TPU v7x, 128 devices: a whole 4x4x4 slice. The times are simulated.
128 devices in a mesh: gx: 8 (over z, x_lo), yt: 16 (over x_hi, y, core).
Axes of the slice: x: 4 (x_hi: 2, x_lo: 2; x = x_hi * 2 + x_lo), y: 4, z: 4, core: 2. Of those that a mesh axis runs over, the one named last changes fastest.
Arguments:
- voltage_old: float32 [4, 4096, 2048], P(None, 'gx', 'yt'), may hold values from -6 to 6
- storage: float32 [4, 4096, 2048], P(None, 'gx', 'yt'), may hold values from 0.5 to 4
- cond_x: float32 [4, 4096, 2048], P(None, 'gx', 'yt'), may hold values from 0.5 to 2
- cond_y: float32 [4, 4096, 2048], P(None, 'gx', 'yt'), may hold values from 0.5 to 2
- cond_via: float32 [3, 4096, 2048], P(None, 'gx', 'yt'), may hold values from 0.5 to 2
- bond_mask: int32 [4096, 2048], P('gx', 'yt'), may hold values from 0 to 1, as said below
- current_blocks: float32 [16384, 8, 128], P(('gx', 'yt')), may hold values from -6 to 6
- block_owner: int32 [16384, 1], P(('gx', 'yt')), may hold values from 0 to 127; in each aligned block of 128 rows (0 to 127, 128 to 255, ...) at most 2 rows name the same one
- block_slot: int32 [16384], P(('gx', 'yt')), may hold values from 0 to 63
Outputs:
- voltage_new: float32 [4, 4096, 2048], P(None, 'gx', 'yt')
- block_voltage: float32 [16384, 8, 128], P(('gx', 'yt'))
Inputs may be any that keep to these rules, and one draw needn't show every extreme that they name: `block_owner`: among the 128 blocks of one device no owner is named more than 2 times; owner o is the tile at x index o // 16 and tier-y index o % 16. bond_mask(i, j) equals bond_mask(i, (j + 1024) mod 2048).
All inputs are finite; a program needn't handle non-finite values.
Results may differ from a plain program's by a relative error of at most 0.00011.
Values sent between devices are 32-bit elements; how exact they have to be, the bound alone decides.
No kernel may reach another device: no remote copies, remote signals or barrier semaphores. Data moves between devices by JAX's collectives and lax.ppermute only.
A program may use at most 128 MiB of HBM per device.

v0:
```python
import jax
import jax.numpy as jnp
from jax import lax
from jax.sharding import PartitionSpec as P

SWEEPS = 3
CAP = 2


bond_conductance = 2.0
cheb_center = 1.0
cheb_halfwidth = 0.97


def from_partner(value, axis, stride):
    mask = 2**stride
    pairs = [(source, source ^ mask) for source in range(lax.axis_size(axis))]
    return lax.ppermute(value, axis, pairs)


def with_halo(block, sides, width):
    for axis, dim in sides:
        count = lax.axis_size(axis)
        forward = [(i, i + 1) for i in range(count - 1)]
        forward.append((count - 1, 0))
        backward = [(target, source) for source, target in forward]
        low = lax.ppermute(
            lax.slice_in_dim(block, block.shape[dim] - width, None, axis=dim), axis, forward
        )
        high = lax.ppermute(lax.slice_in_dim(block, 0, width, axis=dim), axis, backward)
        block = jnp.concatenate([low, block, high], axis=dim)
    return block


def facing(layer_top):
    top_bit = lax.axis_size("yt").bit_length() - 2
    return from_partner(layer_top, "yt", top_bit)


def off_diagonal(field_in, link_arrays, cond_via, bond_weight):
    down_x, up_x, down_y, up_y = link_arrays
    padded = with_halo(field_in, (("gx", 1), ("yt", 2)), 1)
    summed = down_x * padded[:, :-2, 1:-1] + up_x * padded[:, 2:, 1:-1]
    summed = summed + down_y * padded[:, 1:-1, :-2] + up_y * padded[:, 1:-1, 2:]
    zero_layer = jnp.zeros_like(field_in[:1])
    summed = (
        summed
        + jnp.concatenate([cond_via * field_in[1:], zero_layer], 0)
        + jnp.concatenate([zero_layer, cond_via * field_in[:-1]], 0)
    )
    partner = facing(field_in[-1])
    return summed.at[-1].add(bond_weight * partner)


def to_owners(values, labels):
    return (
        lax.all_to_all(values, ("gx", "yt"), split_axis=0, concat_axis=0, tiled=True),
        lax.all_to_all(labels, ("gx", "yt"), split_axis=0, concat_axis=0, tiled=True),
    )


def from_owners(values):
    return lax.all_to_all(values, ("gx", "yt"), split_axis=0, concat_axis=0, tiled=True)


def on_device(
    voltage_old,
    storage,
    cond_x,
    cond_y,
    cond_via,
    bond_mask,
    current_blocks,
    block_owner,
    block_slot,
):
    layers, rows_x, cols_y = voltage_old.shape
    count_gx = lax.axis_size("gx")
    count_yt = lax.axis_size("yt")
    total_x = rows_x * count_gx
    total_y = cols_y * count_yt
    half_y = total_y // 2
    seam = cols_y // 2
    x_global = lax.axis_index("gx") * rows_x + jnp.arange(rows_x)
    y_global = lax.axis_index("yt") * cols_y + jnp.arange(cols_y)
    y_next = (y_global + 1) % total_y
    keep_down_x = (x_global > 0).astype(jnp.float32)[:, None]
    keep_up_x = (x_global < total_x - 1).astype(jnp.float32)[:, None]
    keep_down_y = ((y_global != seam) & (y_global != seam + half_y)).astype(jnp.float32)[None, :]
    keep_up_y = ((y_next != seam) & (y_next != seam + half_y)).astype(jnp.float32)[None, :]
    coeff_stack = jnp.concatenate([cond_x, cond_y], 0)
    coeff_rims = with_halo(coeff_stack, (("gx", 1), ("yt", 2)), 1)
    rim_x = coeff_rims[:layers]
    rim_y = coeff_rims[layers:]
    down_x = 0.5 * (cond_x + rim_x[:, :-2, 1:-1]) * keep_down_x
    up_x = 0.5 * (cond_x + rim_x[:, 2:, 1:-1]) * keep_up_x
    down_y = 0.5 * (cond_y + rim_y[:, 1:-1, :-2]) * keep_down_y
    up_y = 0.5 * (cond_y + rim_y[:, 1:-1, 2:]) * keep_up_y
    link_arrays = (down_x, up_x, down_y, up_y)
    bond_weight = bond_conductance * bond_mask.astype(jnp.float32)
    zero_layer = jnp.zeros_like(cond_via[:1])
    diagonal = storage + (down_x + up_x + down_y + up_y)
    diagonal = (
        diagonal
        + jnp.concatenate([cond_via, zero_layer], 0)
        + jnp.concatenate([zero_layer, cond_via], 0)
    )
    diagonal = diagonal.at[-1].add(bond_weight)
    owners = block_owner[:, 0]
    position = jnp.arange(owners.shape[0])
    earlier = (owners[:, None] == owners[None, :]) & (position[None, :] < position[:, None])
    rank_in_owner = jnp.sum(earlier.astype(jnp.int32), axis=1)
    destination = owners * CAP + rank_in_owner
    devices = count_gx * count_yt
    outgoing = (
        jnp.zeros((devices * CAP,) + current_blocks.shape[1:], jnp.float32)
        .at[destination]
        .set(current_blocks)
    )
    labels = jnp.full((devices * CAP,), -1, jnp.int32).at[destination].set(block_slot)
    arrived, arrived_labels = to_owners(outgoing, labels)
    block_rows = current_blocks.shape[1]
    strip_count = rows_x // block_rows
    one_hot = (arrived_labels[None, :] == jnp.arange(strip_count)[:, None]).astype(jnp.float32)
    strips = jnp.dot(one_hot, arrived.reshape(devices * CAP, -1), precision=lax.Precision.HIGHEST)
    current_map = strips.reshape(rows_x, cols_y)
    right_side = (storage * voltage_old).at[0].add(current_map)

    def apply_operator(field_in):
        return diagonal * field_in - off_diagonal(field_in, link_arrays, cond_via, bond_weight)

    field_now = voltage_old
    residual = right_side - apply_operator(field_now)
    sigma_ratio = cheb_center / cheb_halfwidth
    rho_now = 1.0 / sigma_ratio
    direction = residual / (cheb_center * diagonal)
    for sweep_index in range(SWEEPS):
        field_now = field_now + direction
        residual = residual - apply_operator(direction)
        rho_next = 1.0 / (2.0 * sigma_ratio - rho_now)
        direction = (
            rho_next * rho_now * direction + 2.0 * rho_next / cheb_halfwidth * residual / diagonal
        )
        rho_now = rho_next
    field_now = field_now + direction
    layer_strips = field_now[0].reshape(strip_count, -1)
    occupied = (arrived_labels >= 0).astype(jnp.float32)
    picked = jnp.take(layer_strips, jnp.maximum(arrived_labels, 0), axis=0) * occupied[:, None]
    returned = from_owners(picked.reshape(arrived.shape))
    block_voltage = returned[destination]
    return (field_now, block_voltage)


def solution(mesh):
    in_specs = (
        P(None, "gx", "yt"),
        P(None, "gx", "yt"),
        P(None, "gx", "yt"),
        P(None, "gx", "yt"),
        P(None, "gx", "yt"),
        P("gx", "yt"),
        P(("gx", "yt"), None, None),
        P(("gx", "yt"), None),
        P(("gx", "yt")),
    )
    out_specs = (P(None, "gx", "yt"), P(("gx", "yt"), None, None))
    return jax.shard_map(
        on_device, mesh=mesh, in_specs=in_specs, out_specs=out_specs, check_vma=False
    )
```

profile of v0, /device:TPU:1, one launch (start us, length us, event | category | flops | bytes accessed | tf_op | source)
XLA Modules:
  0.0 226.9 jit_solution(17310934968353888500)
XLA Ops:
  3.6 2.1 collective-permute-start
  5.7 3.6 %collective-permute-start.1 = (f32[8,1,128]{2,1,0:T(1,128)S(1)}, f32[8,1,128]{2,1,0:T(1,128)S(1)}, u32[]{:S(2)}, u32[]{:S(2)}) collective-permute-start(f32[8,1,128]{2,1,0:T(1,128)S(1)} %get-tuple-element.90), channel_id=1, source_target_pairs={{16,0},{32,16},{48,32},{64,48},{80,64},{96,80},{112,96},{0,112},{1... | collective-permute-start | bytes 12296 | tf_op jit(solution)/shard_map/ppermute | solution.py:30
  9.4 3.6 %collective-permute-start.5 = (f32[4,1,128]{2,1,0:T(1,128)S(1)}, f32[4,1,128]{2,1,0:T(1,128)S(1)}, u32[]{:S(2)}, u32[]{:S(2)}) collective-permute-start(f32[4,1,128]{2,1,0:T(1,128)S(1)} %get-tuple-element.116), channel_id=1, source_target_pairs={{16,0},{32,16},{48,32},{64,48},{80,64},{96,80},{112,96},{0,112},{1... | collective-permute-start | bytes 6152 | tf_op jit(solution)/shard_map/ppermute | solution.py:30
  15.0 8.2 %all-to-all-start = ((s32[128,2,1]{1,2,0:T(1,128)}), s32[128,2,1]{1,2,0:T(1,128)S(1)}, u32[]{:S(2)}, u32[]{:S(2)}) async-start(s32[128,2,1]{1,2,0:T(1,128)} %bitcast.3), calls=%async_computation | async-start | bytes 131072 | tf_op jit(solution)/shard_map/all_to_all | solution.py:58
  23.2 3.0 %collective-permute-start.8 = (f32[512,128]{1,0:T(8,128)S(1)}, f32[512,128]{1,0:T(8,128)}, u32[]{:S(2)}, u32[]{:S(2)}) collective-permute-start(f32[512,128]{1,0:T(8,128)S(1)} %slice_bitcast_fusion.3), channel_id=1, source_target_pairs={{0,8},{1,9},{2,10},{3,11},{4,12},{5,13},{6,14},{7,15},{8,0},{9,1},... | collective-permute-start | bytes 786440 | tf_op jit(solution)/shard_map/ppermute | solution.py:18
  28.7 12.4 %scatter_fusion = f32[256,8,128]{2,1,0:T(8,128)} fusion(f32[256,8,128]{2,1,0:T(8,128)} %broadcast_in_dim.15, s32[128]{0:T(128)S(1)} %fusion.62, f32[128,8,128]{2,1,0:T(8,128)S(1)} %copy-done.22), kind=kCustom, calls=%fused_computation.3 | custom fusion | bytes 1573376 | tf_op jit(solution)/shard_map/scatter | solution.py:118
  41.1 8.5 %all-to-all-start.1 = ((f32[256,8,128]{2,1,0:T(8,128)}), f32[256,8,128]{2,1,0:T(8,128)}, u32[]{:S(2)}, u32[]{:S(2)}) async-start(f32[256,8,128]{2,1,0:T(8,128)} %scatter_fusion), calls=%async_computation.1 | async-start | bytes 2097152 | tf_op jit(solution)/shard_map/all_to_all | solution.py:57
  59.9 2.7 %fusion.69 = (f32[8,514,1]{2,1,0:T(8,128)}, f32[8,514,1]{2,1,0:T(8,128)}) fusion(f32[8,514,128]{2,1,0:T(8,128)S(1)} %pad_maximum_fusion), kind=kLoop, calls=%fused_computation.160 | loop fusion | bytes 65792 | tf_op jit(solution)/shard_map/slice | solution.py:30
  62.6 2.4 %copy.162 = f32[8,514,1]{1,0,2:T(8,128)S(1)} copy(f32[8,514,1]{2,1,0:T(8,128)} %get-tuple-element.88) | data formatting | bytes 32896 | tf_op jit(solution)/shard_map/slice | solution.py:28
  66.7 2.4 %copy.164 = f32[8,514,1]{1,0,2:T(8,128)S(1)} copy(f32[8,514,1]{2,1,0:T(8,128)} %get-tuple-element.87) | data formatting | bytes 32896 | tf_op jit(solution)/shard_map/slice | solution.py:30
  69.1 3.4 %collective-permute-start.3 = (f32[8,514,1]{1,0,2:T(8,128)S(1)}, f32[8,514,1]{1,0,2:T(8,128)S(1)}, u32[]{:S(2)}, u32[]{:S(2)}) collective-permute-start(f32[8,514,1]{1,0,2:T(8,128)S(1)} %copy.164), channel_id=1, source_target_pairs={{1,0},{2,1},{3,2},{4,3},{5,4},{6,5},{7,6},{8,7},{9,8},{10,9},{11,1... | collective-permute-start | bytes 49352 | tf_op jit(solution)/shard_map/ppermute | solution.py:30
  75.3 2.0 copy.163
  77.3 2.0 copy.165
  79.4 6.7 %fusion.34 = (f32[4,512,128]{2,1,0:T(8,128)}, f32[4,512,128]{2,1,0:T(8,128)S(1)}, f32[4,512,128]{2,1,0:T(8,128)S(1)}, f32[4,512,128]{2,1,0:T(8,128)S(1)}, f32[4,512,128]{2,1,0:T(8,128)S(1)}) fusion(f32[4,514,1]{2,1,0:T(8,128)} %copy.169, f32[4,1,128]{2,1,0:T(1,128)S(1)} %collective-permute-done.5, f32[4,512,128]{2,1,0:T(8,128)S(1)} %copy-done, ...), kind=kLoop, calls=%fused_computation.69 | loop fusion | flops 8650752 | bytes 12125376 | tf_op jit(solution)/shard_map/add | solution.py:47
  88.4 1.9 fusion.52
  90.2 1.8 fusion.1
  95.6 3.5 %collective-permute-start.10 = (f32[4,1,128]{2,1,0:T(1,128)S(1)}, f32[4,1,128]{2,1,0:T(1,128)S(1)}, u32[]{:S(2)}, u32[]{:S(2)}) collective-permute-start(f32[4,1,128]{2,1,0:T(1,128)S(1)} %get-tuple-element.112), channel_id=1, source_target_pairs={{16,0},{32,16},{48,32},{64,48},{80,64},{96,80},{112,96},{0,112},{1... | collective-permute-start | bytes 6152 | tf_op jit(solution)/shard_map/ppermute | solution.py:30
  100.4 3.2 %collective-permute-done.9 = f32[4,1,128]{2,1,0:T(1,128)S(1)} collective-permute-done((f32[4,1,128]{2,1,0:T(1,128)S(1)}, f32[4,1,128]{2,1,0:T(1,128)S(1)}, u32[]{:S(2)}, u32[]{:S(2)}) %collective-permute-start.9) | collective-permute-done | bytes 2080 | tf_op jit(solution)/shard_map/ppermute | solution.py:27
  109.3 6.1 %collective-permute-start.12 = (f32[4,514,1]{1,0,2:T(4,128)S(1)}, f32[4,514,1]{1,0,2:T(4,128)S(1)}, u32[]{:S(2)}, u32[]{:S(2)}) collective-permute-start(f32[4,514,1]{1,0,2:T(4,128)S(1)} %copy.172), channel_id=1, source_target_pairs={{1,0},{2,1},{3,2},{4,3},{5,4},{6,5},{7,6},{8,7},{9,8},{10,9},{11,1... | collective-permute-start | bytes 24680 | tf_op jit(solution)/shard_map/ppermute | solution.py:30
  116.2 2.4 %collective-permute-start.13 = (f32[512,128]{1,0:T(8,128)}, f32[512,128]{1,0:T(8,128)}, u32[]{:S(2)}, u32[]{:S(2)}) collective-permute-start(f32[512,128]{1,0:T(8,128)} %slice_bitcast_fusion.2), channel_id=1, source_target_pairs={{0,8},{1,9},{2,10},{3,11},{4,12},{5,13},{6,14},{7,15},{8,0},{9,1},... | collective-permute-start | bytes 786440 | tf_op jit(solution)/shard_map/ppermute | solution.py:18
  121.4 4.2 %fusion.25 = f32[4,512,128]{2,1,0:T(8,128)S(1)} fusion(f32[4,512,128]{2,1,0:T(8,128)} %copy-done.4, f32[4,514,1]{2,1,0:T(8,128)} %copy.173, f32[4,1,128]{2,1,0:T(1,128)S(1)} %collective-permute-done.10, f32[4,512,128]{2,1,0:T(8,128)S(1)} %fusion.48, f32[4,1,128]{2,1,0:T(1,128)S(1)} %collective-permute-done.9, f32[4,512,128]{2,1,0:T(8,128)} %copy-done.3, ...), kind=kLoop, calls=%fused_computation.52 | loop fusion | flops 4456448 | bytes 7884864 | tf_op jit(solution)/shard_map/add | solution.py:47
  126.9 2.7 %divide_add_fusion.1 = (f32[4,512,128]{2,1,0:T(8,128)S(1)}, f32[4,512,128]{2,1,0:T(8,128)}) fusion(f32[4,512,128]{2,1,0:T(8,128)S(1)} %get-tuple-element.118, f32[4,512,128]{2,1,0:T(8,128)S(1)} %fusion.48, f32[4,512,128]{2,1,0:T(8,128)S(1)} %fusion.51, f32[4,512,128]{2,1,0:T(8,128)S(1)} %copy-done.14, f32[4,512,128]{2,1,0:T(8,128)} %get-tuple-element.117, ...), kind=kLoop, calls=%fused_computation.101 | loop fusion | flops 2621440 | bytes 8388608 | tf_op jit(solution)/shard_map/add | solution.py:142
  129.7 3.6 %collective-permute-start.15 = (f32[4,1,128]{2,1,0:T(1,128)S(1)}, f32[4,1,128]{2,1,0:T(1,128)S(1)}, u32[]{:S(2)}, u32[]{:S(2)}) collective-permute-start(f32[4,1,128]{2,1,0:T(1,128)S(1)} %get-tuple-element.110), channel_id=1, source_target_pairs={{16,0},{32,16},{48,32},{64,48},{80,64},{96,80},{112,96},{0,112},{1... | collective-permute-start | bytes 6152 | tf_op jit(solution)/shard_map/ppermute | solution.py:30
  139.7 6.4 %collective-permute-start.17 = (f32[4,514,1]{1,0,2:T(4,128)S(1)}, f32[4,514,1]{1,0,2:T(4,128)S(1)}, u32[]{:S(2)}, u32[]{:S(2)}) collective-permute-start(f32[4,514,1]{1,0,2:T(4,128)S(1)} %copy.176), channel_id=1, source_target_pairs={{1,0},{2,1},{3,2},{4,3},{5,4},{6,5},{7,6},{8,7},{9,8},{10,9},{11,1... | collective-permute-start | bytes 24680 | tf_op jit(solution)/shard_map/ppermute | solution.py:30
  151.3 5.5 %fusion.16 = f32[4,512,128]{2,1,0:T(8,128)S(1)} fusion(f32[4,512,128]{2,1,0:T(8,128)} %copy-done.4, f32[4,514,1]{2,1,0:T(8,128)} %copy.177, f32[4,1,128]{2,1,0:T(1,128)S(1)} %collective-permute-done.15, f32[4,512,128]{2,1,0:T(8,128)} %copy-done.6, f32[4,1,128]{2,1,0:T(1,128)S(1)} %collective-permute-done.14, f32[4,512,128]{2,1,0:T(8,128)} %copy-done.3, ...), kind=kLoop, calls=%fused_computation.35 | loop fusion | flops 4456448 | bytes 7884864 | tf_op jit(solution)/shard_map/add | solution.py:47
  159.1 3.6 %collective-permute-start.20 = (f32[4,1,128]{2,1,0:T(1,128)S(1)}, f32[4,1,128]{2,1,0:T(1,128)S(1)}, u32[]{:S(2)}, u32[]{:S(2)}) collective-permute-start(f32[4,1,128]{2,1,0:T(1,128)S(1)} %get-tuple-element.108), channel_id=1, source_target_pairs={{16,0},{32,16},{48,32},{64,48},{80,64},{96,80},{112,96},{0,112},{1... | collective-permute-start | bytes 6152 | tf_op jit(solution)/shard_map/ppermute | solution.py:30
  169.0 6.5 %collective-permute-start.22 = (f32[4,514,1]{1,0,2:T(4,128)S(1)}, f32[4,514,1]{1,0,2:T(4,128)S(1)}, u32[]{:S(2)}, u32[]{:S(2)}) collective-permute-start(f32[4,514,1]{1,0,2:T(4,128)S(1)} %copy.180), channel_id=1, source_target_pairs={{1,0},{2,1},{3,2},{4,3},{5,4},{6,5},{7,6},{8,7},{9,8},{10,9},{11,1... | collective-permute-start | bytes 24680 | tf_op jit(solution)/shard_map/ppermute | solution.py:30
  177.2 2.9 %collective-permute-start.23 = (f32[512,128]{1,0:T(8,128)}, f32[512,128]{1,0:T(8,128)}, u32[]{:S(2)}, u32[]{:S(2)}) collective-permute-start(f32[512,128]{1,0:T(8,128)} %slice_bitcast_fusion), channel_id=1, source_target_pairs={{0,8},{1,9},{2,10},{3,11},{4,12},{5,13},{6,14},{7,15},{8,0},{9,1},... | collective-permute-start | bytes 786440 | tf_op jit(solution)/shard_map/ppermute | solution.py:18
  182.8 6.1 %fusion.7 = f32[4,512,128]{2,1,0:T(8,128)S(1)} fusion(f32[4,512,128]{2,1,0:T(8,128)} %copy-done.4, f32[4,514,1]{2,1,0:T(8,128)} %copy.181, f32[4,1,128]{2,1,0:T(1,128)S(1)} %collective-permute-done.20, f32[4,512,128]{2,1,0:T(8,128)} %copy-done.5, f32[4,1,128]{2,1,0:T(1,128)S(1)} %collective-permute-done.19, f32[4,512,128]{2,1,0:T(8,128)} %copy-done.3, ...), kind=kLoop, calls=%fused_computation.18 | loop fusion | flops 4456448 | bytes 7884864 | tf_op jit(solution)/shard_map/add | solution.py:47
  193.5 2.4 %fusion = f32[256,8,128]{2,1,0:T(8,128)} fusion(f32[32,8,8,128]{3,2,1,0:T(8,128)S(1)} %copy.183, f32[256]{0:T(256)S(1)} %get-tuple-element.120, pred[256]{0:T(512)(128)(4,1)S(1)} %get-tuple-element.119), kind=kLoop, calls=%fused_computation.10 | loop fusion | flops 524288 | bytes 2098432 | tf_op jit(solution)/shard_map/mul | solution.py:148
  195.9 10.4 %all-to-all-start.2 = ((f32[256,8,128]{2,1,0:T(8,128)}), f32[256,8,128]{2,1,0:T(8,128)S(1)}, u32[]{:S(2)}, u32[]{:S(2)}) async-start(f32[256,8,128]{2,1,0:T(8,128)} %fusion), calls=%async_computation.2 | async-start | bytes 2097152 | tf_op jit(solution)/shard_map/all_to_all | solution.py:63
  206.4 19.0 %all-to-all-done.2 = f32[256,8,128]{2,1,0:T(8,128)S(1)} async-done(((f32[256,8,128]{2,1,0:T(8,128)}), f32[256,8,128]{2,1,0:T(8,128)S(1)}, u32[]{:S(2)}, u32[]{:S(2)}) %all-to-all-start.2) | async-done | bytes 1048608 | tf_op jit(solution)/shard_map/all_to_all | solution.py:63
  (152 shorter events, 70.9 us)
Async XLA Ops:
  2.2 7.1 %copy-start = (f32[4,512,128]{2,1,0:T(8,128)S(1)}, f32[4,512,128]{2,1,0:T(8,128)}, u32[]{:S(2)}) copy-start(f32[4,512,128]{2,1,0:T(8,128)} %param.21) | copy-start | bytes 3145732
  2.2 10.8 %copy-start.23 = (s32[128,1]{0,1:T(1,128)S(1)}, s32[128,1]{0,1:T(1,128)}, u32[]{:S(2)}) copy-start(s32[128,1]{0,1:T(1,128)} %param.28) | copy-start | bytes 1540
  2.2 24.0 %copy-start.7 = (f32[3,512,128]{2,1,0:T(8,128)S(1)}, f32[3,512,128]{2,1,0:T(8,128)}, u32[]{:S(2)}) copy-start(f32[3,512,128]{2,1,0:T(8,128)} %param.25) | copy-start | bytes 2359300
  3.6 54.5 %collective-permute-start = (f32[8,1,128]{2,1,0:T(1,128)S(1)}, f32[8,1,128]{2,1,0:T(1,128)S(1)}, u32[]{:S(2)}, u32[]{:S(2)}) collective-permute-start(f32[8,1,128]{2,1,0:T(1,128)S(1)} %get-tuple-element.89), channel_id=1, source_target_pairs={{0,16},{16,32},{32,48},{48,64},{64,80},{80,96},{96,112},{112,0},{1... | collective-permute-start | bytes 12296 | tf_op jit(solution)/shard_map/ppermute | solution.py:27
  5.7 52.4 %collective-permute-start.1 = (f32[8,1,128]{2,1,0:T(1,128)S(1)}, f32[8,1,128]{2,1,0:T(1,128)S(1)}, u32[]{:S(2)}, u32[]{:S(2)}) collective-permute-start(f32[8,1,128]{2,1,0:T(1,128)S(1)} %get-tuple-element.90), channel_id=1, source_target_pairs={{16,0},{32,16},{48,32},{64,48},{80,64},{96,80},{112,96},{0,112},{1... | collective-permute-start | bytes 12296 | tf_op jit(solution)/shard_map/ppermute | solution.py:30
  9.3 42.1 %collective-permute-start.4 = (f32[4,1,128]{2,1,0:T(1,128)S(1)}, f32[4,1,128]{2,1,0:T(1,128)S(1)}, u32[]{:S(2)}, u32[]{:S(2)}) collective-permute-start(f32[4,1,128]{2,1,0:T(1,128)S(1)} %get-tuple-element.115), channel_id=1, source_target_pairs={{0,16},{16,32},{32,48},{48,64},{64,80},{80,96},{96,112},{112,0},{1... | collective-permute-start | bytes 6152 | tf_op jit(solution)/shard_map/ppermute | solution.py:27
  9.4 42.0 %collective-permute-start.5 = (f32[4,1,128]{2,1,0:T(1,128)S(1)}, f32[4,1,128]{2,1,0:T(1,128)S(1)}, u32[]{:S(2)}, u32[]{:S(2)}) collective-permute-start(f32[4,1,128]{2,1,0:T(1,128)S(1)} %get-tuple-element.116), channel_id=1, source_target_pairs={{16,0},{32,16},{48,32},{64,48},{80,64},{96,80},{112,96},{0,112},{1... | collective-permute-start | bytes 6152 | tf_op jit(solution)/shard_map/ppermute | solution.py:30
  15.0 26.0 %all-to-all-start = ((s32[128,2,1]{1,2,0:T(1,128)}), s32[128,2,1]{1,2,0:T(1,128)S(1)}, u32[]{:S(2)}, u32[]{:S(2)}) async-start(s32[128,2,1]{1,2,0:T(1,128)} %bitcast.3), calls=%async_computation | async-start | bytes 131072 | tf_op jit(solution)/shard_map/all_to_all | solution.py:58
  23.2 65.1 %collective-permute-start.8 = (f32[512,128]{1,0:T(8,128)S(1)}, f32[512,128]{1,0:T(8,128)}, u32[]{:S(2)}, u32[]{:S(2)}) collective-permute-start(f32[512,128]{1,0:T(8,128)S(1)} %slice_bitcast_fusion.3), channel_id=1, source_target_pairs={{0,8},{1,9},{2,10},{3,11},{4,12},{5,13},{6,14},{7,15},{8,0},{9,1},... | collective-permute-start | bytes 786440 | tf_op jit(solution)/shard_map/ppermute | solution.py:18
  41.1 49.2 %all-to-all-start.1 = ((f32[256,8,128]{2,1,0:T(8,128)}), f32[256,8,128]{2,1,0:T(8,128)}, u32[]{:S(2)}, u32[]{:S(2)}) async-start(f32[256,8,128]{2,1,0:T(8,128)} %scatter_fusion), calls=%async_computation.1 | async-start | bytes 2097152 | tf_op jit(solution)/shard_map/all_to_all | solution.py:57
  54.8 17.7 %collective-permute-start.6 = (f32[4,514,1]{1,0,2:T(4,128)S(1)}, f32[4,514,1]{1,0,2:T(4,128)S(1)}, u32[]{:S(2)}, u32[]{:S(2)}) collective-permute-start(f32[4,514,1]{1,0,2:T(4,128)S(1)} %copy.166), channel_id=1, source_target_pairs={{0,1},{1,2},{2,3},{3,4},{4,5},{5,6},{6,7},{7,8},{8,9},{9,10},{10,1... | collective-permute-start | bytes 24680 | tf_op jit(solution)/shard_map/ppermute | solution.py:27
  58.1 15.8 %collective-permute-start.7 = (f32[4,514,1]{1,0,2:T(4,128)S(1)}, f32[4,514,1]{1,0,2:T(4,128)S(1)}, u32[]{:S(2)}, u32[]{:S(2)}) collective-permute-start(f32[4,514,1]{1,0,2:T(4,128)S(1)} %copy.168), channel_id=1, source_target_pairs={{1,0},{2,1},{3,2},{4,3},{5,4},{6,5},{7,6},{8,7},{9,8},{10,9},{11,1... | collective-permute-start | bytes 24680 | tf_op jit(solution)/shard_map/ppermute | solution.py:30
  65.0 10.3 %collective-permute-start.2 = (f32[8,514,1]{1,0,2:T(8,128)S(1)}, f32[8,514,1]{1,0,2:T(8,128)S(1)}, u32[]{:S(2)}, u32[]{:S(2)}) collective-permute-start(f32[8,514,1]{1,0,2:T(8,128)S(1)} %copy.162), channel_id=1, source_target_pairs={{0,1},{1,2},{2,3},{3,4},{4,5},{5,6},{6,7},{7,8},{8,9},{9,10},{10,1... | collective-permute-start | bytes 49352 | tf_op jit(solution)/shard_map/ppermute | solution.py:27
  69.1 8.2 %collective-permute-start.3 = (f32[8,514,1]{1,0,2:T(8,128)S(1)}, f32[8,514,1]{1,0,2:T(8,128)S(1)}, u32[]{:S(2)}, u32[]{:S(2)}) collective-permute-start(f32[8,514,1]{1,0,2:T(8,128)S(1)} %copy.164), channel_id=1, source_target_pairs={{1,0},{2,1},{3,2},{4,3},{5,4},{6,5},{7,6},{8,7},{9,8},{10,9},{11,1... | collective-permute-start | bytes 49352 | tf_op jit(solution)/shard_map/ppermute | solution.py:30
  79.4 6.7 %copy-start.21 = (f32[4,512,128]{2,1,0:T(8,128)S(1)}, f32[4,512,128]{2,1,0:T(8,128)}, u32[]{:S(2)}) copy-start(f32[4,512,128]{2,1,0:T(8,128)} %param.22) | copy-start | bytes 3145732
  95.6 4.8 %collective-permute-start.10 = (f32[4,1,128]{2,1,0:T(1,128)S(1)}, f32[4,1,128]{2,1,0:T(1,128)S(1)}, u32[]{:S(2)}, u32[]{:S(2)}) collective-permute-start(f32[4,1,128]{2,1,0:T(1,128)S(1)} %get-tuple-element.112), channel_id=1, source_target_pairs={{16,0},{32,16},{48,32},{64,48},{80,64},{96,80},{112,96},{0,112},{1... | collective-permute-start | bytes 6152 | tf_op jit(solution)/shard_map/ppermute | solution.py:30
  99.1 4.5 %collective-permute-start.9 = (f32[4,1,128]{2,1,0:T(1,128)S(1)}, f32[4,1,128]{2,1,0:T(1,128)S(1)}, u32[]{:S(2)}, u32[]{:S(2)}) collective-permute-start(f32[4,1,128]{2,1,0:T(1,128)S(1)} %get-tuple-element.111), channel_id=1, source_target_pairs={{0,16},{16,32},{32,48},{48,64},{64,80},{80,96},{96,112},{112,0},{1... | collective-permute-start | bytes 6152 | tf_op jit(solution)/shard_map/ppermute | solution.py:27
  107.0 11.6 %collective-permute-start.11 = (f32[4,514,1]{1,0,2:T(4,128)S(1)}, f32[4,514,1]{1,0,2:T(4,128)S(1)}, u32[]{:S(2)}, u32[]{:S(2)}) collective-permute-start(f32[4,514,1]{1,0,2:T(4,128)S(1)} %copy.170), channel_id=1, source_target_pairs={{0,1},{1,2},{2,3},{3,4},{4,5},{5,6},{6,7},{7,8},{8,9},{9,10},{10,1... | collective-permute-start | bytes 24680 | tf_op jit(solution)/shard_map/ppermute | solution.py:27
  109.3 10.7 %collective-permute-start.12 = (f32[4,514,1]{1,0,2:T(4,128)S(1)}, f32[4,514,1]{1,0,2:T(4,128)S(1)}, u32[]{:S(2)}, u32[]{:S(2)}) collective-permute-start(f32[4,514,1]{1,0,2:T(4,128)S(1)} %copy.172), channel_id=1, source_target_pairs={{1,0},{2,1},{3,2},{4,3},{5,4},{6,5},{7,6},{8,7},{9,8},{10,9},{11,1... | collective-permute-start | bytes 24680 | tf_op jit(solution)/shard_map/ppermute | solution.py:30
  116.2 9.4 %collective-permute-start.13 = (f32[512,128]{1,0:T(8,128)}, f32[512,128]{1,0:T(8,128)}, u32[]{:S(2)}, u32[]{:S(2)}) collective-permute-start(f32[512,128]{1,0:T(8,128)} %slice_bitcast_fusion.2), channel_id=1, source_target_pairs={{0,8},{1,9},{2,10},{3,11},{4,12},{5,13},{6,14},{7,15},{8,0},{9,1},... | collective-permute-start | bytes 786440 | tf_op jit(solution)/shard_map/ppermute | solution.py:18
  129.6 5.0 %collective-permute-start.14 = (f32[4,1,128]{2,1,0:T(1,128)S(1)}, f32[4,1,128]{2,1,0:T(1,128)S(1)}, u32[]{:S(2)}, u32[]{:S(2)}) collective-permute-start(f32[4,1,128]{2,1,0:T(1,128)S(1)} %get-tuple-element.109), channel_id=1, source_target_pairs={{0,16},{16,32},{32,48},{48,64},{64,80},{80,96},{96,112},{112,0},{1... | collective-permute-start | bytes 6152 | tf_op jit(solution)/shard_map/ppermute | solution.py:27
  129.7 4.9 %collective-permute-start.15 = (f32[4,1,128]{2,1,0:T(1,128)S(1)}, f32[4,1,128]{2,1,0:T(1,128)S(1)}, u32[]{:S(2)}, u32[]{:S(2)}) collective-permute-start(f32[4,1,128]{2,1,0:T(1,128)S(1)} %get-tuple-element.110), channel_id=1, source_target_pairs={{16,0},{32,16},{48,32},{64,48},{80,64},{96,80},{112,96},{0,112},{1... | collective-permute-start | bytes 6152 | tf_op jit(solution)/shard_map/ppermute | solution.py:30
  138.1 10.5 %collective-permute-start.16 = (f32[4,514,1]{1,0,2:T(4,128)S(1)}, f32[4,514,1]{1,0,2:T(4,128)S(1)}, u32[]{:S(2)}, u32[]{:S(2)}) collective-permute-start(f32[4,514,1]{1,0,2:T(4,128)S(1)} %copy.174), channel_id=1, source_target_pairs={{0,1},{1,2},{2,3},{3,4},{4,5},{5,6},{6,7},{7,8},{8,9},{9,10},{10,1... | collective-permute-start | bytes 24680 | tf_op jit(solution)/shard_map/ppermute | solution.py:27
  139.7 10.2 %collective-permute-start.17 = (f32[4,514,1]{1,0,2:T(4,128)S(1)}, f32[4,514,1]{1,0,2:T(4,128)S(1)}, u32[]{:S(2)}, u32[]{:S(2)}) collective-permute-start(f32[4,514,1]{1,0,2:T(4,128)S(1)} %copy.176), channel_id=1, source_target_pairs={{1,0},{2,1},{3,2},{4,3},{5,4},{6,5},{7,6},{8,7},{9,8},{10,9},{11,1... | collective-permute-start | bytes 24680 | tf_op jit(solution)/shard_map/ppermute | solution.py:30
  147.8 9.0 %collective-permute-start.18 = (f32[512,128]{1,0:T(8,128)}, f32[512,128]{1,0:T(8,128)}, u32[]{:S(2)}, u32[]{:S(2)}) collective-permute-start(f32[512,128]{1,0:T(8,128)} %slice_bitcast_fusion.1), channel_id=1, source_target_pairs={{0,8},{1,9},{2,10},{3,11},{4,12},{5,13},{6,14},{7,15},{8,0},{9,1},... | collective-permute-start | bytes 786440 | tf_op jit(solution)/shard_map/ppermute | solution.py:18
  159.0 4.9 %collective-permute-start.19 = (f32[4,1,128]{2,1,0:T(1,128)S(1)}, f32[4,1,128]{2,1,0:T(1,128)S(1)}, u32[]{:S(2)}, u32[]{:S(2)}) collective-permute-start(f32[4,1,128]{2,1,0:T(1,128)S(1)} %get-tuple-element.107), channel_id=1, source_target_pairs={{0,16},{16,32},{32,48},{48,64},{64,80},{80,96},{96,112},{112,0},{1... | collective-permute-start | bytes 6152 | tf_op jit(solution)/shard_map/ppermute | solution.py:27
  159.1 4.9 %collective-permute-start.20 = (f32[4,1,128]{2,1,0:T(1,128)S(1)}, f32[4,1,128]{2,1,0:T(1,128)S(1)}, u32[]{:S(2)}, u32[]{:S(2)}) collective-permute-start(f32[4,1,128]{2,1,0:T(1,128)S(1)} %get-tuple-element.108), channel_id=1, source_target_pairs={{16,0},{32,16},{48,32},{64,48},{80,64},{96,80},{112,96},{0,112},{1... | collective-permute-start | bytes 6152 | tf_op jit(solution)/shard_map/ppermute | solution.py:30
  167.3 12.7 %collective-permute-start.21 = (f32[4,514,1]{1,0,2:T(4,128)S(1)}, f32[4,514,1]{1,0,2:T(4,128)S(1)}, u32[]{:S(2)}, u32[]{:S(2)}) collective-permute-start(f32[4,514,1]{1,0,2:T(4,128)S(1)} %copy.178), channel_id=1, source_target_pairs={{0,1},{1,2},{2,3},{3,4},{4,5},{5,6},{6,7},{7,8},{8,9},{9,10},{10,1... | collective-permute-start | bytes 24680 | tf_op jit(solution)/shard_map/ppermute | solution.py:27
  169.0 12.4 %collective-permute-start.22 = (f32[4,514,1]{1,0,2:T(4,128)S(1)}, f32[4,514,1]{1,0,2:T(4,128)S(1)}, u32[]{:S(2)}, u32[]{:S(2)}) collective-permute-start(f32[4,514,1]{1,0,2:T(4,128)S(1)} %copy.180), channel_id=1, source_target_pairs={{1,0},{2,1},{3,2},{4,3},{5,4},{6,5},{7,6},{8,7},{9,8},{10,9},{11,1... | collective-permute-start | bytes 24680 | tf_op jit(solution)/shard_map/ppermute | solution.py:30
  177.2 11.8 %collective-permute-start.23 = (f32[512,128]{1,0:T(8,128)}, f32[512,128]{1,0:T(8,128)}, u32[]{:S(2)}, u32[]{:S(2)}) collective-permute-start(f32[512,128]{1,0:T(8,128)} %slice_bitcast_fusion), channel_id=1, source_target_pairs={{0,8},{1,9},{2,10},{3,11},{4,12},{5,13},{6,14},{7,15},{8,0},{9,1},... | collective-permute-start | bytes 786440 | tf_op jit(solution)/shard_map/ppermute | solution.py:18
  182.8 7.3 %copy-start.16 = (f32[4,512,128]{2,1,0:T(8,128)S(1)}, f32[4,512,128]{2,1,0:T(8,128)}, u32[]{:S(2)}) copy-start(f32[4,512,128]{2,1,0:T(8,128)} %get-tuple-element.81) | copy-start | bytes 3145732
  195.9 29.5 %all-to-all-start.2 = ((f32[256,8,128]{2,1,0:T(8,128)}), f32[256,8,128]{2,1,0:T(8,128)S(1)}, u32[]{:S(2)}, u32[]{:S(2)}) async-start(f32[256,8,128]{2,1,0:T(8,128)} %fusion), calls=%async_computation.2 | async-start | bytes 2097152 | tf_op jit(solution)/shard_map/all_to_all | solution.py:63
  (19 other events, 48.2 us)
where the time goes:
time: 228 us; the launch traced here: 227 us
  starting transfers between devices  82.8 us (36%)
  local copies, waits for them, and re-layouts  71 us (31%)
  other arithmetic  48 us (21%)
  waiting for transfers between devices  22.3 us (10%)
    ppermute x10, starting transfers between devices, with_halo(): lax.ppermute(lax.slice_in_dim(block, 0, width, axis=dim), axis, backward)  40.1 us
    add x4, other arithmetic, off_diagonal(): summed + jnp.concatenate([cond_via * field_in[1:], zero_layer], 0)  22.5 us
    all_to_all x1, waiting for transfers between devices, from_owners(): lax.all_to_all(values, ('gx', 'yt'), split_axis=0, concat_axis=0, tiled=T...  19 us
    slice x14, local copies, waits for them, and re-layouts, with_halo(): lax.slice_in_dim(block, block.shape[dim] - width, None, axis=dim)  15.7 us
    scatter x1, local copies, waits for them, and re-layouts, on_device(): outgoing = jnp.zeros((devices * CAP,) + current_blocks.shape[1:], jnp.flo...  12.4 us
    slice x6, local copies, waits for them, and re-layouts, with_halo(): lax.slice_in_dim(block, 0, width, axis=dim)  11.6 us
    all_to_all x1, starting transfers between devices, from_owners(): lax.all_to_all(values, ('gx', 'yt'), split_axis=0, concat_axis=0, tiled=T...  10.4 us
    ppermute x4, starting transfers between devices, from_partner(): return lax.ppermute(value, axis, pairs)  8.97 us
  transfers between devices with their start and end apart: 27, of which 2 were waited for; matrix products, arithmetic and copies ran while one was open for 38% of the time, Pallas kernels for 0%

commit v1 on v0

v1 whole, which is shorter than its diff:
```python
import functools

import jax
import jax.numpy as jnp
from jax import lax
from jax.experimental import pallas as pl
from jax.experimental.pallas import tpu as pltpu
from jax.sharding import PartitionSpec as P

CAP = 2
BOND = 2.0
CENTER = 1.0
HALFWIDTH = 0.97
SIGMA = CENTER / HALFWIDTH
RHO0 = 1.0 / SIGMA
RHO1 = 1.0 / (2.0 * SIGMA - RHO0)
RHO2 = 1.0 / (2.0 * SIGMA - RHO1)
RHO3 = 1.0 / (2.0 * SIGMA - RHO2)
A1, B1 = RHO1 * RHO0, 2.0 * RHO1 / HALFWIDTH
A2, B2 = RHO2 * RHO1, 2.0 * RHO2 / HALFWIDTH
A3, B3 = RHO3 * RHO2, 2.0 * RHO3 / HALFWIDTH

ALL = ("gx", "yt")
F32 = jnp.float32
W = 128
H = 8
PAD = 16
Q = 4
STEP = 16
ROWS_MSG = CAP * 8 + 1


def full(ndim):
    return lambda *_: (0,) * ndim


def call(kernel, out, args, scratch=(), specs=None, out_specs=None, vmem=40, cost=1_000_000):
    specs = specs or {}
    in_specs = [
        specs.get(i, pl.BlockSpec(memory_space=pltpu.VMEM)) for i in range(len(args))
    ]
    many = isinstance(out, (list, tuple))
    outs = list(out) if many else [out]
    o_specs = out_specs or [pl.BlockSpec(memory_space=pltpu.VMEM)] * len(outs)
    return pl.pallas_call(
        kernel,
        out_shape=outs if many else outs[0],
        in_specs=in_specs,
        out_specs=o_specs if many else o_specs[0],
        scratch_shapes=list(scratch),
        compiler_params=pltpu.CompilerParams(vmem_limit_bytes=vmem << 20),
        cost_estimate=pl.CostEstimate(flops=cost, bytes_accessed=cost, transcendentals=0),
    )(*args)


def shape(*dims):
    return jax.ShapeDtypeStruct(dims, F32)


SMEM = pl.BlockSpec(memory_space=pltpu.SMEM)


def from_right(x):
    return pltpu.roll(x, x.shape[-1] - 1, axis=1)


def from_left(x):
    return pltpu.roll(x, 1, axis=1)


def lanes(rows, width=W):
    return lax.broadcasted_iota(jnp.int32, (rows, width), 1)


def each_chunk(first, count, body, step=STEP):
    @pl.loop(0, count)
    def _(k):
        body(pl.multiple_of(first + k * step, 8))


def send_kernel(owner_ref, slot_ref, blocks_ref, out_ref, dest_ref, count_ref, buf, slots):
    devices = count_ref.shape[0]

    @pl.loop(0, devices, unroll=8)
    def _(o):
        count_ref[o] = 0

    buf[...] = jnp.zeros_like(buf)
    slots[...] = jnp.full(slots.shape, 64, jnp.int32)
    lane = lanes(1)

    @pl.loop(0, blocks_ref.shape[0], unroll=4)
    def _(k):
        owner = owner_ref[k]
        rank = count_ref[owner]
        count_ref[owner] = rank + 1
        dest = owner * CAP + rank
        dest_ref[k] = dest
        buf[pl.ds(pl.multiple_of(dest * 8, 8), 8), :] = blocks_ref[k]
        row = slots[pl.ds(owner, 1), :]
        slots[pl.ds(owner, 1), :] = jnp.where(lane == rank, slot_ref[k], row)

    @pl.loop(0, devices // 8)
    def _(g):
        data = buf[pl.ds(pl.multiple_of(g * CAP * 64, 8), CAP * 64), :]
        label = slots[pl.ds(pl.multiple_of(g * 8, 8), 8), :].astype(F32)
        pieces = []
        for j in range(8):
            pieces += [data[CAP * 8 * j : CAP * 8 * (j + 1)], label[j : j + 1]]
        out_ref[pl.ds(pl.multiple_of(g * ROWS_MSG * 8, 8), ROWS_MSG * 8), :] = (
            jnp.concatenate(pieces, axis=0)
        )


def pack_x_kernel(*refs):
    firsts, lasts, v3, mid = refs[:6], refs[6:12], refs[12], refs[13:]
    first_out, last_out, v3_out = mid
    for group, out in ((firsts, first_out), (lasts, last_out)):
        p = 0
        for ref in group[:5]:
            n = ref.shape[0]
            out[p : p + n] = ref[...]
            p += n
        out[p] = BOND * group[5][...].astype(F32)
    v3_out[...] = v3[0]


def pack_y_kernel(v, cx, cy, st, via, mask, vp, lo, hi, vph, to_left, to_right):
    rows = v.shape[1]

    def pack(planes, at, n):
        lane = lanes(n)
        left = jnp.zeros((n, W), F32)
        right = jnp.zeros((n, W), F32)
        for p, x in enumerate(planes):
            here = (lane >= Q * p) & (lane < Q * p + Q)
            left = jnp.where(here, x if p == 0 else pltpu.roll(x, Q * p, axis=1), left)
            right = jnp.where(here, pltpu.roll(x, (Q * p + Q) % W, axis=1), right)
        to_left[pl.ds(at, n), :] = left
        to_right[pl.ds(at, n), :] = right

    def tile(i):
        at = pl.ds(i, STEP)
        planes = [ref[l, at, :] for ref in (v, cx, cy, st, via) for l in range(ref.shape[0])]
        planes += [BOND * mask[at, :].astype(F32), vp[at, :]]
        pack(planes, pl.multiple_of(i + H, 8), STEP)

    each_chunk(0, rows // STEP, tile)
    count = lo.shape[0]
    pack([lo[p] for p in range(count)] + [vph[0:H, :]], 0, H)
    pack([hi[p] for p in range(count)] + [vph[H : 2 * H, :]], H + rows, H)


def transpose_side(u_ref, out, at, rows):
    for j in range(u_ref.shape[1] // W):
        n = min(W, rows - W * j)
        block = u_ref[:, W * j : W * j + W].T
        out(at + W * j, n, block[:n])


def weighted(x, s, n, gx, gy, l_g):
    low = pl.multiple_of(s - 8, 8)
    near = x(low, n + 16)
    gnear = gx(l_g, low, n + 8)
    c = near[8 : 8 + n]
    g = gy(l_g, s, n)
    up = gnear[8 : 8 + n] * near[9 : 9 + n]
    down = (gnear * near[0 : n + 8])[7 : 7 + n]
    return up + down + g * from_right(c) + from_left(g * c)


def at(ref, l=None):
    if l is None:
        return lambda s, n: ref[pl.ds(s, n), :]
    return lambda s, n: ref[l, pl.ds(s, n), :]


def planes(ref):
    return lambda l, s, n: ref[l, pl.ds(s, n), :]


def base_kernel(
    place, v, cx, cy, st, via, mask, vp, lo, hi, vph, f_left, f_right,
    gx, gy, inv, viae, bond, d0, d1, z1, d2, z2, sb0, vd0, msg,
    ev, ecx, ecy, est, evp, side,
):
    rows = v.shape[1]
    total = rows + 2 * H
    layers = v.shape[0]
    dests = (
        [(ev, l) for l in range(layers)]
        + [(ecx, l) for l in range(layers)]
        + [(ecy, l) for l in range(layers)]
        + [(est, l) for l in range(layers)]
        + [(viae, l) for l in range(layers - 1)]
        + [(bond, None), (evp, None)]
    )

    def put(dest, s, n, cols, x):
        ref, l = dest
        if l is None:
            ref[pl.ds(s, n), cols] = x
        else:
            ref[l, pl.ds(s, n), cols] = x

    main, edge = slice(0, W), slice(W, 2 * W)

    def sides(s, n):
        r = pl.multiple_of(s - H, 8)
        a = f_right[pl.ds(r, n), :]
        b = f_left[pl.ds(r, n), :]
        low = lanes(n) < W // 2
        for p, dest in enumerate(dests):
            x = a if p == 0 else pltpu.roll(a, W - Q * p, axis=1)
            y = pltpu.roll(b, W - Q - Q * p, axis=1)
            put(dest, s, n, edge, jnp.where(low, x, y))

    each_chunk(H, total // STEP, lambda s: sides(s, STEP))

    def tile(i):
        a = pl.ds(i, STEP)
        xs = [ref[l, a, :] for ref in (v, cx, cy, st, via) for l in range(ref.shape[0])]
        xs += [BOND * mask[a, :].astype(F32), vp[a, :]]
        for x, dest in zip(xs, dests):
            put(dest, pl.multiple_of(i + PAD, 8), STEP, main, x)

    each_chunk(0, rows // STEP, tile)
    for p, dest in enumerate(dests):
        is_vp = p == len(dests) - 1
        put(dest, H, H, main, vph[0:H, :] if is_vp else lo[p])
        put(dest, PAD + rows, H, main, vph[H : 2 * H, :] if is_vp else hi[p])

    x_first, x_total, y_first, y_total = place[0], place[1], place[2], place[3]
    col = lanes(1, 2 * W)
    col = y_first + jnp.where(col < W + W // 2, col, col - 2 * W)
    nxt = lax.rem(col + 1 + y_total, y_total)
    seam = W // 2
    keep_y = jnp.where((nxt != seam) & (nxt != seam + y_total // 2), 0.5, 0.0).astype(F32)

    def conductances(s):
        row = x_first + s - PAD + lax.broadcasted_iota(jnp.int32, (STEP, 1), 0)
        keep_x = jnp.where((row != -1) & (row != x_total - 1), 0.5, 0.0).astype(F32)
        for l in range(layers):
            c = ecx[l, pl.ds(s, STEP + 8), :]
            gx[l, pl.ds(s, STEP), :] = keep_x * (c[0:STEP] + c[1 : STEP + 1])
            c = ecy[l, pl.ds(s, STEP), :]
            gy[l, pl.ds(s, STEP), :] = keep_y * (c + from_right(c))

    each_chunk(H, total // STEP, conductances)

    pgx, pgy = planes(gx), planes(gy)

    def start(s):
        n = STEP
        a = pl.ds(s, n)
        for l in range(layers):
            near = gx[l, pl.ds(pl.multiple_of(s - 8, 8), n + 8), :]
            up, down, right = near[8 : 8 + n], near[7 : 7 + n], gy[l, a, :]
            off = up + down + right + from_left(right)
            nb = weighted(at(ev, l), s, n, pgx, pgy, l)
            if l < layers - 1:
                off = off + viae[l, a, :]
                nb = nb + viae[l, a, :] * ev[l + 1, a, :]
            else:
                off = off + bond[a, :]
                nb = nb + bond[a, :] * evp[a, :]
            if l > 0:
                off = off + viae[l - 1, a, :]
                nb = nb + viae[l - 1, a, :] * ev[l - 1, a, :]
            c = ev[l, a, :]
            inverse = 1.0 / (est[l, a, :] + off)
            inv[l, a, :] = inverse
            d0[l, a, :] = (nb - off * c) * inverse

    each_chunk(H, total // STEP, start)

    def links(d, l, s, n, top=layers):
        nb = weighted(at(d, l), s, n, pgx, pgy, l)
        if l < layers - 1:
            nb = nb + viae[l, pl.ds(s, n), :] * d[l + 1, pl.ds(s, n), :]
        if l > 0:
            nb = nb + viae[l - 1, pl.ds(s, n), :] * d[l - 1, pl.ds(s, n), :]
        return inv[l, pl.ds(s, n), :] * nb

    def first(s):
        a = pl.ds(s, STEP)
        side[pl.ds(s - H, STEP), :] = d0[layers - 1, a, edge]
        msg[pl.ds(s - H, STEP), :] = d0[layers - 1, a, main]
        for l in range(layers - 1):
            z = links(d0, l, s, STEP)
            z1[l, a, :] = z
            d1[l, a, :] = A1 * d0[l, a, :] + B1 * z

    each_chunk(H, total // STEP, first)
    pack_side(side, msg, total)

    def second(s):
        a = pl.ds(s, STEP)
        for l in range(2):
            z = z1[l, a, :] - d1[l, a, :] + links(d1, l, s, STEP)
            z2[l, a, :] = z
            d2[l, a, :] = A2 * d1[l, a, :] + B2 * z

    each_chunk(H, total // STEP, second)

    def third(s):
        a = pl.ds(s, STEP)
        o = pl.ds(pl.multiple_of(s - PAD, 8), STEP)
        nb = weighted(at(d2, 0), s, STEP, pgx, pgy, 0)[:, main]
        nb = inv[0, a, main] * (nb + viae[0, a, main] * d2[1, a, main])
        d = d2[0, a, main]
        z = z2[0, a, main] - d + nb
        sb0[o, :] = v[0, o, :] + d0[0, a, main] + d1[0, a, main] + (1.0 + A3) * d + B3 * z
        for l in range(1, layers):
            vd0[l - 1, o, :] = v[l, o, :] + d0[l, a, main]

    each_chunk(PAD, rows // STEP, third)


def pack_side(side, msg, total):
    for j in range(-(-total // W)):
        t = side[W * j : W * j + W, :].T
        msg[total + 8 * j : total + 8 * j + Q, :] = t[0:Q]
        msg[total + 8 * j + Q : total + 8 * j + 2 * Q, :] = t[W - Q : W]


def unpack_side(msg, total, u, ref):
    u[...] = jnp.zeros_like(u)
    for j in range(-(-total // W)):
        u[0:Q, :] = msg[total + 8 * j : total + 8 * j + Q, :]
        u[W - Q : W, :] = msg[total + 8 * j + Q : total + 8 * j + 2 * Q, :]
        n = min(W, total - W * j)
        t = u[...].T
        ref[H + W * j : H + W * j + n, W : 2 * W] = t[:n]


def mid_kernel(d0, part, gx, gy, inv, viae, bond, d1, z1, msg, ep, side, u):
    top = gx.shape[0] - 1
    total = part.shape[0] - 8 * (u.shape[1] * 5 // W)
    unpack_side(part, total, u, ep)

    def body(s):
        a = pl.ds(s, STEP)
        r = pl.ds(pl.multiple_of(s - H, 8), STEP)
        other = jnp.concatenate([part[r, :], ep[a, W : 2 * W]], axis=1)
        nb = weighted(at(d0, top), s, STEP, planes(gx), planes(gy), top)
        nb = nb + viae[top - 1, a, :] * d0[top - 1, a, :] + bond[a, :] * other
        z = inv[top, a, :] * nb
        d = A1 * d0[top, a, :] + B1 * z
        z1[a, :] = z
        d1[a, :] = d
        side[r, :] = d[:, W:]
        msg[r, :] = d[:, :W]

    each_chunk(H, total // STEP, body)
    pack_side(side, msg, total)


def late_kernel(
    d1, e11, z1, d13, z13, part, gx, gy, inv, viae, bond,
    d22, d23, z22, z23, msg, ep, u,
):
    top = gx.shape[0] - 1
    total = part.shape[0] - 8 * (u.shape[1] * 5 // W)
    unpack_side(part, total, u, ep)

    def body(s):
        a = pl.ds(s, STEP)
        r = pl.ds(pl.multiple_of(s - H, 8), STEP)
        under = d1[top - 2, a, :] + e11[a, :]
        this, above = d1[top - 1, a, :], d13[a, :]
        nb = weighted(at(d1, top - 1), s, STEP, planes(gx), planes(gy), top - 1)
        nb = nb + viae[top - 2, a, :] * under + viae[top - 1, a, :] * above
        z = z1[top - 1, a, :] - this + inv[top - 1, a, :] * nb
        z22[a, :] = z
        d22[a, :] = A2 * this + B2 * z
        other = jnp.concatenate([part[r, :], ep[a, W : 2 * W]], axis=1)
        nb = weighted(at(d13), s, STEP, planes(gx), planes(gy), top)
        nb = nb + viae[top - 1, a, :] * this + bond[a, :] * other
        z = z13[a, :] - above + inv[top, a, :] * nb
        z23[a, :] = z
        d23[a, :] = A2 * above + B2 * z

    each_chunk(H, total // STEP, body)
    rows = msg.shape[0]
    msg[...] = d23[PAD : PAD + rows, 0:W]


def final_kernel(
    v0, vd0, d1, e11, d13, d20, d21, d22, d23, z21, z22, z23, part, gx, gy, inv, viae, bond, out
):
    main = slice(0, W)
    top = gx.shape[0] - 1

    def body(i):
        s = pl.multiple_of(i + PAD, 8)
        a, o = pl.ds(s, STEP), pl.ds(i, STEP)
        out[0, o, :] = v0[o, :]
        d2 = [None, d21, d22, d23]
        z2 = [None, z21, z22, z23]
        first = [None, d1[1, a, main] + e11[a, main], d1[2, a, main], d13[a, main]]
        below = d20[o, :]
        for l in range(1, top + 1):
            nb = weighted(at(d2[l]), s, STEP, planes(gx), planes(gy), l)[:, main]
            nb = nb + viae[l - 1, a, main] * below
            below = d2[l][a, main]
            if l < top:
                nb = nb + viae[l, a, main] * d2[l + 1][a, main]
            else:
                nb = nb + bond[a, main] * part[o, :]
            z = z2[l][a, main] - below + inv[l, a, main] * nb
            out[l, o, :] = vd0[l - 1, o, :] + first[l] + (1.0 + A3) * below + B3 * z

    each_chunk(0, out.shape[1] // STEP, body)


def map_kernel(arrived, out, first, last, labels, vec, lab, acc, sem):
    devices = vec.shape[0]
    rows = out.shape[0]
    vec[...] = arrived[pl.ds(CAP * 8, devices, stride=ROWS_MSG), :].astype(jnp.int32)
    copy = pltpu.make_async_copy(vec, lab, sem)
    copy.start()
    acc[...] = jnp.zeros_like(acc)
    copy.wait()

    @pl.loop(0, devices // 8)
    def _(g):
        n = ROWS_MSG * 8
        data = arrived[pl.ds(pl.multiple_of(g * n, 8), n), :]
        for j in range(8):
            for r in range(CAP):
                slot = lab[g * 8 + j, r]
                labels[(g * 8 + j) * CAP + r] = slot
                a = pl.ds(pl.multiple_of(slot * 8, 8), 8)
                acc[a, :] += data[j * ROWS_MSG + r * 8 : j * ROWS_MSG + r * 8 + 8]

    out[...] = acc[0:rows, :]
    first[...] = acc[0:8, :]
    last[...] = acc[rows - 8 : rows, :]


def edges_kernel(cur, lo, hi, to_left, to_right, ext):
    rows = cur.shape[0]
    ext[0:H, :] = lo[...]
    ext[H : H + rows, :] = cur[...]
    ext[H + rows : rows + 2 * H, :] = hi[...]
    for j in range(to_left.shape[1] // W):
        t = ext[W * j : W * j + W, :].T
        to_left[:, W * j : W * j + W] = t[0:8]
        to_right[:, W * j : W * j + W] = t[W - 8 : W]


def effect_kernel(
    labels, cur, lo, hi, f_left, f_right, gx, gy, inv, viae, sb0, d2, z2,
    v0, picked, e11, d20, d21, z21,
    ec, e0, e1, z10, z11, e2, z20, u, acc,
):
    rows = cur.shape[0]
    total = rows + 2 * H
    main, edge = slice(0, W), slice(W, 2 * W)
    ec[H : 2 * H, main] = lo[...]
    ec[PAD : PAD + rows, main] = cur[...]
    ec[PAD + rows : PAD + rows + H, main] = hi[...]
    u[...] = jnp.zeros_like(u)
    for j in range(f_left.shape[1] // W):
        u[0:8, :] = f_right[:, W * j : W * j + W]
        u[W - 8 : W, :] = f_left[:, W * j : W * j + W]
        n = min(W, total - W * j)
        ec[H + W * j : H + W * j + n, edge] = u[...].T[:n]
    pgx, pgy = planes(gx), planes(gy)

    def zeroth(s):
        a = pl.ds(s, STEP)
        e0[a, :] = inv[0, a, :] * ec[a, :]

    each_chunk(H, total // STEP, zeroth)

    def first(s):
        a = pl.ds(s, STEP)
        here = e0[a, :]
        z = inv[0, a, :] * weighted(at(e0), s, STEP, pgx, pgy, 0)
        z10[a, :] = z
        e1[a, :] = A1 * here + B1 * z
        z = inv[1, a, :] * viae[0, a, :] * here
        z11[a, :] = z
        e11[a, :] = B1 * z

    each_chunk(H, total // STEP, first)

    def second(s):
        a = pl.ds(s, STEP)
        low, high, between = e1[a, :], e11[a, :], viae[0, a, :]
        nb = weighted(at(e1), s, STEP, pgx, pgy, 0) + between * high
        z = z10[a, :] - low + inv[0, a, :] * nb
        z20[a, :] = z
        e2[a, :] = A2 * low + B2 * z
        nb = weighted(at(e11), s, STEP, pgx, pgy, 1) + between * low
        z = z11[a, :] - high + inv[1, a, :] * nb
        z21[a, :] = z2[1, a, :] + z
        d21[a, :] = d2[1, a, :] + A2 * high + B2 * z

    each_chunk(H, total // STEP, second)

    def third(i):
        s = pl.multiple_of(i + PAD, 8)
        a, o = pl.ds(s, STEP), pl.ds(i, STEP)
        here = e2[a, main]
        upper = d21[a, main] - d2[1, a, main]
        nb = weighted(at(e2), s, STEP, pgx, pgy, 0)[:, main] + viae[0, a, main] * upper
        z = z20[a, main] - here + inv[0, a, main] * nb
        whole = sb0[o, :] + e0[a, main] + e1[a, main] + (1.0 + A3) * here + B3 * z
        v0[o, :] = whole
        acc[o, :] = whole
        d20[o, :] = d2[0, a, main] + here

    each_chunk(0, rows // STEP, third)
    acc[rows : rows + 8, :] = jnp.zeros((8, W), F32)

    @pl.loop(0, labels.shape[0], unroll=8)
    def _(k):
        picked[pl.ds(pl.multiple_of(k * 8, 8), 8), :] = acc[
            pl.ds(pl.multiple_of(labels[k] * 8, 8), 8), :
        ]


def give_kernel(dest, back, out):
    @pl.loop(0, out.shape[0], unroll=8)
    def _(k):
        out[k] = back[pl.ds(pl.multiple_of(dest[k] * 8, 8), 8), :]


def ring(axis, step):
    n = lax.axis_size(axis)
    return [(i, (i + step) % n) for i in range(n)]


def shift(x, axis, step):
    return lax.ppermute(x, axis, ring(axis, step))


def facing(x):
    n = lax.axis_size("yt")
    return lax.ppermute(x, "yt", [(i, i ^ (n // 2)) for i in range(n)])


def on_device(v, st, cx, cy, via, mask, blocks, owner, slot):
    layers, rows, cols = v.shape
    devices = lax.axis_size("gx") * lax.axis_size("yt")
    nb = blocks.shape[0]
    total = rows + 2 * H
    nr = total + 2 * H
    side_blocks = -(-total // W)
    place = jnp.stack(
        [
            lax.axis_index("gx") * rows,
            jnp.int32(rows * lax.axis_size("gx")),
            lax.axis_index("yt") * cols,
            jnp.int32(cols * lax.axis_size("yt")),
        ]
    ).astype(jnp.int32)

    outgoing, dest = call(
        send_kernel,
        [shape(devices * ROWS_MSG, W), jax.ShapeDtypeStruct((nb,), jnp.int32)],
        [owner.reshape(nb), slot, blocks],
        scratch=[
            pltpu.SMEM((devices,), jnp.int32),
            pltpu.VMEM((devices * CAP * 8, W), F32),
            pltpu.VMEM((devices, W), jnp.int32),
        ],
        specs={0: SMEM, 1: SMEM},
        out_specs=[pl.BlockSpec(memory_space=pltpu.VMEM), SMEM],
    )
    arrived = lax.all_to_all(outgoing, ALL, 0, 0, tiled=True)

    sources = [v, cx, cy, st, via]
    args = sources + [mask] + sources + [mask, v]
    specs = {}
    last = rows // 8 - 1
    for i in range(5):
        n = sources[i].shape[0]
        specs[i] = pl.BlockSpec((n, 8, W), lambda _: (0, 0, 0))
        specs[6 + i] = pl.BlockSpec((n, 8, W), lambda _: (0, last, 0))
    specs[5] = pl.BlockSpec((8, W), lambda _: (0, 0))
    specs[11] = pl.BlockSpec((8, W), lambda _: (last, 0))
    specs[12] = pl.BlockSpec((1, rows, W), lambda _: (layers - 1, 0, 0))
    count = 5 * layers
    first_rows, last_rows, v_top = pl.pallas_call(
        pack_x_kernel,
        grid=(1,),
        out_shape=[shape(count, 8, W), shape(count, 8, W), shape(rows, W)],
        in_specs=[specs[i] for i in range(13)],
        out_specs=[
            pl.BlockSpec((count, 8, W), lambda _: (0, 0, 0)),
            pl.BlockSpec((count, 8, W), lambda _: (0, 0, 0)),
            pl.BlockSpec((rows, W), lambda _: (0, 0)),
        ],
        cost_estimate=pl.CostEstimate(flops=1, bytes_accessed=1_000_000, transcendentals=0),
    )(*args)
    lo = shift(last_rows, "gx", 1)
    hi = shift(first_rows, "gx", -1)
    v_part = facing(v_top)
    v_part_rims = facing(jnp.concatenate([lo[layers - 1], hi[layers - 1]], 0))
    tiles = [v, cx, cy, st, via, mask, v_part, lo, hi, v_part_rims]
    to_left, to_right = call(pack_y_kernel, [shape(total, W), shape(total, W)], tiles)
    f_left = shift(to_right, "yt", 1)
    f_right = shift(to_left, "yt", -1)

    ext = lambda n: shape(n, nr, 2 * W)
    one = shape(nr, 2 * W)
    buffer = lambda *d: pltpu.VMEM(d, F32)
    msg_shape = shape(total + 8 * side_blocks, W)
    gx, gy, inv, viae, bond, d0, d1, z1, d2, z2, sb0, vd0, msg0 = call(
        base_kernel,
        [ext(layers), ext(layers), ext(layers), ext(layers - 1), one, ext(layers), ext(3), ext(3),
         ext(2), ext(2), shape(rows, W), shape(layers - 1, rows, W), msg_shape],
        [place, *tiles, f_left, f_right],
        scratch=[buffer(layers, nr, 2 * W)] * 4
        + [buffer(nr, 2 * W), buffer(side_blocks * W, W)],
        specs={0: SMEM},
        vmem=56,
        cost=20_000_000,
    )
    part0 = facing(msg0)
    d13, z13, msg1 = call(
        mid_kernel,
        [one, one, msg_shape],
        [d0, part0, gx, gy, inv, viae, bond],
        scratch=[buffer(nr, 2 * W), buffer(side_blocks * W, W), buffer(W, W)],
    )
    part1 = facing(msg1)

    cur, cur_first, cur_last, labels = call(
        map_kernel,
        [shape(rows, W), shape(8, W), shape(8, W), jax.ShapeDtypeStruct((devices * CAP,), jnp.int32)],
        [arrived],
        scratch=[
            pltpu.VMEM((devices, W), jnp.int32),
            pltpu.SMEM((devices, W), jnp.int32),
            buffer(rows + 8, W),
            pltpu.SemaphoreType.DMA,
        ],
        out_specs=[pl.BlockSpec(memory_space=pltpu.VMEM)] * 3 + [SMEM],
    )
    cur_lo = shift(cur_last, "gx", 1)
    cur_hi = shift(cur_first, "gx", -1)
    cur_left, cur_right = call(
        edges_kernel,
        [shape(8, side_blocks * W)] * 2,
        [cur, cur_lo, cur_hi],
        scratch=[buffer(side_blocks * W, W)],
    )
    cur_f_left = shift(cur_right, "yt", 1)
    cur_f_right = shift(cur_left, "yt", -1)
    v0, picked, e11, d20, d21, z21 = call(
        effect_kernel,
        [shape(rows, W), shape(devices * CAP * 8, W), one, shape(rows, W), one, one],
        [labels, cur, cur_lo, cur_hi, cur_f_left, cur_f_right, gx, gy, inv, viae, sb0, d2, z2],
        scratch=[buffer(nr, 2 * W)] * 7 + [buffer(W, W), buffer(rows + 8, W)],
        specs={0: SMEM},
        vmem=56,
    )
    back = lax.all_to_all(picked, ALL, 0, 0, tiled=True)

    d22, d23, z22, z23, msg2 = call(
        late_kernel,
        [one, one, one, one, shape(rows, W)],
        [d1, e11, z1, d13, z13, part1, gx, gy, inv, viae, bond],
        scratch=[buffer(nr, 2 * W), buffer(W, W)],
        vmem=56,
        cost=10_000_000,
    )
    part2 = facing(msg2)
    voltage = call(
        final_kernel,
        shape(layers, rows, W),
        [v0, vd0, d1, e11, d13, d20, d21, d22, d23, z21, z22, z23, part2, gx, gy, inv, viae, bond],
        vmem=56,
        cost=10_000_000,
    )
    block_voltage = call(
        give_kernel, shape(nb, 8, W), [dest, back], specs={0: SMEM}
    )
    return voltage, block_voltage


def solution(mesh):
    tile = P(None, "gx", "yt")
    return jax.shard_map(
        on_device,
        mesh=mesh,
        in_specs=(tile, tile, tile, tile, tile, P("gx", "yt"), P(ALL, None, None), P(ALL, None), P(ALL)),
        out_specs=(tile, P(ALL, None, None)),
        check_vma=False,
    )
```

time: 228 us -> 207 us (0.908)
  Pallas kernels: 0 us -> 85.6 us
  local copies, waits for them, and re-layouts: 71 us -> 18.8 us
  other arithmetic: 48 us -> 0.62 us
  starting transfers between devices: 82.8 us -> 46.8 us
  waiting for transfers between devices: 22.3 us -> 52.7 us
    pallas_call x0 -> x11, Pallas kernels: none -> 85.6 us  [the longest x10 83.6 us: call(): pl.pallas_call(kernel, out_shape=outs if many else outs[0], in_specs=in_s...]
    ppermute x24 -> x13, waiting for transfers between devices: 3.24 us -> 52.7 us  [the longest x5 37.5 us: facing(): return lax.ppermute(x, 'yt', [(i, i ^ n // 2) for i in range(n)])]
    ppermute x24 -> x13, starting transfers between devices: 55.7 us -> 23.1 us  [the longest x8 15.5 us: shift(): return lax.ppermute(x, axis, ring(axis, step))]
    slice x21 -> x0, local copies, waits for them, and re-layouts: 27.2 us -> none  [the longest x14 15.7 us: with_halo(): lax.slice_in_dim(block, block.shape[dim] - width, None, axis=dim)]
    add x7 -> x0, other arithmetic: 26.5 us -> none  [the longest x4 22.5 us: off_diagonal(): summed + jnp.concatenate([cond_via * field_in[1:], zero_layer], 0)]
    all_to_all x3 -> x2, waiting for transfers between devices: 19 us -> 0.01 us  [the longest x1 0.01 us: on_device(): arrived = lax.all_to_all(outgoing, ALL, 0, 0, tiled=True)]
    ppermute x10 -> x0, local copies, waits for them, and re-layouts: 15.3 us -> none  [the longest x5 7.68 us: with_halo(): lax.ppermute(lax.slice_in_dim(block, 0, width, axis=dim), axis, backward)]
    scatter x2 -> x0, local copies, waits for them, and re-layouts: 13.5 us -> none  [the longest x1 12.4 us: on_device(): outgoing = jnp.zeros((devices * CAP,) + current_blocks.shape[1:], jnp.flo...]
  transfers between devices with their start and end apart: 27 -> 15, of which waited for: 2 -> 6; matrix products, arithmetic and copies ran while one was open for 38% -> 0% of each run, Pallas kernels for 0% -> 32%
where the time goes in v1:
time: 207 us; the launch traced here: 205 us
  Pallas kernels  85.6 us (41%)
  waiting for transfers between devices  52.7 us (25%)
  starting transfers between devices  46.8 us (23%)
  local copies, waits for them, and re-layouts  18.8 us (9%)
    pallas_call x10, Pallas kernels, call(): pl.pallas_call(kernel, out_shape=outs if many else outs[0], in_specs=in_s...  83.6 us
    ppermute x5, waiting for transfers between devices, facing(): return lax.ppermute(x, 'yt', [(i, i ^ n // 2) for i in range(n)])  37.5 us
    unnamed x64, local copies, waits for them, and re-layouts  16.2 us
    ppermute x8, starting transfers between devices, shift(): return lax.ppermute(x, axis, ring(axis, step))  15.5 us
    ppermute x8, waiting for transfers between devices, shift(): return lax.ppermute(x, axis, ring(axis, step))  15.2 us
    all_to_all x1, starting transfers between devices, on_device(): arrived = lax.all_to_all(outgoing, ALL, 0, 0, tiled=True)  11.9 us
    all_to_all x1, starting transfers between devices, on_device(): back = lax.all_to_all(picked, ALL, 0, 0, tiled=True)  11.7 us
    ppermute x5, starting transfers between devices, facing(): return lax.ppermute(x, 'yt', [(i, i ^ n // 2) for i in range(n)])  7.63 us
  transfers between devices with their start and end apart: 15, of which 6 were waited for; matrix products, arithmetic and copies ran while one was open for 0% of the time, Pallas kernels for 32%

profile of v1, /device:TPU:1, one launch (start us, length us, event | category | flops | bytes accessed | tf_op | source)
XLA Modules:
  0.0 205.4 jit_solution(9824091824030452209)
XLA Ops:
  3.0 2.3 %shard_map.104 = (f32[2176,128]{1,0:T(8,128)S(1)}, s32[128]{0:T(128)S(1)}) custom-call(s32[128]{0:T(128)S(1)} %bitcast.9, s32[128]{0:T(128)S(1)} %copy-done.24, f32[128,8,128]{2,1,0:T(8,128)S(1)} %copy-done.16), custom_call_target="tpu_custom_call" | custom-call | flops 1000000 | bytes 1000000 | tf_op jit(solution)/shard_map/pallas_call | solution.py:45
  5.2 1.2 all_to_all.14
  6.5 11.9 %all-to-all-start = ((f32[128,17,128]{2,1,0:T(8,128)}), f32[128,17,128]{2,1,0:T(8,128)}, u32[]{:S(2)}, u32[]{:S(2)}) async-start(f32[128,17,128]{2,1,0:T(8,128)} %all_to_all.14), calls=%async_computation | async-start | bytes 3145728 | tf_op jit(solution)/shard_map/all_to_all | solution.py:574
  18.4 2.0 shard_map.107
  20.4 1.4 collective-permute-start.5
  21.8 2.8 %collective-permute-start.6 = (f32[20,8,128]{2,1,0:T(8,128)}, f32[20,8,128]{2,1,0:T(8,128)S(1)}, u32[]{:S(2)}, u32[]{:S(2)}) collective-permute-start(f32[20,8,128]{2,1,0:T(8,128)} %get-tuple-element.51), channel_id=1, source_target_pairs={{0,112},{16,0},{32,16},{48,32},{64,48},{80,64},{96,80},{112,96},{1... | collective-permute-start | bytes 245768 | tf_op jit(solution)/shard_map/ppermute | solution.py:538
  24.7 2.4 %collective-permute-start.4 = (f32[512,128]{1,0:T(8,128)}, f32[512,128]{1,0:T(8,128)S(1)}, u32[]{:S(2)}, u32[]{:S(2)}) collective-permute-start(f32[512,128]{1,0:T(8,128)} %get-tuple-element.49), channel_id=1, source_target_pairs={{0,8},{1,9},{2,10},{3,11},{4,12},{5,13},{6,14},{7,15},{8,0},{9,1},... | collective-permute-start | bytes 786440 | tf_op jit(solution)/shard_map/ppermute | solution.py:543
  27.1 14.2 %collective-permute-done.5.lo = f32[20,8,128]{2,1,0:T(8,128)S(1)} collective-permute-done((f32[20,8,128]{2,1,0:T(8,128)}, f32[20,8,128]{2,1,0:T(8,128)S(1)}, u32[]{:S(2)}, u32[]{:S(2)}) %collective-permute-start.5) | collective-permute-done | bytes 81952 | tf_op jit(solution)/shard_map/ppermute | solution.py:538
  41.3 2.2 %collective-permute-start.7 = (f32[16,128]{1,0:T(8,128)S(1)}, f32[16,128]{1,0:T(8,128)S(1)}, u32[]{:S(2)}, u32[]{:S(2)}) collective-permute-start(f32[16,128]{1,0:T(8,128)S(1)} %pad_maximum_fusion), channel_id=1, source_target_pairs={{0,8},{1,9},{2,10},{3,11},{4,12},{5,13},{6,14},{7,15},{8,0},{9,1},... | collective-permute-start | bytes 24584 | tf_op jit(solution)/shard_map/ppermute | solution.py:543
  43.5 3.7 %collective-permute-done.7.vph = f32[16,128]{1,0:T(8,128)S(1)} collective-permute-done((f32[16,128]{1,0:T(8,128)S(1)}, f32[16,128]{1,0:T(8,128)S(1)}, u32[]{:S(2)}, u32[]{:S(2)}) %collective-permute-start.7) | collective-permute-done | bytes 8224 | tf_op jit(solution)/shard_map/ppermute | solution.py:543
  49.6 5.9 %shard_map.108 = (f32[528,128]{1,0:T(8,128)}, f32[528,128]{1,0:T(8,128)}) custom-call(f32[4,512,128]{2,1,0:T(8,128)S(1)} %copy-done.4, f32[4,512,128]{2,1,0:T(8,128)S(1)} %copy-done.5, f32[4,512,128]{2,1,0:T(8,128)S(1)} %copy-done.6, f32[4,512,128]{2,1,0:T(8,128)S(1)} %copy-done.7, f32[3,512,128]{2,1,0:T(8,128)S(1)} %copy-done.8, s32[512,128]{1,0:T(8,128)S(1)} %copy-done.10, ...), custom_call_target="tpu_custom_call" | custom-call | flops 1000000 | bytes 1000000 | tf_op jit(solution)/shard_map/pallas_call | solution.py:45
  55.5 1.9 collective-permute-start.8
  57.5 1.4 all_to_all.16.arrived
  58.9 3.3 %shard_map.105 = (f32[512,128]{1,0:T(8,128)S(1)}, f32[8,128]{1,0:T(8,128)S(1)}, f32[8,128]{1,0:T(8,128)S(1)}, s32[256]{0:T(256)S(1)}) custom-call(f32[2176,128]{1,0:T(8,128)S(1)} %all_to_all.16.arrived), custom_call_target="tpu_custom_call" | custom-call | flops 1000000 | bytes 1000000 | tf_op jit(solution)/shard_map/pallas_call | solution.py:45
  62.7 3.2 %collective-permute-start.1 = (f32[8,128]{1,0:T(8,128)S(1)}, f32[8,128]{1,0:T(8,128)S(1)}, u32[]{:S(2)}, u32[]{:S(2)}) collective-permute-start(f32[8,128]{1,0:T(8,128)S(1)} %get-tuple-element.46), channel_id=1, source_target_pairs={{0,112},{16,0},{32,16},{48,32},{64,48},{80,64},{96,80},{112,96},{1... | collective-permute-start | bytes 12296 | tf_op jit(solution)/shard_map/ppermute | solution.py:538
  67.0 3.0 %collective-permute-start.2 = (f32[8,640]{1,0:T(8,128)S(1)}, f32[8,640]{1,0:T(8,128)S(1)}, u32[]{:S(2)}, u32[]{:S(2)}) collective-permute-start(f32[8,640]{1,0:T(8,128)S(1)} %get-tuple-element.47), channel_id=1, source_target_pairs={{0,1},{1,2},{2,3},{3,4},{4,5},{5,6},{6,7},{7,8},{8,9},{9,10},{10,1... | collective-permute-start | bytes 61448 | tf_op jit(solution)/shard_map/ppermute | solution.py:538
  70.0 2.7 %collective-permute-start.3 = (f32[8,640]{1,0:T(8,128)S(1)}, f32[8,640]{1,0:T(8,128)S(1)}, u32[]{:S(2)}, u32[]{:S(2)}) collective-permute-start(f32[8,640]{1,0:T(8,128)S(1)} %get-tuple-element.48), channel_id=1, source_target_pairs={{0,15},{1,0},{2,1},{3,2},{4,3},{5,4},{6,5},{7,6},{8,7},{9,8},{10,9... | collective-permute-start | bytes 61448 | tf_op jit(solution)/shard_map/ppermute | solution.py:538
  74.7 31.3 %shard_map.109 = (f32[4,544,256]{2,1,0:T(8,128)}, f32[4,544,256]{2,1,0:T(8,128)}, f32[4,544,256]{2,1,0:T(8,128)}, f32[3,544,256]{2,1,0:T(8,128)}, f32[544,256]{1...) custom-call(s32[4]{0:T(128)} %pad_add_fusion.place, ...), custom_call_target="tpu_custom_call" | custom-call | flops 20000000 | bytes 20000000 | tf_op jit(solution)/shard_map/pallas_call | solution.py:45
  106.7 15.4 %shard_map.110 = (f32[512,128]{1,0:T(8,128)}, f32[2048,128]{1,0:T(8,128)}, f32[544,256]{1,0:T(8,128)}, f32[512,128]{1,0:T(8,128)}, f32[544,256]{1,0:T(8,128)}, /*index=5*/f32[544,256]{1,0:T(8,128)}) custom-call(s32[256]{0:T(256)} %copy-done.22, f32[512,128]{1,0:T(8,128)} %copy-done.14, f32[8,128]{1,0:T(8,128)} %copy-done.20, f32[8,128]{1,0:T(8,128)} %copy-done.21, ...), custom_call_target="tpu_custom_call" | custom-call | flops 1000000 | bytes 1000000 | tf_op jit(solution)/shard_map/pallas_call | solution.py:45
  122.1 11.7 %all-to-all-start.1 = ((f32[128,16,128]{2,1,0:T(8,128)}), f32[128,16,128]{2,1,0:T(8,128)}, u32[]{:S(2)}, u32[]{:S(2)}) async-start(f32[128,16,128]{2,1,0:T(8,128)} %bitcast.10), calls=%async_computation.1 | async-start | bytes 2097152 | tf_op jit(solution)/shard_map/all_to_all | solution.py:663
  133.9 3.0 %collective-permute-start.10 = (f32[568,128]{1,0:T(8,128)S(1)}, f32[568,128]{1,0:T(8,128)S(1)}, u32[]{:S(2)}, u32[]{:S(2)}) collective-permute-start(f32[568,128]{1,0:T(8,128)S(1)} %copy-done.31), channel_id=1, source_target_pairs={{0,8},{1,9},{2,10},{3,11},{4,12},{5,13},{6,14},{7,15},{8,0},{9,1},... | collective-permute-start | bytes 872456 | tf_op jit(solution)/shard_map/ppermute | solution.py:543
  136.8 17.0 %collective-permute-done.10.part = f32[568,128]{1,0:T(8,128)S(1)} collective-permute-done((f32[568,128]{1,0:T(8,128)S(1)}, f32[568,128]{1,0:T(8,128)S(1)}, u32[]{:S(2)}, u32[]{:S(2)}) %collective-permute-start.10) | collective-permute-done | bytes 290848 | tf_op jit(solution)/shard_map/ppermute | solution.py:543
  153.9 1.6 copy-done.1
  155.5 1.6 copy-done.2
  157.1 1.4 copy-done.3
  158.6 1.6 copy-done.12
  160.2 3.2 %shard_map.111 = (f32[544,256]{1,0:T(8,128)S(1)}, f32[544,256]{1,0:T(8,128)S(1)}, f32[568,128]{1,0:T(8,128)S(1)}) custom-call(f32[4,544,256]{2,1,0:T(8,128)S(1)} %copy-done.12, f32[568,128]{1,0:T(8,128)S(1)} %collective-permute-done.10.part, f32[4,544,256]{2,1,0:T(8,128)S(1)} %copy-done, f32[4,544,256]{2,1,0:T(8,128)S(1)} %copy-done.1, ...), custom_call_target="tpu_custom_call" | custom-call | flops 1000000 | bytes 1000000 | tf_op jit(solution)/shard_map/pallas_call | solution.py:45
  165.1 9.1 %collective-permute-done.11.part = f32[568,128]{1,0:T(8,128)S(1)} collective-permute-done((f32[568,128]{1,0:T(8,128)S(1)}, f32[568,128]{1,0:T(8,128)S(1)}, u32[]{:S(2)}, u32[]{:S(2)}) %collective-permute-start.11) | collective-permute-done | bytes 290848 | tf_op jit(solution)/shard_map/ppermute | solution.py:543
  174.8 9.9 %shard_map.112 = (f32[544,256]{1,0:T(8,128)}, f32[544,256]{1,0:T(8,128)}, f32[544,256]{1,0:T(8,128)}, f32[544,256]{1,0:T(8,128)}, f32[512,128]{1,0:T(8,128)}) custom-call(f32[3,544,256]{2,1,0:T(8,128)} %get-tuple-element.63.d1, f32[544,256]{1,0:T(8,128)} %get-tuple-element.64.e11, f32[3,544,256]{2,1,0:T(8,128)} %get-tuple-element.71.z1, ...), custom_call_target="tpu_custom_call" | custom-call | flops 10000000 | bytes 10000000 | tf_op jit(solution)/shard_map/pallas_call | solution.py:45
  184.8 7.7 %collective-permute-done.12.part = f32[512,128]{1,0:T(8,128)S(1)} collective-permute-done((f32[512,128]{1,0:T(8,128)}, f32[512,128]{1,0:T(8,128)S(1)}, u32[]{:S(2)}, u32[]{:S(2)}) %collective-permute-start.12) | collective-permute-done | bytes 262176 | tf_op jit(solution)/shard_map/ppermute | solution.py:543
  193.2 10.0 %shard_map.113 = f32[4,512,128]{2,1,0:T(8,128)} custom-call(f32[512,128]{1,0:T(8,128)} %get-tuple-element.61.v0, f32[3,512,128]{2,1,0:T(8,128)} %get-tuple-element.62.vd0, f32[3,544,256]{2,1,0:T(8,128)} %get-tuple-element.63.d1, f32[544,256]{1,0:T(8,128)} %get-tuple-element.64.e11, f32[544,256]{1,0:T(8,128)} %copy-done.11, ...), custom_call_target="tpu_custom_call" | custom-call | flops 10000000 | bytes 10000000 | tf_op jit(solution)/shard_map/pallas_call | solution.py:45
  203.2 2.2 %shard_map.114 = f32[128,8,128]{2,1,0:T(8,128)} custom-call(s32[128]{0:T(128)S(1)} %get-tuple-element.80.dest, f32[2048,128]{1,0:T(8,128)} %bitcast.6.back), custom_call_target="tpu_custom_call" | custom-call | flops 1000000 | bytes 1000000 | tf_op jit(solution)/shard_map/pallas_call | solution.py:45
  (79 shorter events, 12.1 us)
Async XLA Ops:
  6.5 51.0 %all-to-all-start = ((f32[128,17,128]{2,1,0:T(8,128)}), f32[128,17,128]{2,1,0:T(8,128)}, u32[]{:S(2)}, u32[]{:S(2)}) async-start(f32[128,17,128]{2,1,0:T(8,128)} %all_to_all.14), calls=%async_computation | async-start | bytes 3145728 | tf_op jit(solution)/shard_map/all_to_all | solution.py:574
  18.4 28.8 %copy-start.4 = (f32[4,512,128]{2,1,0:T(8,128)S(1)}, f32[4,512,128]{2,1,0:T(8,128)}, u32[]{:S(2)}) copy-start(f32[4,512,128]{2,1,0:T(8,128)} %v.3) | copy-start | bytes 3145732
  18.4 28.8 %copy-start.5 = (f32[4,512,128]{2,1,0:T(8,128)S(1)}, f32[4,512,128]{2,1,0:T(8,128)}, u32[]{:S(2)}) copy-start(f32[4,512,128]{2,1,0:T(8,128)} %cx.3) | copy-start | bytes 3145732
  18.4 28.8 %copy-start.6 = (f32[4,512,128]{2,1,0:T(8,128)S(1)}, f32[4,512,128]{2,1,0:T(8,128)}, u32[]{:S(2)}) copy-start(f32[4,512,128]{2,1,0:T(8,128)} %cy.3) | copy-start | bytes 3145732
  18.4 28.8 %copy-start.10 = (s32[512,128]{1,0:T(8,128)S(1)}, s32[512,128]{1,0:T(8,128)}, u32[]{:S(2)}) copy-start(s32[512,128]{1,0:T(8,128)} %mask.3) | copy-start | bytes 786436
  20.4 20.8 %collective-permute-start.5 = (f32[20,8,128]{2,1,0:T(8,128)}, f32[20,8,128]{2,1,0:T(8,128)S(1)}, u32[]{:S(2)}, u32[]{:S(2)}) collective-permute-start(f32[20,8,128]{2,1,0:T(8,128)} %get-tuple-element.50), channel_id=1, source_target_pairs={{0,16},{16,32},{32,48},{48,64},{64,80},{80,96},{96,112},{112,0},{1... | collective-permute-start | bytes 245768 | tf_op jit(solution)/shard_map/ppermute | solution.py:538
  21.8 19.4 %collective-permute-start.6 = (f32[20,8,128]{2,1,0:T(8,128)}, f32[20,8,128]{2,1,0:T(8,128)S(1)}, u32[]{:S(2)}, u32[]{:S(2)}) collective-permute-start(f32[20,8,128]{2,1,0:T(8,128)} %get-tuple-element.51), channel_id=1, source_target_pairs={{0,112},{16,0},{32,16},{48,32},{64,48},{80,64},{96,80},{112,96},{1... | collective-permute-start | bytes 245768 | tf_op jit(solution)/shard_map/ppermute | solution.py:538
  24.7 22.6 %collective-permute-start.4 = (f32[512,128]{1,0:T(8,128)}, f32[512,128]{1,0:T(8,128)S(1)}, u32[]{:S(2)}, u32[]{:S(2)}) collective-permute-start(f32[512,128]{1,0:T(8,128)} %get-tuple-element.49), channel_id=1, source_target_pairs={{0,8},{1,9},{2,10},{3,11},{4,12},{5,13},{6,14},{7,15},{8,0},{9,1},... | collective-permute-start | bytes 786440 | tf_op jit(solution)/shard_map/ppermute | solution.py:543
  41.2 14.3 %copy-start.17 = (f32[20,8,128]{2,1,0:T(8,128)}, f32[20,8,128]{2,1,0:T(8,128)S(1)}, u32[]{:S(2)}) copy-start(f32[20,8,128]{2,1,0:T(8,128)S(1)} %collective-permute-done.5.lo) | copy-start | bytes 245764
  41.2 14.3 %copy-start.18 = (f32[20,8,128]{2,1,0:T(8,128)}, f32[20,8,128]{2,1,0:T(8,128)S(1)}, u32[]{:S(2)}) copy-start(f32[20,8,128]{2,1,0:T(8,128)S(1)} %collective-permute-done.6.hi) | copy-start | bytes 245764
  41.3 5.9 %collective-permute-start.7 = (f32[16,128]{1,0:T(8,128)S(1)}, f32[16,128]{1,0:T(8,128)S(1)}, u32[]{:S(2)}, u32[]{:S(2)}) collective-permute-start(f32[16,128]{1,0:T(8,128)S(1)} %pad_maximum_fusion), channel_id=1, source_target_pairs={{0,8},{1,9},{2,10},{3,11},{4,12},{5,13},{6,14},{7,15},{8,0},{9,1},... | collective-permute-start | bytes 24584 | tf_op jit(solution)/shard_map/ppermute | solution.py:543
  47.2 8.3 %copy-start.19 = (f32[16,128]{1,0:T(8,128)}, f32[16,128]{1,0:T(8,128)S(1)}, u32[]{:S(2)}) copy-start(f32[16,128]{1,0:T(8,128)S(1)} %collective-permute-done.7.vph) | copy-start | bytes 24580
  49.6 5.9 %copy-start.13 = (f32[512,128]{1,0:T(8,128)}, f32[512,128]{1,0:T(8,128)S(1)}, u32[]{:S(2)}) copy-start(f32[512,128]{1,0:T(8,128)S(1)} %collective-permute-done.4.vp) | copy-start | bytes 786436
  55.5 17.8 %collective-permute-start.8 = (f32[528,128]{1,0:T(8,128)}, f32[528,128]{1,0:T(8,128)S(1)}, u32[]{:S(2)}, u32[]{:S(2)}) collective-permute-start(f32[528,128]{1,0:T(8,128)} %get-tuple-element.52), channel_id=1, source_target_pairs={{0,1},{1,2},{2,3},{3,4},{4,5},{5,6},{6,7},{7,8},{8,9},{9,10},{10,1... | collective-permute-start | bytes 811016 | tf_op jit(solution)/shard_map/ppermute | solution.py:538
  57.5 15.9 %collective-permute-start.9 = (f32[528,128]{1,0:T(8,128)}, f32[528,128]{1,0:T(8,128)S(1)}, u32[]{:S(2)}, u32[]{:S(2)}) collective-permute-start(f32[528,128]{1,0:T(8,128)} %get-tuple-element.53), channel_id=1, source_target_pairs={{0,15},{1,0},{2,1},{3,2},{4,3},{5,4},{6,5},{7,6},{8,7},{9,8},{10,9... | collective-permute-start | bytes 811016 | tf_op jit(solution)/shard_map/ppermute | solution.py:538
  62.2 43.9 %copy-start.14 = (f32[512,128]{1,0:T(8,128)}, f32[512,128]{1,0:T(8,128)S(1)}, u32[]{:S(2)}) copy-start(f32[512,128]{1,0:T(8,128)S(1)} %get-tuple-element.44.cur) | copy-start | bytes 786436
  62.2 43.9 %copy-start.22 = (s32[256]{0:T(256)}, s32[256]{0:T(256)S(1)}, u32[]{:S(2)}) copy-start(s32[256]{0:T(256)S(1)} %get-tuple-element.43.labels) | copy-start | bytes 3076
  62.2 4.6 %collective-permute-start = (f32[8,128]{1,0:T(8,128)S(1)}, f32[8,128]{1,0:T(8,128)S(1)}, u32[]{:S(2)}, u32[]{:S(2)}) collective-permute-start(f32[8,128]{1,0:T(8,128)S(1)} %get-tuple-element.45), channel_id=1, source_target_pairs={{0,16},{16,32},{32,48},{48,64},{64,80},{80,96},{96,112},{112,0},{1... | collective-permute-start | bytes 12296 | tf_op jit(solution)/shard_map/ppermute | solution.py:538
  62.7 4.2 %collective-permute-start.1 = (f32[8,128]{1,0:T(8,128)S(1)}, f32[8,128]{1,0:T(8,128)S(1)}, u32[]{:S(2)}, u32[]{:S(2)}) collective-permute-start(f32[8,128]{1,0:T(8,128)S(1)} %get-tuple-element.46), channel_id=1, source_target_pairs={{0,112},{16,0},{32,16},{48,32},{64,48},{80,64},{96,80},{112,96},{1... | collective-permute-start | bytes 12296 | tf_op jit(solution)/shard_map/ppermute | solution.py:538
  66.9 39.2 %copy-start.20 = (f32[8,128]{1,0:T(8,128)}, f32[8,128]{1,0:T(8,128)S(1)}, u32[]{:S(2)}) copy-start(f32[8,128]{1,0:T(8,128)S(1)} %collective-permute-done.lo) | copy-start | bytes 12292
  66.9 39.2 %copy-start.21 = (f32[8,128]{1,0:T(8,128)}, f32[8,128]{1,0:T(8,128)S(1)}, u32[]{:S(2)}) copy-start(f32[8,128]{1,0:T(8,128)S(1)} %collective-permute-done.1.hi) | copy-start | bytes 12292
  67.0 39.1 %collective-permute-start.2 = (f32[8,640]{1,0:T(8,128)S(1)}, f32[8,640]{1,0:T(8,128)S(1)}, u32[]{:S(2)}, u32[]{:S(2)}) collective-permute-start(f32[8,640]{1,0:T(8,128)S(1)} %get-tuple-element.47), channel_id=1, source_target_pairs={{0,1},{1,2},{2,3},{3,4},{4,5},{5,6},{6,7},{7,8},{8,9},{9,10},{10,1... | collective-permute-start | bytes 61448 | tf_op jit(solution)/shard_map/ppermute | solution.py:538
  70.0 36.1 %collective-permute-start.3 = (f32[8,640]{1,0:T(8,128)S(1)}, f32[8,640]{1,0:T(8,128)S(1)}, u32[]{:S(2)}, u32[]{:S(2)}) collective-permute-start(f32[8,640]{1,0:T(8,128)S(1)} %get-tuple-element.48), channel_id=1, source_target_pairs={{0,15},{1,0},{2,1},{3,2},{4,3},{5,4},{6,5},{7,6},{8,7},{9,8},{10,9... | collective-permute-start | bytes 61448 | tf_op jit(solution)/shard_map/ppermute | solution.py:538
  106.7 47.1 %copy-start = (f32[4,544,256]{2,1,0:T(8,128)S(1)}, f32[4,544,256]{2,1,0:T(8,128)}, u32[]{:S(2)}) copy-start(f32[4,544,256]{2,1,0:T(8,128)} %get-tuple-element.54.gx) | copy-start | bytes 6684676
  122.1 11.7 %copy-start.31 = (f32[568,128]{1,0:T(8,128)S(1)}, f32[568,128]{1,0:T(8,128)}, u32[]{:S(2)}) copy-start(f32[568,128]{1,0:T(8,128)} %get-tuple-element.66) | copy-start | bytes 872452
  122.1 31.7 %copy-start.9 = (f32[544,256]{1,0:T(8,128)S(1)}, f32[544,256]{1,0:T(8,128)}, u32[]{:S(2)}) copy-start(f32[544,256]{1,0:T(8,128)} %get-tuple-element.67.bond) | copy-start | bytes 1671172
  122.1 81.0 %all-to-all-start.1 = ((f32[128,16,128]{2,1,0:T(8,128)}), f32[128,16,128]{2,1,0:T(8,128)}, u32[]{:S(2)}, u32[]{:S(2)}) async-start(f32[128,16,128]{2,1,0:T(8,128)} %bitcast.10), calls=%async_computation.1 | async-start | bytes 2097152 | tf_op jit(solution)/shard_map/all_to_all | solution.py:663
  133.9 20.0 %collective-permute-start.10 = (f32[568,128]{1,0:T(8,128)S(1)}, f32[568,128]{1,0:T(8,128)S(1)}, u32[]{:S(2)}, u32[]{:S(2)}) collective-permute-start(f32[568,128]{1,0:T(8,128)S(1)} %copy-done.31), channel_id=1, source_target_pairs={{0,8},{1,9},{2,10},{3,11},{4,12},{5,13},{6,14},{7,15},{8,0},{9,1},... | collective-permute-start | bytes 872456 | tf_op jit(solution)/shard_map/ppermute | solution.py:543
  153.9 1.6 copy-start.1
  155.5 1.6 copy-start.2
  165.1 9.1 %collective-permute-start.11 = (f32[568,128]{1,0:T(8,128)S(1)}, f32[568,128]{1,0:T(8,128)S(1)}, u32[]{:S(2)}, u32[]{:S(2)}) collective-permute-start(f32[568,128]{1,0:T(8,128)S(1)} %get-tuple-element.73), channel_id=1, source_target_pairs={{0,8},{1,9},{2,10},{3,11},{4,12},{5,13},{6,14},{7,15},{8,0},{9,1},... | collective-permute-start | bytes 872456 | tf_op jit(solution)/shard_map/ppermute | solution.py:543
  184.8 7.7 %collective-permute-start.12 = (f32[512,128]{1,0:T(8,128)}, f32[512,128]{1,0:T(8,128)S(1)}, u32[]{:S(2)}, u32[]{:S(2)}) collective-permute-start(f32[512,128]{1,0:T(8,128)} %get-tuple-element.79), channel_id=1, source_target_pairs={{0,8},{1,9},{2,10},{3,11},{4,12},{5,13},{6,14},{7,15},{8,0},{9,1},... | collective-permute-start | bytes 786440 | tf_op jit(solution)/shard_map/ppermute | solution.py:543
  (15 other events, 13.5 us)

commit v2 on v1

v2 whole, which is shorter than its diff:
```python
import jax
import jax.numpy as jnp
from jax import lax
from jax.experimental import pallas as pl
from jax.experimental.pallas import tpu as pltpu
from jax.sharding import PartitionSpec as P

CAP = 2
BOND = 2.0
CENTER = 1.0
HALFWIDTH = 0.97
SIGMA = CENTER / HALFWIDTH
RHO0 = 1.0 / SIGMA
RHO1 = 1.0 / (2.0 * SIGMA - RHO0)
RHO2 = 1.0 / (2.0 * SIGMA - RHO1)
RHO3 = 1.0 / (2.0 * SIGMA - RHO2)
A1, B1 = RHO1 * RHO0, 2.0 * RHO1 / HALFWIDTH
A2, B2 = RHO2 * RHO1, 2.0 * RHO2 / HALFWIDTH
A3, B3 = RHO3 * RHO2, 2.0 * RHO3 / HALFWIDTH

VMEM_BASE, VMEM_TOP, VMEM_EFFECT, VMEM_FINAL = 58, 58, 58, 58

ALL = ("gx", "yt")
F32 = jnp.float32
W = 128
H = 8
PAD = 16
Q = 4
WIDE = 48
STEP = 64
ROWS_MSG = CAP * 8 + 1


def call(kernel, out, args, scratch=(), specs=None, out_specs=None, vmem=6, cost=1_000_000):
    specs = specs or {}
    in_specs = [
        specs.get(i, pl.BlockSpec(memory_space=pltpu.VMEM)) for i in range(len(args))
    ]
    many = isinstance(out, (list, tuple))
    outs = list(out) if many else [out]
    o_specs = out_specs or [pl.BlockSpec(memory_space=pltpu.VMEM)] * len(outs)
    return pl.pallas_call(
        kernel,
        out_shape=outs if many else outs[0],
        in_specs=in_specs,
        out_specs=o_specs if many else o_specs[0],
        scratch_shapes=list(scratch),
        name=kernel.__name__,
        compiler_params=pltpu.CompilerParams(vmem_limit_bytes=vmem << 20),
        cost_estimate=pl.CostEstimate(flops=cost, bytes_accessed=cost, transcendentals=0),
    )(*args)


def shape(*dims):
    return jax.ShapeDtypeStruct(dims, F32)


SMEM = pl.BlockSpec(memory_space=pltpu.SMEM)


def from_right(x):
    return pltpu.roll(x, x.shape[-1] - 1, axis=1)


def from_left(x):
    return pltpu.roll(x, 1, axis=1)


def lanes(rows, width=W):
    return lax.broadcasted_iota(jnp.int32, (rows, width), 1)


def each_chunk(first, rows, body, step):
    @pl.loop(0, rows // step)
    def _(k):
        body(pl.multiple_of(first + k * step, 8))


def send_kernel(owner_ref, slot_ref, blocks_ref, out_ref, dest_ref, count_ref, buf, slots):
    devices = count_ref.shape[0]

    @pl.loop(0, devices, unroll=8)
    def _(o):
        count_ref[o] = 0

    buf[...] = jnp.zeros_like(buf)
    slots[...] = jnp.full(slots.shape, 64, jnp.int32)
    lane = lanes(1)

    @pl.loop(0, blocks_ref.shape[0], unroll=4)
    def _(k):
        owner = owner_ref[k]
        rank = count_ref[owner]
        count_ref[owner] = rank + 1
        dest = owner * CAP + rank
        dest_ref[k] = dest
        buf[pl.ds(pl.multiple_of(dest * 8, 8), 8), :] = blocks_ref[k]
        row = slots[pl.ds(owner, 1), :]
        slots[pl.ds(owner, 1), :] = jnp.where(lane == rank, slot_ref[k], row)

    @pl.loop(0, devices // 8)
    def _(g):
        data = buf[pl.ds(pl.multiple_of(g * CAP * 64, 8), CAP * 64), :]
        label = slots[pl.ds(pl.multiple_of(g * 8, 8), 8), :].astype(F32)
        pieces = []
        for j in range(8):
            pieces += [data[CAP * 8 * j : CAP * 8 * (j + 1)], label[j : j + 1]]
        out_ref[pl.ds(pl.multiple_of(g * ROWS_MSG * 8, 8), ROWS_MSG * 8), :] = (
            jnp.concatenate(pieces, axis=0)
        )


def pack_x_kernel(*refs):
    firsts, lasts, v3 = refs[:6], refs[6:12], refs[12]
    first_out, last_out, v3_out, v3_first, v3_last = refs[13:]
    for group, out in ((firsts, first_out), (lasts, last_out)):
        p = 0
        for ref in group[:5]:
            n = ref.shape[0]
            out[p : p + n] = ref[...]
            p += n
        out[p] = BOND * group[5][...].astype(F32)
    rows = v3.shape[1]
    v3_out[...] = v3[0]
    v3_first[...] = v3[0, 0:H, :]
    v3_last[...] = v3[0, rows - H : rows, :]


def pack_y_kernel(v, cx, cy, st, via, mask, vp, lo, hi, vlo, vhi, to_left, to_right):
    rows = v.shape[1]

    def pack(planes, at, n):
        lane = lanes(n)
        left = jnp.zeros((n, W), F32)
        right = jnp.zeros((n, W), F32)
        for p, x in enumerate(planes):
            here = (lane >= Q * p) & (lane < Q * p + Q)
            left = jnp.where(here, x if p == 0 else pltpu.roll(x, Q * p, axis=1), left)
            right = jnp.where(here, pltpu.roll(x, (Q * p + Q) % W, axis=1), right)
        to_left[pl.ds(at, n), :] = left
        to_right[pl.ds(at, n), :] = right

    def tile(i):
        at = pl.ds(i, STEP)
        planes = [ref[l, at, :] for ref in (v, cx, cy, st, via) for l in range(ref.shape[0])]
        planes += [BOND * mask[at, :].astype(F32), vp[at, :]]
        pack(planes, pl.multiple_of(i + H, 8), STEP)

    each_chunk(0, rows, tile, STEP)
    count = lo.shape[0]
    pack([lo[p] for p in range(count)] + [vlo[...]], 0, H)
    pack([hi[p] for p in range(count)] + [vhi[...]], H + rows, H)


def rows_of(ref, l=None):
    if l is None:
        return lambda s, n: ref[pl.ds(s, n), :]
    return lambda s, n: ref[l, pl.ds(s, n), :]


def weighted(x, s, n, gx, gy):
    low = pl.multiple_of(s - 8, 8)
    near = rows_of(x)(low, n + 16)
    gnear = rows_of(gx)(low, n + 8)
    c = near[8 : 8 + n]
    g = rows_of(gy)(s, n)
    up = gnear[8 : 8 + n] * near[9 : 9 + n]
    down = (gnear * near[0 : n + 8])[7 : 7 + n]
    return up + down + g * from_right(c) + from_left(g * c)


def base_kernel(*refs):
    place, v, cx, cy, st, via, mask, vp, lo, hi, vlo, vhi, f_left, f_right = refs[:14]
    refs = list(refs[14:])
    layers, rows = v.shape[0], v.shape[1]
    total = rows + 2 * H

    def take(n):
        got = refs[:n]
        del refs[:n]
        return got

    gx, gy, inv, viae = take(layers), take(layers), take(layers), take(layers - 1)
    bond, d02, d03, d11, d12, z12, d20, d21, z21, sb0, vd0, msg = take(12)
    ev, ecx, ecy, est = take(layers), take(layers), take(layers), take(layers)
    evp, side, d00, d01, d10, z10, z11, z20, e20 = take(9)
    d0 = [d00, d01, d02, d03]
    d1, z1 = [d10, d11, d12], [z10, z11, z12]
    d2, z2 = [e20, d21], [z20, z21]
    dests = [*ev, *ecx, *ecy, *est, *viae, bond, evp]
    main, edge = slice(0, W), slice(W, 2 * W)

    def sides(s):
        r = pl.multiple_of(s - H, 8)
        a = f_right[pl.ds(r, WIDE), :]
        b = f_left[pl.ds(r, WIDE), :]
        low = lanes(WIDE) < W // 2
        for p, dest in enumerate(dests):
            x = a if p == 0 else pltpu.roll(a, W - Q * p, axis=1)
            y = pltpu.roll(b, W - Q - Q * p, axis=1)
            dest[pl.ds(s, WIDE), edge] = jnp.where(low, x, y)

    each_chunk(H, total, sides, WIDE)

    def tile(i):
        a = pl.ds(i, STEP)
        xs = [ref[l, a, :] for ref in (v, cx, cy, st, via) for l in range(ref.shape[0])]
        xs += [BOND * mask[a, :].astype(F32), vp[a, :]]
        for x, dest in zip(xs, dests):
            dest[pl.ds(pl.multiple_of(i + PAD, 8), STEP), main] = x

    each_chunk(0, rows, tile, STEP)
    for p, dest in enumerate(dests):
        is_vp = p == len(dests) - 1
        dest[H : 2 * H, main] = vlo[...] if is_vp else lo[p]
        dest[PAD + rows : PAD + rows + H, main] = vhi[...] if is_vp else hi[p]

    x_first, x_total, y_first, y_total = place[0], place[1], place[2], place[3]
    col = lanes(1, 2 * W)
    col = y_first + jnp.where(col < W + W // 2, col, col - 2 * W)
    nxt = lax.rem(col + 1 + y_total, y_total)
    seam = W // 2
    keep_y = jnp.where((nxt != seam) & (nxt != seam + y_total // 2), 0.5, 0.0).astype(F32)

    def conductances(s):
        row = x_first + s - PAD + lax.broadcasted_iota(jnp.int32, (WIDE, 1), 0)
        keep_x = jnp.where((row != -1) & (row != x_total - 1), 0.5, 0.0).astype(F32)
        for l in range(layers):
            c = ecx[l][pl.ds(s, WIDE + 8), :]
            gx[l][pl.ds(s, WIDE), :] = keep_x * (c[0:WIDE] + c[1 : WIDE + 1])
            c = ecy[l][pl.ds(s, WIDE), :]
            gy[l][pl.ds(s, WIDE), :] = keep_y * (c + from_right(c))

    each_chunk(H, total, conductances, WIDE)

    def start(s):
        n = WIDE
        a = pl.ds(s, n)
        for l in range(layers):
            near = gx[l][pl.ds(pl.multiple_of(s - 8, 8), n + 8), :]
            up, down, right = near[8 : 8 + n], near[7 : 7 + n], gy[l][a, :]
            off = up + down + right + from_left(right)
            nb = weighted(ev[l], s, n, gx[l], gy[l])
            if l < layers - 1:
                off = off + viae[l][a, :]
                nb = nb + viae[l][a, :] * ev[l + 1][a, :]
            else:
                off = off + bond[a, :]
                nb = nb + bond[a, :] * evp[a, :]
            if l > 0:
                off = off + viae[l - 1][a, :]
                nb = nb + viae[l - 1][a, :] * ev[l - 1][a, :]
            c = ev[l][a, :]
            inverse = 1.0 / (est[l][a, :] + off)
            inv[l][a, :] = inverse
            d0[l][a, :] = (nb - off * c) * inverse

    each_chunk(H, total, start, WIDE)

    def links(d, l, s, n):
        nb = weighted(d[l], s, n, gx[l], gy[l])
        if l < layers - 1:
            nb = nb + viae[l][pl.ds(s, n), :] * d[l + 1][pl.ds(s, n), :]
        if l > 0:
            nb = nb + viae[l - 1][pl.ds(s, n), :] * d[l - 1][pl.ds(s, n), :]
        return inv[l][pl.ds(s, n), :] * nb

    def first(s):
        a = pl.ds(s, WIDE)
        r = pl.ds(pl.multiple_of(s - H, 8), WIDE)
        side[r, :] = d03[a, edge]
        msg[r, :] = d03[a, main]
        for l in range(layers - 1):
            z = links(d0, l, s, WIDE)
            z1[l][a, :] = z
            d1[l][a, :] = A1 * d0[l][a, :] + B1 * z

    each_chunk(H, total, first, WIDE)
    pack_side(side, msg, total)

    def second(s):
        a = pl.ds(s, WIDE)
        for l in range(2):
            z = z1[l][a, :] - d1[l][a, :] + links(d1, l, s, WIDE)
            z2[l][a, :] = z
            d2[l][a, :] = A2 * d1[l][a, :] + B2 * z

    each_chunk(H, total, second, WIDE)

    def third(s):
        a = pl.ds(s, STEP)
        o = pl.ds(pl.multiple_of(s - PAD, 8), STEP)
        nb = weighted(e20, s, STEP, gx[0], gy[0])[:, main]
        nb = inv[0][a, main] * (nb + viae[0][a, main] * d21[a, main])
        d = e20[a, main]
        z = z20[a, main] - d + nb
        d20[o, :] = d
        sb0[o, :] = v[0, o, :] + d00[a, main] + d10[a, main] + (1.0 + A3) * d + B3 * z
        for l in range(1, layers):
            vd0[l - 1, o, :] = v[l, o, :] + d0[l][a, main]

    each_chunk(PAD, rows, third, STEP)


def pack_side(side, msg, total):
    for j in range(-(-total // W)):
        t = side[W * j : W * j + W, :].T
        msg[total + 8 * j : total + 8 * j + Q, :] = t[0:Q]
        msg[total + 8 * j + Q : total + 8 * j + 2 * Q, :] = t[W - Q : W]


def unpack_side(msg, total, u, ref):
    u[...] = jnp.zeros_like(u)
    for j in range(-(-total // W)):
        u[0:Q, :] = msg[total + 8 * j : total + 8 * j + Q, :]
        u[W - Q : W, :] = msg[total + 8 * j + Q : total + 8 * j + 2 * Q, :]
        n = min(W, total - W * j)
        t = u[...].T
        ref[H + W * j : H + W * j + n, W : 2 * W] = t[:n]


def top_kernel(low, here, z, part, gx, gy, inv, via, bond, *rest):
    again = z is not None
    if again:
        d_out, z_out, msg, weight, ep, side, u = rest
    else:
        d_out, z_out, msg, ep, side, u = rest
    total = part.shape[0] - 8 * (side.shape[0] // W)
    unpack_side(part, total, u, ep)

    def body(s):
        a = pl.ds(s, WIDE)
        r = pl.ds(pl.multiple_of(s - H, 8), WIDE)
        other = jnp.concatenate([part[r, :], ep[a, W : 2 * W]], axis=1)
        nb = weighted(here, s, WIDE, gx, gy) + via[a, :] * low[a, :] + bond[a, :] * other
        c = here[a, :]
        x = inv[a, :] * nb
        if again:
            x = z[a, :] - c + x
        d = (A2 if again else A1) * c + (B2 if again else B1) * x
        z_out[a, :] = x
        d_out[a, :] = d
        if not again:
            side[r, :] = d[:, W:]
            msg[r, :] = d[:, :W]

    each_chunk(H, total, body, WIDE)
    if not again:
        pack_side(side, msg, total)
    else:
        rows = msg.shape[0]
        msg[...] = d_out[PAD : PAD + rows, 0:W]
        weight[...] = inv[PAD : PAD + rows, 0:W] * bond[PAD : PAD + rows, 0:W]


def first_top_kernel(low, here, *rest):
    top_kernel(low, here, None, *rest)


def second_top_kernel(*refs):
    top_kernel(*refs)


def final_kernel(
    v0, vd0, d11, d12, z12, e11, d13, d20, d21, d23, z21, z23,
    gx1, gx2, gx3, gy1, gy2, gy3, inv1, inv2, inv3, via0, via1, via2,
    out, d22, z22,
):
    main = slice(0, W)
    rows = out.shape[1]

    def middle(s):
        a = pl.ds(s, WIDE)
        this = d12[a, :]
        nb = weighted(d12, s, WIDE, gx2, gy2)
        nb = nb + via1[a, :] * (d11[a, :] + e11[a, :]) + via2[a, :] * d13[a, :]
        z = z12[a, :] - this + inv2[a, :] * nb
        z22[a, :] = z
        d22[a, :] = A2 * this + B2 * z

    each_chunk(H, rows + 2 * H, middle, WIDE)
    gx, gy, inv = [None, gx1, gx2, gx3], [None, gy1, gy2, gy3], [None, inv1, inv2, inv3]
    via = [via0, via1, via2]
    d2, z2 = [None, d21, d22, d23], [None, z21, z22, z23]

    def body(i):
        s = pl.multiple_of(i + PAD, 8)
        a, o = pl.ds(s, STEP), pl.ds(i, STEP)
        out[0, o, :] = v0[o, :]
        first = [None, d11[a, main] + e11[a, main], d12[a, main], d13[a, main]]
        below = d20[o, :]
        for l in range(1, 4):
            nb = weighted(d2[l], s, STEP, gx[l], gy[l])[:, main]
            nb = nb + via[l - 1][a, main] * below
            below = d2[l][a, main]
            if l < 3:
                nb = nb + via[l][a, main] * d2[l + 1][a, main]
            z = z2[l][a, main] - below + inv[l][a, main] * nb
            out[l, o, :] = vd0[l - 1, o, :] + first[l] + (1.0 + A3) * below + B3 * z

    each_chunk(0, rows, body, STEP)


def bond_kernel(field, part, weight, out):
    out[0] = field[0] + B3 * weight[...] * part[...]


def map_kernel(arrived, out, first, last, labels, vec, lab, acc, sem):
    devices = vec.shape[0]
    rows = out.shape[0]
    vec[...] = arrived[pl.ds(CAP * 8, devices, stride=ROWS_MSG), :].astype(jnp.int32)
    copy = pltpu.make_async_copy(vec, lab, sem)
    copy.start()
    acc[...] = jnp.zeros_like(acc)
    copy.wait()

    @pl.loop(0, devices // 8)
    def _(g):
        n = ROWS_MSG * 8
        data = arrived[pl.ds(pl.multiple_of(g * n, 8), n), :]
        for j in range(8):
            for r in range(CAP):
                slot = lab[g * 8 + j, r]
                labels[(g * 8 + j) * CAP + r] = slot
                a = pl.ds(pl.multiple_of(slot * 8, 8), 8)
                acc[a, :] += data[j * ROWS_MSG + r * 8 : j * ROWS_MSG + r * 8 + 8]

    out[...] = acc[0:rows, :]
    first[...] = acc[0:8, :]
    last[...] = acc[rows - 8 : rows, :]


def edges_kernel(cur, lo, hi, to_left, to_right, ext):
    rows = cur.shape[0]
    ext[0:H, :] = lo[...]
    ext[H : H + rows, :] = cur[...]
    ext[H + rows : rows + 2 * H, :] = hi[...]
    for j in range(to_left.shape[1] // W):
        t = ext[W * j : W * j + W, :].T
        to_left[:, W * j : W * j + W] = t[0:8]
        to_right[:, W * j : W * j + W] = t[W - 8 : W]


def effect_kernel(
    labels, cur, lo, hi, f_left, f_right, gx0, gx1, gy0, gy1, inv0, inv1, via0, sb0, d20, d21, z21,
    v0, picked, e11, d20_out, d21_out, z21_out,
    ec, e0, e1, z10, z11, e2, z20, e21, u, acc,
):
    rows = cur.shape[0]
    total = rows + 2 * H
    main, edge = slice(0, W), slice(W, 2 * W)
    ec[H : 2 * H, main] = lo[...]
    ec[PAD : PAD + rows, main] = cur[...]
    ec[PAD + rows : PAD + rows + H, main] = hi[...]
    u[...] = jnp.zeros_like(u)
    for j in range(f_left.shape[1] // W):
        u[0:8, :] = f_right[:, W * j : W * j + W]
        u[W - 8 : W, :] = f_left[:, W * j : W * j + W]
        n = min(W, total - W * j)
        ec[H + W * j : H + W * j + n, edge] = u[...].T[:n]

    def zeroth(s):
        a = pl.ds(s, WIDE)
        e0[a, :] = inv0[a, :] * ec[a, :]

    each_chunk(H, total, zeroth, WIDE)

    def first(s):
        a = pl.ds(s, WIDE)
        here = e0[a, :]
        z = inv0[a, :] * weighted(e0, s, WIDE, gx0, gy0)
        z10[a, :] = z
        e1[a, :] = A1 * here + B1 * z
        z = inv1[a, :] * via0[a, :] * here
        z11[a, :] = z
        e11[a, :] = B1 * z

    each_chunk(H, total, first, WIDE)

    def second(s):
        a = pl.ds(s, WIDE)
        low, high, between = e1[a, :], e11[a, :], via0[a, :]
        nb = weighted(e1, s, WIDE, gx0, gy0) + between * high
        z = z10[a, :] - low + inv0[a, :] * nb
        z20[a, :] = z
        e2[a, :] = A2 * low + B2 * z
        nb = weighted(e11, s, WIDE, gx1, gy1) + between * low
        z = z11[a, :] - high + inv1[a, :] * nb
        z21_out[a, :] = z21[a, :] + z
        d = A2 * high + B2 * z
        e21[a, :] = d
        d21_out[a, :] = d21[a, :] + d

    each_chunk(H, total, second, WIDE)

    def third(i):
        s = pl.multiple_of(i + PAD, 8)
        a, o = pl.ds(s, STEP), pl.ds(i, STEP)
        here = e2[a, main]
        nb = weighted(e2, s, STEP, gx0, gy0)[:, main] + via0[a, main] * e21[a, main]
        z = z20[a, main] - here + inv0[a, main] * nb
        whole = sb0[o, :] + e0[a, main] + e1[a, main] + (1.0 + A3) * here + B3 * z
        v0[o, :] = whole
        acc[o, :] = whole
        d20_out[o, :] = d20[o, :] + here

    each_chunk(0, rows, third, STEP)
    acc[rows : rows + 8, :] = jnp.zeros((8, W), F32)

    @pl.loop(0, labels.shape[0], unroll=8)
    def _(k):
        picked[pl.ds(pl.multiple_of(k * 8, 8), 8), :] = acc[
            pl.ds(pl.multiple_of(labels[k] * 8, 8), 8), :
        ]


def give_kernel(dest, back, out):
    @pl.loop(0, out.shape[0], unroll=8)
    def _(k):
        out[k] = back[pl.ds(pl.multiple_of(dest[k] * 8, 8), 8), :]


def ring(axis, step):
    n = lax.axis_size(axis)
    return [(i, (i + step) % n) for i in range(n)]


def shift(x, axis, step):
    return lax.ppermute(x, axis, ring(axis, step))


def facing(x, step=0):
    n, m = lax.axis_size("gx"), lax.axis_size("yt")
    pairs = [
        (g * m + t, ((g + step) % n) * m + (t ^ (m // 2))) for g in range(n) for t in range(m)
    ]
    return lax.ppermute(x, ALL, pairs)


def on_device(v, st, cx, cy, via, mask, blocks, owner, slot):
    layers, rows, cols = v.shape
    devices = lax.axis_size("gx") * lax.axis_size("yt")
    nb = blocks.shape[0]
    total = rows + 2 * H
    nr = total + 2 * H
    side_blocks = -(-total // W)
    place = jnp.stack(
        [
            lax.axis_index("gx") * rows,
            jnp.int32(rows * lax.axis_size("gx")),
            lax.axis_index("yt") * cols,
            jnp.int32(cols * lax.axis_size("yt")),
        ]
    ).astype(jnp.int32)

    outgoing, dest = call(
        send_kernel,
        [shape(devices * ROWS_MSG, W), jax.ShapeDtypeStruct((nb,), jnp.int32)],
        [owner.reshape(nb), slot, blocks],
        scratch=[
            pltpu.SMEM((devices,), jnp.int32),
            pltpu.VMEM((devices * CAP * 8, W), F32),
            pltpu.VMEM((devices, W), jnp.int32),
        ],
        specs={0: SMEM, 1: SMEM},
        out_specs=[pl.BlockSpec(memory_space=pltpu.VMEM), SMEM],
    )
    sources = [v, cx, cy, st, via]
    args = sources + [mask] + sources + [mask, v]
    specs = {}
    last = rows // 8 - 1
    for i in range(5):
        n = sources[i].shape[0]
        specs[i] = pl.BlockSpec((n, 8, W), lambda _: (0, 0, 0))
        specs[6 + i] = pl.BlockSpec((n, 8, W), lambda _: (0, last, 0))
    specs[5] = pl.BlockSpec((8, W), lambda _: (0, 0))
    specs[11] = pl.BlockSpec((8, W), lambda _: (last, 0))
    specs[12] = pl.BlockSpec((1, rows, W), lambda _: (layers - 1, 0, 0))
    count = 5 * layers
    first_rows, last_rows, v_top, v_first, v_last = pl.pallas_call(
        pack_x_kernel,
        grid=(1,),
        out_shape=[shape(count, 8, W)] * 2 + [shape(rows, W), shape(H, W), shape(H, W)],
        in_specs=[specs[i] for i in range(13)],
        out_specs=[
            pl.BlockSpec((count, 8, W), lambda _: (0, 0, 0)),
            pl.BlockSpec((count, 8, W), lambda _: (0, 0, 0)),
            pl.BlockSpec((rows, W), lambda _: (0, 0)),
            pl.BlockSpec((H, W), lambda _: (0, 0)),
            pl.BlockSpec((H, W), lambda _: (0, 0)),
        ],
        name="pack_x_kernel",
        compiler_params=pltpu.CompilerParams(vmem_limit_bytes=58 << 20),
        cost_estimate=pl.CostEstimate(flops=1, bytes_accessed=1_000_000, transcendentals=0),
    )(*args)
    lo = shift(last_rows, "gx", 1)
    hi = shift(first_rows, "gx", -1)
    v_part = facing(v_top)
    v_lo, v_hi = facing(v_last, 1), facing(v_first, -1)
    tiles = [v, cx, cy, st, via, mask, v_part, lo, hi, v_lo, v_hi]
    to_left, to_right = call(pack_y_kernel, [shape(total, W), shape(total, W)], tiles, vmem=8)
    f_left = shift(to_right, "yt", 1)
    f_right = shift(to_left, "yt", -1)
    outgoing, f_left, f_right = lax.optimization_barrier((outgoing, f_left, f_right))
    arrived = lax.all_to_all(
        outgoing.reshape(devices, ROWS_MSG, 1, W), ALL, 0, 0, tiled=True
    ).reshape(devices * ROWS_MSG, W)

    one = shape(nr, 2 * W)
    tile = shape(rows, W)
    buffer = lambda *d: pltpu.VMEM(d, F32)
    msg_shape = shape(total + 8 * side_blocks, W)
    outs = call(
        base_kernel,
        [one] * (4 * layers + 5) + [tile, one, one, tile, shape(layers - 1, rows, W), msg_shape],
        [place, *tiles, f_left, f_right],
        scratch=[buffer(nr, 2 * W)] * (4 * layers + 1)
        + [buffer(side_blocks * W, W)]
        + [buffer(nr, 2 * W)] * 7,
        specs={0: SMEM},
        vmem=VMEM_BASE,
        cost=20_000_000,
    )
    gx, gy, inv, via_e = outs[0:4], outs[4:8], outs[8:12], outs[12:15]
    bond, d02, d03, d11, d12, z12, d20, d21, z21, sb0, vd0, msg0 = outs[15:]
    part0 = facing(msg0)

    cur, cur_first, cur_last, labels = call(
        map_kernel,
        [tile, shape(8, W), shape(8, W), jax.ShapeDtypeStruct((devices * CAP,), jnp.int32)],
        [arrived],
        scratch=[
            pltpu.VMEM((devices, W), jnp.int32),
            pltpu.SMEM((devices, W), jnp.int32),
            buffer(rows + 8, W),
            pltpu.SemaphoreType.DMA,
        ],
        out_specs=[pl.BlockSpec(memory_space=pltpu.VMEM)] * 3 + [SMEM],
    )
    cur_lo = shift(cur_last, "gx", 1)
    cur_hi = shift(cur_first, "gx", -1)
    cur_lo, cur_hi, part0 = lax.optimization_barrier((cur_lo, cur_hi, part0))
    top = [gx[3], gy[3], inv[3], via_e[2], bond]
    d13, z13, msg1 = call(
        first_top_kernel,
        [one, one, msg_shape],
        [d02, d03, part0, *top],
        scratch=[buffer(nr, 2 * W), buffer(side_blocks * W, W), buffer(W, W)],
        vmem=VMEM_TOP,
    )
    part1 = facing(msg1)
    d23, z23, msg2, weight = call(
        second_top_kernel,
        [one, one, tile, tile],
        [d12, d13, z13, part1, *top],
        scratch=[buffer(nr, 2 * W), buffer(side_blocks * W, W), buffer(W, W)],
        vmem=VMEM_TOP,
    )

    cur_left, cur_right = call(
        edges_kernel,
        [shape(8, side_blocks * W)] * 2,
        [cur, cur_lo, cur_hi],
        scratch=[buffer(side_blocks * W, W)],
    )
    cur_f_left = shift(cur_right, "yt", 1)
    cur_f_right = shift(cur_left, "yt", -1)
    v0, picked, e11, d20, d21, z21 = call(
        effect_kernel,
        [tile, shape(devices * CAP * 8, W), one, tile, one, one],
        [labels, cur, cur_lo, cur_hi, cur_f_left, cur_f_right, *gx[:2], *gy[:2], *inv[:2],
         via_e[0], sb0, d20, d21, z21],
        scratch=[buffer(nr, 2 * W)] * 8 + [buffer(W, W), buffer(rows + 8, W)],
        specs={0: SMEM},
        vmem=VMEM_EFFECT,
    )
    part2 = facing(msg2)
    back = lax.all_to_all(picked, ALL, 0, 0, tiled=True)

    voltage = call(
        final_kernel,
        shape(layers, rows, W),
        [v0, vd0, d11, d12, z12, e11, d13, d20, d21, d23, z21, z23,
         *gx[1:], *gy[1:], *inv[1:], *via_e],
        scratch=[buffer(nr, 2 * W)] * 2,
        vmem=VMEM_FINAL,
        cost=10_000_000,
    )
    voltage = pl.pallas_call(
        bond_kernel,
        grid=(1,),
        out_shape=shape(layers, rows, W),
        in_specs=[
            pl.BlockSpec((1, rows, W), lambda _: (layers - 1, 0, 0)),
            pl.BlockSpec((rows, W), lambda _: (0, 0)),
            pl.BlockSpec((rows, W), lambda _: (0, 0)),
        ],
        out_specs=pl.BlockSpec((1, rows, W), lambda _: (layers - 1, 0, 0)),
        input_output_aliases={0: 0},
        name="bond_kernel",
        compiler_params=pltpu.CompilerParams(vmem_limit_bytes=6 << 20),
    )(voltage, part2, weight)
    block_voltage = call(
        give_kernel, shape(nb, 8, W), [dest, back], specs={0: SMEM}
    )
    return voltage, block_voltage


def solution(mesh):
    tile = P(None, "gx", "yt")
    return jax.shard_map(
        on_device,
        mesh=mesh,
        in_specs=(tile, tile, tile, tile, tile, P("gx", "yt"), P(ALL, None, None), P(ALL, None), P(ALL)),
        out_specs=(tile, P(ALL, None, None)),
        check_vma=False,
    )
```

time: 207 us -> 143 us (0.69)
  waiting for transfers between devices: 52.7 us -> 25.4 us
  Pallas kernels: 85.6 us -> 63.3 us
  local copies, waits for them, and re-layouts: 18.8 us -> 2.66 us
  starting transfers between devices: 46.8 us -> 49.7 us
    pallas_call x10, Pallas kernels: 83.6 us -> 59.7 us  [call(): pl.pallas_call(kernel, out_shape=outs if many else outs[0], in_specs=in_s...]
    ppermute x5 -> x6, waiting for transfers between devices: 37.5 us -> 14.3 us  [facing(): return lax.ppermute(x, ALL, pairs)]
    unnamed x64 -> x50, local copies, waits for them, and re-layouts: 16.2 us -> 2.66 us
    ppermute x5 -> x6, starting transfers between devices: 7.63 us -> 14.2 us  [facing(): return lax.ppermute(x, ALL, pairs)]
    ppermute x8, waiting for transfers between devices: 15.2 us -> 11 us  [shift(): return lax.ppermute(x, axis, ring(axis, step))]
    all_to_all x2 -> x0, local copies, waits for them, and re-layouts: 2.69 us -> none  [on_device(): arrived = lax.all_to_all(outgoing, ALL, 0, 0, tiled=True)]
  transfers between devices with their start and end apart: 15 -> 16, of which waited for: 6 -> 9; matrix products, arithmetic and copies ran while one was open for 0% -> 0% of each run, Pallas kernels for 32% -> 33%
where the time goes in v2:
time: 143 us
  Pallas kernels  63.3 us (44%)
  starting transfers between devices  49.7 us (35%)
  waiting for transfers between devices  25.4 us (18%)
  local copies, waits for them, and re-layouts  2.66 us (2%)
    pallas_call x10, Pallas kernels, call(): pl.pallas_call(kernel, out_shape=outs if many else outs[0], in_specs=in_s...  59.7 us
    ppermute x6, waiting for transfers between devices, facing(): return lax.ppermute(x, ALL, pairs)  14.3 us
    ppermute x6, starting transfers between devices, facing(): return lax.ppermute(x, ALL, pairs)  14.2 us
    ppermute x8, starting transfers between devices, shift(): return lax.ppermute(x, axis, ring(axis, step))  13.8 us
    ppermute x8, waiting for transfers between devices, shift(): return lax.ppermute(x, axis, ring(axis, step))  11 us
    all_to_all x1, starting transfers between devices, on_device(): back = lax.all_to_all(picked, ALL, 0, 0, tiled=True)  11 us
    all_to_all x1, starting transfers between devices, on_device(): lax.all_to_all(outgoing.reshape(devices, ROWS_MSG, 1, W), ALL, 0, 0, tile...  10.7 us
  transfers between devices with their start and end apart: 16, of which 9 were waited for; matrix products, arithmetic and copies ran while one was open for 0% of the time, Pallas kernels for 33%

profile of v2, /device:TPU:1, one launch (start us, length us, event | category | flops | bytes accessed | tf_op | source)
XLA Modules:
  0.0 142.5 jit_solution(15418209474496150051)
XLA Ops:
  0.7 2.0 %pack_x_kernel.1 = (f32[20,8,128]{2,1,0:T(8,128)}, f32[20,8,128]{2,1,0:T(8,128)}, f32[512,128]{1,0:T(8,128)}, f32[8,128]{1,0:T(8,128)}, f32[8,128]{1,0:T(8,128)}) custom-call(f32[4,512,128]{2,1,0:T(8,128)} %refs_1_.3, f32[4,512,128]{2,1,0:T(8,128)} %refs_2_.3, f32[4,512,128]{2,1,0:T(8,128)} %refs_3_.3, f32[4,512,128]{2,1,0:T(8,128)} %refs_4_.3, ...), custom_call_target="tpu_custom_call" | custom-call | flops 1 | bytes 1000000 | tf_op jit(solution)/shard_map/pack_x_kernel/pallas_call | solution.py:580
  2.7 3.6 %collective-permute-start = (f32[512,128]{1,0:T(8,128)}, f32[512,128]{1,0:T(8,128)S(1)}, u32[]{:S(2)}, u32[]{:S(2)}) collective-permute-start(f32[512,128]{1,0:T(8,128)} %get-tuple-element.64), channel_id=1, source_target_pairs={{0,8},{1,9},{2,10},{3,11},{4,12},{5,13},{6,14},{7,15},{8,0},{9,1},... | collective-permute-start | bytes 786440 | tf_op jit(solution)/shard_map/ppermute | solution.py:537
  6.6 3.5 %collective-permute-start.2 = (f32[20,8,128]{2,1,0:T(8,128)}, f32[20,8,128]{2,1,0:T(8,128)S(1)}, u32[]{:S(2)}, u32[]{:S(2)}) collective-permute-start(f32[20,8,128]{2,1,0:T(8,128)} %get-tuple-element.66), channel_id=1, source_target_pairs={{0,112},{16,0},{32,16},{48,32},{64,48},{80,64},{96,80},{112,96},{1... | collective-permute-start | bytes 245768 | tf_op jit(solution)/shard_map/ppermute | solution.py:529
  10.1 4.8 %collective-permute-start.4 = (f32[8,128]{1,0:T(8,128)}, f32[8,128]{1,0:T(8,128)S(1)}, u32[]{:S(2)}, u32[]{:S(2)}) collective-permute-start(f32[8,128]{1,0:T(8,128)} %get-tuple-element.68), channel_id=1, source_target_pairs={{0,120},{1,121},{2,122},{3,123},{4,124},{5,125},{6,126},{7,127},{8... | collective-permute-start | bytes 12296 | tf_op jit(solution)/shard_map/ppermute | solution.py:537
  14.8 1.2 collective-permute-done.3.vlo.refs_10_
  16.1 1.6 %collective-permute-done.1.lo.refs_8_ = f32[20,8,128]{2,1,0:T(8,128)S(1)} collective-permute-done((f32[20,8,128]{2,1,0:T(8,128)}, f32[20,8,128]{2,1,0:T(8,128)S(1)}, u32[]{:S(2)}, u32[]{:S(2)}) %collective-permute-start.1) | collective-permute-done | bytes 81952 | tf_op jit(solution)/shard_map/ppermute | solution.py:529
  17.8 3.5 %pack_y_kernel.1 = (f32[528,128]{1,0:T(8,128)S(1)}, f32[528,128]{1,0:T(8,128)S(1)}) custom-call(f32[4,512,128]{2,1,0:T(8,128)S(1)} %copy-done, f32[4,512,128]{2,1,0:T(8,128)S(1)} %copy-done.1, f32[4,512,128]{2,1,0:T(8,128)S(1)} %copy-done.2, f32[4,512,128]{2,1,0:T(8,128)S(1)} %copy-done.3, f32[3,512,128]{2,1,0:T(8,128)S(1)} %copy-done.4, ...), custom_call_target="tpu_custom_call" | custom-call | flops 1000000 | bytes 1000000 | tf_op jit(solution)/shard_map/pack_y_kernel/pallas_call | solution.py:42
  21.3 3.7 %collective-permute-start.5 = (f32[528,128]{1,0:T(8,128)S(1)}, f32[528,128]{1,0:T(8,128)S(1)}, u32[]{:S(2)}, u32[]{:S(2)}) collective-permute-start(f32[528,128]{1,0:T(8,128)S(1)} %get-tuple-element.69), channel_id=1, source_target_pairs={{0,1},{1,2},{2,3},{3,4},{4,5},{5,6},{6,7},{7,8},{8,9},{9,10},{10,1... | collective-permute-start | bytes 811016 | tf_op jit(solution)/shard_map/ppermute | solution.py:529
  25.0 2.7 %send_kernel.1 = (f32[2176,128]{1,0:T(8,128)}, s32[128]{0:T(128)S(1)}) custom-call(s32[128]{0:T(128)S(1)} %bitcast.9, s32[128]{0:T(128)S(1)} %copy-done.18, f32[128,8,128]{2,1,0:T(8,128)S(1)} %copy-done.8), custom_call_target="tpu_custom_call" | custom-call | flops 1000000 | bytes 1000000 | tf_op jit(solution)/shard_map/send_kernel/pallas_call | solution.py:42
  27.8 0.7 collective-permute-done.5.refs_12_
  28.4 2.8 %collective-permute-done.6.refs_13_ = f32[528,128]{1,0:T(8,128)S(1)} collective-permute-done((f32[528,128]{1,0:T(8,128)S(1)}, f32[528,128]{1,0:T(8,128)S(1)}, u32[]{:S(2)}, u32[]{:S(2)}) %collective-permute-start.6) | collective-permute-done | bytes 270368 | tf_op jit(solution)/shard_map/ppermute | solution.py:529
  31.2 0.7 copy-done.22
  31.9 10.7 %all-to-all-start = ((f32[128,17,1,128]{3,2,1,0:T(1,128)}), f32[128,17,1,128]{3,2,1,0:T(1,128)S(1)}, u32[]{:S(2)}, u32[]{:S(2)}) async-start(f32[128,17,1,128]{3,2,1,0:T(1,128)} %bitcast.1), calls=%async_computation | async-start | bytes 2228224 | tf_op jit(solution)/shard_map/all_to_all | solution.py:605
  43.2 21.9 %base_kernel.1 = (f32[544,256]{1,0:T(8,128)}, f32[544,256]{1,0:T(8,128)}, f32[544,256]{1,0:T(8,128)}, f32[544,256]{1,0:T(8,128)}, f32[544,256]{1,0:T(8,128)}, /*...) custom-call(s32[4]{0:T(128)} %pad_add_fusion.refs_0_, ...), custom_call_target="tpu_custom_call" | custom-call | flops 20000000 | bytes 20000000 | tf_op jit(solution)/shard_map/base_kernel/pallas_call | solution.py:42
  65.1 3.0 %collective-permute-start.9 = (f32[568,128]{1,0:T(8,128)}, f32[568,128]{1,0:T(8,128)S(1)}, u32[]{:S(2)}, u32[]{:S(2)}) collective-permute-start(f32[568,128]{1,0:T(8,128)} %get-tuple-element.78), channel_id=1, source_target_pairs={{0,8},{1,9},{2,10},{3,11},{4,12},{5,13},{6,14},{7,15},{8,0},{9,1},... | collective-permute-start | bytes 872456 | tf_op jit(solution)/shard_map/ppermute | solution.py:537
  68.1 3.1 %map_kernel.1 = (f32[512,128]{1,0:T(8,128)S(1)}, f32[8,128]{1,0:T(8,128)S(1)}, f32[8,128]{1,0:T(8,128)S(1)}, s32[256]{0:T(256)S(1)}) custom-call(f32[2176,128]{1,0:T(8,128)S(1)} %bitcast.7), custom_call_target="tpu_custom_call" | custom-call | flops 1000000 | bytes 1000000 | tf_op jit(solution)/shard_map/map_kernel/pallas_call | solution.py:42
  72.2 3.2 %collective-permute-start.8 = (f32[8,128]{1,0:T(8,128)S(1)}, f32[8,128]{1,0:T(8,128)S(1)}, u32[]{:S(2)}, u32[]{:S(2)}) collective-permute-start(f32[8,128]{1,0:T(8,128)S(1)} %get-tuple-element.75), channel_id=1, source_target_pairs={{0,112},{16,0},{32,16},{48,32},{64,48},{80,64},{96,80},{112,96},{1... | collective-permute-start | bytes 12296 | tf_op jit(solution)/shard_map/ppermute | solution.py:529
  75.4 2.5 %collective-permute-done.7.lo = f32[8,128]{1,0:T(8,128)S(1)} collective-permute-done((f32[8,128]{1,0:T(8,128)S(1)}, f32[8,128]{1,0:T(8,128)S(1)}, u32[]{:S(2)}, u32[]{:S(2)}) %collective-permute-start.7) | collective-permute-done | bytes 4128 | tf_op jit(solution)/shard_map/ppermute | solution.py:529
  78.0 2.7 %collective-permute-start.10 = (f32[8,640]{1,0:T(8,128)S(1)}, f32[8,640]{1,0:T(8,128)S(1)}, u32[]{:S(2)}, u32[]{:S(2)}) collective-permute-start(f32[8,640]{1,0:T(8,128)S(1)} %get-tuple-element.81), channel_id=1, source_target_pairs={{0,1},{1,2},{2,3},{3,4},{4,5},{5,6},{6,7},{7,8},{8,9},{9,10},{10,1... | collective-permute-start | bytes 61448 | tf_op jit(solution)/shard_map/ppermute | solution.py:529
  80.8 0.9 collective-permute-done.10.f_left
  81.7 2.6 %collective-permute-done.11.f_right = f32[8,640]{1,0:T(8,128)S(1)} collective-permute-done((f32[8,640]{1,0:T(8,128)S(1)}, f32[8,640]{1,0:T(8,128)S(1)}, u32[]{:S(2)}, u32[]{:S(2)}) %collective-permute-start.11) | collective-permute-done | bytes 20512 | tf_op jit(solution)/shard_map/ppermute | solution.py:529
  84.3 0.6 copy-done.24
  84.9 8.7 %effect_kernel.1 = (f32[512,128]{1,0:T(8,128)}, f32[2048,128]{1,0:T(8,128)}, f32[544,256]{1,0:T(8,128)}, f32[512,128]{1,0:T(8,128)}, f32[544,256]{1,0:T(8,128)}, /*index=5*/f32[544,256]{1,0:T(8,128)}) custom-call(s32[256]{0:T(256)} %copy-done.16, f32[512,128]{1,0:T(8,128)} %copy-done.7, f32[8,128]{1,0:T(8,128)} %copy-done.12, f32[8,128]{1,0:T(8,128)} %copy-done.13, ...), custom_call_target="tpu_custom_call" | custom-call | flops 1000000 | bytes 1000000 | tf_op jit(solution)/shard_map/effect_kernel/pallas_call | solution.py:42
  93.5 11.0 %all-to-all-start.1 = ((f32[128,16,128]{2,1,0:T(8,128)}), f32[128,16,128]{2,1,0:T(8,128)S(1)}, u32[]{:S(2)}, u32[]{:S(2)}) async-start(f32[128,16,128]{2,1,0:T(8,128)} %bitcast.10), calls=%async_computation.1 | async-start | bytes 2097152 | tf_op jit(solution)/shard_map/all_to_all | solution.py:678
  104.5 4.7 %first_top_kernel.1 = (f32[544,256]{1,0:T(8,128)}, f32[544,256]{1,0:T(8,128)}, f32[568,128]{1,0:T(8,128)}) custom-call(f32[544,256]{1,0:T(8,128)} %get-tuple-element.100.low, f32[544,256]{1,0:T(8,128)} %get-tuple-element.101.here, f32[568,128]{1,0:T(8,128)} %copy-done.19, f32[544,256]{1,0:T(8,128)} %get-tuple-element.103.rest_1_.refs_4_.gx3, ...), custom_call_target="tpu_custom_call" | custom-call | flops 1000000 | bytes 1000000 | tf_op jit(solution)/shard_map/first_top_kernel/pallas_call | solution.py:42
  109.2 2.9 %collective-permute-start.12 = (f32[568,128]{1,0:T(8,128)}, f32[568,128]{1,0:T(8,128)S(1)}, u32[]{:S(2)}, u32[]{:S(2)}) collective-permute-start(f32[568,128]{1,0:T(8,128)} %get-tuple-element.112), channel_id=1, source_target_pairs={{0,8},{1,9},{2,10},{3,11},{4,12},{5,13},{6,14},{7,15},{8,0},{9,1},... | collective-permute-start | bytes 872456 | tf_op jit(solution)/shard_map/ppermute | solution.py:537
  112.1 12.9 %collective-permute-done.12.refs_3_ = f32[568,128]{1,0:T(8,128)S(1)} collective-permute-done((f32[568,128]{1,0:T(8,128)}, f32[568,128]{1,0:T(8,128)S(1)}, u32[]{:S(2)}, u32[]{:S(2)}) %collective-permute-start.12) | collective-permute-done | bytes 290848 | tf_op jit(solution)/shard_map/ppermute | solution.py:537
  125.0 0.7 copy-done.20
  125.7 4.9 %second_top_kernel.1 = (f32[544,256]{1,0:T(8,128)}, f32[544,256]{1,0:T(8,128)}, f32[512,128]{1,0:T(8,128)}, f32[512,128]{1,0:T(8,128)}) custom-call(f32[544,256]{1,0:T(8,128)} %get-tuple-element.97.refs_0_.d12, f32[544,256]{1,0:T(8,128)} %get-tuple-element.108.refs_1_.d13, f32[544,256]{1,0:T(8,128)} %get-tuple-element.111.refs_2_, f32[568,128]{1,0:T(8,128)} %copy-done.20, ...), custom_call_target="tpu_custom_call" | custom-call | flops 1000000 | bytes 1000000 | tf_op jit(solution)/shard_map/second_top_kernel/pallas_call | solution.py:42
  130.6 8.5 %final_kernel.1.field = f32[4,512,128]{2,1,0:T(8,128)} custom-call(f32[512,128]{1,0:T(8,128)} %get-tuple-element.94.v0, f32[3,512,128]{2,1,0:T(8,128)} %get-tuple-element.95.vd0, f32[544,256]{1,0:T(8,128)} %get-tuple-element.96.d11, f32[544,256]{1,0:T(8,128)} %get-tuple-element.97.refs_0_.d12, f32[544,256]{1,0:T(8,128)} %get-tuple-element.98.z12, ...), custom_call_target="tpu_custom_call" | custom-call | flops 10000000 | bytes 10000000 | tf_op jit(solution)/shard_map/final_kernel/pallas_call | solution.py:42
  139.3 1.7 %bond_kernel.1 = f32[4,512,128]{2,1,0:T(8,128)} custom-call(f32[4,512,128]{2,1,0:T(8,128)} %final_kernel.1.field, f32[512,128]{1,0:T(8,128)S(1)} %collective-permute-done.13.part, f32[512,128]{1,0:T(8,128)S(1)} %copy-done.11), custom_call_target="tpu_custom_call", output_to_operand_aliasing={{}: (0, {})} | custom-call | tf_op jit(solution)/shard_map/bond_kernel/pallas_call | solution.py:689
  141.0 1.6 %give_kernel.1 = f32[128,8,128]{2,1,0:T(8,128)} custom-call(s32[128]{0:T(128)S(1)} %get-tuple-element.122.dest, f32[2048,128]{1,0:T(8,128)S(1)} %bitcast.8), custom_call_target="tpu_custom_call" | custom-call | flops 1000000 | bytes 1000000 | tf_op jit(solution)/shard_map/give_kernel/pallas_call | solution.py:42
  (63 shorter events, 2.3 us)
Async XLA Ops:
  0.6 17.1 %copy-start.5 = (s32[512,128]{1,0:T(8,128)S(1)}, s32[512,128]{1,0:T(8,128)}, u32[]{:S(2)}) copy-start(s32[512,128]{1,0:T(8,128)} %refs_6_.3) | copy-start | bytes 786436
  0.6 17.1 %copy-start.4 = (f32[3,512,128]{2,1,0:T(8,128)S(1)}, f32[3,512,128]{2,1,0:T(8,128)}, u32[]{:S(2)}) copy-start(f32[3,512,128]{2,1,0:T(8,128)} %refs_5_.3) | copy-start | bytes 2359300
  0.7 17.1 %copy-start.2 = (f32[4,512,128]{2,1,0:T(8,128)S(1)}, f32[4,512,128]{2,1,0:T(8,128)}, u32[]{:S(2)}) copy-start(f32[4,512,128]{2,1,0:T(8,128)} %refs_3_.3) | copy-start | bytes 3145732
  0.7 17.1 %copy-start.1 = (f32[4,512,128]{2,1,0:T(8,128)S(1)}, f32[4,512,128]{2,1,0:T(8,128)}, u32[]{:S(2)}) copy-start(f32[4,512,128]{2,1,0:T(8,128)} %refs_2_.3) | copy-start | bytes 3145732
  0.7 17.1 %copy-start.3 = (f32[4,512,128]{2,1,0:T(8,128)S(1)}, f32[4,512,128]{2,1,0:T(8,128)}, u32[]{:S(2)}) copy-start(f32[4,512,128]{2,1,0:T(8,128)} %refs_4_.3) | copy-start | bytes 3145732
  0.7 17.1 %copy-start = (f32[4,512,128]{2,1,0:T(8,128)S(1)}, f32[4,512,128]{2,1,0:T(8,128)}, u32[]{:S(2)}) copy-start(f32[4,512,128]{2,1,0:T(8,128)} %refs_1_.3) | copy-start | bytes 3145732
  2.7 15.0 %collective-permute-start = (f32[512,128]{1,0:T(8,128)}, f32[512,128]{1,0:T(8,128)S(1)}, u32[]{:S(2)}, u32[]{:S(2)}) collective-permute-start(f32[512,128]{1,0:T(8,128)} %get-tuple-element.64), channel_id=1, source_target_pairs={{0,8},{1,9},{2,10},{3,11},{4,12},{5,13},{6,14},{7,15},{8,0},{9,1},... | collective-permute-start | bytes 786440 | tf_op jit(solution)/shard_map/ppermute | solution.py:537
  6.2 11.5 %collective-permute-start.1 = (f32[20,8,128]{2,1,0:T(8,128)}, f32[20,8,128]{2,1,0:T(8,128)S(1)}, u32[]{:S(2)}, u32[]{:S(2)}) collective-permute-start(f32[20,8,128]{2,1,0:T(8,128)} %get-tuple-element.65), channel_id=1, source_target_pairs={{0,16},{16,32},{32,48},{48,64},{64,80},{80,96},{96,112},{112,0},{1... | collective-permute-start | bytes 245768 | tf_op jit(solution)/shard_map/ppermute | solution.py:529
  6.6 11.2 %collective-permute-start.2 = (f32[20,8,128]{2,1,0:T(8,128)}, f32[20,8,128]{2,1,0:T(8,128)S(1)}, u32[]{:S(2)}, u32[]{:S(2)}) collective-permute-start(f32[20,8,128]{2,1,0:T(8,128)} %get-tuple-element.66), channel_id=1, source_target_pairs={{0,112},{16,0},{32,16},{48,32},{64,48},{80,64},{96,80},{112,96},{1... | collective-permute-start | bytes 245768 | tf_op jit(solution)/shard_map/ppermute | solution.py:529
  10.0 6.0 %collective-permute-start.3 = (f32[8,128]{1,0:T(8,128)}, f32[8,128]{1,0:T(8,128)S(1)}, u32[]{:S(2)}, u32[]{:S(2)}) collective-permute-start(f32[8,128]{1,0:T(8,128)} %get-tuple-element.67), channel_id=1, source_target_pairs={{0,24},{1,25},{2,26},{3,27},{4,28},{5,29},{6,30},{7,31},{8,16},{9,... | collective-permute-start | bytes 12296 | tf_op jit(solution)/shard_map/ppermute | solution.py:537
  10.0 15.0 %copy-start.8 = (f32[128,8,128]{2,1,0:T(8,128)S(1)}, f32[128,8,128]{2,1,0:T(8,128)}, u32[]{:S(2)}) copy-start(f32[128,8,128]{2,1,0:T(8,128)} %blocks_ref.1) | copy-start | bytes 1572868
  10.0 15.0 %copy-start.17 = (s32[128,1]{0,1:T(1,128)S(1)}, s32[128,1]{0,1:T(1,128)}, u32[]{:S(2)}) copy-start(s32[128,1]{0,1:T(1,128)} %param.16) | copy-start | bytes 1540
  10.0 15.0 %copy-start.18 = (s32[128]{0:T(128)S(1)}, s32[128]{0:T(128)}, u32[]{:S(2)}) copy-start(s32[128]{0:T(128)} %slot_ref.1) | copy-start | bytes 1540
  10.1 6.0 %collective-permute-start.4 = (f32[8,128]{1,0:T(8,128)}, f32[8,128]{1,0:T(8,128)S(1)}, u32[]{:S(2)}, u32[]{:S(2)}) collective-permute-start(f32[8,128]{1,0:T(8,128)} %get-tuple-element.68), channel_id=1, source_target_pairs={{0,120},{1,121},{2,122},{3,123},{4,124},{5,125},{6,126},{7,127},{8... | collective-permute-start | bytes 12296 | tf_op jit(solution)/shard_map/ppermute | solution.py:537
  16.1 5.2 %copy-start.14 = (f32[8,128]{1,0:T(8,128)}, f32[8,128]{1,0:T(8,128)S(1)}, u32[]{:S(2)}) copy-start(f32[8,128]{1,0:T(8,128)S(1)} %collective-permute-done.3.vlo.refs_10_) | copy-start | bytes 12292
  16.1 5.2 %copy-start.15 = (f32[8,128]{1,0:T(8,128)}, f32[8,128]{1,0:T(8,128)S(1)}, u32[]{:S(2)}) copy-start(f32[8,128]{1,0:T(8,128)S(1)} %collective-permute-done.4.vhi.refs_11_) | copy-start | bytes 12292
  21.3 7.1 %collective-permute-start.5 = (f32[528,128]{1,0:T(8,128)S(1)}, f32[528,128]{1,0:T(8,128)S(1)}, u32[]{:S(2)}, u32[]{:S(2)}) collective-permute-start(f32[528,128]{1,0:T(8,128)S(1)} %get-tuple-element.69), channel_id=1, source_target_pairs={{0,1},{1,2},{2,3},{3,4},{4,5},{5,6},{6,7},{7,8},{8,9},{9,10},{10,1... | collective-permute-start | bytes 811016 | tf_op jit(solution)/shard_map/ppermute | solution.py:529
  25.0 6.2 %collective-permute-start.6 = (f32[528,128]{1,0:T(8,128)S(1)}, f32[528,128]{1,0:T(8,128)S(1)}, u32[]{:S(2)}, u32[]{:S(2)}) collective-permute-start(f32[528,128]{1,0:T(8,128)S(1)} %get-tuple-element.70), channel_id=1, source_target_pairs={{0,15},{1,0},{2,1},{3,2},{4,3},{5,4},{6,5},{7,6},{8,7},{9,8},{10,9... | collective-permute-start | bytes 811016 | tf_op jit(solution)/shard_map/ppermute | solution.py:529
  31.9 36.2 %all-to-all-start = ((f32[128,17,1,128]{3,2,1,0:T(1,128)}), f32[128,17,1,128]{3,2,1,0:T(1,128)S(1)}, u32[]{:S(2)}, u32[]{:S(2)}) async-start(f32[128,17,1,128]{3,2,1,0:T(1,128)} %bitcast.1), calls=%async_computation | async-start | bytes 2228224 | tf_op jit(solution)/shard_map/all_to_all | solution.py:605
  65.1 10.3 %collective-permute-start.9 = (f32[568,128]{1,0:T(8,128)}, f32[568,128]{1,0:T(8,128)S(1)}, u32[]{:S(2)}, u32[]{:S(2)}) collective-permute-start(f32[568,128]{1,0:T(8,128)} %get-tuple-element.78), channel_id=1, source_target_pairs={{0,8},{1,9},{2,10},{3,11},{4,12},{5,13},{6,14},{7,15},{8,0},{9,1},... | collective-permute-start | bytes 872456 | tf_op jit(solution)/shard_map/ppermute | solution.py:537
  71.8 12.4 %copy-start.7 = (f32[512,128]{1,0:T(8,128)}, f32[512,128]{1,0:T(8,128)S(1)}, u32[]{:S(2)}) copy-start(f32[512,128]{1,0:T(8,128)S(1)} %get-tuple-element.73.cur) | copy-start | bytes 786436
  71.8 6.0 %collective-permute-start.7 = (f32[8,128]{1,0:T(8,128)S(1)}, f32[8,128]{1,0:T(8,128)S(1)}, u32[]{:S(2)}, u32[]{:S(2)}) collective-permute-start(f32[8,128]{1,0:T(8,128)S(1)} %get-tuple-element.74), channel_id=1, source_target_pairs={{0,16},{16,32},{32,48},{48,64},{64,80},{80,96},{96,112},{112,0},{1... | collective-permute-start | bytes 12296 | tf_op jit(solution)/shard_map/ppermute | solution.py:529
  72.2 5.7 %collective-permute-start.8 = (f32[8,128]{1,0:T(8,128)S(1)}, f32[8,128]{1,0:T(8,128)S(1)}, u32[]{:S(2)}, u32[]{:S(2)}) collective-permute-start(f32[8,128]{1,0:T(8,128)S(1)} %get-tuple-element.75), channel_id=1, source_target_pairs={{0,112},{16,0},{32,16},{48,32},{64,48},{80,64},{96,80},{112,96},{1... | collective-permute-start | bytes 12296 | tf_op jit(solution)/shard_map/ppermute | solution.py:529
  75.4 18.1 %copy-start.19 = (f32[568,128]{1,0:T(8,128)}, f32[568,128]{1,0:T(8,128)S(1)}, u32[]{:S(2)}) copy-start(f32[568,128]{1,0:T(8,128)S(1)} %collective-permute-done.9.rest_0_) | copy-start | bytes 872452
  77.9 6.4 %copy-start.12 = (f32[8,128]{1,0:T(8,128)}, f32[8,128]{1,0:T(8,128)S(1)}, u32[]{:S(2)}) copy-start(f32[8,128]{1,0:T(8,128)S(1)} %collective-permute-done.7.lo) | copy-start | bytes 12292
  77.9 6.4 %copy-start.13 = (f32[8,128]{1,0:T(8,128)}, f32[8,128]{1,0:T(8,128)S(1)}, u32[]{:S(2)}) copy-start(f32[8,128]{1,0:T(8,128)S(1)} %collective-permute-done.8.hi) | copy-start | bytes 12292
  78.0 3.6 %collective-permute-start.10 = (f32[8,640]{1,0:T(8,128)S(1)}, f32[8,640]{1,0:T(8,128)S(1)}, u32[]{:S(2)}, u32[]{:S(2)}) collective-permute-start(f32[8,640]{1,0:T(8,128)S(1)} %get-tuple-element.81), channel_id=1, source_target_pairs={{0,1},{1,2},{2,3},{3,4},{4,5},{5,6},{6,7},{7,8},{8,9},{9,10},{10,1... | collective-permute-start | bytes 61448 | tf_op jit(solution)/shard_map/ppermute | solution.py:529
  80.8 3.5 %collective-permute-start.11 = (f32[8,640]{1,0:T(8,128)S(1)}, f32[8,640]{1,0:T(8,128)S(1)}, u32[]{:S(2)}, u32[]{:S(2)}) collective-permute-start(f32[8,640]{1,0:T(8,128)S(1)} %get-tuple-element.82), channel_id=1, source_target_pairs={{0,15},{1,0},{2,1},{3,2},{4,3},{5,4},{6,5},{7,6},{8,7},{9,8},{10,9... | collective-permute-start | bytes 61448 | tf_op jit(solution)/shard_map/ppermute | solution.py:529
  93.5 47.4 %all-to-all-start.1 = ((f32[128,16,128]{2,1,0:T(8,128)}), f32[128,16,128]{2,1,0:T(8,128)S(1)}, u32[]{:S(2)}, u32[]{:S(2)}) async-start(f32[128,16,128]{2,1,0:T(8,128)} %bitcast.10), calls=%async_computation.1 | async-start | bytes 2097152 | tf_op jit(solution)/shard_map/all_to_all | solution.py:678
  109.2 15.8 %collective-permute-start.12 = (f32[568,128]{1,0:T(8,128)}, f32[568,128]{1,0:T(8,128)S(1)}, u32[]{:S(2)}, u32[]{:S(2)}) collective-permute-start(f32[568,128]{1,0:T(8,128)} %get-tuple-element.112), channel_id=1, source_target_pairs={{0,8},{1,9},{2,10},{3,11},{4,12},{5,13},{6,14},{7,15},{8,0},{9,1},... | collective-permute-start | bytes 872456 | tf_op jit(solution)/shard_map/ppermute | solution.py:537
  130.6 8.7 %collective-permute-start.13 = (f32[512,128]{1,0:T(8,128)}, f32[512,128]{1,0:T(8,128)S(1)}, u32[]{:S(2)}, u32[]{:S(2)}) collective-permute-start(f32[512,128]{1,0:T(8,128)} %get-tuple-element.120), channel_id=1, source_target_pairs={{0,8},{1,9},{2,10},{3,11},{4,12},{5,13},{6,14},{7,15},{8,0},{9,1},... | collective-permute-start | bytes 786440 | tf_op jit(solution)/shard_map/ppermute | solution.py:537
  130.6 8.7 %copy-start.11 = (f32[512,128]{1,0:T(8,128)S(1)}, f32[512,128]{1,0:T(8,128)}, u32[]{:S(2)}) copy-start(f32[512,128]{1,0:T(8,128)} %get-tuple-element.121.weight) | copy-start | bytes 786436
  (9 other events, 18.7 us)

commit v3 on v2

--- a/solution.py
+++ b/solution.py
@@ -56,6 +56,26 @@
 
 
 SMEM = pl.BlockSpec(memory_space=pltpu.SMEM)
+ANY = pl.BlockSpec(memory_space=pl.ANY)
+
+
+class Copies:
+    def __init__(self, sems):
+        self.sems, self.made = sems, []
+
+    def start(self, *pairs):
+        begun = []
+        for source, target in pairs:
+            copy = pltpu.make_async_copy(source, target, self.sems.at[len(self.made)])
+            copy.start()
+            self.made.append(copy)
+            begun.append(copy)
+        return begun
+
+
+def wait(copies):
+    for copy in copies:
+        copy.wait()
 
 
 def from_right(x):
@@ -134,9 +154,9 @@
         left = jnp.zeros((n, W), F32)
         right = jnp.zeros((n, W), F32)
         for p, x in enumerate(planes):
-            here = (lane >= Q * p) & (lane < Q * p + Q)
-            left = jnp.where(here, x if p == 0 else pltpu.roll(x, Q * p, axis=1), left)
-            right = jnp.where(here, pltpu.roll(x, (Q * p + Q) % W, axis=1), right)
+            turned = x if p == 0 else pltpu.roll(x, Q * p, axis=1)
+            left = jnp.where(lane // Q == p, turned, left)
+            right = jnp.where(lane // Q == (p - 1) % (W // Q), turned, right)
         to_left[pl.ds(at, n), :] = left
         to_right[pl.ds(at, n), :] = right
 
@@ -180,40 +200,55 @@
         del refs[:n]
         return got
 
+    outs = take(4 * layers + 11)
+    helds = take(4 * layers + 11)
+    ev, ecx, ecy, est = take(layers), take(layers), take(layers), take(layers)
+    evp, side, d00, d01, d10, z10, z11, z20, e20, sems = take(10)
+    copies = Copies(sems)
+    home = dict(zip(map(id, helds), outs))
+
+    def give(*held):
+        return copies.start(*[(h, home[id(h)]) for h in held])
+
+    refs = list(helds)
     gx, gy, inv, viae = take(layers), take(layers), take(layers), take(layers - 1)
     bond, d02, d03, d11, d12, z12, d20, d21, z21, sb0, vd0, msg = take(12)
-    ev, ecx, ecy, est = take(layers), take(layers), take(layers), take(layers)
-    evp, side, d00, d01, d10, z10, z11, z20, e20 = take(9)
     d0 = [d00, d01, d02, d03]
     d1, z1 = [d10, d11, d12], [z10, z11, z12]
     d2, z2 = [e20, d21], [z20, z21]
     dests = [*ev, *ecx, *ecy, *est, *viae, bond, evp]
     main, edge = slice(0, W), slice(W, 2 * W)
+    sources = [ref.at[l] for ref in (v, cx, cy, st, via) for l in range(ref.shape[0])]
+    arriving = copies.start(
+        *[
+            (source, dest.at[pl.ds(PAD, rows), pl.ds(0, W)])
+            for source, dest in zip([*sources, vp], [*dests[:-2], evp])
+        ]
+    )
 
     def sides(s):
         r = pl.multiple_of(s - H, 8)
         a = f_right[pl.ds(r, WIDE), :]
         b = f_left[pl.ds(r, WIDE), :]
-        low = lanes(WIDE) < W // 2
+        even = lanes(WIDE) // Q % 2 == 0
+        both = [jnp.where(even, a, b), jnp.where(even, b, a)]
         for p, dest in enumerate(dests):
-            x = a if p == 0 else pltpu.roll(a, W - Q * p, axis=1)
-            y = pltpu.roll(b, W - Q - Q * p, axis=1)
-            dest[pl.ds(s, WIDE), edge] = jnp.where(low, x, y)
+            x = both[p % 2]
+            dest[pl.ds(s, WIDE), edge] = x if p == 0 else pltpu.roll(x, W - Q * p, axis=1)
 
     each_chunk(H, total, sides, WIDE)
 
-    def tile(i):
-        a = pl.ds(i, STEP)
-        xs = [ref[l, a, :] for ref in (v, cx, cy, st, via) for l in range(ref.shape[0])]
-        xs += [BOND * mask[a, :].astype(F32), vp[a, :]]
-        for x, dest in zip(xs, dests):
-            dest[pl.ds(pl.multiple_of(i + PAD, 8), STEP), main] = x
-
-    each_chunk(0, rows, tile, STEP)
+    def bonds(i):
+        weight = BOND * mask[pl.ds(i, STEP), :].astype(F32)
+        bond[pl.ds(pl.multiple_of(i + PAD, 8), STEP), main] = weight
+
+    each_chunk(0, rows, bonds, STEP)
     for p, dest in enumerate(dests):
         is_vp = p == len(dests) - 1
         dest[H : 2 * H, main] = vlo[...] if is_vp else lo[p]
         dest[PAD + rows : PAD + rows + H, main] = vhi[...] if is_vp else hi[p]
+
+    wait(arriving)
 
     x_first, x_total, y_first, y_total = place[0], place[1], place[2], place[3]
     col = lanes(1, 2 * W)
@@ -232,6 +267,7 @@
             gy[l][pl.ds(s, WIDE), :] = keep_y * (c + from_right(c))
 
     each_chunk(H, total, conductances, WIDE)
+    leaving = give(*gx, *gy, *viae, bond)
 
     def start(s):
         n = WIDE
@@ -256,6 +292,7 @@
             d0[l][a, :] = (nb - off * c) * inverse
 
     each_chunk(H, total, start, WIDE)
+    leaving += give(*inv, d02, d03)
 
     def links(d, l, s, n):
         nb = weighted(d[l], s, n, gx[l], gy[l])
@@ -277,6 +314,7 @@
 
     each_chunk(H, total, first, WIDE)
     pack_side(side, msg, total)
+    leaving += give(d11, d12, z12, msg)
 
     def second(s):
         a = pl.ds(s, WIDE)
@@ -286,6 +324,7 @@
             d2[l][a, :] = A2 * d1[l][a, :] + B2 * z
 
     each_chunk(H, total, second, WIDE)
+    leaving += give(d21, z21)
 
     def third(s):
         a = pl.ds(s, STEP)
@@ -295,11 +334,13 @@
         d = e20[a, main]
         z = z20[a, main] - d + nb
         d20[o, :] = d
-        sb0[o, :] = v[0, o, :] + d00[a, main] + d10[a, main] + (1.0 + A3) * d + B3 * z
+        sb0[o, :] = ev[0][a, main] + d00[a, main] + d10[a, main] + (1.0 + A3) * d + B3 * z
         for l in range(1, layers):
-            vd0[l - 1, o, :] = v[l, o, :] + d0[l][a, main]
+            vd0[l - 1, o, :] = ev[l][a, main] + d0[l][a, main]
 
     each_chunk(PAD, rows, third, STEP)
+    leaving += give(d20, sb0, vd0)
+    wait(leaving)
 
 
 def pack_side(side, msg, total):
@@ -362,9 +403,9 @@
 
 
 def final_kernel(
-    v0, vd0, d11, d12, z12, e11, d13, d20, d21, d23, z21, z23,
+    v0, vd0, d11, d12, z12, e11, d13, d20, b21, e21, d23, z21, ze21, z23,
     gx1, gx2, gx3, gy1, gy2, gy3, inv1, inv2, inv3, via0, via1, via2,
-    out, d22, z22,
+    out, d22, z22, d21,
 ):
     main = slice(0, W)
     rows = out.shape[1]
@@ -377,11 +418,12 @@
         z = z12[a, :] - this + inv2[a, :] * nb
         z22[a, :] = z
         d22[a, :] = A2 * this + B2 * z
+        d21[a, :] = b21[a, :] + e21[a, :]
 
     each_chunk(H, rows + 2 * H, middle, WIDE)
     gx, gy, inv = [None, gx1, gx2, gx3], [None, gy1, gy2, gy3], [None, inv1, inv2, inv3]
     via = [via0, via1, via2]
-    d2, z2 = [None, d21, d22, d23], [None, z21, z22, z23]
+    d2, z2 = [None, d21, d22, d23], [None, None, z22, z23]
 
     def body(i):
         s = pl.multiple_of(i + PAD, 8)
@@ -395,23 +437,21 @@
             below = d2[l][a, main]
             if l < 3:
                 nb = nb + via[l][a, main] * d2[l + 1][a, main]
-            z = z2[l][a, main] - below + inv[l][a, main] * nb
+            z = (z21[a, main] + ze21[o, :] if l == 1 else z2[l][a, main]) - below + inv[l][a, main] * nb
             out[l, o, :] = vd0[l - 1, o, :] + first[l] + (1.0 + A3) * below + B3 * z
 
     each_chunk(0, rows, body, STEP)
 
 
-def bond_kernel(field, part, weight, out):
-    out[0] = field[0] + B3 * weight[...] * part[...]
-
-
-def map_kernel(arrived, out, first, last, labels, vec, lab, acc, sem):
+def map_kernel(arrived, out, first, last, labels, vec, lab, a0, a1, a2, a3, sem):
     devices = vec.shape[0]
     rows = out.shape[0]
     vec[...] = arrived[pl.ds(CAP * 8, devices, stride=ROWS_MSG), :].astype(jnp.int32)
     copy = pltpu.make_async_copy(vec, lab, sem)
     copy.start()
-    acc[...] = jnp.zeros_like(acc)
+    parts = (a0, a1, a2, a3)
+    for acc in parts:
+        acc[...] = jnp.zeros_like(acc)
     copy.wait()
 
     @pl.loop(0, devices // 8)
@@ -423,11 +463,12 @@
                 slot = lab[g * 8 + j, r]
                 labels[(g * 8 + j) * CAP + r] = slot
                 a = pl.ds(pl.multiple_of(slot * 8, 8), 8)
+                acc = parts[(j * CAP + r) % 4]
                 acc[a, :] += data[j * ROWS_MSG + r * 8 : j * ROWS_MSG + r * 8 + 8]
 
-    out[...] = acc[0:rows, :]
-    first[...] = acc[0:8, :]
-    last[...] = acc[rows - 8 : rows, :]
+    out[...] = (a0[0:rows, :] + a1[0:rows, :]) + (a2[0:rows, :] + a3[0:rows, :])
+    first[...] = out[0:8, :]
+    last[...] = out[rows - 8 : rows, :]
 
 
 def edges_kernel(cur, lo, hi, to_left, to_right, ext):
@@ -442,10 +483,14 @@
 
 
 def effect_kernel(
-    labels, cur, lo, hi, f_left, f_right, gx0, gx1, gy0, gy1, inv0, inv1, via0, sb0, d20, d21, z21,
-    v0, picked, e11, d20_out, d21_out, z21_out,
-    ec, e0, e1, z10, z11, e2, z20, e21, u, acc,
+    labels, cur, lo, hi, f_left, f_right, *refs
 ):
+    coefficients, (v0, picked, e11_out, e21_out, z21, d20_out) = refs[:9], refs[9:15]
+    held, refs = refs[15:24], refs[24:]
+    inv0, gx0, gy0, via0, inv1, gx1, gy1, sb0, d20 = held
+    ec, e0, e1, z10, z11, e2, z20, e11, e21, u, acc, sems = refs
+    copies = Copies(sems)
+    arriving = copies.start(*zip(coefficients, held))
     rows = cur.shape[0]
     total = rows + 2 * H
     main, edge = slice(0, W), slice(W, 2 * W)
@@ -459,11 +504,14 @@
         n = min(W, total - W * j)
         ec[H + W * j : H + W * j + n, edge] = u[...].T[:n]
 
+    wait(arriving[0:1])
+
     def zeroth(s):
         a = pl.ds(s, WIDE)
         e0[a, :] = inv0[a, :] * ec[a, :]
 
     each_chunk(H, total, zeroth, WIDE)
+    wait(arriving[1:5])
 
     def first(s):
         a = pl.ds(s, WIDE)
@@ -476,6 +524,7 @@
         e11[a, :] = B1 * z
 
     each_chunk(H, total, first, WIDE)
+    wait(arriving[5:7])
 
     def second(s):
         a = pl.ds(s, WIDE)
@@ -486,12 +535,12 @@
         e2[a, :] = A2 * low + B2 * z
         nb = weighted(e11, s, WIDE, gx1, gy1) + between * low
         z = z11[a, :] - high + inv1[a, :] * nb
-        z21_out[a, :] = z21[a, :] + z
-        d = A2 * high + B2 * z
-        e21[a, :] = d
-        d21_out[a, :] = d21[a, :] + d
+        z11[a, :] = z
+        e21[a, :] = A2 * high + B2 * z
 
     each_chunk(H, total, second, WIDE)
+    leaving = copies.start((e11, e11_out), (e21, e21_out))
+    wait(arriving[7:])
 
     def third(i):
         s = pl.multiple_of(i + PAD, 8)
@@ -503,6 +552,7 @@
         v0[o, :] = whole
         acc[o, :] = whole
         d20_out[o, :] = d20[o, :] + here
+        z21[o, :] = z11[a, main]
 
     each_chunk(0, rows, third, STEP)
     acc[rows : rows + 8, :] = jnp.zeros((8, W), F32)
@@ -513,8 +563,12 @@
             pl.ds(pl.multiple_of(labels[k] * 8, 8), 8), :
         ]
 
-
-def give_kernel(dest, back, out):
+    wait(leaving)
+
+
+def last_kernel(dest, back, field, part, weight, out, top):
+    top[0] = field[0] + B3 * weight[...] * part[...]
+
     @pl.loop(0, out.shape[0], unroll=8)
     def _(k):
         out[k] = back[pl.ds(pl.multiple_of(dest[k] * 8, 8), 8), :]
@@ -610,14 +664,19 @@
     tile = shape(rows, W)
     buffer = lambda *d: pltpu.VMEM(d, F32)
     msg_shape = shape(total + 8 * side_blocks, W)
+    held = [one] * (4 * layers + 5)
+    held += [tile, one, one, tile, shape(layers - 1, rows, W), msg_shape]
     outs = call(
         base_kernel,
-        [one] * (4 * layers + 5) + [tile, one, one, tile, shape(layers - 1, rows, W), msg_shape],
+        held,
         [place, *tiles, f_left, f_right],
-        scratch=[buffer(nr, 2 * W)] * (4 * layers + 1)
+        scratch=[buffer(*h.shape) for h in held]
+        + [buffer(nr, 2 * W)] * (4 * layers + 1)
         + [buffer(side_blocks * W, W)]
-        + [buffer(nr, 2 * W)] * 7,
-        specs={0: SMEM},
+        + [buffer(nr, 2 * W)] * 7
+        + [pltpu.SemaphoreType.DMA((9 * layers + 20,))],
+        specs={0: SMEM, 1: ANY, 2: ANY, 3: ANY, 4: ANY, 5: ANY, 7: ANY},
+        out_specs=[ANY] * len(held),
         vmem=VMEM_BASE,
         cost=20_000_000,
     )
@@ -632,14 +691,13 @@
         scratch=[
             pltpu.VMEM((devices, W), jnp.int32),
             pltpu.SMEM((devices, W), jnp.int32),
-            buffer(rows + 8, W),
+            *[buffer(rows + 8, W)] * 4,
             pltpu.SemaphoreType.DMA,
         ],
         out_specs=[pl.BlockSpec(memory_space=pltpu.VMEM)] * 3 + [SMEM],
     )
     cur_lo = shift(cur_last, "gx", 1)
     cur_hi = shift(cur_first, "gx", -1)
-    cur_lo, cur_hi, part0 = lax.optimization_barrier((cur_lo, cur_hi, part0))
     top = [gx[3], gy[3], inv[3], via_e[2], bond]
     d13, z13, msg1 = call(
         first_top_kernel,
@@ -648,6 +706,13 @@
         scratch=[buffer(nr, 2 * W), buffer(side_blocks * W, W), buffer(W, W)],
         vmem=VMEM_TOP,
     )
+    cur_left, cur_right = call(
+        edges_kernel,
+        [shape(8, side_blocks * W)] * 2,
+        [cur, cur_lo, cur_hi],
+        scratch=[buffer(side_blocks * W, W)],
+    )
+    cur_left, cur_right, msg1 = lax.optimization_barrier((cur_left, cur_right, msg1))
     part1 = facing(msg1)
     d23, z23, msg2, weight = call(
         second_top_kernel,
@@ -656,53 +721,48 @@
         scratch=[buffer(nr, 2 * W), buffer(side_blocks * W, W), buffer(W, W)],
         vmem=VMEM_TOP,
     )
-
-    cur_left, cur_right = call(
-        edges_kernel,
-        [shape(8, side_blocks * W)] * 2,
-        [cur, cur_lo, cur_hi],
-        scratch=[buffer(side_blocks * W, W)],
-    )
     cur_f_left = shift(cur_right, "yt", 1)
     cur_f_right = shift(cur_left, "yt", -1)
-    v0, picked, e11, d20, d21, z21 = call(
+    v0, picked, e11, e21, ze21, d20 = call(
         effect_kernel,
-        [tile, shape(devices * CAP * 8, W), one, tile, one, one],
-        [labels, cur, cur_lo, cur_hi, cur_f_left, cur_f_right, *gx[:2], *gy[:2], *inv[:2],
-         via_e[0], sb0, d20, d21, z21],
-        scratch=[buffer(nr, 2 * W)] * 8 + [buffer(W, W), buffer(rows + 8, W)],
-        specs={0: SMEM},
+        [tile, shape(devices * CAP * 8, W), one, one, tile, tile],
+        [labels, cur, cur_lo, cur_hi, cur_f_left, cur_f_right,
+         inv[0], gx[0], gy[0], via_e[0], inv[1], gx[1], gy[1], sb0, d20],
+        scratch=[buffer(nr, 2 * W)] * 7
+        + [buffer(rows, W)] * 2
+        + [buffer(nr, 2 * W)] * 9
+        + [buffer(W, W), buffer(rows + 8, W), pltpu.SemaphoreType.DMA((11,))],
+        specs={0: SMEM} | {i: ANY for i in range(6, 15)},
+        out_specs=[pl.BlockSpec(memory_space=pltpu.VMEM)] * 2
+        + [ANY] * 2
+        + [pl.BlockSpec(memory_space=pltpu.VMEM)] * 2,
         vmem=VMEM_EFFECT,
     )
+    picked, _ = lax.optimization_barrier((picked, part1))
     part2 = facing(msg2)
     back = lax.all_to_all(picked, ALL, 0, 0, tiled=True)
 
     voltage = call(
         final_kernel,
         shape(layers, rows, W),
-        [v0, vd0, d11, d12, z12, e11, d13, d20, d21, d23, z21, z23,
+        [v0, vd0, d11, d12, z12, e11, d13, d20, d21, e21, d23, z21, ze21, z23,
          *gx[1:], *gy[1:], *inv[1:], *via_e],
-        scratch=[buffer(nr, 2 * W)] * 2,
+        scratch=[buffer(nr, 2 * W)] * 3,
         vmem=VMEM_FINAL,
         cost=10_000_000,
     )
-    voltage = pl.pallas_call(
-        bond_kernel,
+    whole = pl.BlockSpec(memory_space=pltpu.VMEM)
+    upper = pl.BlockSpec((1, rows, W), lambda _: (layers - 1, 0, 0))
+    block_voltage, voltage = pl.pallas_call(
+        last_kernel,
         grid=(1,),
-        out_shape=shape(layers, rows, W),
-        in_specs=[
-            pl.BlockSpec((1, rows, W), lambda _: (layers - 1, 0, 0)),
-            pl.BlockSpec((rows, W), lambda _: (0, 0)),
-            pl.BlockSpec((rows, W), lambda _: (0, 0)),
-        ],
-        out_specs=pl.BlockSpec((1, rows, W), lambda _: (layers - 1, 0, 0)),
-        input_output_aliases={0: 0},
-        name="bond_kernel",
-        compiler_params=pltpu.CompilerParams(vmem_limit_bytes=6 << 20),
-    )(voltage, part2, weight)
-    block_voltage = call(
-        give_kernel, shape(nb, 8, W), [dest, back], specs={0: SMEM}
-    )
+        out_shape=[shape(nb, 8, W), shape(layers, rows, W)],
+        in_specs=[SMEM, whole, upper, whole, whole],
+        out_specs=[whole, upper],
+        input_output_aliases={2: 1},
+        name="last_kernel",
+        compiler_params=pltpu.CompilerParams(vmem_limit_bytes=58 << 20),
+    )(dest, back, voltage, part2, weight)
     return voltage, block_voltage
 
 

time: 143 us -> 126 us (0.88)
  waiting for transfers between devices: 25.4 us -> 13.5 us
  Pallas kernels: 63.3 us -> 53.7 us
  starting transfers between devices: 49.7 us -> 52 us
  local copies, waits for them, and re-layouts: 2.66 us -> 4.36 us
    pallas_call x10 -> x9, Pallas kernels: 59.7 us -> 49.2 us  [call(): pl.pallas_call(kernel, out_shape=outs if many else outs[0], in_specs=in_s...]
    ppermute x6, waiting for transfers between devices: 14.3 us -> 4.68 us  [facing(): return lax.ppermute(x, ALL, pairs)]
    ppermute x8, waiting for transfers between devices: 11 us -> 7.96 us  [shift(): return lax.ppermute(x, axis, ring(axis, step))]
    ppermute x6, starting transfers between devices: 14.2 us -> 16.3 us  [facing(): return lax.ppermute(x, ALL, pairs)]
    unnamed x50 -> x54, local copies, waits for them, and re-layouts: 2.66 us -> 4.36 us
  transfers between devices with their start and end apart: 16 -> 16, of which waited for: 9 -> 8; matrix products, arithmetic and copies ran while one was open for 0% -> 0% of each run, Pallas kernels for 33% -> 38%
where the time goes in v3:
time: 126 us; the launch traced here: 125 us
  Pallas kernels  53.7 us (43%)
  starting transfers between devices  52 us (41%)
  waiting for transfers between devices  13.5 us (11%)
  local copies, waits for them, and re-layouts  4.36 us (3%)
    pallas_call x9, Pallas kernels, call(): pl.pallas_call(kernel, out_shape=outs if many else outs[0], in_specs=in_s...  49.2 us
    ppermute x6, starting transfers between devices, facing(): return lax.ppermute(x, ALL, pairs)  16.3 us
    ppermute x8, starting transfers between devices, shift(): return lax.ppermute(x, axis, ring(axis, step))  13.6 us
    all_to_all x1, starting transfers between devices, on_device(): back = lax.all_to_all(picked, ALL, 0, 0, tiled=True)  11.3 us
    all_to_all x1, starting transfers between devices, on_device(): lax.all_to_all(outgoing.reshape(devices, ROWS_MSG, 1, W), ALL, 0, 0, tile...  10.7 us
    ppermute x8, waiting for transfers between devices, shift(): return lax.ppermute(x, axis, ring(axis, step))  7.96 us
    ppermute x6, waiting for transfers between devices, facing(): return lax.ppermute(x, ALL, pairs)  4.68 us
    unnamed x54, local copies, waits for them, and re-layouts  4.36 us
  transfers between devices with their start and end apart: 16, of which 8 were waited for; matrix products, arithmetic and copies ran while one was open for 0% of the time, Pallas kernels for 38%

profile of v3, /device:TPU:1, one launch (start us, length us, event | category | flops | bytes accessed | tf_op | source)
XLA Modules:
  0.0 125.2 jit_solution(1106479866362409208)
XLA Ops:
  0.7 2.0 %pack_x_kernel.1 = (f32[20,8,128]{2,1,0:T(8,128)}, f32[20,8,128]{2,1,0:T(8,128)}, f32[512,128]{1,0:T(8,128)}, f32[8,128]{1,0:T(8,128)}, f32[8,128]{1,0:T(8,128)}) custom-call(f32[4,512,128]{2,1,0:T(8,128)} %refs_1_.3, f32[4,512,128]{2,1,0:T(8,128)} %refs_2_.3, f32[4,512,128]{2,1,0:T(8,128)} %refs_3_.3, f32[4,512,128]{2,1,0:T(8,128)} %refs_4_.3, ...), custom_call_target="tpu_custom_call" | custom-call | flops 1 | bytes 1000000 | tf_op jit(solution)/shard_map/pack_x_kernel/pallas_call | solution.py:634
  2.7 3.6 %collective-permute-start = (f32[512,128]{1,0:T(8,128)}, f32[512,128]{1,0:T(8,128)S(1)}, u32[]{:S(2)}, u32[]{:S(2)}) collective-permute-start(f32[512,128]{1,0:T(8,128)} %get-tuple-element.68), channel_id=1, source_target_pairs={{0,8},{1,9},{2,10},{3,11},{4,12},{5,13},{6,14},{7,15},{8,0},{9,1},... | collective-permute-start | bytes 786440 | tf_op jit(solution)/shard_map/ppermute | solution.py:591
  6.6 3.5 %collective-permute-start.2 = (f32[20,8,128]{2,1,0:T(8,128)}, f32[20,8,128]{2,1,0:T(8,128)S(1)}, u32[]{:S(2)}, u32[]{:S(2)}) collective-permute-start(f32[20,8,128]{2,1,0:T(8,128)} %get-tuple-element.70), channel_id=1, source_target_pairs={{0,112},{16,0},{32,16},{48,32},{64,48},{80,64},{96,80},{112,96},{1... | collective-permute-start | bytes 245768 | tf_op jit(solution)/shard_map/ppermute | solution.py:583
  10.1 4.8 %collective-permute-start.4 = (f32[8,128]{1,0:T(8,128)}, f32[8,128]{1,0:T(8,128)S(1)}, u32[]{:S(2)}, u32[]{:S(2)}) collective-permute-start(f32[8,128]{1,0:T(8,128)} %get-tuple-element.72), channel_id=1, source_target_pairs={{0,120},{1,121},{2,122},{3,123},{4,124},{5,125},{6,126},{7,127},{8... | collective-permute-start | bytes 12296 | tf_op jit(solution)/shard_map/ppermute | solution.py:591
  14.8 1.2 collective-permute-done.3.vlo.refs_10_
  16.1 1.6 %collective-permute-done.1.lo.refs_8_ = f32[20,8,128]{2,1,0:T(8,128)S(1)} collective-permute-done((f32[20,8,128]{2,1,0:T(8,128)}, f32[20,8,128]{2,1,0:T(8,128)S(1)}, u32[]{:S(2)}, u32[]{:S(2)}) %collective-permute-start.1) | collective-permute-done | bytes 81952 | tf_op jit(solution)/shard_map/ppermute | solution.py:583
  17.8 2.0 %pack_y_kernel.1 = (f32[528,128]{1,0:T(8,128)S(1)}, f32[528,128]{1,0:T(8,128)S(1)}) custom-call(f32[4,512,128]{2,1,0:T(8,128)S(1)} %copy-done, f32[4,512,128]{2,1,0:T(8,128)S(1)} %copy-done.1, f32[4,512,128]{2,1,0:T(8,128)S(1)} %copy-done.2, f32[4,512,128]{2,1,0:T(8,128)S(1)} %copy-done.3, f32[3,512,128]{2,1,0:T(8,128)S(1)} %copy-done.4, ...), custom_call_target="tpu_custom_call" | custom-call | flops 1000000 | bytes 1000000 | tf_op jit(solution)/shard_map/pack_y_kernel/pallas_call | solution.py:42
  19.8 3.7 %collective-permute-start.5 = (f32[528,128]{1,0:T(8,128)S(1)}, f32[528,128]{1,0:T(8,128)S(1)}, u32[]{:S(2)}, u32[]{:S(2)}) collective-permute-start(f32[528,128]{1,0:T(8,128)S(1)} %get-tuple-element.73), channel_id=1, source_target_pairs={{0,1},{1,2},{2,3},{3,4},{4,5},{5,6},{6,7},{7,8},{8,9},{9,10},{10,1... | collective-permute-start | bytes 811016 | tf_op jit(solution)/shard_map/ppermute | solution.py:583
  23.5 2.7 %send_kernel.1 = (f32[2176,128]{1,0:T(8,128)}, s32[128]{0:T(128)S(1)}) custom-call(s32[128]{0:T(128)S(1)} %bitcast.8, s32[128]{0:T(128)S(1)} %copy-done.17, f32[128,8,128]{2,1,0:T(8,128)S(1)} %copy-done.8), custom_call_target="tpu_custom_call" | custom-call | flops 1000000 | bytes 1000000 | tf_op jit(solution)/shard_map/send_kernel/pallas_call | solution.py:42
  26.9 2.8 %collective-permute-done.6.refs_13_ = f32[528,128]{1,0:T(8,128)S(1)} collective-permute-done((f32[528,128]{1,0:T(8,128)S(1)}, f32[528,128]{1,0:T(8,128)S(1)}, u32[]{:S(2)}, u32[]{:S(2)}) %collective-permute-start.6) | collective-permute-done | bytes 270368 | tf_op jit(solution)/shard_map/ppermute | solution.py:583
  29.7 0.7 copy-done.23
  30.4 10.7 %all-to-all-start = ((f32[128,17,1,128]{3,2,1,0:T(1,128)}), f32[128,17,1,128]{3,2,1,0:T(1,128)S(1)}, u32[]{:S(2)}, u32[]{:S(2)}) async-start(f32[128,17,1,128]{3,2,1,0:T(1,128)} %bitcast.1), calls=%async_computation | async-start | bytes 2228224 | tf_op jit(solution)/shard_map/all_to_all | solution.py:659
  41.1 0.6 pad_add_fusion.refs_0_
  41.8 15.2 %base_kernel.1 = (f32[544,256]{1,0:T(8,128)}, f32[544,256]{1,0:T(8,128)}, f32[544,256]{1,0:T(8,128)}, f32[544,256]{1,0:T(8,128)}, f32[544,256]{1,0:T(8,128)}, /*...) custom-call(s32[4]{0:T(128)} %pad_add_fusion.refs_0_, ...), custom_call_target="tpu_custom_call" | custom-call | flops 20000000 | bytes 20000000 | tf_op jit(solution)/shard_map/base_kernel/pallas_call | solution.py:42
  57.0 3.0 %collective-permute-start.9 = (f32[568,128]{1,0:T(8,128)}, f32[568,128]{1,0:T(8,128)S(1)}, u32[]{:S(2)}, u32[]{:S(2)}) collective-permute-start(f32[568,128]{1,0:T(8,128)} %get-tuple-element.86), channel_id=1, source_target_pairs={{0,8},{1,9},{2,10},{3,11},{4,12},{5,13},{6,14},{7,15},{8,0},{9,1},... | collective-permute-start | bytes 872456 | tf_op jit(solution)/shard_map/ppermute | solution.py:591
  59.9 0.9 all-to-all-done
  60.8 2.8 %map_kernel.1 = (f32[512,128]{1,0:T(8,128)S(1)}, f32[8,128]{1,0:T(8,128)S(1)}, f32[8,128]{1,0:T(8,128)S(1)}, s32[256]{0:T(256)S(1)}) custom-call(f32[2176,128]{1,0:T(8,128)S(1)} %bitcast.7), custom_call_target="tpu_custom_call" | custom-call | flops 1000000 | bytes 1000000 | tf_op jit(solution)/shard_map/map_kernel/pallas_call | solution.py:42
  64.5 3.3 %collective-permute-start.8 = (f32[8,128]{1,0:T(8,128)S(1)}, f32[8,128]{1,0:T(8,128)S(1)}, u32[]{:S(2)}, u32[]{:S(2)}) collective-permute-start(f32[8,128]{1,0:T(8,128)S(1)} %get-tuple-element.79), channel_id=1, source_target_pairs={{0,112},{16,0},{32,16},{48,32},{64,48},{80,64},{96,80},{112,96},{1... | collective-permute-start | bytes 12296 | tf_op jit(solution)/shard_map/ppermute | solution.py:583
  67.8 0.7 copy-done.20
  68.5 4.7 %first_top_kernel.1 = (f32[544,256]{1,0:T(8,128)}, f32[544,256]{1,0:T(8,128)}, f32[568,128]{1,0:T(8,128)}) custom-call(f32[544,256]{1,0:T(8,128)} %get-tuple-element.84.low, f32[544,256]{1,0:T(8,128)} %get-tuple-element.85.here, f32[568,128]{1,0:T(8,128)} %copy-done.20, f32[544,256]{1,0:T(8,128)} %get-tuple-element.87.rest_1_.refs_4_.gx3, ...), custom_call_target="tpu_custom_call" | custom-call | flops 1000000 | bytes 1000000 | tf_op jit(solution)/shard_map/first_top_kernel/pallas_call | solution.py:42
  73.4 2.1 %collective-permute-start.12 = (f32[568,128]{1,0:T(8,128)}, f32[568,128]{1,0:T(8,128)S(1)}, u32[]{:S(2)}, u32[]{:S(2)}) collective-permute-start(f32[568,128]{1,0:T(8,128)} %get-tuple-element.105), channel_id=1, source_target_pairs={{0,8},{1,9},{2,10},{3,11},{4,12},{5,13},{6,14},{7,15},{8,0},{9,1},... | collective-permute-start | bytes 872456 | tf_op jit(solution)/shard_map/ppermute | solution.py:591
  75.5 2.6 %collective-permute-start.10 = (f32[8,640]{1,0:T(8,128)S(1)}, f32[8,640]{1,0:T(8,128)S(1)}, u32[]{:S(2)}, u32[]{:S(2)}) collective-permute-start(f32[8,640]{1,0:T(8,128)S(1)} %get-tuple-element.93), channel_id=1, source_target_pairs={{0,1},{1,2},{2,3},{3,4},{4,5},{5,6},{6,7},{7,8},{8,9},{9,10},{10,1... | collective-permute-start | bytes 61448 | tf_op jit(solution)/shard_map/ppermute | solution.py:583
  78.1 0.9 collective-permute-done.10.f_left
  79.0 2.6 %collective-permute-done.11.f_right = f32[8,640]{1,0:T(8,128)S(1)} collective-permute-done((f32[8,640]{1,0:T(8,128)S(1)}, f32[8,640]{1,0:T(8,128)S(1)}, u32[]{:S(2)}, u32[]{:S(2)}) %collective-permute-start.11) | collective-permute-done | bytes 20512 | tf_op jit(solution)/shard_map/ppermute | solution.py:583
  82.2 8.1 %effect_kernel.1 = (f32[512,128]{1,0:T(8,128)}, f32[2048,128]{1,0:T(8,128)}, f32[544,256]{1,0:T(8,128)}, f32[544,256]{1,0:T(8,128)}, f32[512,128]{1,0:T(8,128)}, /*index=5*/f32[512,128]{1,0:T(8,128)}) custom-call(s32[256]{0:T(256)} %copy-done.15, f32[512,128]{1,0:T(8,128)} %copy-done.7, f32[8,128]{1,0:T(8,128)} %copy-done.13, f32[8,128]{1,0:T(8,128)} %copy-done.14, ...), custom_call_target="tpu_custom_call" | custom-call | flops 1000000 | bytes 1000000 | tf_op jit(solution)/shard_map/effect_kernel/pallas_call | solution.py:42
  90.3 11.3 %all-to-all-start.1 = ((f32[128,16,128]{2,1,0:T(8,128)}), f32[128,16,128]{2,1,0:T(8,128)S(1)}, u32[]{:S(2)}, u32[]{:S(2)}) async-start(f32[128,16,128]{2,1,0:T(8,128)} %bitcast.10), calls=%async_computation.1 | async-start | bytes 2097152 | tf_op jit(solution)/shard_map/all_to_all | solution.py:743
  101.7 4.9 %second_top_kernel.1 = (f32[544,256]{1,0:T(8,128)}, f32[544,256]{1,0:T(8,128)}, f32[512,128]{1,0:T(8,128)}, f32[512,128]{1,0:T(8,128)}) custom-call(f32[544,256]{1,0:T(8,128)} %get-tuple-element.110.refs_0_.d12, f32[544,256]{1,0:T(8,128)} %get-tuple-element.113.refs_1_.d13, f32[544,256]{1,0:T(8,128)} %get-tuple-element.117.refs_2_, f32[568,128]{1,0:T(8,128)} %copy-done.21, ...), custom_call_target="tpu_custom_call" | custom-call | flops 1000000 | bytes 1000000 | tf_op jit(solution)/shard_map/second_top_kernel/pallas_call | solution.py:42
  106.6 2.9 %collective-permute-start.13 = (f32[512,128]{1,0:T(8,128)}, f32[512,128]{1,0:T(8,128)S(1)}, u32[]{:S(2)}, u32[]{:S(2)}) collective-permute-start(f32[512,128]{1,0:T(8,128)} %get-tuple-element.126), channel_id=1, source_target_pairs={{0,8},{1,9},{2,10},{3,11},{4,12},{5,13},{6,14},{7,15},{8,0},{9,1},... | collective-permute-start | bytes 786440 | tf_op jit(solution)/shard_map/ppermute | solution.py:591
  109.5 8.6 %final_kernel.1.field = f32[4,512,128]{2,1,0:T(8,128)} custom-call(f32[512,128]{1,0:T(8,128)} %get-tuple-element.107.v0, f32[3,512,128]{2,1,0:T(8,128)} %get-tuple-element.108.vd0, f32[544,256]{1,0:T(8,128)} %get-tuple-element.109.d11, f32[544,256]{1,0:T(8,128)} %get-tuple-element.110.refs_0_.d12, f32[544,256]{1,0:T(8,128)} %get-tuple-element.111.z12, ...), custom_call_target="tpu_custom_call" | custom-call | flops 10000000 | bytes 10000000 | tf_op jit(solution)/shard_map/final_kernel/pallas_call | solution.py:42
  118.1 3.4 %collective-permute-done.13.part = f32[512,128]{1,0:T(8,128)S(1)} collective-permute-done((f32[512,128]{1,0:T(8,128)}, f32[512,128]{1,0:T(8,128)S(1)}, u32[]{:S(2)}, u32[]{:S(2)}) %collective-permute-start.13) | collective-permute-done | bytes 262176 | tf_op jit(solution)/shard_map/ppermute | solution.py:591
  121.5 0.7 copy-done.24
  122.6 2.6 %last_kernel.1 = (f32[128,8,128]{2,1,0:T(8,128)}, f32[4,512,128]{2,1,0:T(8,128)}) custom-call(s32[128]{0:T(128)} %copy-done.18, f32[2048,128]{1,0:T(8,128)} %bitcast.9, f32[4,512,128]{2,1,0:T(8,128)} %final_kernel.1.field, f32[512,128]{1,0:T(8,128)} %copy-done.24, f32[512,128]{1,0:T(8,128)} %get-tuple-element.127.weight), custom_call_target="tpu_custom_call", output_to_operand_aliasing={{1}: (2, {})} | custom-call | tf_op jit(solution)/shard_map/last_kernel/pallas_call | solution.py:756
  (66 shorter events, 3.1 us)
Async XLA Ops:
  0.6 17.1 %copy-start.5 = (s32[512,128]{1,0:T(8,128)S(1)}, s32[512,128]{1,0:T(8,128)}, u32[]{:S(2)}) copy-start(s32[512,128]{1,0:T(8,128)} %refs_6_.3) | copy-start | bytes 786436
  0.6 17.1 %copy-start.4 = (f32[3,512,128]{2,1,0:T(8,128)S(1)}, f32[3,512,128]{2,1,0:T(8,128)}, u32[]{:S(2)}) copy-start(f32[3,512,128]{2,1,0:T(8,128)} %refs_5_.3) | copy-start | bytes 2359300
  0.7 17.1 %copy-start.2 = (f32[4,512,128]{2,1,0:T(8,128)S(1)}, f32[4,512,128]{2,1,0:T(8,128)}, u32[]{:S(2)}) copy-start(f32[4,512,128]{2,1,0:T(8,128)} %refs_3_.3) | copy-start | bytes 3145732
  0.7 17.1 %copy-start.1 = (f32[4,512,128]{2,1,0:T(8,128)S(1)}, f32[4,512,128]{2,1,0:T(8,128)}, u32[]{:S(2)}) copy-start(f32[4,512,128]{2,1,0:T(8,128)} %refs_2_.3) | copy-start | bytes 3145732
  0.7 17.1 %copy-start.3 = (f32[4,512,128]{2,1,0:T(8,128)S(1)}, f32[4,512,128]{2,1,0:T(8,128)}, u32[]{:S(2)}) copy-start(f32[4,512,128]{2,1,0:T(8,128)} %refs_4_.3) | copy-start | bytes 3145732
  0.7 17.1 %copy-start = (f32[4,512,128]{2,1,0:T(8,128)S(1)}, f32[4,512,128]{2,1,0:T(8,128)}, u32[]{:S(2)}) copy-start(f32[4,512,128]{2,1,0:T(8,128)} %refs_1_.3) | copy-start | bytes 3145732
  2.7 15.0 %collective-permute-start = (f32[512,128]{1,0:T(8,128)}, f32[512,128]{1,0:T(8,128)S(1)}, u32[]{:S(2)}, u32[]{:S(2)}) collective-permute-start(f32[512,128]{1,0:T(8,128)} %get-tuple-element.68), channel_id=1, source_target_pairs={{0,8},{1,9},{2,10},{3,11},{4,12},{5,13},{6,14},{7,15},{8,0},{9,1},... | collective-permute-start | bytes 786440 | tf_op jit(solution)/shard_map/ppermute | solution.py:591
  6.2 11.5 %collective-permute-start.1 = (f32[20,8,128]{2,1,0:T(8,128)}, f32[20,8,128]{2,1,0:T(8,128)S(1)}, u32[]{:S(2)}, u32[]{:S(2)}) collective-permute-start(f32[20,8,128]{2,1,0:T(8,128)} %get-tuple-element.69), channel_id=1, source_target_pairs={{0,16},{16,32},{32,48},{48,64},{64,80},{80,96},{96,112},{112,0},{1... | collective-permute-start | bytes 245768 | tf_op jit(solution)/shard_map/ppermute | solution.py:583
  6.6 11.2 %collective-permute-start.2 = (f32[20,8,128]{2,1,0:T(8,128)}, f32[20,8,128]{2,1,0:T(8,128)S(1)}, u32[]{:S(2)}, u32[]{:S(2)}) collective-permute-start(f32[20,8,128]{2,1,0:T(8,128)} %get-tuple-element.70), channel_id=1, source_target_pairs={{0,112},{16,0},{32,16},{48,32},{64,48},{80,64},{96,80},{112,96},{1... | collective-permute-start | bytes 245768 | tf_op jit(solution)/shard_map/ppermute | solution.py:583
  10.0 6.0 %collective-permute-start.3 = (f32[8,128]{1,0:T(8,128)}, f32[8,128]{1,0:T(8,128)S(1)}, u32[]{:S(2)}, u32[]{:S(2)}) collective-permute-start(f32[8,128]{1,0:T(8,128)} %get-tuple-element.71), channel_id=1, source_target_pairs={{0,24},{1,25},{2,26},{3,27},{4,28},{5,29},{6,30},{7,31},{8,16},{9,... | collective-permute-start | bytes 12296 | tf_op jit(solution)/shard_map/ppermute | solution.py:591
  10.0 13.5 %copy-start.8 = (f32[128,8,128]{2,1,0:T(8,128)S(1)}, f32[128,8,128]{2,1,0:T(8,128)}, u32[]{:S(2)}) copy-start(f32[128,8,128]{2,1,0:T(8,128)} %blocks_ref.1) | copy-start | bytes 1572868
  10.0 13.5 %copy-start.16 = (s32[128,1]{0,1:T(1,128)S(1)}, s32[128,1]{0,1:T(1,128)}, u32[]{:S(2)}) copy-start(s32[128,1]{0,1:T(1,128)} %param.16) | copy-start | bytes 1540
  10.0 13.5 %copy-start.17 = (s32[128]{0:T(128)S(1)}, s32[128]{0:T(128)}, u32[]{:S(2)}) copy-start(s32[128]{0:T(128)} %slot_ref.1) | copy-start | bytes 1540
  10.1 6.0 %collective-permute-start.4 = (f32[8,128]{1,0:T(8,128)}, f32[8,128]{1,0:T(8,128)S(1)}, u32[]{:S(2)}, u32[]{:S(2)}) collective-permute-start(f32[8,128]{1,0:T(8,128)} %get-tuple-element.72), channel_id=1, source_target_pairs={{0,120},{1,121},{2,122},{3,123},{4,124},{5,125},{6,126},{7,127},{8... | collective-permute-start | bytes 12296 | tf_op jit(solution)/shard_map/ppermute | solution.py:591
  16.1 3.7 %copy-start.11 = (f32[8,128]{1,0:T(8,128)}, f32[8,128]{1,0:T(8,128)S(1)}, u32[]{:S(2)}) copy-start(f32[8,128]{1,0:T(8,128)S(1)} %collective-permute-done.3.vlo.refs_10_) | copy-start | bytes 12292
  16.1 3.7 %copy-start.12 = (f32[8,128]{1,0:T(8,128)}, f32[8,128]{1,0:T(8,128)S(1)}, u32[]{:S(2)}) copy-start(f32[8,128]{1,0:T(8,128)S(1)} %collective-permute-done.4.vhi.refs_11_) | copy-start | bytes 12292
  19.8 7.1 %collective-permute-start.5 = (f32[528,128]{1,0:T(8,128)S(1)}, f32[528,128]{1,0:T(8,128)S(1)}, u32[]{:S(2)}, u32[]{:S(2)}) collective-permute-start(f32[528,128]{1,0:T(8,128)S(1)} %get-tuple-element.73), channel_id=1, source_target_pairs={{0,1},{1,2},{2,3},{3,4},{4,5},{5,6},{6,7},{7,8},{8,9},{9,10},{10,1... | collective-permute-start | bytes 811016 | tf_op jit(solution)/shard_map/ppermute | solution.py:583
  23.5 6.2 %collective-permute-start.6 = (f32[528,128]{1,0:T(8,128)S(1)}, f32[528,128]{1,0:T(8,128)S(1)}, u32[]{:S(2)}, u32[]{:S(2)}) collective-permute-start(f32[528,128]{1,0:T(8,128)S(1)} %get-tuple-element.74), channel_id=1, source_target_pairs={{0,15},{1,0},{2,1},{3,2},{4,3},{5,4},{6,5},{7,6},{8,7},{9,8},{10,9... | collective-permute-start | bytes 811016 | tf_op jit(solution)/shard_map/ppermute | solution.py:583
  26.9 2.8 %copy-start.22 = (f32[528,128]{1,0:T(8,128)}, f32[528,128]{1,0:T(8,128)S(1)}, u32[]{:S(2)}) copy-start(f32[528,128]{1,0:T(8,128)S(1)} %collective-permute-done.5.refs_12_) | copy-start | bytes 811012
  30.4 30.4 %all-to-all-start = ((f32[128,17,1,128]{3,2,1,0:T(1,128)}), f32[128,17,1,128]{3,2,1,0:T(1,128)S(1)}, u32[]{:S(2)}, u32[]{:S(2)}) async-start(f32[128,17,1,128]{3,2,1,0:T(1,128)} %bitcast.1), calls=%async_computation | async-start | bytes 2228224 | tf_op jit(solution)/shard_map/all_to_all | solution.py:659
  57.0 10.8 %collective-permute-start.9 = (f32[568,128]{1,0:T(8,128)}, f32[568,128]{1,0:T(8,128)S(1)}, u32[]{:S(2)}, u32[]{:S(2)}) collective-permute-start(f32[568,128]{1,0:T(8,128)} %get-tuple-element.86), channel_id=1, source_target_pairs={{0,8},{1,9},{2,10},{3,11},{4,12},{5,13},{6,14},{7,15},{8,0},{9,1},... | collective-permute-start | bytes 872456 | tf_op jit(solution)/shard_map/ppermute | solution.py:591
  64.2 9.1 %copy-start.7 = (f32[512,128]{1,0:T(8,128)}, f32[512,128]{1,0:T(8,128)S(1)}, u32[]{:S(2)}) copy-start(f32[512,128]{1,0:T(8,128)S(1)} %get-tuple-element.77.cur) | copy-start | bytes 786436
  64.2 9.0 %collective-permute-start.7 = (f32[8,128]{1,0:T(8,128)S(1)}, f32[8,128]{1,0:T(8,128)S(1)}, u32[]{:S(2)}, u32[]{:S(2)}) collective-permute-start(f32[8,128]{1,0:T(8,128)S(1)} %get-tuple-element.78), channel_id=1, source_target_pairs={{0,16},{16,32},{32,48},{48,64},{64,80},{80,96},{96,112},{112,0},{1... | collective-permute-start | bytes 12296 | tf_op jit(solution)/shard_map/ppermute | solution.py:583
  64.5 8.7 %collective-permute-start.8 = (f32[8,128]{1,0:T(8,128)S(1)}, f32[8,128]{1,0:T(8,128)S(1)}, u32[]{:S(2)}, u32[]{:S(2)}) collective-permute-start(f32[8,128]{1,0:T(8,128)S(1)} %get-tuple-element.79), channel_id=1, source_target_pairs={{0,112},{16,0},{32,16},{48,32},{64,48},{80,64},{96,80},{112,96},{1... | collective-permute-start | bytes 12296 | tf_op jit(solution)/shard_map/ppermute | solution.py:583
  73.2 8.4 %copy-start.13 = (f32[8,128]{1,0:T(8,128)}, f32[8,128]{1,0:T(8,128)S(1)}, u32[]{:S(2)}) copy-start(f32[8,128]{1,0:T(8,128)S(1)} %collective-permute-done.7.lo) | copy-start | bytes 12292
  73.2 8.4 %copy-start.14 = (f32[8,128]{1,0:T(8,128)}, f32[8,128]{1,0:T(8,128)S(1)}, u32[]{:S(2)}) copy-start(f32[8,128]{1,0:T(8,128)S(1)} %collective-permute-done.8.hi) | copy-start | bytes 12292
  73.4 16.9 %collective-permute-start.12 = (f32[568,128]{1,0:T(8,128)}, f32[568,128]{1,0:T(8,128)S(1)}, u32[]{:S(2)}, u32[]{:S(2)}) collective-permute-start(f32[568,128]{1,0:T(8,128)} %get-tuple-element.105), channel_id=1, source_target_pairs={{0,8},{1,9},{2,10},{3,11},{4,12},{5,13},{6,14},{7,15},{8,0},{9,1},... | collective-permute-start | bytes 872456 | tf_op jit(solution)/shard_map/ppermute | solution.py:591
  75.5 3.5 %collective-permute-start.10 = (f32[8,640]{1,0:T(8,128)S(1)}, f32[8,640]{1,0:T(8,128)S(1)}, u32[]{:S(2)}, u32[]{:S(2)}) collective-permute-start(f32[8,640]{1,0:T(8,128)S(1)} %get-tuple-element.93), channel_id=1, source_target_pairs={{0,1},{1,2},{2,3},{3,4},{4,5},{5,6},{6,7},{7,8},{8,9},{9,10},{10,1... | collective-permute-start | bytes 61448 | tf_op jit(solution)/shard_map/ppermute | solution.py:583
  78.1 3.5 %collective-permute-start.11 = (f32[8,640]{1,0:T(8,128)S(1)}, f32[8,640]{1,0:T(8,128)S(1)}, u32[]{:S(2)}, u32[]{:S(2)}) collective-permute-start(f32[8,640]{1,0:T(8,128)S(1)} %get-tuple-element.94), channel_id=1, source_target_pairs={{0,15},{1,0},{2,1},{3,2},{4,3},{5,4},{6,5},{7,6},{8,7},{9,8},{10,9... | collective-permute-start | bytes 61448 | tf_op jit(solution)/shard_map/ppermute | solution.py:583
  90.3 11.4 %copy-start.21 = (f32[568,128]{1,0:T(8,128)}, f32[568,128]{1,0:T(8,128)S(1)}, u32[]{:S(2)}) copy-start(f32[568,128]{1,0:T(8,128)S(1)} %collective-permute-done.12.refs_3_) | copy-start | bytes 872452
  90.3 31.2 %all-to-all-start.1 = ((f32[128,16,128]{2,1,0:T(8,128)}), f32[128,16,128]{2,1,0:T(8,128)S(1)}, u32[]{:S(2)}, u32[]{:S(2)}) async-start(f32[128,16,128]{2,1,0:T(8,128)} %bitcast.10), calls=%async_computation.1 | async-start | bytes 2097152 | tf_op jit(solution)/shard_map/all_to_all | solution.py:743
  106.6 14.9 %collective-permute-start.13 = (f32[512,128]{1,0:T(8,128)}, f32[512,128]{1,0:T(8,128)S(1)}, u32[]{:S(2)}, u32[]{:S(2)}) collective-permute-start(f32[512,128]{1,0:T(8,128)} %get-tuple-element.126), channel_id=1, source_target_pairs={{0,8},{1,9},{2,10},{3,11},{4,12},{5,13},{6,14},{7,15},{8,0},{9,1},... | collective-permute-start | bytes 786440 | tf_op jit(solution)/shard_map/ppermute | solution.py:591
  (11 other events, 13.9 us)

commit v4 on v3

--- a/solution.py
+++ b/solution.py
@@ -57,6 +57,7 @@
 
 SMEM = pl.BlockSpec(memory_space=pltpu.SMEM)
 ANY = pl.BlockSpec(memory_space=pl.ANY)
+HBM = pl.BlockSpec(memory_space=pltpu.HBM)
 
 
 class Copies:
@@ -96,7 +97,7 @@
         body(pl.multiple_of(first + k * step, 8))
 
 
-def send_kernel(owner_ref, slot_ref, blocks_ref, out_ref, dest_ref, count_ref, buf, slots):
+def send_kernel(owner_ref, slot_ref, blocks_ref, out_hbm, dest_ref, count_ref, buf, slots, out_ref, sems):
     devices = count_ref.shape[0]
 
     @pl.loop(0, devices, unroll=8)
@@ -118,8 +119,7 @@
         row = slots[pl.ds(owner, 1), :]
         slots[pl.ds(owner, 1), :] = jnp.where(lane == rank, slot_ref[k], row)
 
-    @pl.loop(0, devices // 8)
-    def _(g):
+    def assemble(g):
         data = buf[pl.ds(pl.multiple_of(g * CAP * 64, 8), CAP * 64), :]
         label = slots[pl.ds(pl.multiple_of(g * 8, 8), 8), :].astype(F32)
         pieces = []
@@ -129,10 +129,19 @@
             jnp.concatenate(pieces, axis=0)
         )
 
+    copies = Copies(sems)
+    groups = devices // 8 // 4
+    for part in range(4):
+        pl.loop(part * groups, (part + 1) * groups)(assemble)
+        n = groups * 8 * ROWS_MSG
+        a = pl.ds(part * n, n)
+        copies.start((out_ref.at[a, :], out_hbm.at[a, :]))
+    wait(copies.made)
+
 
 def pack_x_kernel(*refs):
     firsts, lasts, v3 = refs[:6], refs[6:12], refs[12]
-    first_out, last_out, v3_out, v3_first, v3_last = refs[13:]
+    first_out, last_out, v3_out = refs[13:]
     for group, out in ((firsts, first_out), (lasts, last_out)):
         p = 0
         for ref in group[:5]:
@@ -140,13 +149,10 @@
             out[p : p + n] = ref[...]
             p += n
         out[p] = BOND * group[5][...].astype(F32)
-    rows = v3.shape[1]
     v3_out[...] = v3[0]
-    v3_first[...] = v3[0, 0:H, :]
-    v3_last[...] = v3[0, rows - H : rows, :]
-
-
-def pack_y_kernel(v, cx, cy, st, via, mask, vp, lo, hi, vlo, vhi, to_left, to_right):
+
+
+def pack_y_kernel(v, cx, cy, st, via, mask, lo, hi, to_left, to_right):
     rows = v.shape[1]
 
     def pack(planes, at, n):
@@ -163,13 +169,13 @@
     def tile(i):
         at = pl.ds(i, STEP)
         planes = [ref[l, at, :] for ref in (v, cx, cy, st, via) for l in range(ref.shape[0])]
-        planes += [BOND * mask[at, :].astype(F32), vp[at, :]]
+        planes += [BOND * mask[at, :].astype(F32)]
         pack(planes, pl.multiple_of(i + H, 8), STEP)
 
     each_chunk(0, rows, tile, STEP)
     count = lo.shape[0]
-    pack([lo[p] for p in range(count)] + [vlo[...]], 0, H)
-    pack([hi[p] for p in range(count)] + [vhi[...]], H + rows, H)
+    pack([lo[p] for p in range(count)], 0, H)
+    pack([hi[p] for p in range(count)], H + rows, H)
 
 
 def rows_of(ref, l=None):
@@ -190,8 +196,8 @@
 
 
 def base_kernel(*refs):
-    place, v, cx, cy, st, via, mask, vp, lo, hi, vlo, vhi, f_left, f_right = refs[:14]
-    refs = list(refs[14:])
+    place, v, cx, cy, st, via, mask, vp, lo, hi, f_left, f_right = refs[:12]
+    refs = list(refs[12:])
     layers, rows = v.shape[0], v.shape[1]
     total = rows + 2 * H
 
@@ -201,6 +207,7 @@
         return got
 
     outs = take(4 * layers + 11)
+    [v3_out] = take(1)
     helds = take(4 * layers + 11)
     ev, ecx, ecy, est = take(layers), take(layers), take(layers), take(layers)
     evp, side, d00, d01, d10, z10, z11, z20, e20, sems = take(10)
@@ -216,13 +223,13 @@
     d0 = [d00, d01, d02, d03]
     d1, z1 = [d10, d11, d12], [z10, z11, z12]
     d2, z2 = [e20, d21], [z20, z21]
-    dests = [*ev, *ecx, *ecy, *est, *viae, bond, evp]
+    dests = [*ev, *ecx, *ecy, *est, *viae, bond]
     main, edge = slice(0, W), slice(W, 2 * W)
     sources = [ref.at[l] for ref in (v, cx, cy, st, via) for l in range(ref.shape[0])]
     arriving = copies.start(
         *[
             (source, dest.at[pl.ds(PAD, rows), pl.ds(0, W)])
-            for source, dest in zip([*sources, vp], [*dests[:-2], evp])
+            for source, dest in zip([*sources, vp], [*dests[:-1], evp])
         ]
     )
 
@@ -235,6 +242,7 @@
         for p, dest in enumerate(dests):
             x = both[p % 2]
             dest[pl.ds(s, WIDE), edge] = x if p == 0 else pltpu.roll(x, W - Q * p, axis=1)
+        evp[pl.ds(s, WIDE), edge] = jnp.zeros((WIDE, W), F32)
 
     each_chunk(H, total, sides, WIDE)
 
@@ -244,10 +252,10 @@
 
     each_chunk(0, rows, bonds, STEP)
     for p, dest in enumerate(dests):
-        is_vp = p == len(dests) - 1
-        dest[H : 2 * H, main] = vlo[...] if is_vp else lo[p]
-        dest[PAD + rows : PAD + rows + H, main] = vhi[...] if is_vp else hi[p]
-
+        dest[H : 2 * H, main] = lo[p]
+        dest[PAD + rows : PAD + rows + H, main] = hi[p]
+    evp[H : 2 * H, main] = jnp.zeros((H, W), F32)
+    evp[PAD + rows : PAD + rows + H, main] = jnp.zeros((H, W), F32)
     wait(arriving)
 
     x_first, x_total, y_first, y_total = place[0], place[1], place[2], place[3]
@@ -268,6 +276,7 @@
 
     each_chunk(H, total, conductances, WIDE)
     leaving = give(*gx, *gy, *viae, bond)
+    leaving += copies.start((ev[layers - 1], v3_out))
 
     def start(s):
         n = WIDE
@@ -313,7 +322,22 @@
             d1[l][a, :] = A1 * d0[l][a, :] + B1 * z
 
     each_chunk(H, total, first, WIDE)
-    pack_side(side, msg, total)
+    pack_side(side, msg, total, total)
+    row = total + 8 * (side.shape[0] // W)
+    for product in (False, True):
+        def rim(x, product=product):
+            part = ev[layers - 1][x]
+            return inv[layers - 1][x] * bond[x] if product else part
+
+        msg[row : row + H, :] = rim((slice(H, 2 * H), main))
+        msg[row + H : row + 2 * H, :] = rim((slice(PAD + rows, PAD + rows + H), main))
+
+        def lay(s, rim=rim):
+            side[pl.ds(pl.multiple_of(s - H, 8), WIDE), :] = rim((pl.ds(s, WIDE), edge))
+
+        each_chunk(H, total, lay, WIDE)
+        pack_side(side, msg, row + 2 * H, total)
+        row += 2 * H + 8 * (side.shape[0] // W)
     leaving += give(d11, d12, z12, msg)
 
     def second(s):
@@ -343,82 +367,117 @@
     wait(leaving)
 
 
-def pack_side(side, msg, total):
+def pack_side(side, msg, row, total):
     for j in range(-(-total // W)):
         t = side[W * j : W * j + W, :].T
-        msg[total + 8 * j : total + 8 * j + Q, :] = t[0:Q]
-        msg[total + 8 * j + Q : total + 8 * j + 2 * Q, :] = t[W - Q : W]
-
-
-def unpack_side(msg, total, u, ref):
+        msg[row + 8 * j : row + 8 * j + Q, :] = t[0:Q]
+        msg[row + 8 * j + Q : row + 8 * j + 2 * Q, :] = t[W - Q : W]
+
+
+def unpack_side(msg, row, total, u):
+    blocks = []
+    for j in range(-(-total // W)):
+        u[0:Q, :] = msg[row + 8 * j : row + 8 * j + Q, :]
+        u[W - Q : W, :] = msg[row + 8 * j + Q : row + 8 * j + 2 * Q, :]
+        blocks.append((H + W * j, min(W, total - W * j), u[...].T))
+    return blocks
+
+
+def first_top_kernel(low, here, v3, part, gx, gy, inv, via, bond, d_out, z_out, msg, delta, d0, ep, side, u, sem):
+    fetch = pltpu.make_async_copy(here, d0, sem)
+    fetch.start()
+    rows = part.shape[0] - 3 * (2 * H + 8 * (side.shape[0] // W))
+    total = rows + 2 * H
+    sides = 8 * (side.shape[0] // W)
+    main, edge = slice(0, W), slice(W, 2 * W)
     u[...] = jnp.zeros_like(u)
-    for j in range(-(-total // W)):
-        u[0:Q, :] = msg[total + 8 * j : total + 8 * j + Q, :]
-        u[W - Q : W, :] = msg[total + 8 * j + Q : total + 8 * j + 2 * Q, :]
-        n = min(W, total - W * j)
-        t = u[...].T
-        ref[H + W * j : H + W * j + n, W : 2 * W] = t[:n]
-
-
-def top_kernel(low, here, z, part, gx, gy, inv, via, bond, *rest):
-    again = z is not None
-    if again:
-        d_out, z_out, msg, weight, ep, side, u = rest
-    else:
-        d_out, z_out, msg, ep, side, u = rest
-    total = part.shape[0] - 8 * (side.shape[0] // W)
-    unpack_side(part, total, u, ep)
+    row = total + sides
+    own = unpack_side(part, row + 2 * H, total, u)
+    others = unpack_side(part, row + 2 * H + sides + 2 * H, total, u)
+    theirs = unpack_side(part, total, total, u)
+    fetch.wait()
+    delta[PAD : PAD + rows, main] = jnp.zeros((rows, W), F32)
+    ep[PAD : PAD + rows, main] = part[H : H + rows, :]
+
+    def halo(a, cols, v_part, weight_part, d_part):
+        x = inv[a, cols] * bond[a, cols] * v_part
+        delta[a, cols] = x
+        d0[a, cols] = d0[a, cols] + x
+        ep[a, cols] = d_part + weight_part * v3[a, cols]
+
+    for k, first in ((0, H), (1, PAD + rows)):
+        at = row + H * k
+        halo(
+            slice(first, first + H), main, part[at : at + H, :],
+            part[at + 2 * H + sides : at + 3 * H + sides, :], part[first - H : first, :],
+        )
+    for (first, n, a), (_, _, b), (_, _, c) in zip(own, others, theirs):
+        halo(slice(first, first + n), edge, a[:n], b[:n], c[:n])
 
     def body(s):
         a = pl.ds(s, WIDE)
         r = pl.ds(pl.multiple_of(s - H, 8), WIDE)
-        other = jnp.concatenate([part[r, :], ep[a, W : 2 * W]], axis=1)
-        nb = weighted(here, s, WIDE, gx, gy) + via[a, :] * low[a, :] + bond[a, :] * other
-        c = here[a, :]
+        nb = weighted(d0, s, WIDE, gx, gy) + via[a, :] * low[a, :] + bond[a, :] * ep[a, :]
         x = inv[a, :] * nb
-        if again:
-            x = z[a, :] - c + x
-        d = (A2 if again else A1) * c + (B2 if again else B1) * x
+        d = A1 * d0[a, :] + B1 * x
         z_out[a, :] = x
         d_out[a, :] = d
-        if not again:
-            side[r, :] = d[:, W:]
-            msg[r, :] = d[:, :W]
+        side[r, :] = d[:, W:]
+        msg[r, :] = d[:, :W]
 
     each_chunk(H, total, body, WIDE)
-    if not again:
-        pack_side(side, msg, total)
-    else:
-        rows = msg.shape[0]
-        msg[...] = d_out[PAD : PAD + rows, 0:W]
-        weight[...] = inv[PAD : PAD + rows, 0:W] * bond[PAD : PAD + rows, 0:W]
-
-
-def first_top_kernel(low, here, *rest):
-    top_kernel(low, here, None, *rest)
-
-
-def second_top_kernel(*refs):
-    top_kernel(*refs)
+    pack_side(side, msg, total, total)
+
+
+def second_top_kernel(low, inv_low, delta, here, z, part, gx, gy, inv, via, bond, d_out, z_out, msg, weight, ep, u):
+    rows = msg.shape[0]
+    total = rows + 2 * H
+    u[...] = jnp.zeros_like(u)
+    for first, n, x in unpack_side(part, total, total, u):
+        ep[first : first + n, :] = x[:n]
+
+    def body(s):
+        a = pl.ds(s, WIDE)
+        r = pl.ds(pl.multiple_of(s - H, 8), WIDE)
+        other = jnp.concatenate([part[r, :], ep[a, :]], axis=1)
+        under = low[a, :] + B1 * inv_low[a, :] * via[a, :] * delta[a, :]
+        nb = weighted(here, s, WIDE, gx, gy) + via[a, :] * under + bond[a, :] * other
+        c = here[a, :]
+        x = z[a, :] - c + inv[a, :] * nb
+        z_out[a, :] = x
+        d_out[a, :] = A2 * c + B2 * x
+
+    each_chunk(H, total, body, WIDE)
+    msg[...] = d_out[PAD : PAD + rows, 0:W]
+    weight[...] = inv[PAD : PAD + rows, 0:W] * bond[PAD : PAD + rows, 0:W]
 
 
 def final_kernel(
-    v0, vd0, d11, d12, z12, e11, d13, d20, b21, e21, d23, z21, ze21, z23,
+    v0, vd0, d11, b12, z12, e11, d13, d20, b21, e21, d23, z21, ze21, z23, delta,
     gx1, gx2, gx3, gy1, gy2, gy3, inv1, inv2, inv3, via0, via1, via2,
-    out, d22, z22, d21,
+    out, d22, z22, d21, d12,
 ):
     main = slice(0, W)
     rows = out.shape[1]
+
+    def amend(s):
+        a = pl.ds(s, WIDE)
+        c = inv2[a, :] * via2[a, :] * delta[a, :]
+        z22[a, :] = z12[a, :] + c
+        c = B1 * c
+        d12[a, :] = b12[a, :] + c
+        d21[a, :] = b21[a, :] + e21[a, :] + B2 * inv1[a, :] * via1[a, :] * c
+
+    each_chunk(H, rows + 2 * H, amend, WIDE)
 
     def middle(s):
         a = pl.ds(s, WIDE)
         this = d12[a, :]
         nb = weighted(d12, s, WIDE, gx2, gy2)
         nb = nb + via1[a, :] * (d11[a, :] + e11[a, :]) + via2[a, :] * d13[a, :]
-        z = z12[a, :] - this + inv2[a, :] * nb
+        z = z22[a, :] - this + inv2[a, :] * nb
         z22[a, :] = z
         d22[a, :] = A2 * this + B2 * z
-        d21[a, :] = b21[a, :] + e21[a, :]
 
     each_chunk(H, rows + 2 * H, middle, WIDE)
     gx, gy, inv = [None, gx1, gx2, gx3], [None, gy1, gy2, gy3], [None, inv1, inv2, inv3]
@@ -615,9 +674,11 @@
             pltpu.SMEM((devices,), jnp.int32),
             pltpu.VMEM((devices * CAP * 8, W), F32),
             pltpu.VMEM((devices, W), jnp.int32),
+            pltpu.VMEM((devices * ROWS_MSG, W), F32),
+            pltpu.SemaphoreType.DMA((4,)),
         ],
         specs={0: SMEM, 1: SMEM},
-        out_specs=[pl.BlockSpec(memory_space=pltpu.VMEM), SMEM],
+        out_specs=[HBM, SMEM],
     )
     sources = [v, cx, cy, st, via]
     args = sources + [mask] + sources + [mask, v]
@@ -631,17 +692,15 @@
     specs[11] = pl.BlockSpec((8, W), lambda _: (last, 0))
     specs[12] = pl.BlockSpec((1, rows, W), lambda _: (layers - 1, 0, 0))
     count = 5 * layers
-    first_rows, last_rows, v_top, v_first, v_last = pl.pallas_call(
+    first_rows, last_rows, v_top = pl.pallas_call(
         pack_x_kernel,
         grid=(1,),
-        out_shape=[shape(count, 8, W)] * 2 + [shape(rows, W), shape(H, W), shape(H, W)],
+        out_shape=[shape(count, 8, W)] * 2 + [shape(rows, W)],
         in_specs=[specs[i] for i in range(13)],
         out_specs=[
             pl.BlockSpec((count, 8, W), lambda _: (0, 0, 0)),
             pl.BlockSpec((count, 8, W), lambda _: (0, 0, 0)),
             pl.BlockSpec((rows, W), lambda _: (0, 0)),
-            pl.BlockSpec((H, W), lambda _: (0, 0)),
-            pl.BlockSpec((H, W), lambda _: (0, 0)),
         ],
         name="pack_x_kernel",
         compiler_params=pltpu.CompilerParams(vmem_limit_bytes=58 << 20),
@@ -649,13 +708,17 @@
     )(*args)
     lo = shift(last_rows, "gx", 1)
     hi = shift(first_rows, "gx", -1)
+    lo, hi, v_top, outgoing = lax.optimization_barrier((lo, hi, v_top, outgoing))
     v_part = facing(v_top)
-    v_lo, v_hi = facing(v_last, 1), facing(v_first, -1)
-    tiles = [v, cx, cy, st, via, mask, v_part, lo, hi, v_lo, v_hi]
-    to_left, to_right = call(pack_y_kernel, [shape(total, W), shape(total, W)], tiles, vmem=8)
+    tiles = [v, cx, cy, st, via, mask]
+    to_left, to_right = call(
+        pack_y_kernel, [shape(total, W), shape(total, W)], [*tiles, lo, hi], vmem=8
+    )
     f_left = shift(to_right, "yt", 1)
     f_right = shift(to_left, "yt", -1)
-    outgoing, f_left, f_right = lax.optimization_barrier((outgoing, f_left, f_right))
+    outgoing, f_left, f_right, v_part = lax.optimization_barrier(
+        (outgoing, f_left, f_right, v_part)
+    )
     arrived = lax.all_to_all(
         outgoing.reshape(devices, ROWS_MSG, 1, W), ALL, 0, 0, tiled=True
     ).reshape(devices * ROWS_MSG, W)
@@ -665,23 +728,24 @@
     buffer = lambda *d: pltpu.VMEM(d, F32)
     msg_shape = shape(total + 8 * side_blocks, W)
     held = [one] * (4 * layers + 5)
-    held += [tile, one, one, tile, shape(layers - 1, rows, W), msg_shape]
+    msg0_shape = shape(3 * (total + 8 * side_blocks) - 2 * rows, W)
+    held += [tile, one, one, tile, shape(layers - 1, rows, W), msg0_shape]
     outs = call(
         base_kernel,
-        held,
-        [place, *tiles, f_left, f_right],
+        [*held, one],
+        [place, *tiles, v_part, lo, hi, f_left, f_right],
         scratch=[buffer(*h.shape) for h in held]
         + [buffer(nr, 2 * W)] * (4 * layers + 1)
         + [buffer(side_blocks * W, W)]
         + [buffer(nr, 2 * W)] * 7
         + [pltpu.SemaphoreType.DMA((9 * layers + 20,))],
         specs={0: SMEM, 1: ANY, 2: ANY, 3: ANY, 4: ANY, 5: ANY, 7: ANY},
-        out_specs=[ANY] * len(held),
+        out_specs=[ANY] * (len(held) + 1),
         vmem=VMEM_BASE,
         cost=20_000_000,
     )
     gx, gy, inv, via_e = outs[0:4], outs[4:8], outs[8:12], outs[12:15]
-    bond, d02, d03, d11, d12, z12, d20, d21, z21, sb0, vd0, msg0 = outs[15:]
+    bond, d02, d03, d11, d12, z12, d20, d21, z21, sb0, vd0, msg0, v3 = outs[15:]
     part0 = facing(msg0)
 
     cur, cur_first, cur_last, labels = call(
@@ -699,28 +763,31 @@
     cur_lo = shift(cur_last, "gx", 1)
     cur_hi = shift(cur_first, "gx", -1)
     top = [gx[3], gy[3], inv[3], via_e[2], bond]
-    d13, z13, msg1 = call(
-        first_top_kernel,
-        [one, one, msg_shape],
-        [d02, d03, part0, *top],
-        scratch=[buffer(nr, 2 * W), buffer(side_blocks * W, W), buffer(W, W)],
-        vmem=VMEM_TOP,
-    )
     cur_left, cur_right = call(
         edges_kernel,
         [shape(8, side_blocks * W)] * 2,
         [cur, cur_lo, cur_hi],
         scratch=[buffer(side_blocks * W, W)],
     )
-    cur_left, cur_right, msg1 = lax.optimization_barrier((cur_left, cur_right, msg1))
+    cur_left, cur_right, part0 = lax.optimization_barrier((cur_left, cur_right, part0))
+    d13, z13, msg1, delta = call(
+        first_top_kernel,
+        [one, one, msg_shape, one],
+        [d02, d03, v3, part0, *top],
+        scratch=[buffer(nr, 2 * W)] * 2
+        + [buffer(side_blocks * W, W), buffer(W, W), pltpu.SemaphoreType.DMA],
+        specs={1: ANY},
+        vmem=VMEM_TOP,
+    )
     part1 = facing(msg1)
     d23, z23, msg2, weight = call(
         second_top_kernel,
         [one, one, tile, tile],
-        [d12, d13, z13, part1, *top],
-        scratch=[buffer(nr, 2 * W), buffer(side_blocks * W, W), buffer(W, W)],
+        [d12, inv[2], delta, d13, z13, part1, *top],
+        scratch=[buffer(nr, W), buffer(W, W)],
         vmem=VMEM_TOP,
     )
+
     cur_f_left = shift(cur_right, "yt", 1)
     cur_f_right = shift(cur_left, "yt", -1)
     v0, picked, e11, e21, ze21, d20 = call(
@@ -738,16 +805,16 @@
         + [pl.BlockSpec(memory_space=pltpu.VMEM)] * 2,
         vmem=VMEM_EFFECT,
     )
-    picked, _ = lax.optimization_barrier((picked, part1))
+    picked, part1 = lax.optimization_barrier((picked, part1))
     part2 = facing(msg2)
     back = lax.all_to_all(picked, ALL, 0, 0, tiled=True)
 
     voltage = call(
         final_kernel,
         shape(layers, rows, W),
-        [v0, vd0, d11, d12, z12, e11, d13, d20, d21, e21, d23, z21, ze21, z23,
+        [v0, vd0, d11, d12, z12, e11, d13, d20, d21, e21, d23, z21, ze21, z23, delta,
          *gx[1:], *gy[1:], *inv[1:], *via_e],
-        scratch=[buffer(nr, 2 * W)] * 3,
+        scratch=[buffer(nr, 2 * W)] * 4,
         vmem=VMEM_FINAL,
         cost=10_000_000,
     )

time: 126 us -> 123 us (0.976)
  starting transfers between devices: 52 us -> 45.6 us
  Pallas kernels: 53.7 us -> 55.6 us
  waiting for transfers between devices: 13.5 us -> 14.8 us
    ppermute x6 -> x4, starting transfers between devices: 16.3 us -> 10.1 us  [facing(): return lax.ppermute(x, ALL, pairs)]
    ppermute x6 -> x4, waiting for transfers between devices: 4.68 us -> 7.21 us  [facing(): return lax.ppermute(x, ALL, pairs)]
    all_to_all x1, starting transfers between devices: 11.3 us -> 9.13 us  [on_device(): back = lax.all_to_all(picked, ALL, 0, 0, tiled=True)]
    pallas_call x9, Pallas kernels: 49.2 us -> 51.1 us  [call(): pl.pallas_call(kernel, out_shape=outs if many else outs[0], in_specs=in_s...]
    all_to_all x1, starting transfers between devices: 10.7 us -> 12.1 us  [on_device(): lax.all_to_all(outgoing.reshape(devices, ROWS_MSG, 1, W), ALL, 0, 0, tile...]
  transfers between devices with their start and end apart: 16 -> 14, of which waited for: 8 -> 6; matrix products, arithmetic and copies ran while one was open for 0% -> 0% of each run, Pallas kernels for 38% -> 35%
where the time goes in v4:
time: 123 us
  Pallas kernels  55.6 us (45%)
  starting transfers between devices  45.6 us (37%)
  waiting for transfers between devices  14.8 us (12%)
  local copies, waits for them, and re-layouts  5.45 us (4%)
    pallas_call x9, Pallas kernels, call(): pl.pallas_call(kernel, out_shape=outs if many else outs[0], in_specs=in_s...  51.1 us
    ppermute x8, starting transfers between devices, shift(): return lax.ppermute(x, axis, ring(axis, step))  14.3 us
    all_to_all x1, starting transfers between devices, on_device(): lax.all_to_all(outgoing.reshape(devices, ROWS_MSG, 1, W), ALL, 0, 0, tile...  12.1 us
    ppermute x4, starting transfers between devices, facing(): return lax.ppermute(x, ALL, pairs)  10.1 us
    all_to_all x1, starting transfers between devices, on_device(): back = lax.all_to_all(picked, ALL, 0, 0, tiled=True)  9.13 us
    ppermute x4, waiting for transfers between devices, facing(): return lax.ppermute(x, ALL, pairs)  7.21 us
    ppermute x8, waiting for transfers between devices, shift(): return lax.ppermute(x, axis, ring(axis, step))  7.2 us
    unnamed x54, local copies, waits for them, and re-layouts  5.45 us
  transfers between devices with their start and end apart: 14, of which 6 were waited for; matrix products, arithmetic and copies ran while one was open for 0% of the time, Pallas kernels for 35%

profile of v4, /device:TPU:1, one launch (start us, length us, event | category | flops | bytes accessed | tf_op | source)
XLA Modules:
  0.0 123.1 jit_solution(6728542328087986893)
XLA Ops:
  0.7 1.9 %pack_x_kernel.1 = (f32[20,8,128]{2,1,0:T(8,128)}, f32[20,8,128]{2,1,0:T(8,128)}, f32[512,128]{1,0:T(8,128)}) custom-call(f32[4,512,128]{2,1,0:T(8,128)} %refs_1_.3, f32[4,512,128]{2,1,0:T(8,128)} %refs_2_.3, f32[4,512,128]{2,1,0:T(8,128)} %refs_3_.3, f32[4,512,128]{2,1,0:T(8,128)} %refs_4_.3, f32[3,512,128]{2,1,0:T(8,128)} %refs_5_.3, s32[512,128]{1,0:T(8,128)} %refs_6_.3, ...), custom_call_target="tpu_custom_call" | custom-call | flops 1 | bytes 1000000 | tf_op jit(solution)/shard_map/pack_x_kernel/pallas_call | solution.py:695
  2.7 2.0 %collective-permute-start = (f32[20,8,128]{2,1,0:T(8,128)}, f32[20,8,128]{2,1,0:T(8,128)S(1)}, u32[]{:S(2)}, u32[]{:S(2)}) collective-permute-start(f32[20,8,128]{2,1,0:T(8,128)} %get-tuple-element.72), channel_id=1, source_target_pairs={{0,16},{16,32},{32,48},{48,64},{64,80},{80,96},{96,112},{112,0},{1... | collective-permute-start | bytes 245768 | tf_op jit(solution)/shard_map/ppermute | solution.py:642
  4.7 3.5 %collective-permute-start.1 = (f32[20,8,128]{2,1,0:T(8,128)}, f32[20,8,128]{2,1,0:T(8,128)S(1)}, u32[]{:S(2)}, u32[]{:S(2)}) collective-permute-start(f32[20,8,128]{2,1,0:T(8,128)} %get-tuple-element.73), channel_id=1, source_target_pairs={{0,112},{16,0},{32,16},{48,32},{64,48},{80,64},{96,80},{112,96},{1... | collective-permute-start | bytes 245768 | tf_op jit(solution)/shard_map/ppermute | solution.py:642
  8.2 2.4 %send_kernel.1 = (f32[2176,128]{1,0:T(8,128)S(1)}, s32[128]{0:T(128)S(1)}) custom-call(s32[128]{0:T(128)S(1)} %bitcast.9, s32[128]{0:T(128)S(1)} %copy-done.15, f32[128,8,128]{2,1,0:T(8,128)S(1)} %copy-done.8), custom_call_target="tpu_custom_call" | custom-call | flops 1000000 | bytes 1000000 | tf_op jit(solution)/shard_map/send_kernel/pallas_call | solution.py:42
  10.7 1.0 copy-done.6
  12.3 1.9 %pack_y_kernel.1 = (f32[528,128]{1,0:T(8,128)S(1)}, f32[528,128]{1,0:T(8,128)S(1)}) custom-call(f32[4,512,128]{2,1,0:T(8,128)S(1)} %copy-done, f32[4,512,128]{2,1,0:T(8,128)S(1)} %copy-done.1, f32[4,512,128]{2,1,0:T(8,128)S(1)} %copy-done.2, f32[4,512,128]{2,1,0:T(8,128)S(1)} %copy-done.3, f32[3,512,128]{2,1,0:T(8,128)S(1)} %copy-done.4, ...), custom_call_target="tpu_custom_call" | custom-call | flops 1000000 | bytes 1000000 | tf_op jit(solution)/shard_map/pack_y_kernel/pallas_call | solution.py:42
  14.3 2.2 %collective-permute-start.2 = (f32[528,128]{1,0:T(8,128)S(1)}, f32[528,128]{1,0:T(8,128)S(1)}, u32[]{:S(2)}, u32[]{:S(2)}) collective-permute-start(f32[528,128]{1,0:T(8,128)S(1)} %get-tuple-element.79), channel_id=1, source_target_pairs={{0,1},{1,2},{2,3},{3,4},{4,5},{5,6},{6,7},{7,8},{8,9},{9,10},{10,1... | collective-permute-start | bytes 811016 | tf_op jit(solution)/shard_map/ppermute | solution.py:642
  16.5 2.5 %collective-permute-start.4 = (f32[512,128]{1,0:T(8,128)S(1)}, f32[512,128]{1,0:T(8,128)S(1)}, u32[]{:S(2)}, u32[]{:S(2)}) collective-permute-start(f32[512,128]{1,0:T(8,128)S(1)} %copy-done.26), channel_id=1, source_target_pairs={{0,8},{1,9},{2,10},{3,11},{4,12},{5,13},{6,14},{7,15},{8,0},{9,1},... | collective-permute-start | bytes 786440 | tf_op jit(solution)/shard_map/ppermute | solution.py:650
  19.0 4.6 %collective-permute-done.4.refs_7_ = f32[512,128]{1,0:T(8,128)S(1)} collective-permute-done((f32[512,128]{1,0:T(8,128)S(1)}, f32[512,128]{1,0:T(8,128)S(1)}, u32[]{:S(2)}, u32[]{:S(2)}) %collective-permute-start.4) | collective-permute-done | bytes 262176 | tf_op jit(solution)/shard_map/ppermute | solution.py:650
  23.5 0.7 copy-done.22
  24.4 12.1 %all-to-all-start = ((f32[128,17,1,128]{3,2,1,0:T(1,128)}), f32[128,17,1,128]{3,2,1,0:T(1,128)S(1)}, u32[]{:S(2)}, u32[]{:S(2)}) async-start(f32[128,17,1,128]{3,2,1,0:T(1,128)} %bitcast.8), calls=%async_computation | async-start | bytes 2228224 | tf_op jit(solution)/shard_map/all_to_all | solution.py:722
  36.5 0.6 pad_add_fusion.refs_0_
  37.1 15.7 %base_kernel.1 = (f32[544,256]{1,0:T(8,128)}, f32[544,256]{1,0:T(8,128)}, f32[544,256]{1,0:T(8,128)}, f32[544,256]{1,0:T(8,128)}, f32[544,256]{1,0:T(8,128)}, /*...) custom-call(s32[4]{0:T(128)} %pad_add_fusion.refs_0_, ...), custom_call_target="tpu_custom_call" | custom-call | flops 20000000 | bytes 20000000 | tf_op jit(solution)/shard_map/base_kernel/pallas_call | solution.py:42
  52.8 3.0 %collective-permute-start.7 = (f32[680,128]{1,0:T(8,128)}, f32[680,128]{1,0:T(8,128)S(1)}, u32[]{:S(2)}, u32[]{:S(2)}) collective-permute-start(f32[680,128]{1,0:T(8,128)} %get-tuple-element.92), channel_id=1, source_target_pairs={{0,8},{1,9},{2,10},{3,11},{4,12},{5,13},{6,14},{7,15},{8,0},{9,1},... | collective-permute-start | bytes 1044488 | tf_op jit(solution)/shard_map/ppermute | solution.py:650
  56.2 2.8 %map_kernel.1 = (f32[512,128]{1,0:T(8,128)S(1)}, f32[8,128]{1,0:T(8,128)S(1)}, f32[8,128]{1,0:T(8,128)S(1)}, s32[256]{0:T(256)S(1)}) custom-call(f32[2176,128]{1,0:T(8,128)S(1)} %bitcast.7), custom_call_target="tpu_custom_call" | custom-call | flops 1000000 | bytes 1000000 | tf_op jit(solution)/shard_map/map_kernel/pallas_call | solution.py:42
  59.8 3.3 %collective-permute-start.6 = (f32[8,128]{1,0:T(8,128)S(1)}, f32[8,128]{1,0:T(8,128)S(1)}, u32[]{:S(2)}, u32[]{:S(2)}) collective-permute-start(f32[8,128]{1,0:T(8,128)S(1)} %get-tuple-element.86), channel_id=1, source_target_pairs={{0,112},{16,0},{32,16},{48,32},{64,48},{80,64},{96,80},{112,96},{1... | collective-permute-start | bytes 12296 | tf_op jit(solution)/shard_map/ppermute | solution.py:642
  63.1 3.7 %collective-permute-done.5.lo = f32[8,128]{1,0:T(8,128)S(1)} collective-permute-done((f32[8,128]{1,0:T(8,128)S(1)}, f32[8,128]{1,0:T(8,128)S(1)}, u32[]{:S(2)}, u32[]{:S(2)}) %collective-permute-start.5) | collective-permute-done | bytes 4128 | tf_op jit(solution)/shard_map/ppermute | solution.py:642
  67.0 0.7 copy-done.18
  67.7 5.8 %first_top_kernel.1 = (f32[544,256]{1,0:T(8,128)}, f32[544,256]{1,0:T(8,128)}, f32[568,128]{1,0:T(8,128)}, f32[544,256]{1,0:T(8,128)}) custom-call(f32[544,256]{1,0:T(8,128)} %get-tuple-element.105.low, f32[544,256]{1,0:T(8,128)} %get-tuple-element.106.here, f32[544,256]{1,0:T(8,128)} %get-tuple-element.107.v3, f32[680,128]{1,0:T(8,128)} %copy-done.18, ...), custom_call_target="tpu_custom_call" | custom-call | flops 1000000 | bytes 1000000 | tf_op jit(solution)/shard_map/first_top_kernel/pallas_call | solution.py:42
  73.5 1.8 %collective-permute-start.10 = (f32[568,128]{1,0:T(8,128)}, f32[568,128]{1,0:T(8,128)S(1)}, u32[]{:S(2)}, u32[]{:S(2)}) collective-permute-start(f32[568,128]{1,0:T(8,128)} %get-tuple-element.114), channel_id=1, source_target_pairs={{0,8},{1,9},{2,10},{3,11},{4,12},{5,13},{6,14},{7,15},{8,0},{9,1},... | collective-permute-start | bytes 872456 | tf_op jit(solution)/shard_map/ppermute | solution.py:650
  75.3 2.9 %collective-permute-start.8 = (f32[8,640]{1,0:T(8,128)S(1)}, f32[8,640]{1,0:T(8,128)S(1)}, u32[]{:S(2)}, u32[]{:S(2)}) collective-permute-start(f32[8,640]{1,0:T(8,128)S(1)} %get-tuple-element.93), channel_id=1, source_target_pairs={{0,1},{1,2},{2,3},{3,4},{4,5},{5,6},{6,7},{7,8},{8,9},{9,10},{10,1... | collective-permute-start | bytes 61448 | tf_op jit(solution)/shard_map/ppermute | solution.py:642
  78.3 0.9 collective-permute-done.8.f_left
  79.2 2.6 %collective-permute-done.9.f_right = f32[8,640]{1,0:T(8,128)S(1)} collective-permute-done((f32[8,640]{1,0:T(8,128)S(1)}, f32[8,640]{1,0:T(8,128)S(1)}, u32[]{:S(2)}, u32[]{:S(2)}) %collective-permute-start.9) | collective-permute-done | bytes 20512 | tf_op jit(solution)/shard_map/ppermute | solution.py:642
  81.8 0.6 copy-done.25
  82.4 8.1 %effect_kernel.1 = (f32[512,128]{1,0:T(8,128)}, f32[2048,128]{1,0:T(8,128)}, f32[544,256]{1,0:T(8,128)}, f32[544,256]{1,0:T(8,128)}, f32[512,128]{1,0:T(8,128)}, /*index=5*/f32[512,128]{1,0:T(8,128)}) custom-call(s32[256]{0:T(256)} %copy-done.13, f32[512,128]{1,0:T(8,128)} %copy-done.7, f32[8,128]{1,0:T(8,128)} %copy-done.11, f32[8,128]{1,0:T(8,128)} %copy-done.12, ...), custom_call_target="tpu_custom_call" | custom-call | flops 1000000 | bytes 1000000 | tf_op jit(solution)/shard_map/effect_kernel/pallas_call | solution.py:42
  90.5 9.1 %all-to-all-start.1 = ((f32[128,16,128]{2,1,0:T(8,128)}), f32[128,16,128]{2,1,0:T(8,128)S(1)}, u32[]{:S(2)}, u32[]{:S(2)}) async-start(f32[128,16,128]{2,1,0:T(8,128)} %bitcast.11), calls=%async_computation.1 | async-start | bytes 2097152 | tf_op jit(solution)/shard_map/all_to_all | solution.py:810
  99.6 5.3 %second_top_kernel.1 = (f32[544,256]{1,0:T(8,128)}, f32[544,256]{1,0:T(8,128)}, f32[512,128]{1,0:T(8,128)}, f32[512,128]{1,0:T(8,128)}) custom-call(f32[544,256]{1,0:T(8,128)} %get-tuple-element.119.low.b12, f32[544,256]{1,0:T(8,128)} %get-tuple-element.126.inv_low.inv2, f32[544,256]{1,0:T(8,128)} %get-tuple-element.127.delta, ...), custom_call_target="tpu_custom_call" | custom-call | flops 1000000 | bytes 1000000 | tf_op jit(solution)/shard_map/second_top_kernel/pallas_call | solution.py:42
  104.9 2.9 %collective-permute-start.11 = (f32[512,128]{1,0:T(8,128)}, f32[512,128]{1,0:T(8,128)S(1)}, u32[]{:S(2)}, u32[]{:S(2)}) collective-permute-start(f32[512,128]{1,0:T(8,128)} %get-tuple-element.136), channel_id=1, source_target_pairs={{0,8},{1,9},{2,10},{3,11},{4,12},{5,13},{6,14},{7,15},{8,0},{9,1},... | collective-permute-start | bytes 786440 | tf_op jit(solution)/shard_map/ppermute | solution.py:650
  107.8 9.0 %final_kernel.1.field = f32[4,512,128]{2,1,0:T(8,128)} custom-call(f32[512,128]{1,0:T(8,128)} %get-tuple-element.116.v0, f32[3,512,128]{2,1,0:T(8,128)} %get-tuple-element.117.vd0, f32[544,256]{1,0:T(8,128)} %get-tuple-element.118.d11, f32[544,256]{1,0:T(8,128)} %get-tuple-element.119.low.b12, f32[544,256]{1,0:T(8,128)} %get-tuple-element.120.z12, ...), custom_call_target="tpu_custom_call" | custom-call | flops 10000000 | bytes 10000000 | tf_op jit(solution)/shard_map/final_kernel/pallas_call | solution.py:42
  116.8 2.6 %collective-permute-done.11.part = f32[512,128]{1,0:T(8,128)S(1)} collective-permute-done((f32[512,128]{1,0:T(8,128)}, f32[512,128]{1,0:T(8,128)S(1)}, u32[]{:S(2)}, u32[]{:S(2)}) %collective-permute-start.11) | collective-permute-done | bytes 262176 | tf_op jit(solution)/shard_map/ppermute | solution.py:650
  119.5 0.7 copy-done.23
  120.5 2.6 %last_kernel.1 = (f32[128,8,128]{2,1,0:T(8,128)}, f32[4,512,128]{2,1,0:T(8,128)}) custom-call(s32[128]{0:T(128)} %copy-done.16, f32[2048,128]{1,0:T(8,128)} %bitcast.10, f32[4,512,128]{2,1,0:T(8,128)} %final_kernel.1.field, f32[512,128]{1,0:T(8,128)} %copy-done.23, f32[512,128]{1,0:T(8,128)} %get-tuple-element.137.weight), custom_call_target="tpu_custom_call", output_to_operand_aliasing={{1}: (2, {})} | custom-call | tf_op jit(solution)/shard_map/last_kernel/pallas_call | solution.py:823
  (62 shorter events, 2.6 us)
Async XLA Ops:
  0.6 11.6 %copy-start.5 = (s32[512,128]{1,0:T(8,128)S(1)}, s32[512,128]{1,0:T(8,128)}, u32[]{:S(2)}) copy-start(s32[512,128]{1,0:T(8,128)} %refs_6_.3) | copy-start | bytes 786436
  0.6 11.6 %copy-start.4 = (f32[3,512,128]{2,1,0:T(8,128)S(1)}, f32[3,512,128]{2,1,0:T(8,128)}, u32[]{:S(2)}) copy-start(f32[3,512,128]{2,1,0:T(8,128)} %refs_5_.3) | copy-start | bytes 2359300
  0.7 7.6 %copy-start.15 = (s32[128]{0:T(128)S(1)}, s32[128]{0:T(128)}, u32[]{:S(2)}) copy-start(s32[128]{0:T(128)} %slot_ref.1) | copy-start | bytes 1540
  0.7 7.6 %copy-start.14 = (s32[128,1]{0,1:T(1,128)S(1)}, s32[128,1]{0,1:T(1,128)}, u32[]{:S(2)}) copy-start(s32[128,1]{0,1:T(1,128)} %param.16) | copy-start | bytes 1540
  0.7 7.6 %copy-start.8 = (f32[128,8,128]{2,1,0:T(8,128)S(1)}, f32[128,8,128]{2,1,0:T(8,128)}, u32[]{:S(2)}) copy-start(f32[128,8,128]{2,1,0:T(8,128)} %blocks_ref.1) | copy-start | bytes 1572868
  0.7 11.6 %copy-start = (f32[4,512,128]{2,1,0:T(8,128)S(1)}, f32[4,512,128]{2,1,0:T(8,128)}, u32[]{:S(2)}) copy-start(f32[4,512,128]{2,1,0:T(8,128)} %refs_1_.3) | copy-start | bytes 3145732
  0.7 11.6 %copy-start.1 = (f32[4,512,128]{2,1,0:T(8,128)S(1)}, f32[4,512,128]{2,1,0:T(8,128)}, u32[]{:S(2)}) copy-start(f32[4,512,128]{2,1,0:T(8,128)} %refs_2_.3) | copy-start | bytes 3145732
  0.7 11.6 %copy-start.2 = (f32[4,512,128]{2,1,0:T(8,128)S(1)}, f32[4,512,128]{2,1,0:T(8,128)}, u32[]{:S(2)}) copy-start(f32[4,512,128]{2,1,0:T(8,128)} %refs_3_.3) | copy-start | bytes 3145732
  0.7 11.6 %copy-start.3 = (f32[4,512,128]{2,1,0:T(8,128)S(1)}, f32[4,512,128]{2,1,0:T(8,128)}, u32[]{:S(2)}) copy-start(f32[4,512,128]{2,1,0:T(8,128)} %refs_4_.3) | copy-start | bytes 3145732
  2.7 9.6 %collective-permute-start = (f32[20,8,128]{2,1,0:T(8,128)}, f32[20,8,128]{2,1,0:T(8,128)S(1)}, u32[]{:S(2)}, u32[]{:S(2)}) collective-permute-start(f32[20,8,128]{2,1,0:T(8,128)} %get-tuple-element.72), channel_id=1, source_target_pairs={{0,16},{16,32},{32,48},{48,64},{64,80},{80,96},{96,112},{112,0},{1... | collective-permute-start | bytes 245768 | tf_op jit(solution)/shard_map/ppermute | solution.py:642
  4.7 7.5 %collective-permute-start.1 = (f32[20,8,128]{2,1,0:T(8,128)}, f32[20,8,128]{2,1,0:T(8,128)S(1)}, u32[]{:S(2)}, u32[]{:S(2)}) collective-permute-start(f32[20,8,128]{2,1,0:T(8,128)} %get-tuple-element.73), channel_id=1, source_target_pairs={{0,112},{16,0},{32,16},{48,32},{64,48},{80,64},{96,80},{112,96},{1... | collective-permute-start | bytes 245768 | tf_op jit(solution)/shard_map/ppermute | solution.py:642
  12.3 2.0 %copy-start.9 = (f32[20,8,128]{2,1,0:T(8,128)}, f32[20,8,128]{2,1,0:T(8,128)S(1)}, u32[]{:S(2)}) copy-start(f32[20,8,128]{2,1,0:T(8,128)S(1)} %collective-permute-done.lo.refs_8_) | copy-start | bytes 245764
  12.3 2.0 %copy-start.10 = (f32[20,8,128]{2,1,0:T(8,128)}, f32[20,8,128]{2,1,0:T(8,128)S(1)}, u32[]{:S(2)}) copy-start(f32[20,8,128]{2,1,0:T(8,128)S(1)} %collective-permute-done.1.hi.refs_9_) | copy-start | bytes 245764
  12.3 4.2 %copy-start.26 = (f32[512,128]{1,0:T(8,128)S(1)}, f32[512,128]{1,0:T(8,128)}, u32[]{:S(2)}) copy-start(f32[512,128]{1,0:T(8,128)} %get-tuple-element.81) | copy-start | bytes 786436
  14.3 9.2 %collective-permute-start.2 = (f32[528,128]{1,0:T(8,128)S(1)}, f32[528,128]{1,0:T(8,128)S(1)}, u32[]{:S(2)}, u32[]{:S(2)}) collective-permute-start(f32[528,128]{1,0:T(8,128)S(1)} %get-tuple-element.79), channel_id=1, source_target_pairs={{0,1},{1,2},{2,3},{3,4},{4,5},{5,6},{6,7},{7,8},{8,9},{9,10},{10,1... | collective-permute-start | bytes 811016 | tf_op jit(solution)/shard_map/ppermute | solution.py:642
  16.5 7.0 %collective-permute-start.3 = (f32[528,128]{1,0:T(8,128)S(1)}, f32[528,128]{1,0:T(8,128)S(1)}, u32[]{:S(2)}, u32[]{:S(2)}) collective-permute-start(f32[528,128]{1,0:T(8,128)S(1)} %get-tuple-element.80), channel_id=1, source_target_pairs={{0,15},{1,0},{2,1},{3,2},{4,3},{5,4},{6,5},{7,6},{8,7},{9,8},{10,9... | collective-permute-start | bytes 811016 | tf_op jit(solution)/shard_map/ppermute | solution.py:642
  16.5 7.0 %collective-permute-start.4 = (f32[512,128]{1,0:T(8,128)S(1)}, f32[512,128]{1,0:T(8,128)S(1)}, u32[]{:S(2)}, u32[]{:S(2)}) collective-permute-start(f32[512,128]{1,0:T(8,128)S(1)} %copy-done.26), channel_id=1, source_target_pairs={{0,8},{1,9},{2,10},{3,11},{4,12},{5,13},{6,14},{7,15},{8,0},{9,1},... | collective-permute-start | bytes 786440 | tf_op jit(solution)/shard_map/ppermute | solution.py:650
  24.4 31.8 %all-to-all-start = ((f32[128,17,1,128]{3,2,1,0:T(1,128)}), f32[128,17,1,128]{3,2,1,0:T(1,128)S(1)}, u32[]{:S(2)}, u32[]{:S(2)}) async-start(f32[128,17,1,128]{3,2,1,0:T(1,128)} %bitcast.8), calls=%async_computation | async-start | bytes 2228224 | tf_op jit(solution)/shard_map/all_to_all | solution.py:722
  52.8 14.1 %collective-permute-start.7 = (f32[680,128]{1,0:T(8,128)}, f32[680,128]{1,0:T(8,128)S(1)}, u32[]{:S(2)}, u32[]{:S(2)}) collective-permute-start(f32[680,128]{1,0:T(8,128)} %get-tuple-element.92), channel_id=1, source_target_pairs={{0,8},{1,9},{2,10},{3,11},{4,12},{5,13},{6,14},{7,15},{8,0},{9,1},... | collective-permute-start | bytes 1044488 | tf_op jit(solution)/shard_map/ppermute | solution.py:650
  59.5 14.0 %copy-start.7 = (f32[512,128]{1,0:T(8,128)}, f32[512,128]{1,0:T(8,128)S(1)}, u32[]{:S(2)}) copy-start(f32[512,128]{1,0:T(8,128)S(1)} %get-tuple-element.84.cur) | copy-start | bytes 786436
  59.5 7.3 %collective-permute-start.5 = (f32[8,128]{1,0:T(8,128)S(1)}, f32[8,128]{1,0:T(8,128)S(1)}, u32[]{:S(2)}, u32[]{:S(2)}) collective-permute-start(f32[8,128]{1,0:T(8,128)S(1)} %get-tuple-element.85), channel_id=1, source_target_pairs={{0,16},{16,32},{32,48},{48,64},{64,80},{80,96},{96,112},{112,0},{1... | collective-permute-start | bytes 12296 | tf_op jit(solution)/shard_map/ppermute | solution.py:642
  59.8 7.0 %collective-permute-start.6 = (f32[8,128]{1,0:T(8,128)S(1)}, f32[8,128]{1,0:T(8,128)S(1)}, u32[]{:S(2)}, u32[]{:S(2)}) collective-permute-start(f32[8,128]{1,0:T(8,128)S(1)} %get-tuple-element.86), channel_id=1, source_target_pairs={{0,112},{16,0},{32,16},{48,32},{64,48},{80,64},{96,80},{112,96},{1... | collective-permute-start | bytes 12296 | tf_op jit(solution)/shard_map/ppermute | solution.py:642
  66.8 6.7 %copy-start.11 = (f32[8,128]{1,0:T(8,128)}, f32[8,128]{1,0:T(8,128)S(1)}, u32[]{:S(2)}) copy-start(f32[8,128]{1,0:T(8,128)S(1)} %collective-permute-done.5.lo) | copy-start | bytes 12292
  66.8 6.7 %copy-start.12 = (f32[8,128]{1,0:T(8,128)}, f32[8,128]{1,0:T(8,128)S(1)}, u32[]{:S(2)}) copy-start(f32[8,128]{1,0:T(8,128)S(1)} %collective-permute-done.6.hi) | copy-start | bytes 12292
  73.5 17.0 %collective-permute-start.10 = (f32[568,128]{1,0:T(8,128)}, f32[568,128]{1,0:T(8,128)S(1)}, u32[]{:S(2)}, u32[]{:S(2)}) collective-permute-start(f32[568,128]{1,0:T(8,128)} %get-tuple-element.114), channel_id=1, source_target_pairs={{0,8},{1,9},{2,10},{3,11},{4,12},{5,13},{6,14},{7,15},{8,0},{9,1},... | collective-permute-start | bytes 872456 | tf_op jit(solution)/shard_map/ppermute | solution.py:650
  75.3 3.9 %collective-permute-start.8 = (f32[8,640]{1,0:T(8,128)S(1)}, f32[8,640]{1,0:T(8,128)S(1)}, u32[]{:S(2)}, u32[]{:S(2)}) collective-permute-start(f32[8,640]{1,0:T(8,128)S(1)} %get-tuple-element.93), channel_id=1, source_target_pairs={{0,1},{1,2},{2,3},{3,4},{4,5},{5,6},{6,7},{7,8},{8,9},{9,10},{10,1... | collective-permute-start | bytes 61448 | tf_op jit(solution)/shard_map/ppermute | solution.py:642
  78.3 3.5 %collective-permute-start.9 = (f32[8,640]{1,0:T(8,128)S(1)}, f32[8,640]{1,0:T(8,128)S(1)}, u32[]{:S(2)}, u32[]{:S(2)}) collective-permute-start(f32[8,640]{1,0:T(8,128)S(1)} %get-tuple-element.94), channel_id=1, source_target_pairs={{0,15},{1,0},{2,1},{3,2},{4,3},{5,4},{6,5},{7,6},{8,7},{9,8},{10,9... | collective-permute-start | bytes 61448 | tf_op jit(solution)/shard_map/ppermute | solution.py:642
  79.2 2.6 %copy-start.24 = (f32[8,640]{1,0:T(8,128)}, f32[8,640]{1,0:T(8,128)S(1)}, u32[]{:S(2)}) copy-start(f32[8,640]{1,0:T(8,128)S(1)} %collective-permute-done.8.f_left) | copy-start | bytes 61444
  90.5 9.2 %copy-start.19 = (f32[568,128]{1,0:T(8,128)}, f32[568,128]{1,0:T(8,128)S(1)}, u32[]{:S(2)}) copy-start(f32[568,128]{1,0:T(8,128)S(1)} %collective-permute-done.10.part) | copy-start | bytes 872452
  90.5 29.0 %all-to-all-start.1 = ((f32[128,16,128]{2,1,0:T(8,128)}), f32[128,16,128]{2,1,0:T(8,128)S(1)}, u32[]{:S(2)}, u32[]{:S(2)}) async-start(f32[128,16,128]{2,1,0:T(8,128)} %bitcast.11), calls=%async_computation.1 | async-start | bytes 2097152 | tf_op jit(solution)/shard_map/all_to_all | solution.py:810
  104.9 14.6 %collective-permute-start.11 = (f32[512,128]{1,0:T(8,128)}, f32[512,128]{1,0:T(8,128)S(1)}, u32[]{:S(2)}, u32[]{:S(2)}) collective-permute-start(f32[512,128]{1,0:T(8,128)} %get-tuple-element.136), channel_id=1, source_target_pairs={{0,8},{1,9},{2,10},{3,11},{4,12},{5,13},{6,14},{7,15},{8,0},{9,1},... | collective-permute-start | bytes 786440 | tf_op jit(solution)/shard_map/ppermute | solution.py:650
  119.5 1.1 copy-start.17
  (9 other events, 6.5 us)

commit v5 on v4

--- a/solution.py
+++ b/solution.py
@@ -6,6 +6,7 @@
 from jax.sharding import PartitionSpec as P
 
 CAP = 2
+TAIL = 24
 BOND = 2.0
 CENTER = 1.0
 HALFWIDTH = 0.97
@@ -18,7 +19,7 @@
 A2, B2 = RHO2 * RHO1, 2.0 * RHO2 / HALFWIDTH
 A3, B3 = RHO3 * RHO2, 2.0 * RHO3 / HALFWIDTH
 
-VMEM_BASE, VMEM_TOP, VMEM_EFFECT, VMEM_FINAL = 58, 58, 58, 58
+VMEM_BASE, VMEM_TOP, VMEM_EFFECT, VMEM_FINAL = 58, 20, 16, 58
 
 ALL = ("gx", "yt")
 F32 = jnp.float32
@@ -31,10 +32,14 @@
 ROWS_MSG = CAP * 8 + 1
 
 
-def call(kernel, out, args, scratch=(), specs=None, out_specs=None, vmem=6, cost=1_000_000):
+def call(kernel, out, args, scratch=(), specs=None, out_specs=None, vmem=6, cost=1_000_000, far=()):
     specs = specs or {}
     in_specs = [
         specs.get(i, pl.BlockSpec(memory_space=pltpu.VMEM)) for i in range(len(args))
+    ]
+    args = [
+        pltpu.with_memory_space_constraint(x, pltpu.HBM) if i in far else x
+        for i, x in enumerate(args)
     ]
     many = isinstance(out, (list, tuple))
     outs = list(out) if many else [out]
@@ -149,7 +154,9 @@
             out[p : p + n] = ref[...]
             p += n
         out[p] = BOND * group[5][...].astype(F32)
-    v3_out[...] = v3[0]
+    rows = v3.shape[1]
+    v3_out[0:rows, :] = v3[0]
+    v3_out[rows:, :] = jnp.zeros((v3_out.shape[0] - rows, W), F32)
 
 
 def pack_y_kernel(v, cx, cy, st, via, mask, lo, hi, to_left, to_right):
@@ -229,7 +236,7 @@
     arriving = copies.start(
         *[
             (source, dest.at[pl.ds(PAD, rows), pl.ds(0, W)])
-            for source, dest in zip([*sources, vp], [*dests[:-1], evp])
+            for source, dest in zip([*sources, vp.at[pl.ds(0, rows), :]], [*dests[:-1], evp])
         ]
     )
 
@@ -383,9 +390,12 @@
     return blocks
 
 
-def first_top_kernel(low, here, v3, part, gx, gy, inv, via, bond, d_out, z_out, msg, delta, d0, ep, side, u, sem):
-    fetch = pltpu.make_async_copy(here, d0, sem)
-    fetch.start()
+def first_top_kernel(part, *refs):
+    inputs, (d_hbm, z_hbm, delta_hbm, msg), held = refs[:8], refs[8:12], refs[12:20]
+    low, d0, v3, gx, gy, inv, via, bond = held
+    d_out, z_out, delta, ep, side, u, sems = refs[20:]
+    copies = Copies(sems)
+    arriving = copies.start(*zip(inputs, held))
     rows = part.shape[0] - 3 * (2 * H + 8 * (side.shape[0] // W))
     total = rows + 2 * H
     sides = 8 * (side.shape[0] // W)
@@ -395,7 +405,7 @@
     own = unpack_side(part, row + 2 * H, total, u)
     others = unpack_side(part, row + 2 * H + sides + 2 * H, total, u)
     theirs = unpack_side(part, total, total, u)
-    fetch.wait()
+    wait(arriving)
     delta[PAD : PAD + rows, main] = jnp.zeros((rows, W), F32)
     ep[PAD : PAD + rows, main] = part[H : H + rows, :]
 
@@ -426,7 +436,9 @@
         msg[r, :] = d[:, :W]
 
     each_chunk(H, total, body, WIDE)
+    leaving = copies.start((d_out, d_hbm), (z_out, z_hbm), (delta, delta_hbm))
     pack_side(side, msg, total, total)
+    wait(leaving)
 
 
 def second_top_kernel(low, inv_low, delta, here, z, part, gx, gy, inv, via, bond, d_out, z_out, msg, weight, ep, u):
@@ -544,12 +556,10 @@
 def effect_kernel(
     labels, cur, lo, hi, f_left, f_right, *refs
 ):
-    coefficients, (v0, picked, e11_out, e21_out, z21, d20_out) = refs[:9], refs[9:15]
-    held, refs = refs[15:24], refs[24:]
-    inv0, gx0, gy0, via0, inv1, gx1, gy1, sb0, d20 = held
-    ec, e0, e1, z10, z11, e2, z20, e11, e21, u, acc, sems = refs
+    (inv0, gx0, gy0, via0, inv1, gx1, gy1, sb0, d20), refs = refs[:9], refs[9:]
+    v0_out, picked_out, e11_out, e21_out, z21_out, d20_out = refs[:6]
+    ec, e0, e1, z10, z11, e2, z20, e11, e21, u, acc, z21, d20_sum, picked, sems = refs[6:]
     copies = Copies(sems)
-    arriving = copies.start(*zip(coefficients, held))
     rows = cur.shape[0]
     total = rows + 2 * H
     main, edge = slice(0, W), slice(W, 2 * W)
@@ -563,15 +573,11 @@
         n = min(W, total - W * j)
         ec[H + W * j : H + W * j + n, edge] = u[...].T[:n]
 
-    wait(arriving[0:1])
-
     def zeroth(s):
         a = pl.ds(s, WIDE)
         e0[a, :] = inv0[a, :] * ec[a, :]
 
     each_chunk(H, total, zeroth, WIDE)
-    wait(arriving[1:5])
-
     def first(s):
         a = pl.ds(s, WIDE)
         here = e0[a, :]
@@ -583,8 +589,6 @@
         e11[a, :] = B1 * z
 
     each_chunk(H, total, first, WIDE)
-    wait(arriving[5:7])
-
     def second(s):
         a = pl.ds(s, WIDE)
         low, high, between = e1[a, :], e11[a, :], via0[a, :]
@@ -598,9 +602,7 @@
         e21[a, :] = A2 * high + B2 * z
 
     each_chunk(H, total, second, WIDE)
-    leaving = copies.start((e11, e11_out), (e21, e21_out))
-    wait(arriving[7:])
-
+    copies.start((e11, e11_out), (e21, e21_out))
     def third(i):
         s = pl.multiple_of(i + PAD, 8)
         a, o = pl.ds(s, STEP), pl.ds(i, STEP)
@@ -608,21 +610,25 @@
         nb = weighted(e2, s, STEP, gx0, gy0)[:, main] + via0[a, main] * e21[a, main]
         z = z20[a, main] - here + inv0[a, main] * nb
         whole = sb0[o, :] + e0[a, main] + e1[a, main] + (1.0 + A3) * here + B3 * z
-        v0[o, :] = whole
         acc[o, :] = whole
-        d20_out[o, :] = d20[o, :] + here
+        d20_sum[o, :] = d20[o, :] + here
         z21[o, :] = z11[a, main]
 
     each_chunk(0, rows, third, STEP)
+    copies.start((acc.at[pl.ds(0, rows), :], v0_out), (z21, z21_out), (d20_sum, d20_out))
     acc[rows : rows + 8, :] = jnp.zeros((8, W), F32)
 
-    @pl.loop(0, labels.shape[0], unroll=8)
-    def _(k):
+    def pick(k):
         picked[pl.ds(pl.multiple_of(k * 8, 8), 8), :] = acc[
             pl.ds(pl.multiple_of(labels[k] * 8, 8), 8), :
         ]
 
-    wait(leaving)
+    count = labels.shape[0] // 4
+    for part in range(4):
+        pl.loop(part * count, (part + 1) * count, unroll=8)(pick)
+        a = pl.ds(part * count * 8, count * 8)
+        copies.start((picked.at[a, :], picked_out.at[a, :]))
+    wait(copies.made)
 
 
 def last_kernel(dest, back, field, part, weight, out, top):
@@ -668,7 +674,7 @@
 
     outgoing, dest = call(
         send_kernel,
-        [shape(devices * ROWS_MSG, W), jax.ShapeDtypeStruct((nb,), jnp.int32)],
+        [pltpu.HBM((devices * ROWS_MSG, W), F32), jax.ShapeDtypeStruct((nb,), jnp.int32)],
         [owner.reshape(nb), slot, blocks],
         scratch=[
             pltpu.SMEM((devices,), jnp.int32),
@@ -695,12 +701,12 @@
     first_rows, last_rows, v_top = pl.pallas_call(
         pack_x_kernel,
         grid=(1,),
-        out_shape=[shape(count, 8, W)] * 2 + [shape(rows, W)],
+        out_shape=[shape(count, 8, W)] * 2 + [shape(rows + TAIL, W)],
         in_specs=[specs[i] for i in range(13)],
         out_specs=[
             pl.BlockSpec((count, 8, W), lambda _: (0, 0, 0)),
             pl.BlockSpec((count, 8, W), lambda _: (0, 0, 0)),
-            pl.BlockSpec((rows, W), lambda _: (0, 0)),
+            pl.BlockSpec((rows + TAIL, W), lambda _: (0, 0)),
         ],
         name="pack_x_kernel",
         compiler_params=pltpu.CompilerParams(vmem_limit_bytes=58 << 20),
@@ -769,40 +775,42 @@
         [cur, cur_lo, cur_hi],
         scratch=[buffer(side_blocks * W, W)],
     )
-    cur_left, cur_right, part0 = lax.optimization_barrier((cur_left, cur_right, part0))
-    d13, z13, msg1, delta = call(
+    labels, part0 = lax.optimization_barrier((labels, part0))
+    far_one = pltpu.HBM((nr, 2 * W), F32)
+    d13, z13, delta, msg1 = call(
         first_top_kernel,
-        [one, one, msg_shape, one],
-        [d02, d03, v3, part0, *top],
-        scratch=[buffer(nr, 2 * W)] * 2
-        + [buffer(side_blocks * W, W), buffer(W, W), pltpu.SemaphoreType.DMA],
-        specs={1: ANY},
+        [far_one, far_one, far_one, msg_shape],
+        [part0, d02, d03, v3, *top],
+        scratch=[buffer(nr, 2 * W)] * 12
+        + [buffer(side_blocks * W, W), buffer(W, W), pltpu.SemaphoreType.DMA((11,))],
+        specs={i: ANY for i in range(1, 9)},
+        out_specs=[ANY] * 3 + [pl.BlockSpec(memory_space=pltpu.VMEM)],
         vmem=VMEM_TOP,
-    )
+        far=range(1, 9),
+    )
+    cur_left, cur_right, msg1 = lax.optimization_barrier((cur_left, cur_right, msg1))
     part1 = facing(msg1)
     d23, z23, msg2, weight = call(
         second_top_kernel,
         [one, one, tile, tile],
         [d12, inv[2], delta, d13, z13, part1, *top],
         scratch=[buffer(nr, W), buffer(W, W)],
-        vmem=VMEM_TOP,
+        vmem=VMEM_FINAL,
     )
 
     cur_f_left = shift(cur_right, "yt", 1)
     cur_f_right = shift(cur_left, "yt", -1)
     v0, picked, e11, e21, ze21, d20 = call(
         effect_kernel,
-        [tile, shape(devices * CAP * 8, W), one, one, tile, tile],
+        [pltpu.HBM(d, F32) for d in (
+            (rows, W), (devices * CAP * 8, W), (nr, 2 * W), (nr, 2 * W), (rows, W), (rows, W))],
         [labels, cur, cur_lo, cur_hi, cur_f_left, cur_f_right,
          inv[0], gx[0], gy[0], via_e[0], inv[1], gx[1], gy[1], sb0, d20],
-        scratch=[buffer(nr, 2 * W)] * 7
-        + [buffer(rows, W)] * 2
-        + [buffer(nr, 2 * W)] * 9
-        + [buffer(W, W), buffer(rows + 8, W), pltpu.SemaphoreType.DMA((11,))],
-        specs={0: SMEM} | {i: ANY for i in range(6, 15)},
-        out_specs=[pl.BlockSpec(memory_space=pltpu.VMEM)] * 2
-        + [ANY] * 2
-        + [pl.BlockSpec(memory_space=pltpu.VMEM)] * 2,
+        scratch=[buffer(nr, 2 * W)] * 9
+        + [buffer(W, W), buffer(rows + 8, W), buffer(rows, W), buffer(rows, W)]
+        + [buffer(devices * CAP * 8, W), pltpu.SemaphoreType.DMA((9,))],
+        specs={0: SMEM},
+        out_specs=[ANY] * 6,
         vmem=VMEM_EFFECT,
     )
     picked, part1 = lax.optimization_barrier((picked, part1))

time: 123 us -> 119 us (0.967)
  local copies, waits for them, and re-layouts: 5.45 us -> 2.01 us
  starting transfers between devices: 45.6 us -> 48.5 us
  Pallas kernels: 55.6 us -> 53.3 us
  waiting for transfers between devices: 14.8 us -> 13.4 us
    ppermute x4, waiting for transfers between devices: 7.21 us -> 3.4 us  [facing(): return lax.ppermute(x, ALL, pairs)]
    unnamed x54, local copies, waits for them, and re-layouts: 5.45 us -> 2.01 us
    ppermute x8, waiting for transfers between devices: 7.2 us -> 9.68 us  [shift(): return lax.ppermute(x, axis, ring(axis, step))]
    pallas_call x9, Pallas kernels: 51.1 us -> 48.8 us  [call(): pl.pallas_call(kernel, out_shape=outs if many else outs[0], in_specs=in_s...]
    all_to_all x1, starting transfers between devices: 9.13 us -> 11.3 us  [on_device(): back = lax.all_to_all(picked, ALL, 0, 0, tiled=True)]
    ppermute x4, starting transfers between devices: 10.1 us -> 12.1 us  [facing(): return lax.ppermute(x, ALL, pairs)]
    all_to_all x1, starting transfers between devices: 12.1 us -> 10.8 us  [on_device(): lax.all_to_all(outgoing.reshape(devices, ROWS_MSG, 1, W), ALL, 0, 0, tile...]
  transfers between devices with their start and end apart: 14 -> 14, of which waited for: 6 -> 7; matrix products, arithmetic and copies ran while one was open for 0% -> 1% of each run, Pallas kernels for 35% -> 41%
where the time goes in v5:
time: 119 us
  Pallas kernels  53.3 us (45%)
  starting transfers between devices  48.5 us (41%)
  waiting for transfers between devices  13.4 us (11%)
  local copies, waits for them, and re-layouts  2.01 us (2%)
    pallas_call x9, Pallas kernels, call(): pl.pallas_call(kernel, out_shape=outs if many else outs[0], in_specs=in_s...  48.8 us
    ppermute x8, starting transfers between devices, shift(): return lax.ppermute(x, axis, ring(axis, step))  14.3 us
    ppermute x4, starting transfers between devices, facing(): return lax.ppermute(x, ALL, pairs)  12.1 us
    all_to_all x1, starting transfers between devices, on_device(): back = lax.all_to_all(picked, ALL, 0, 0, tiled=True)  11.3 us
    all_to_all x1, starting transfers between devices, on_device(): lax.all_to_all(outgoing.reshape(devices, ROWS_MSG, 1, W), ALL, 0, 0, tile...  10.8 us
    ppermute x8, waiting for transfers between devices, shift(): return lax.ppermute(x, axis, ring(axis, step))  9.68 us
    ppermute x4, waiting for transfers between devices, facing(): return lax.ppermute(x, ALL, pairs)  3.4 us
    pallas_call x1, Pallas kernels, on_device(): pl.pallas_call(last_kernel, grid=(1,), out_shape=[shape(nb, 8, W), shape(...  2.56 us
  transfers between devices with their start and end apart: 14, of which 7 were waited for; matrix products, arithmetic and copies ran while one was open for 1% of the time, Pallas kernels for 41%

profile of v5, /device:TPU:1, one launch (start us, length us, event | category | flops | bytes accessed | tf_op | source)
XLA Modules:
  0.0 119.0 jit_solution(14179351660105280497)
XLA Ops:
  0.7 1.9 %pack_x_kernel.1 = (f32[20,8,128]{2,1,0:T(8,128)}, f32[20,8,128]{2,1,0:T(8,128)}, f32[536,128]{1,0:T(8,128)}) custom-call(f32[4,512,128]{2,1,0:T(8,128)} %refs_1_.3, f32[4,512,128]{2,1,0:T(8,128)} %refs_2_.3, f32[4,512,128]{2,1,0:T(8,128)} %refs_3_.3, f32[4,512,128]{2,1,0:T(8,128)} %refs_4_.3, f32[3,512,128]{2,1,0:T(8,128)} %refs_5_.3, s32[512,128]{1,0:T(8,128)} %refs_6_.3, ...), custom_call_target="tpu_custom_call" | custom-call | flops 1 | bytes 1000000 | tf_op jit(solution)/shard_map/pack_x_kernel/pallas_call | solution.py:701
  2.7 2.0 %collective-permute-start = (f32[20,8,128]{2,1,0:T(8,128)}, f32[20,8,128]{2,1,0:T(8,128)S(1)}, u32[]{:S(2)}, u32[]{:S(2)}) collective-permute-start(f32[20,8,128]{2,1,0:T(8,128)} %get-tuple-element.74), channel_id=1, source_target_pairs={{0,16},{16,32},{32,48},{48,64},{64,80},{80,96},{96,112},{112,0},{1... | collective-permute-start | bytes 245768 | tf_op jit(solution)/shard_map/ppermute | solution.py:648
  4.7 3.5 %collective-permute-start.1 = (f32[20,8,128]{2,1,0:T(8,128)}, f32[20,8,128]{2,1,0:T(8,128)S(1)}, u32[]{:S(2)}, u32[]{:S(2)}) collective-permute-start(f32[20,8,128]{2,1,0:T(8,128)} %get-tuple-element.75), channel_id=1, source_target_pairs={{0,112},{16,0},{32,16},{48,32},{64,48},{80,64},{96,80},{112,96},{1... | collective-permute-start | bytes 245768 | tf_op jit(solution)/shard_map/ppermute | solution.py:648
  8.2 3.2 %send_kernel.1 = (f32[2176,128]{1,0:T(8,128)}, s32[128]{0:T(128)S(1)}) custom-call(s32[128]{0:T(128)S(1)} %bitcast.8, s32[128]{0:T(128)S(1)} %copy-done.19, f32[128,8,128]{2,1,0:T(8,128)S(1)} %copy-done.13), custom_call_target="tpu_custom_call" | custom-call | flops 1000000 | bytes 1000000 | tf_op jit(solution)/shard_map/send_kernel/pallas_call | solution.py:47
  11.5 2.5 %collective-permute-start.4 = (f32[536,128]{1,0:T(8,128)}, f32[536,128]{1,0:T(8,128)S(1)}, u32[]{:S(2)}, u32[]{:S(2)}) collective-permute-start(f32[536,128]{1,0:T(8,128)} %get-tuple-element.83), channel_id=1, source_target_pairs={{0,8},{1,9},{2,10},{3,11},{4,12},{5,13},{6,14},{7,15},{8,0},{9,1},... | collective-permute-start | bytes 823304 | tf_op jit(solution)/shard_map/ppermute | solution.py:656
  14.1 1.9 %pack_y_kernel.1 = (f32[528,128]{1,0:T(8,128)S(1)}, f32[528,128]{1,0:T(8,128)S(1)}) custom-call(f32[4,512,128]{2,1,0:T(8,128)S(1)} %copy-done, f32[4,512,128]{2,1,0:T(8,128)S(1)} %copy-done.1, f32[4,512,128]{2,1,0:T(8,128)S(1)} %copy-done.2, f32[4,512,128]{2,1,0:T(8,128)S(1)} %copy-done.3, f32[3,512,128]{2,1,0:T(8,128)S(1)} %copy-done.4, ...), custom_call_target="tpu_custom_call" | custom-call | flops 1000000 | bytes 1000000 | tf_op jit(solution)/shard_map/pack_y_kernel/pallas_call | solution.py:47
  16.0 2.5 %collective-permute-start.2 = (f32[528,128]{1,0:T(8,128)S(1)}, f32[528,128]{1,0:T(8,128)S(1)}, u32[]{:S(2)}, u32[]{:S(2)}) collective-permute-start(f32[528,128]{1,0:T(8,128)S(1)} %get-tuple-element.81), channel_id=1, source_target_pairs={{0,1},{1,2},{2,3},{3,4},{4,5},{5,6},{6,7},{7,8},{8,9},{9,10},{10,1... | collective-permute-start | bytes 811016 | tf_op jit(solution)/shard_map/ppermute | solution.py:648
  18.5 3.4 %collective-permute-done.2.refs_10_ = f32[528,128]{1,0:T(8,128)S(1)} collective-permute-done((f32[528,128]{1,0:T(8,128)S(1)}, f32[528,128]{1,0:T(8,128)S(1)}, u32[]{:S(2)}, u32[]{:S(2)}) %collective-permute-start.2) | collective-permute-done | bytes 270368 | tf_op jit(solution)/shard_map/ppermute | solution.py:648
  21.9 2.8 %collective-permute-done.3.refs_11_ = f32[528,128]{1,0:T(8,128)S(1)} collective-permute-done((f32[528,128]{1,0:T(8,128)S(1)}, f32[528,128]{1,0:T(8,128)S(1)}, u32[]{:S(2)}, u32[]{:S(2)}) %collective-permute-start.3) | collective-permute-done | bytes 270368 | tf_op jit(solution)/shard_map/ppermute | solution.py:648
  24.7 0.7 copy-done.25
  25.5 10.8 %all-to-all-start = ((f32[128,17,1,128]{3,2,1,0:T(1,128)}), f32[128,17,1,128]{3,2,1,0:T(1,128)S(1)}, u32[]{:S(2)}, u32[]{:S(2)}) async-start(f32[128,17,1,128]{3,2,1,0:T(1,128)} %bitcast.10), calls=%async_computation | async-start | bytes 2228224 | tf_op jit(solution)/shard_map/all_to_all | solution.py:728
  36.3 0.7 pad_add_fusion.refs_0_
  37.0 15.7 %base_kernel.1 = (f32[544,256]{1,0:T(8,128)}, f32[544,256]{1,0:T(8,128)}, f32[544,256]{1,0:T(8,128)}, f32[544,256]{1,0:T(8,128)}, f32[544,256]{1,0:T(8,128)}, /*...) custom-call(s32[4]{0:T(128)} %pad_add_fusion.refs_0_, ...), custom_call_target="tpu_custom_call" | custom-call | flops 20000000 | bytes 20000000 | tf_op jit(solution)/shard_map/base_kernel/pallas_call | solution.py:47
  52.7 3.0 %collective-permute-start.5 = (f32[680,128]{1,0:T(8,128)}, f32[680,128]{1,0:T(8,128)S(1)}, u32[]{:S(2)}, u32[]{:S(2)}) collective-permute-start(f32[680,128]{1,0:T(8,128)} %get-tuple-element.89), channel_id=1, source_target_pairs={{0,8},{1,9},{2,10},{3,11},{4,12},{5,13},{6,14},{7,15},{8,0},{9,1},... | collective-permute-start | bytes 1044488 | tf_op jit(solution)/shard_map/ppermute | solution.py:656
  56.0 2.8 %map_kernel.1 = (f32[512,128]{1,0:T(8,128)S(1)}, f32[8,128]{1,0:T(8,128)S(1)}, f32[8,128]{1,0:T(8,128)S(1)}, s32[256]{0:T(256)S(1)}) custom-call(f32[2176,128]{1,0:T(8,128)S(1)} %bitcast.7), custom_call_target="tpu_custom_call" | custom-call | flops 1000000 | bytes 1000000 | tf_op jit(solution)/shard_map/map_kernel/pallas_call | solution.py:47
  58.8 0.3 collective-permute-start.6
  59.1 3.3 %collective-permute-start.7 = (f32[8,128]{1,0:T(8,128)S(1)}, f32[8,128]{1,0:T(8,128)S(1)}, u32[]{:S(2)}, u32[]{:S(2)}) collective-permute-start(f32[8,128]{1,0:T(8,128)S(1)} %get-tuple-element.93), channel_id=1, source_target_pairs={{0,112},{16,0},{32,16},{48,32},{64,48},{80,64},{96,80},{112,96},{1... | collective-permute-start | bytes 12296 | tf_op jit(solution)/shard_map/ppermute | solution.py:648
  62.4 0.7 collective-permute-done.5.part
  63.2 5.0 %first_top_kernel.1 = (f32[544,256]{1,0:T(8,128)}, f32[544,256]{1,0:T(8,128)}, f32[544,256]{1,0:T(8,128)}, f32[568,128]{1,0:T(8,128)S(1)}) custom-call(f32[680,128]{1,0:T(8,128)S(1)} %collective-permute-done.5.part, f32[544,256]{1,0:T(8,128)} %get-tuple-element.97.refs_0_, f32[544,256]{1,0:T(8,128)} %get-tuple-element.98.refs_1_, ...), custom_call_target="tpu_custom_call" | custom-call | flops 1000000 | bytes 1000000 | tf_op jit(solution)/shard_map/first_top_kernel/pallas_call | solution.py:47
  68.4 3.7 %collective-permute-start.10 = (f32[568,128]{1,0:T(8,128)S(1)}, f32[568,128]{1,0:T(8,128)S(1)}, u32[]{:S(2)}, u32[]{:S(2)}) collective-permute-start(f32[568,128]{1,0:T(8,128)S(1)} %get-tuple-element.118), channel_id=1, source_target_pairs={{0,8},{1,9},{2,10},{3,11},{4,12},{5,13},{6,14},{7,15},{8,0},{9,1},... | collective-permute-start | bytes 872456 | tf_op jit(solution)/shard_map/ppermute | solution.py:656
  72.1 2.6 %collective-permute-start.8 = (f32[8,640]{1,0:T(8,128)S(1)}, f32[8,640]{1,0:T(8,128)S(1)}, u32[]{:S(2)}, u32[]{:S(2)}) collective-permute-start(f32[8,640]{1,0:T(8,128)S(1)} %get-tuple-element.106), channel_id=1, source_target_pairs={{0,1},{1,2},{2,3},{3,4},{4,5},{5,6},{6,7},{7,8},{8,9},{9,10},{10,1... | collective-permute-start | bytes 61448 | tf_op jit(solution)/shard_map/ppermute | solution.py:648
  74.7 0.9 collective-permute-done.8.f_left
  75.6 2.6 %collective-permute-done.9.f_right = f32[8,640]{1,0:T(8,128)S(1)} collective-permute-done((f32[8,640]{1,0:T(8,128)S(1)}, f32[8,640]{1,0:T(8,128)S(1)}, u32[]{:S(2)}, u32[]{:S(2)}) %collective-permute-start.9) | collective-permute-done | bytes 20512 | tf_op jit(solution)/shard_map/ppermute | solution.py:648
  78.3 5.8 %effect_kernel.1 = (f32[512,128]{1,0:T(8,128)}, f32[2048,128]{1,0:T(8,128)}, f32[544,256]{1,0:T(8,128)}, f32[544,256]{1,0:T(8,128)}, f32[512,128]{1,0:T(8,128)}, /*index=5*/f32[512,128]{1,0:T(8,128)}) custom-call(s32[256]{0:T(256)S(1)} %get-tuple-element.90.labels, f32[512,128]{1,0:T(8,128)S(1)} %get-tuple-element.91.cur, ...), custom_call_target="tpu_custom_call" | custom-call | flops 1000000 | bytes 1000000 | tf_op jit(solution)/shard_map/effect_kernel/pallas_call | solution.py:47
  84.1 11.3 %all-to-all-start.1 = ((f32[128,16,128]{2,1,0:T(8,128)}), f32[128,16,128]{2,1,0:T(8,128)S(1)}, u32[]{:S(2)}, u32[]{:S(2)}) async-start(f32[128,16,128]{2,1,0:T(8,128)} %bitcast.11), calls=%async_computation.1 | async-start | bytes 2097152 | tf_op jit(solution)/shard_map/all_to_all | solution.py:818
  95.4 5.2 %second_top_kernel.1 = (f32[544,256]{1,0:T(8,128)}, f32[544,256]{1,0:T(8,128)}, f32[512,128]{1,0:T(8,128)}, f32[512,128]{1,0:T(8,128)}) custom-call(f32[544,256]{1,0:T(8,128)} %get-tuple-element.123.low.b12, f32[544,256]{1,0:T(8,128)} %get-tuple-element.130.inv_low.inv2, f32[544,256]{1,0:T(8,128)} %get-tuple-element.131.delta, ...), custom_call_target="tpu_custom_call" | custom-call | flops 1000000 | bytes 1000000 | tf_op jit(solution)/shard_map/second_top_kernel/pallas_call | solution.py:47
  100.7 2.9 %collective-permute-start.11 = (f32[512,128]{1,0:T(8,128)}, f32[512,128]{1,0:T(8,128)S(1)}, u32[]{:S(2)}, u32[]{:S(2)}) collective-permute-start(f32[512,128]{1,0:T(8,128)} %get-tuple-element.140), channel_id=1, source_target_pairs={{0,8},{1,9},{2,10},{3,11},{4,12},{5,13},{6,14},{7,15},{8,0},{9,1},... | collective-permute-start | bytes 786440 | tf_op jit(solution)/shard_map/ppermute | solution.py:656
  103.6 9.0 %final_kernel.1.field = f32[4,512,128]{2,1,0:T(8,128)} custom-call(f32[512,128]{1,0:T(8,128)} %get-tuple-element.120.v0, f32[3,512,128]{2,1,0:T(8,128)} %get-tuple-element.121.vd0, f32[544,256]{1,0:T(8,128)} %get-tuple-element.122.d11, f32[544,256]{1,0:T(8,128)} %get-tuple-element.123.low.b12, f32[544,256]{1,0:T(8,128)} %get-tuple-element.124.z12, ...), custom_call_target="tpu_custom_call" | custom-call | flops 10000000 | bytes 10000000 | tf_op jit(solution)/shard_map/final_kernel/pallas_call | solution.py:47
  112.6 2.7 %collective-permute-done.11.part = f32[512,128]{1,0:T(8,128)S(1)} collective-permute-done((f32[512,128]{1,0:T(8,128)}, f32[512,128]{1,0:T(8,128)S(1)}, u32[]{:S(2)}, u32[]{:S(2)}) %collective-permute-start.11) | collective-permute-done | bytes 262176 | tf_op jit(solution)/shard_map/ppermute | solution.py:656
  115.3 0.7 copy-done.26
  116.0 0.4 copy-done.21
  116.4 2.6 %last_kernel.1 = (f32[128,8,128]{2,1,0:T(8,128)}, f32[4,512,128]{2,1,0:T(8,128)}) custom-call(s32[128]{0:T(128)} %copy-done.20, f32[2048,128]{1,0:T(8,128)} %bitcast.9, f32[4,512,128]{2,1,0:T(8,128)} %final_kernel.1.field, f32[512,128]{1,0:T(8,128)} %copy-done.26, f32[512,128]{1,0:T(8,128)} %get-tuple-element.141.weight), custom_call_target="tpu_custom_call", output_to_operand_aliasing={{1}: (2, {})} | custom-call | tf_op jit(solution)/shard_map/last_kernel/pallas_call | solution.py:831
  (62 shorter events, 0.7 us)
Async XLA Ops:
  0.6 13.4 %copy-start.5 = (s32[512,128]{1,0:T(8,128)S(1)}, s32[512,128]{1,0:T(8,128)}, u32[]{:S(2)}) copy-start(s32[512,128]{1,0:T(8,128)} %refs_6_.3) | copy-start | bytes 786436
  0.6 13.4 %copy-start.4 = (f32[3,512,128]{2,1,0:T(8,128)S(1)}, f32[3,512,128]{2,1,0:T(8,128)}, u32[]{:S(2)}) copy-start(f32[3,512,128]{2,1,0:T(8,128)} %refs_5_.3) | copy-start | bytes 2359300
  0.7 7.6 %copy-start.19 = (s32[128]{0:T(128)S(1)}, s32[128]{0:T(128)}, u32[]{:S(2)}) copy-start(s32[128]{0:T(128)} %slot_ref.1) | copy-start | bytes 1540
  0.7 7.6 %copy-start.18 = (s32[128,1]{0,1:T(1,128)S(1)}, s32[128,1]{0,1:T(1,128)}, u32[]{:S(2)}) copy-start(s32[128,1]{0,1:T(1,128)} %param.16) | copy-start | bytes 1540
  0.7 13.3 %copy-start = (f32[4,512,128]{2,1,0:T(8,128)S(1)}, f32[4,512,128]{2,1,0:T(8,128)}, u32[]{:S(2)}) copy-start(f32[4,512,128]{2,1,0:T(8,128)} %refs_1_.3) | copy-start | bytes 3145732
  0.7 13.3 %copy-start.1 = (f32[4,512,128]{2,1,0:T(8,128)S(1)}, f32[4,512,128]{2,1,0:T(8,128)}, u32[]{:S(2)}) copy-start(f32[4,512,128]{2,1,0:T(8,128)} %refs_2_.3) | copy-start | bytes 3145732
  0.7 13.3 %copy-start.2 = (f32[4,512,128]{2,1,0:T(8,128)S(1)}, f32[4,512,128]{2,1,0:T(8,128)}, u32[]{:S(2)}) copy-start(f32[4,512,128]{2,1,0:T(8,128)} %refs_3_.3) | copy-start | bytes 3145732
  0.7 13.3 %copy-start.3 = (f32[4,512,128]{2,1,0:T(8,128)S(1)}, f32[4,512,128]{2,1,0:T(8,128)}, u32[]{:S(2)}) copy-start(f32[4,512,128]{2,1,0:T(8,128)} %refs_4_.3) | copy-start | bytes 3145732
  2.7 8.8 %collective-permute-start = (f32[20,8,128]{2,1,0:T(8,128)}, f32[20,8,128]{2,1,0:T(8,128)S(1)}, u32[]{:S(2)}, u32[]{:S(2)}) collective-permute-start(f32[20,8,128]{2,1,0:T(8,128)} %get-tuple-element.74), channel_id=1, source_target_pairs={{0,16},{16,32},{32,48},{48,64},{64,80},{80,96},{96,112},{112,0},{1... | collective-permute-start | bytes 245768 | tf_op jit(solution)/shard_map/ppermute | solution.py:648
  4.7 6.8 %collective-permute-start.1 = (f32[20,8,128]{2,1,0:T(8,128)}, f32[20,8,128]{2,1,0:T(8,128)S(1)}, u32[]{:S(2)}, u32[]{:S(2)}) collective-permute-start(f32[20,8,128]{2,1,0:T(8,128)} %get-tuple-element.75), channel_id=1, source_target_pairs={{0,112},{16,0},{32,16},{48,32},{64,48},{80,64},{96,80},{112,96},{1... | collective-permute-start | bytes 245768 | tf_op jit(solution)/shard_map/ppermute | solution.py:648
  11.5 13.2 %collective-permute-start.4 = (f32[536,128]{1,0:T(8,128)}, f32[536,128]{1,0:T(8,128)S(1)}, u32[]{:S(2)}, u32[]{:S(2)}) collective-permute-start(f32[536,128]{1,0:T(8,128)} %get-tuple-element.83), channel_id=1, source_target_pairs={{0,8},{1,9},{2,10},{3,11},{4,12},{5,13},{6,14},{7,15},{8,0},{9,1},... | collective-permute-start | bytes 823304 | tf_op jit(solution)/shard_map/ppermute | solution.py:656
  16.0 5.9 %collective-permute-start.2 = (f32[528,128]{1,0:T(8,128)S(1)}, f32[528,128]{1,0:T(8,128)S(1)}, u32[]{:S(2)}, u32[]{:S(2)}) collective-permute-start(f32[528,128]{1,0:T(8,128)S(1)} %get-tuple-element.81), channel_id=1, source_target_pairs={{0,1},{1,2},{2,3},{3,4},{4,5},{5,6},{6,7},{7,8},{8,9},{9,10},{10,1... | collective-permute-start | bytes 811016 | tf_op jit(solution)/shard_map/ppermute | solution.py:648
  18.5 6.2 %collective-permute-start.3 = (f32[528,128]{1,0:T(8,128)S(1)}, f32[528,128]{1,0:T(8,128)S(1)}, u32[]{:S(2)}, u32[]{:S(2)}) collective-permute-start(f32[528,128]{1,0:T(8,128)S(1)} %get-tuple-element.82), channel_id=1, source_target_pairs={{0,15},{1,0},{2,1},{3,2},{4,3},{5,4},{6,5},{7,6},{8,7},{9,8},{10,9... | collective-permute-start | bytes 811016 | tf_op jit(solution)/shard_map/ppermute | solution.py:648
  25.5 30.5 %all-to-all-start = ((f32[128,17,1,128]{3,2,1,0:T(1,128)}), f32[128,17,1,128]{3,2,1,0:T(1,128)S(1)}, u32[]{:S(2)}, u32[]{:S(2)}) async-start(f32[128,17,1,128]{3,2,1,0:T(1,128)} %bitcast.10), calls=%async_computation | async-start | bytes 2228224 | tf_op jit(solution)/shard_map/all_to_all | solution.py:728
  52.7 10.5 %collective-permute-start.5 = (f32[680,128]{1,0:T(8,128)}, f32[680,128]{1,0:T(8,128)S(1)}, u32[]{:S(2)}, u32[]{:S(2)}) collective-permute-start(f32[680,128]{1,0:T(8,128)} %get-tuple-element.89), channel_id=1, source_target_pairs={{0,8},{1,9},{2,10},{3,11},{4,12},{5,13},{6,14},{7,15},{8,0},{9,1},... | collective-permute-start | bytes 1044488 | tf_op jit(solution)/shard_map/ppermute | solution.py:656
  58.8 9.4 %collective-permute-start.6 = (f32[8,128]{1,0:T(8,128)S(1)}, f32[8,128]{1,0:T(8,128)S(1)}, u32[]{:S(2)}, u32[]{:S(2)}) collective-permute-start(f32[8,128]{1,0:T(8,128)S(1)} %get-tuple-element.92), channel_id=1, source_target_pairs={{0,16},{16,32},{32,48},{48,64},{64,80},{80,96},{96,112},{112,0},{1... | collective-permute-start | bytes 12296 | tf_op jit(solution)/shard_map/ppermute | solution.py:648
  59.1 9.1 %collective-permute-start.7 = (f32[8,128]{1,0:T(8,128)S(1)}, f32[8,128]{1,0:T(8,128)S(1)}, u32[]{:S(2)}, u32[]{:S(2)}) collective-permute-start(f32[8,128]{1,0:T(8,128)S(1)} %get-tuple-element.93), channel_id=1, source_target_pairs={{0,112},{16,0},{32,16},{48,32},{64,48},{80,64},{96,80},{112,96},{1... | collective-permute-start | bytes 12296 | tf_op jit(solution)/shard_map/ppermute | solution.py:648
  63.2 15.1 %copy-start.6 = (f32[544,256]{1,0:T(8,128)S(1)}, f32[544,256]{1,0:T(8,128)}, u32[]{:S(2)}) copy-start(f32[544,256]{1,0:T(8,128)} %get-tuple-element.113.refs_5_.gx1) | copy-start | bytes 1671172
  63.2 15.1 %copy-start.7 = (f32[544,256]{1,0:T(8,128)S(1)}, f32[544,256]{1,0:T(8,128)}, u32[]{:S(2)}) copy-start(f32[544,256]{1,0:T(8,128)} %get-tuple-element.114.refs_6_.gy1) | copy-start | bytes 1671172
  63.2 15.1 %copy-start.8 = (f32[544,256]{1,0:T(8,128)S(1)}, f32[544,256]{1,0:T(8,128)}, u32[]{:S(2)}) copy-start(f32[544,256]{1,0:T(8,128)} %get-tuple-element.112.refs_4_.inv1) | copy-start | bytes 1671172
  63.2 15.1 %copy-start.9 = (f32[544,256]{1,0:T(8,128)S(1)}, f32[544,256]{1,0:T(8,128)}, u32[]{:S(2)}) copy-start(f32[544,256]{1,0:T(8,128)} %get-tuple-element.111.refs_3_.via0) | copy-start | bytes 1671172
  63.2 15.1 %copy-start.10 = (f32[544,256]{1,0:T(8,128)S(1)}, f32[544,256]{1,0:T(8,128)}, u32[]{:S(2)}) copy-start(f32[544,256]{1,0:T(8,128)} %get-tuple-element.109.refs_1_) | copy-start | bytes 1671172
  63.2 15.1 %copy-start.11 = (f32[544,256]{1,0:T(8,128)S(1)}, f32[544,256]{1,0:T(8,128)}, u32[]{:S(2)}) copy-start(f32[544,256]{1,0:T(8,128)} %get-tuple-element.110.refs_2_) | copy-start | bytes 1671172
  63.2 15.1 %copy-start.12 = (f32[544,256]{1,0:T(8,128)S(1)}, f32[544,256]{1,0:T(8,128)}, u32[]{:S(2)}) copy-start(f32[544,256]{1,0:T(8,128)} %get-tuple-element.108.refs_0_) | copy-start | bytes 1671172
  63.2 15.1 %copy-start.16 = (f32[512,128]{1,0:T(8,128)S(1)}, f32[512,128]{1,0:T(8,128)}, u32[]{:S(2)}) copy-start(f32[512,128]{1,0:T(8,128)} %get-tuple-element.116.refs_8_) | copy-start | bytes 786436
  63.2 15.1 %copy-start.17 = (f32[512,128]{1,0:T(8,128)S(1)}, f32[512,128]{1,0:T(8,128)}, u32[]{:S(2)}) copy-start(f32[512,128]{1,0:T(8,128)} %get-tuple-element.115.refs_7_) | copy-start | bytes 786436
  68.4 15.7 %collective-permute-start.10 = (f32[568,128]{1,0:T(8,128)S(1)}, f32[568,128]{1,0:T(8,128)S(1)}, u32[]{:S(2)}, u32[]{:S(2)}) collective-permute-start(f32[568,128]{1,0:T(8,128)S(1)} %get-tuple-element.118), channel_id=1, source_target_pairs={{0,8},{1,9},{2,10},{3,11},{4,12},{5,13},{6,14},{7,15},{8,0},{9,1},... | collective-permute-start | bytes 872456 | tf_op jit(solution)/shard_map/ppermute | solution.py:656
  72.1 3.5 %collective-permute-start.8 = (f32[8,640]{1,0:T(8,128)S(1)}, f32[8,640]{1,0:T(8,128)S(1)}, u32[]{:S(2)}, u32[]{:S(2)}) collective-permute-start(f32[8,640]{1,0:T(8,128)S(1)} %get-tuple-element.106), channel_id=1, source_target_pairs={{0,1},{1,2},{2,3},{3,4},{4,5},{5,6},{6,7},{7,8},{8,9},{9,10},{10,1... | collective-permute-start | bytes 61448 | tf_op jit(solution)/shard_map/ppermute | solution.py:648
  74.7 3.5 %collective-permute-start.9 = (f32[8,640]{1,0:T(8,128)S(1)}, f32[8,640]{1,0:T(8,128)S(1)}, u32[]{:S(2)}, u32[]{:S(2)}) collective-permute-start(f32[8,640]{1,0:T(8,128)S(1)} %get-tuple-element.107), channel_id=1, source_target_pairs={{0,15},{1,0},{2,1},{3,2},{4,3},{5,4},{6,5},{7,6},{8,7},{9,8},{10,9... | collective-permute-start | bytes 61448 | tf_op jit(solution)/shard_map/ppermute | solution.py:648
  84.1 11.3 %copy-start.22 = (f32[568,128]{1,0:T(8,128)}, f32[568,128]{1,0:T(8,128)S(1)}, u32[]{:S(2)}) copy-start(f32[568,128]{1,0:T(8,128)S(1)} %collective-permute-done.10.part) | copy-start | bytes 872452
  84.1 31.2 %all-to-all-start.1 = ((f32[128,16,128]{2,1,0:T(8,128)}), f32[128,16,128]{2,1,0:T(8,128)S(1)}, u32[]{:S(2)}, u32[]{:S(2)}) async-start(f32[128,16,128]{2,1,0:T(8,128)} %bitcast.11), calls=%async_computation.1 | async-start | bytes 2097152 | tf_op jit(solution)/shard_map/all_to_all | solution.py:818
  100.7 14.6 %collective-permute-start.11 = (f32[512,128]{1,0:T(8,128)}, f32[512,128]{1,0:T(8,128)S(1)}, u32[]{:S(2)}, u32[]{:S(2)}) collective-permute-start(f32[512,128]{1,0:T(8,128)} %get-tuple-element.140), channel_id=1, source_target_pairs={{0,8},{1,9},{2,10},{3,11},{4,12},{5,13},{6,14},{7,15},{8,0},{9,1},... | collective-permute-start | bytes 786440 | tf_op jit(solution)/shard_map/ppermute | solution.py:656
  (9 other events, 27.3 us)

commit v6 on v5

--- a/solution.py
+++ b/solution.py
@@ -27,7 +27,7 @@
 H = 8
 PAD = 16
 Q = 4
-WIDE = 48
+WIDE = 88
 STEP = 64
 ROWS_MSG = CAP * 8 + 1
 
@@ -102,8 +102,15 @@
         body(pl.multiple_of(first + k * step, 8))
 
 
-def send_kernel(owner_ref, slot_ref, blocks_ref, out_hbm, dest_ref, count_ref, buf, slots, out_ref, sems):
+def send_kernel(
+    owner_ref, slot_ref, blocks_ref, v_ref, out_hbm, dest_ref, top_hbm,
+    count_ref, buf, slots, out_ref, top_ref, sems,
+):
     devices = count_ref.shape[0]
+    copies = Copies(sems)
+    rows = v_ref.shape[1]
+    top = v_ref.at[v_ref.shape[0] - 1]
+    [fetch] = copies.start((top, top_ref.at[pl.ds(0, rows), :]))
 
     @pl.loop(0, devices, unroll=8)
     def _(o):
@@ -134,19 +141,21 @@
             jnp.concatenate(pieces, axis=0)
         )
 
-    copies = Copies(sems)
+    fetch.wait()
+    top_ref[rows:, :] = jnp.zeros((TAIL, W), F32)
+    leaving = copies.start((top_ref, top_hbm))
     groups = devices // 8 // 4
     for part in range(4):
         pl.loop(part * groups, (part + 1) * groups)(assemble)
         n = groups * 8 * ROWS_MSG
         a = pl.ds(part * n, n)
-        copies.start((out_ref.at[a, :], out_hbm.at[a, :]))
-    wait(copies.made)
+        leaving += copies.start((out_ref.at[a, :], out_hbm.at[a, :]))
+    wait(leaving)
 
 
 def pack_x_kernel(*refs):
-    firsts, lasts, v3 = refs[:6], refs[6:12], refs[12]
-    first_out, last_out, v3_out = refs[13:]
+    firsts, lasts = refs[:6], refs[6:12]
+    first_out, last_out = refs[12:]
     for group, out in ((firsts, first_out), (lasts, last_out)):
         p = 0
         for ref in group[:5]:
@@ -154,9 +163,6 @@
             out[p : p + n] = ref[...]
             p += n
         out[p] = BOND * group[5][...].astype(F32)
-    rows = v3.shape[1]
-    v3_out[0:rows, :] = v3[0]
-    v3_out[rows:, :] = jnp.zeros((v3_out.shape[0] - rows, W), F32)
 
 
 def pack_y_kernel(v, cx, cy, st, via, mask, lo, hi, to_left, to_right):
@@ -393,14 +399,17 @@
 def first_top_kernel(part, *refs):
     inputs, (d_hbm, z_hbm, delta_hbm, msg), held = refs[:8], refs[8:12], refs[12:20]
     low, d0, v3, gx, gy, inv, via, bond = held
-    d_out, z_out, delta, ep, side, u, sems = refs[20:]
+    d_out, z_out, delta, ep, side, u, part_held, sems = refs[20:]
     copies = Copies(sems)
+    [came] = copies.start((part, part_held))
+    part = part_held
     arriving = copies.start(*zip(inputs, held))
     rows = part.shape[0] - 3 * (2 * H + 8 * (side.shape[0] // W))
     total = rows + 2 * H
     sides = 8 * (side.shape[0] // W)
     main, edge = slice(0, W), slice(W, 2 * W)
     u[...] = jnp.zeros_like(u)
+    came.wait()
     row = total + sides
     own = unpack_side(part, row + 2 * H, total, u)
     others = unpack_side(part, row + 2 * H + sides + 2 * H, total, u)
@@ -672,22 +681,28 @@
         ]
     ).astype(jnp.int32)
 
-    outgoing, dest = call(
+    outgoing, dest, v_top = call(
         send_kernel,
-        [pltpu.HBM((devices * ROWS_MSG, W), F32), jax.ShapeDtypeStruct((nb,), jnp.int32)],
-        [owner.reshape(nb), slot, blocks],
+        [
+            pltpu.HBM((devices * ROWS_MSG, W), F32),
+            jax.ShapeDtypeStruct((nb,), jnp.int32),
+            pltpu.HBM((rows + TAIL, W), F32),
+        ],
+        [owner.reshape(nb), slot, blocks, v],
         scratch=[
             pltpu.SMEM((devices,), jnp.int32),
             pltpu.VMEM((devices * CAP * 8, W), F32),
             pltpu.VMEM((devices, W), jnp.int32),
             pltpu.VMEM((devices * ROWS_MSG, W), F32),
-            pltpu.SemaphoreType.DMA((4,)),
+            pltpu.VMEM((rows + TAIL, W), F32),
+            pltpu.SemaphoreType.DMA((6,)),
         ],
-        specs={0: SMEM, 1: SMEM},
-        out_specs=[HBM, SMEM],
+        specs={0: SMEM, 1: SMEM, 3: ANY},
+        out_specs=[ANY, SMEM, ANY],
+        far=(3,),
     )
     sources = [v, cx, cy, st, via]
-    args = sources + [mask] + sources + [mask, v]
+    args = sources + [mask] + sources + [mask]
     specs = {}
     last = rows // 8 - 1
     for i in range(5):
@@ -696,17 +711,15 @@
         specs[6 + i] = pl.BlockSpec((n, 8, W), lambda _: (0, last, 0))
     specs[5] = pl.BlockSpec((8, W), lambda _: (0, 0))
     specs[11] = pl.BlockSpec((8, W), lambda _: (last, 0))
-    specs[12] = pl.BlockSpec((1, rows, W), lambda _: (layers - 1, 0, 0))
     count = 5 * layers
-    first_rows, last_rows, v_top = pl.pallas_call(
+    first_rows, last_rows = pl.pallas_call(
         pack_x_kernel,
         grid=(1,),
-        out_shape=[shape(count, 8, W)] * 2 + [shape(rows + TAIL, W)],
-        in_specs=[specs[i] for i in range(13)],
+        out_shape=[shape(count, 8, W)] * 2,
+        in_specs=[specs[i] for i in range(12)],
         out_specs=[
             pl.BlockSpec((count, 8, W), lambda _: (0, 0, 0)),
             pl.BlockSpec((count, 8, W), lambda _: (0, 0, 0)),
-            pl.BlockSpec((rows + TAIL, W), lambda _: (0, 0)),
         ],
         name="pack_x_kernel",
         compiler_params=pltpu.CompilerParams(vmem_limit_bytes=58 << 20),
@@ -782,11 +795,12 @@
         [far_one, far_one, far_one, msg_shape],
         [part0, d02, d03, v3, *top],
         scratch=[buffer(nr, 2 * W)] * 12
-        + [buffer(side_blocks * W, W), buffer(W, W), pltpu.SemaphoreType.DMA((11,))],
-        specs={i: ANY for i in range(1, 9)},
+        + [buffer(side_blocks * W, W), buffer(W, W), buffer(*msg0_shape.shape)]
+        + [pltpu.SemaphoreType.DMA((12,))],
+        specs={i: ANY for i in range(9)},
         out_specs=[ANY] * 3 + [pl.BlockSpec(memory_space=pltpu.VMEM)],
         vmem=VMEM_TOP,
-        far=range(1, 9),
+        far=range(9),
     )
     cur_left, cur_right, msg1 = lax.optimization_barrier((cur_left, cur_right, msg1))
     part1 = facing(msg1)
@@ -836,7 +850,7 @@
         out_specs=[whole, upper],
         input_output_aliases={2: 1},
         name="last_kernel",
-        compiler_params=pltpu.CompilerParams(vmem_limit_bytes=58 << 20),
+        compiler_params=pltpu.CompilerParams(vmem_limit_bytes=8 << 20),
     )(dest, back, voltage, part2, weight)
     return voltage, block_voltage
 

time: 119 us -> 117 us (0.983)
  Pallas kernels: 53.3 us -> 50.7 us
    pallas_call x9, Pallas kernels: 48.8 us -> 47 us  [call(): pl.pallas_call(kernel, out_shape=outs if many else outs[0], in_specs=in_s...]
  transfers between devices with their start and end apart: 14 -> 14, of which waited for: 7 -> 6; matrix products, arithmetic and copies ran while one was open for 1% -> 0% of each run, Pallas kernels for 41% -> 40%
where the time goes in v6:
time: 117 us; the launch traced here: 116 us
  Pallas kernels  50.7 us (43%)
  starting transfers between devices  48.5 us (41%)
  waiting for transfers between devices  13.9 us (12%)
  local copies, waits for them, and re-layouts  1.62 us (1%)
    pallas_call x9, Pallas kernels, call(): pl.pallas_call(kernel, out_shape=outs if many else outs[0], in_specs=in_s...  47 us
    ppermute x8, starting transfers between devices, shift(): return lax.ppermute(x, axis, ring(axis, step))  14.4 us
    ppermute x4, starting transfers between devices, facing(): return lax.ppermute(x, ALL, pairs)  12 us
    all_to_all x1, starting transfers between devices, on_device(): back = lax.all_to_all(picked, ALL, 0, 0, tiled=True)  11.3 us
    all_to_all x1, starting transfers between devices, on_device(): lax.all_to_all(outgoing.reshape(devices, ROWS_MSG, 1, W), ALL, 0, 0, tile...  10.8 us
    ppermute x8, waiting for transfers between devices, shift(): return lax.ppermute(x, axis, ring(axis, step))  9.68 us
    ppermute x4, waiting for transfers between devices, facing(): return lax.ppermute(x, ALL, pairs)  3.18 us
  transfers between devices with their start and end apart: 14, of which 6 were waited for; matrix products, arithmetic and copies ran while one was open for 0% of the time, Pallas kernels for 40%

profile of v6, /device:TPU:1, one launch (start us, length us, event | category | flops | bytes accessed | tf_op | source)
XLA Modules:
  0.0 116.3 jit_solution(17696219079899302168)
XLA Ops:
  0.7 1.6 %pack_x_kernel.1 = (f32[20,8,128]{2,1,0:T(8,128)}, f32[20,8,128]{2,1,0:T(8,128)}) custom-call(f32[4,512,128]{2,1,0:T(8,128)} %refs_1_.3, f32[4,512,128]{2,1,0:T(8,128)} %refs_2_.3, f32[4,512,128]{2,1,0:T(8,128)} %refs_3_.3, f32[4,512,128]{2,1,0:T(8,128)} %refs_4_.3, f32[3,512,128]{2,1,0:T(8,128)} %refs_5_.3, s32[512,128]{1,0:T(8,128)} %refs_6_.3, ...), custom_call_target="tpu_custom_call" | custom-call | flops 1 | bytes 1000000 | tf_op jit(solution)/shard_map/pack_x_kernel/pallas_call | solution.py:715
  2.3 2.1 %collective-permute-start = (f32[20,8,128]{2,1,0:T(8,128)}, f32[20,8,128]{2,1,0:T(8,128)S(1)}, u32[]{:S(2)}, u32[]{:S(2)}) collective-permute-start(f32[20,8,128]{2,1,0:T(8,128)} %get-tuple-element.74), channel_id=1, source_target_pairs={{0,16},{16,32},{32,48},{48,64},{64,80},{80,96},{96,112},{112,0},{1... | collective-permute-start | bytes 245768 | tf_op jit(solution)/shard_map/ppermute | solution.py:657
  4.5 3.6 %collective-permute-start.1 = (f32[20,8,128]{2,1,0:T(8,128)}, f32[20,8,128]{2,1,0:T(8,128)S(1)}, u32[]{:S(2)}, u32[]{:S(2)}) collective-permute-start(f32[20,8,128]{2,1,0:T(8,128)} %get-tuple-element.75), channel_id=1, source_target_pairs={{0,112},{16,0},{32,16},{48,32},{64,48},{80,64},{96,80},{112,96},{1... | collective-permute-start | bytes 245768 | tf_op jit(solution)/shard_map/ppermute | solution.py:657
  8.0 3.2 %send_kernel.1 = (f32[2176,128]{1,0:T(8,128)}, s32[128]{0:T(128)S(1)}, f32[536,128]{1,0:T(8,128)}) custom-call(s32[128]{0:T(128)S(1)} %bitcast.9, s32[128]{0:T(128)S(1)} %copy-done.20, f32[128,8,128]{2,1,0:T(8,128)S(1)} %copy-done.13, f32[4,512,128]{2,1,0:T(8,128)} %refs_1_.3), custom_call_target="tpu_custom_call" | custom-call | flops 1000000 | bytes 1000000 | tf_op jit(solution)/shard_map/send_kernel/pallas_call | solution.py:47
  11.3 2.5 %collective-permute-start.4 = (f32[536,128]{1,0:T(8,128)}, f32[536,128]{1,0:T(8,128)S(1)}, u32[]{:S(2)}, u32[]{:S(2)}) collective-permute-start(f32[536,128]{1,0:T(8,128)} %get-tuple-element.83), channel_id=1, source_target_pairs={{0,8},{1,9},{2,10},{3,11},{4,12},{5,13},{6,14},{7,15},{8,0},{9,1},... | collective-permute-start | bytes 823304 | tf_op jit(solution)/shard_map/ppermute | solution.py:665
  13.9 1.9 %pack_y_kernel.1 = (f32[528,128]{1,0:T(8,128)S(1)}, f32[528,128]{1,0:T(8,128)S(1)}) custom-call(f32[4,512,128]{2,1,0:T(8,128)S(1)} %copy-done, f32[4,512,128]{2,1,0:T(8,128)S(1)} %copy-done.1, f32[4,512,128]{2,1,0:T(8,128)S(1)} %copy-done.2, f32[4,512,128]{2,1,0:T(8,128)S(1)} %copy-done.3, f32[3,512,128]{2,1,0:T(8,128)S(1)} %copy-done.4, ...), custom_call_target="tpu_custom_call" | custom-call | flops 1000000 | bytes 1000000 | tf_op jit(solution)/shard_map/pack_y_kernel/pallas_call | solution.py:47
  15.8 2.5 %collective-permute-start.2 = (f32[528,128]{1,0:T(8,128)S(1)}, f32[528,128]{1,0:T(8,128)S(1)}, u32[]{:S(2)}, u32[]{:S(2)}) collective-permute-start(f32[528,128]{1,0:T(8,128)S(1)} %get-tuple-element.81), channel_id=1, source_target_pairs={{0,1},{1,2},{2,3},{3,4},{4,5},{5,6},{6,7},{7,8},{8,9},{9,10},{10,1... | collective-permute-start | bytes 811016 | tf_op jit(solution)/shard_map/ppermute | solution.py:657
  18.3 3.4 %collective-permute-done.2.refs_10_ = f32[528,128]{1,0:T(8,128)S(1)} collective-permute-done((f32[528,128]{1,0:T(8,128)S(1)}, f32[528,128]{1,0:T(8,128)S(1)}, u32[]{:S(2)}, u32[]{:S(2)}) %collective-permute-start.2) | collective-permute-done | bytes 270368 | tf_op jit(solution)/shard_map/ppermute | solution.py:657
  21.7 2.8 %collective-permute-done.3.refs_11_ = f32[528,128]{1,0:T(8,128)S(1)} collective-permute-done((f32[528,128]{1,0:T(8,128)S(1)}, f32[528,128]{1,0:T(8,128)S(1)}, u32[]{:S(2)}, u32[]{:S(2)}) %collective-permute-start.3) | collective-permute-done | bytes 270368 | tf_op jit(solution)/shard_map/ppermute | solution.py:657
  24.5 0.7 copy-done.25
  25.3 10.8 %all-to-all-start = ((f32[128,17,1,128]{3,2,1,0:T(1,128)}), f32[128,17,1,128]{3,2,1,0:T(1,128)S(1)}, u32[]{:S(2)}, u32[]{:S(2)}) async-start(f32[128,17,1,128]{3,2,1,0:T(1,128)} %bitcast.1), calls=%async_computation | async-start | bytes 2228224 | tf_op jit(solution)/shard_map/all_to_all | solution.py:741
  36.1 0.6 pad_add_fusion.refs_0_
  36.6 15.0 %base_kernel.1 = (f32[544,256]{1,0:T(8,128)}, f32[544,256]{1,0:T(8,128)}, f32[544,256]{1,0:T(8,128)}, f32[544,256]{1,0:T(8,128)}, f32[544,256]{1,0:T(8,128)}, /*...) custom-call(s32[4]{0:T(128)} %pad_add_fusion.refs_0_, ...), custom_call_target="tpu_custom_call" | custom-call | flops 20000000 | bytes 20000000 | tf_op jit(solution)/shard_map/base_kernel/pallas_call | solution.py:47
  51.7 3.0 %collective-permute-start.5 = (f32[680,128]{1,0:T(8,128)}, f32[680,128]{1,0:T(8,128)S(1)}, u32[]{:S(2)}, u32[]{:S(2)}) collective-permute-start(f32[680,128]{1,0:T(8,128)} %get-tuple-element.89), channel_id=1, source_target_pairs={{0,8},{1,9},{2,10},{3,11},{4,12},{5,13},{6,14},{7,15},{8,0},{9,1},... | collective-permute-start | bytes 1044488 | tf_op jit(solution)/shard_map/ppermute | solution.py:665
  54.6 1.1 all-to-all-done
  55.7 2.8 %map_kernel.1 = (f32[512,128]{1,0:T(8,128)S(1)}, f32[8,128]{1,0:T(8,128)S(1)}, f32[8,128]{1,0:T(8,128)S(1)}, s32[256]{0:T(256)S(1)}) custom-call(f32[2176,128]{1,0:T(8,128)S(1)} %bitcast.7), custom_call_target="tpu_custom_call" | custom-call | flops 1000000 | bytes 1000000 | tf_op jit(solution)/shard_map/map_kernel/pallas_call | solution.py:47
  58.5 0.4 collective-permute-start.6
  58.9 3.3 %collective-permute-start.7 = (f32[8,128]{1,0:T(8,128)S(1)}, f32[8,128]{1,0:T(8,128)S(1)}, u32[]{:S(2)}, u32[]{:S(2)}) collective-permute-start(f32[8,128]{1,0:T(8,128)S(1)} %get-tuple-element.93), channel_id=1, source_target_pairs={{0,112},{16,0},{32,16},{48,32},{64,48},{80,64},{96,80},{112,96},{1... | collective-permute-start | bytes 12296 | tf_op jit(solution)/shard_map/ppermute | solution.py:657
  62.2 0.7 copy-done.21
  63.0 4.8 %first_top_kernel.1 = (f32[544,256]{1,0:T(8,128)}, f32[544,256]{1,0:T(8,128)}, f32[544,256]{1,0:T(8,128)}, f32[568,128]{1,0:T(8,128)S(1)}) custom-call(f32[680,128]{1,0:T(8,128)} %copy-done.21, f32[544,256]{1,0:T(8,128)} %get-tuple-element.97.refs_0_, f32[544,256]{1,0:T(8,128)} %get-tuple-element.98.refs_1_, f32[544,256]{1,0:T(8,128)} %get-tuple-element.99.refs_2_, ...), custom_call_target="tpu_custom_call" | custom-call | flops 1000000 | bytes 1000000 | tf_op jit(solution)/shard_map/first_top_kernel/pallas_call | solution.py:47
  67.8 0.1 edges_kernel.1
  67.9 3.6 %collective-permute-start.10 = (f32[568,128]{1,0:T(8,128)S(1)}, f32[568,128]{1,0:T(8,128)S(1)}, u32[]{:S(2)}, u32[]{:S(2)}) collective-permute-start(f32[568,128]{1,0:T(8,128)S(1)} %get-tuple-element.118), channel_id=1, source_target_pairs={{0,8},{1,9},{2,10},{3,11},{4,12},{5,13},{6,14},{7,15},{8,0},{9,1},... | collective-permute-start | bytes 872456 | tf_op jit(solution)/shard_map/ppermute | solution.py:665
  71.6 2.6 %collective-permute-start.8 = (f32[8,640]{1,0:T(8,128)S(1)}, f32[8,640]{1,0:T(8,128)S(1)}, u32[]{:S(2)}, u32[]{:S(2)}) collective-permute-start(f32[8,640]{1,0:T(8,128)S(1)} %get-tuple-element.106), channel_id=1, source_target_pairs={{0,1},{1,2},{2,3},{3,4},{4,5},{5,6},{6,7},{7,8},{8,9},{9,10},{10,1... | collective-permute-start | bytes 61448 | tf_op jit(solution)/shard_map/ppermute | solution.py:657
  74.2 0.9 collective-permute-done.8.f_left
  75.1 2.6 %collective-permute-done.9.f_right = f32[8,640]{1,0:T(8,128)S(1)} collective-permute-done((f32[8,640]{1,0:T(8,128)S(1)}, f32[8,640]{1,0:T(8,128)S(1)}, u32[]{:S(2)}, u32[]{:S(2)}) %collective-permute-start.9) | collective-permute-done | bytes 20512 | tf_op jit(solution)/shard_map/ppermute | solution.py:657
  77.8 5.3 %effect_kernel.1 = (f32[512,128]{1,0:T(8,128)}, f32[2048,128]{1,0:T(8,128)}, f32[544,256]{1,0:T(8,128)}, f32[544,256]{1,0:T(8,128)}, f32[512,128]{1,0:T(8,128)}, /*index=5*/f32[512,128]{1,0:T(8,128)}) custom-call(s32[256]{0:T(256)S(1)} %get-tuple-element.90.labels, f32[512,128]{1,0:T(8,128)S(1)} %get-tuple-element.91.cur, ...), custom_call_target="tpu_custom_call" | custom-call | flops 1000000 | bytes 1000000 | tf_op jit(solution)/shard_map/effect_kernel/pallas_call | solution.py:47
  83.1 11.3 %all-to-all-start.1 = ((f32[128,16,128]{2,1,0:T(8,128)}), f32[128,16,128]{2,1,0:T(8,128)S(1)}, u32[]{:S(2)}, u32[]{:S(2)}) async-start(f32[128,16,128]{2,1,0:T(8,128)} %bitcast.10), calls=%async_computation.1 | async-start | bytes 2097152 | tf_op jit(solution)/shard_map/all_to_all | solution.py:832
  94.4 4.9 %second_top_kernel.1 = (f32[544,256]{1,0:T(8,128)}, f32[544,256]{1,0:T(8,128)}, f32[512,128]{1,0:T(8,128)}, f32[512,128]{1,0:T(8,128)}) custom-call(f32[544,256]{1,0:T(8,128)} %get-tuple-element.123.low.b12, f32[544,256]{1,0:T(8,128)} %get-tuple-element.130.inv_low.inv2, f32[544,256]{1,0:T(8,128)} %get-tuple-element.131.delta, ...), custom_call_target="tpu_custom_call" | custom-call | flops 1000000 | bytes 1000000 | tf_op jit(solution)/shard_map/second_top_kernel/pallas_call | solution.py:47
  99.3 2.9 %collective-permute-start.11 = (f32[512,128]{1,0:T(8,128)}, f32[512,128]{1,0:T(8,128)S(1)}, u32[]{:S(2)}, u32[]{:S(2)}) collective-permute-start(f32[512,128]{1,0:T(8,128)} %get-tuple-element.140), channel_id=1, source_target_pairs={{0,8},{1,9},{2,10},{3,11},{4,12},{5,13},{6,14},{7,15},{8,0},{9,1},... | collective-permute-start | bytes 786440 | tf_op jit(solution)/shard_map/ppermute | solution.py:665
  102.2 8.9 %final_kernel.1.field = f32[4,512,128]{2,1,0:T(8,128)} custom-call(f32[512,128]{1,0:T(8,128)} %get-tuple-element.120.v0, f32[3,512,128]{2,1,0:T(8,128)} %get-tuple-element.121.vd0, f32[544,256]{1,0:T(8,128)} %get-tuple-element.122.d11, f32[544,256]{1,0:T(8,128)} %get-tuple-element.123.low.b12, f32[544,256]{1,0:T(8,128)} %get-tuple-element.124.z12, ...), custom_call_target="tpu_custom_call" | custom-call | flops 10000000 | bytes 10000000 | tf_op jit(solution)/shard_map/final_kernel/pallas_call | solution.py:47
  111.1 3.2 %collective-permute-done.11.part = f32[512,128]{1,0:T(8,128)S(1)} collective-permute-done((f32[512,128]{1,0:T(8,128)}, f32[512,128]{1,0:T(8,128)S(1)}, u32[]{:S(2)}, u32[]{:S(2)}) %collective-permute-start.11) | collective-permute-done | bytes 262176 | tf_op jit(solution)/shard_map/ppermute | solution.py:665
  114.2 2.1 %last_kernel.1 = (f32[128,8,128]{2,1,0:T(8,128)}, f32[4,512,128]{2,1,0:T(8,128)}) custom-call(s32[128]{0:T(128)S(1)} %get-tuple-element.73.dest, f32[2048,128]{1,0:T(8,128)S(1)} %bitcast.8, f32[4,512,128]{2,1,0:T(8,128)} %final_kernel.1.field, f32[512,128]{1,0:T(8,128)S(1)} %collective-permute-done.11.part, ...), custom_call_target="tpu_custom_call", output_to_operand_aliasing={{1}: (2, {})} | custom-call | tf_op jit(solution)/shard_map/last_kernel/pallas_call | solution.py:845
  (60 shorter events, 0.2 us)
Async XLA Ops:
  0.6 7.4 %copy-start.20 = (s32[128]{0:T(128)S(1)}, s32[128]{0:T(128)}, u32[]{:S(2)}) copy-start(s32[128]{0:T(128)} %slot_ref.1) | copy-start | bytes 1540
  0.7 13.2 %copy-start.1 = (f32[4,512,128]{2,1,0:T(8,128)S(1)}, f32[4,512,128]{2,1,0:T(8,128)}, u32[]{:S(2)}) copy-start(f32[4,512,128]{2,1,0:T(8,128)} %refs_2_.3) | copy-start | bytes 3145732
  0.7 13.2 %copy-start.2 = (f32[4,512,128]{2,1,0:T(8,128)S(1)}, f32[4,512,128]{2,1,0:T(8,128)}, u32[]{:S(2)}) copy-start(f32[4,512,128]{2,1,0:T(8,128)} %refs_3_.3) | copy-start | bytes 3145732
  0.7 13.1 %copy-start.3 = (f32[4,512,128]{2,1,0:T(8,128)S(1)}, f32[4,512,128]{2,1,0:T(8,128)}, u32[]{:S(2)}) copy-start(f32[4,512,128]{2,1,0:T(8,128)} %refs_4_.3) | copy-start | bytes 3145732
  0.7 13.1 %copy-start.4 = (f32[3,512,128]{2,1,0:T(8,128)S(1)}, f32[3,512,128]{2,1,0:T(8,128)}, u32[]{:S(2)}) copy-start(f32[3,512,128]{2,1,0:T(8,128)} %refs_5_.3) | copy-start | bytes 2359300
  2.3 11.5 %copy-start = (f32[4,512,128]{2,1,0:T(8,128)S(1)}, f32[4,512,128]{2,1,0:T(8,128)}, u32[]{:S(2)}) copy-start(f32[4,512,128]{2,1,0:T(8,128)} %refs_1_.3) | copy-start | bytes 3145732
  2.3 11.5 %copy-start.5 = (s32[512,128]{1,0:T(8,128)S(1)}, s32[512,128]{1,0:T(8,128)}, u32[]{:S(2)}) copy-start(s32[512,128]{1,0:T(8,128)} %refs_6_.3) | copy-start | bytes 786436
  2.3 8.9 %collective-permute-start = (f32[20,8,128]{2,1,0:T(8,128)}, f32[20,8,128]{2,1,0:T(8,128)S(1)}, u32[]{:S(2)}, u32[]{:S(2)}) collective-permute-start(f32[20,8,128]{2,1,0:T(8,128)} %get-tuple-element.74), channel_id=1, source_target_pairs={{0,16},{16,32},{32,48},{48,64},{64,80},{80,96},{96,112},{112,0},{1... | collective-permute-start | bytes 245768 | tf_op jit(solution)/shard_map/ppermute | solution.py:657
  4.5 6.8 %collective-permute-start.1 = (f32[20,8,128]{2,1,0:T(8,128)}, f32[20,8,128]{2,1,0:T(8,128)S(1)}, u32[]{:S(2)}, u32[]{:S(2)}) collective-permute-start(f32[20,8,128]{2,1,0:T(8,128)} %get-tuple-element.75), channel_id=1, source_target_pairs={{0,112},{16,0},{32,16},{48,32},{64,48},{80,64},{96,80},{112,96},{1... | collective-permute-start | bytes 245768 | tf_op jit(solution)/shard_map/ppermute | solution.py:657
  11.3 13.2 %collective-permute-start.4 = (f32[536,128]{1,0:T(8,128)}, f32[536,128]{1,0:T(8,128)S(1)}, u32[]{:S(2)}, u32[]{:S(2)}) collective-permute-start(f32[536,128]{1,0:T(8,128)} %get-tuple-element.83), channel_id=1, source_target_pairs={{0,8},{1,9},{2,10},{3,11},{4,12},{5,13},{6,14},{7,15},{8,0},{9,1},... | collective-permute-start | bytes 823304 | tf_op jit(solution)/shard_map/ppermute | solution.py:665
  15.8 5.9 %collective-permute-start.2 = (f32[528,128]{1,0:T(8,128)S(1)}, f32[528,128]{1,0:T(8,128)S(1)}, u32[]{:S(2)}, u32[]{:S(2)}) collective-permute-start(f32[528,128]{1,0:T(8,128)S(1)} %get-tuple-element.81), channel_id=1, source_target_pairs={{0,1},{1,2},{2,3},{3,4},{4,5},{5,6},{6,7},{7,8},{8,9},{9,10},{10,1... | collective-permute-start | bytes 811016 | tf_op jit(solution)/shard_map/ppermute | solution.py:657
  18.3 6.2 %collective-permute-start.3 = (f32[528,128]{1,0:T(8,128)S(1)}, f32[528,128]{1,0:T(8,128)S(1)}, u32[]{:S(2)}, u32[]{:S(2)}) collective-permute-start(f32[528,128]{1,0:T(8,128)S(1)} %get-tuple-element.82), channel_id=1, source_target_pairs={{0,15},{1,0},{2,1},{3,2},{4,3},{5,4},{6,5},{7,6},{8,7},{9,8},{10,9... | collective-permute-start | bytes 811016 | tf_op jit(solution)/shard_map/ppermute | solution.py:657
  25.3 30.4 %all-to-all-start = ((f32[128,17,1,128]{3,2,1,0:T(1,128)}), f32[128,17,1,128]{3,2,1,0:T(1,128)S(1)}, u32[]{:S(2)}, u32[]{:S(2)}) async-start(f32[128,17,1,128]{3,2,1,0:T(1,128)} %bitcast.1), calls=%async_computation | async-start | bytes 2228224 | tf_op jit(solution)/shard_map/all_to_all | solution.py:741
  51.7 10.5 %collective-permute-start.5 = (f32[680,128]{1,0:T(8,128)}, f32[680,128]{1,0:T(8,128)S(1)}, u32[]{:S(2)}, u32[]{:S(2)}) collective-permute-start(f32[680,128]{1,0:T(8,128)} %get-tuple-element.89), channel_id=1, source_target_pairs={{0,8},{1,9},{2,10},{3,11},{4,12},{5,13},{6,14},{7,15},{8,0},{9,1},... | collective-permute-start | bytes 1044488 | tf_op jit(solution)/shard_map/ppermute | solution.py:665
  58.5 9.3 %collective-permute-start.6 = (f32[8,128]{1,0:T(8,128)S(1)}, f32[8,128]{1,0:T(8,128)S(1)}, u32[]{:S(2)}, u32[]{:S(2)}) collective-permute-start(f32[8,128]{1,0:T(8,128)S(1)} %get-tuple-element.92), channel_id=1, source_target_pairs={{0,16},{16,32},{32,48},{48,64},{64,80},{80,96},{96,112},{112,0},{1... | collective-permute-start | bytes 12296 | tf_op jit(solution)/shard_map/ppermute | solution.py:657
  58.9 8.9 %collective-permute-start.7 = (f32[8,128]{1,0:T(8,128)S(1)}, f32[8,128]{1,0:T(8,128)S(1)}, u32[]{:S(2)}, u32[]{:S(2)}) collective-permute-start(f32[8,128]{1,0:T(8,128)S(1)} %get-tuple-element.93), channel_id=1, source_target_pairs={{0,112},{16,0},{32,16},{48,32},{64,48},{80,64},{96,80},{112,96},{1... | collective-permute-start | bytes 12296 | tf_op jit(solution)/shard_map/ppermute | solution.py:657
  62.9 14.8 %copy-start.6 = (f32[544,256]{1,0:T(8,128)S(1)}, f32[544,256]{1,0:T(8,128)}, u32[]{:S(2)}) copy-start(f32[544,256]{1,0:T(8,128)} %get-tuple-element.113.refs_5_.gx1) | copy-start | bytes 1671172
  62.9 14.8 %copy-start.7 = (f32[544,256]{1,0:T(8,128)S(1)}, f32[544,256]{1,0:T(8,128)}, u32[]{:S(2)}) copy-start(f32[544,256]{1,0:T(8,128)} %get-tuple-element.114.refs_6_.gy1) | copy-start | bytes 1671172
  62.9 14.8 %copy-start.8 = (f32[544,256]{1,0:T(8,128)S(1)}, f32[544,256]{1,0:T(8,128)}, u32[]{:S(2)}) copy-start(f32[544,256]{1,0:T(8,128)} %get-tuple-element.112.refs_4_.inv1) | copy-start | bytes 1671172
  62.9 14.8 %copy-start.9 = (f32[544,256]{1,0:T(8,128)S(1)}, f32[544,256]{1,0:T(8,128)}, u32[]{:S(2)}) copy-start(f32[544,256]{1,0:T(8,128)} %get-tuple-element.111.refs_3_.via0) | copy-start | bytes 1671172
  62.9 14.8 %copy-start.10 = (f32[544,256]{1,0:T(8,128)S(1)}, f32[544,256]{1,0:T(8,128)}, u32[]{:S(2)}) copy-start(f32[544,256]{1,0:T(8,128)} %get-tuple-element.109.refs_1_) | copy-start | bytes 1671172
  62.9 14.8 %copy-start.11 = (f32[544,256]{1,0:T(8,128)S(1)}, f32[544,256]{1,0:T(8,128)}, u32[]{:S(2)}) copy-start(f32[544,256]{1,0:T(8,128)} %get-tuple-element.110.refs_2_) | copy-start | bytes 1671172
  62.9 14.8 %copy-start.12 = (f32[544,256]{1,0:T(8,128)S(1)}, f32[544,256]{1,0:T(8,128)}, u32[]{:S(2)}) copy-start(f32[544,256]{1,0:T(8,128)} %get-tuple-element.108.refs_0_) | copy-start | bytes 1671172
  62.9 14.8 %copy-start.17 = (f32[512,128]{1,0:T(8,128)S(1)}, f32[512,128]{1,0:T(8,128)}, u32[]{:S(2)}) copy-start(f32[512,128]{1,0:T(8,128)} %get-tuple-element.116.refs_8_) | copy-start | bytes 786436
  63.0 14.8 %copy-start.18 = (f32[512,128]{1,0:T(8,128)S(1)}, f32[512,128]{1,0:T(8,128)}, u32[]{:S(2)}) copy-start(f32[512,128]{1,0:T(8,128)} %get-tuple-element.115.refs_7_) | copy-start | bytes 786436
  67.9 15.1 %collective-permute-start.10 = (f32[568,128]{1,0:T(8,128)S(1)}, f32[568,128]{1,0:T(8,128)S(1)}, u32[]{:S(2)}, u32[]{:S(2)}) collective-permute-start(f32[568,128]{1,0:T(8,128)S(1)} %get-tuple-element.118), channel_id=1, source_target_pairs={{0,8},{1,9},{2,10},{3,11},{4,12},{5,13},{6,14},{7,15},{8,0},{9,1},... | collective-permute-start | bytes 872456 | tf_op jit(solution)/shard_map/ppermute | solution.py:665
  71.6 3.5 %collective-permute-start.8 = (f32[8,640]{1,0:T(8,128)S(1)}, f32[8,640]{1,0:T(8,128)S(1)}, u32[]{:S(2)}, u32[]{:S(2)}) collective-permute-start(f32[8,640]{1,0:T(8,128)S(1)} %get-tuple-element.106), channel_id=1, source_target_pairs={{0,1},{1,2},{2,3},{3,4},{4,5},{5,6},{6,7},{7,8},{8,9},{9,10},{10,1... | collective-permute-start | bytes 61448 | tf_op jit(solution)/shard_map/ppermute | solution.py:657
  74.2 3.5 %collective-permute-start.9 = (f32[8,640]{1,0:T(8,128)S(1)}, f32[8,640]{1,0:T(8,128)S(1)}, u32[]{:S(2)}, u32[]{:S(2)}) collective-permute-start(f32[8,640]{1,0:T(8,128)S(1)} %get-tuple-element.107), channel_id=1, source_target_pairs={{0,15},{1,0},{2,1},{3,2},{4,3},{5,4},{6,5},{7,6},{8,7},{9,8},{10,9... | collective-permute-start | bytes 61448 | tf_op jit(solution)/shard_map/ppermute | solution.py:657
  83.1 11.3 %copy-start.22 = (f32[568,128]{1,0:T(8,128)}, f32[568,128]{1,0:T(8,128)S(1)}, u32[]{:S(2)}) copy-start(f32[568,128]{1,0:T(8,128)S(1)} %collective-permute-done.10.part) | copy-start | bytes 872452
  83.1 31.2 %all-to-all-start.1 = ((f32[128,16,128]{2,1,0:T(8,128)}), f32[128,16,128]{2,1,0:T(8,128)S(1)}, u32[]{:S(2)}, u32[]{:S(2)}) async-start(f32[128,16,128]{2,1,0:T(8,128)} %bitcast.10), calls=%async_computation.1 | async-start | bytes 2097152 | tf_op jit(solution)/shard_map/all_to_all | solution.py:832
  99.3 14.9 %collective-permute-start.11 = (f32[512,128]{1,0:T(8,128)}, f32[512,128]{1,0:T(8,128)S(1)}, u32[]{:S(2)}, u32[]{:S(2)}) collective-permute-start(f32[512,128]{1,0:T(8,128)} %get-tuple-element.140), channel_id=1, source_target_pairs={{0,8},{1,9},{2,10},{3,11},{4,12},{5,13},{6,14},{7,15},{8,0},{9,1},... | collective-permute-start | bytes 786440 | tf_op jit(solution)/shard_map/ppermute | solution.py:665
  102.2 12.0 %copy-start.16 = (f32[512,128]{1,0:T(8,128)S(1)}, f32[512,128]{1,0:T(8,128)}, u32[]{:S(2)}) copy-start(f32[512,128]{1,0:T(8,128)} %get-tuple-element.141.weight) | copy-start | bytes 786436
  (8 other events, 28.8 us)

commit v7 on v6

--- a/solution.py
+++ b/solution.py
@@ -28,7 +28,7 @@
 PAD = 16
 Q = 4
 WIDE = 88
-STEP = 64
+STEP = 128
 ROWS_MSG = CAP * 8 + 1
 
 
@@ -120,7 +120,7 @@
     slots[...] = jnp.full(slots.shape, 64, jnp.int32)
     lane = lanes(1)
 
-    @pl.loop(0, blocks_ref.shape[0], unroll=4)
+    @pl.loop(0, blocks_ref.shape[0], unroll=8)
     def _(k):
         owner = owner_ref[k]
         rank = count_ref[owner]
@@ -146,7 +146,7 @@
     leaving = copies.start((top_ref, top_hbm))
     groups = devices // 8 // 4
     for part in range(4):
-        pl.loop(part * groups, (part + 1) * groups)(assemble)
+        pl.loop(part * groups, (part + 1) * groups, unroll=2)(assemble)
         n = groups * 8 * ROWS_MSG
         a = pl.ds(part * n, n)
         leaving += copies.start((out_ref.at[a, :], out_hbm.at[a, :]))
@@ -324,6 +324,14 @@
             nb = nb + viae[l - 1][pl.ds(s, n), :] * d[l - 1][pl.ds(s, n), :]
         return inv[l][pl.ds(s, n), :] * nb
 
+    def upper(i):
+        a, o = pl.ds(pl.multiple_of(i + PAD, 8), STEP), pl.ds(i, STEP)
+        for l in range(1, layers):
+            vd0[l - 1, o, :] = ev[l][a, main] + d0[l][a, main]
+
+    each_chunk(0, rows, upper, STEP)
+    leaving += give(vd0)
+
     def first(s):
         a = pl.ds(s, WIDE)
         r = pl.ds(pl.multiple_of(s - H, 8), WIDE)
@@ -372,11 +380,9 @@
         z = z20[a, main] - d + nb
         d20[o, :] = d
         sb0[o, :] = ev[0][a, main] + d00[a, main] + d10[a, main] + (1.0 + A3) * d + B3 * z
-        for l in range(1, layers):
-            vd0[l - 1, o, :] = ev[l][a, main] + d0[l][a, main]
 
     each_chunk(PAD, rows, third, STEP)
-    leaving += give(d20, sb0, vd0)
+    leaving += give(d20, sb0)
     wait(leaving)
 
 
@@ -524,9 +530,10 @@
 
 
 def map_kernel(arrived, out, first, last, labels, vec, lab, a0, a1, a2, a3, sem):
-    devices = vec.shape[0]
+    devices = vec.shape[1]
     rows = out.shape[0]
-    vec[...] = arrived[pl.ds(CAP * 8, devices, stride=ROWS_MSG), :].astype(jnp.int32)
+    slots = arrived[pl.ds(CAP * 8, devices, stride=ROWS_MSG), :]
+    vec[...] = slots.T[0:8].astype(jnp.int32)
     copy = pltpu.make_async_copy(vec, lab, sem)
     copy.start()
     parts = (a0, a1, a2, a3)
@@ -534,13 +541,13 @@
         acc[...] = jnp.zeros_like(acc)
     copy.wait()
 
-    @pl.loop(0, devices // 8)
+    @pl.loop(0, devices // 8, unroll=4)
     def _(g):
         n = ROWS_MSG * 8
         data = arrived[pl.ds(pl.multiple_of(g * n, 8), n), :]
         for j in range(8):
             for r in range(CAP):
-                slot = lab[g * 8 + j, r]
+                slot = lab[r, g * 8 + j]
                 labels[(g * 8 + j) * CAP + r] = slot
                 a = pl.ds(pl.multiple_of(slot * 8, 8), 8)
                 acc = parts[(j * CAP + r) % 4]
@@ -643,7 +650,7 @@
 def last_kernel(dest, back, field, part, weight, out, top):
     top[0] = field[0] + B3 * weight[...] * part[...]
 
-    @pl.loop(0, out.shape[0], unroll=8)
+    @pl.loop(0, out.shape[0], unroll=16)
     def _(k):
         out[k] = back[pl.ds(pl.multiple_of(dest[k] * 8, 8), 8), :]
 
@@ -772,8 +779,8 @@
         [tile, shape(8, W), shape(8, W), jax.ShapeDtypeStruct((devices * CAP,), jnp.int32)],
         [arrived],
         scratch=[
-            pltpu.VMEM((devices, W), jnp.int32),
-            pltpu.SMEM((devices, W), jnp.int32),
+            pltpu.VMEM((8, devices), jnp.int32),
+            pltpu.SMEM((8, devices), jnp.int32),
             *[buffer(rows + 8, W)] * 4,
             pltpu.SemaphoreType.DMA,
         ],

time: 117 us -> 116 us (level)
  Pallas kernels: 50.7 us -> 48.5 us
    pallas_call x9, Pallas kernels: 47 us -> 44.9 us  [call(): pl.pallas_call(kernel, out_shape=outs if many else outs[0], in_specs=in_s...]
  transfers between devices with their start and end apart: 14 -> 14, of which waited for: 6 -> 7; matrix products, arithmetic and copies ran while one was open for 0% -> 0% of each run, Pallas kernels for 40% -> 39%
where the time goes in v7:
time: 116 us; the launch traced here: 115 us
  starting transfers between devices  48.6 us (42%)
  Pallas kernels  48.5 us (42%)
  waiting for transfers between devices  14.9 us (13%)
  local copies, waits for them, and re-layouts  1.62 us (1%)
    pallas_call x9, Pallas kernels, call(): pl.pallas_call(kernel, out_shape=outs if many else outs[0], in_specs=in_s...  44.9 us
    ppermute x8, starting transfers between devices, shift(): return lax.ppermute(x, axis, ring(axis, step))  14.4 us
    ppermute x4, starting transfers between devices, facing(): return lax.ppermute(x, ALL, pairs)  12.1 us
    all_to_all x1, starting transfers between devices, on_device(): back = lax.all_to_all(picked, ALL, 0, 0, tiled=True)  11.3 us
    all_to_all x1, starting transfers between devices, on_device(): lax.all_to_all(outgoing.reshape(devices, ROWS_MSG, 1, W), ALL, 0, 0, tile...  10.8 us
    ppermute x8, waiting for transfers between devices, shift(): return lax.ppermute(x, axis, ring(axis, step))  9.68 us
    ppermute x4, waiting for transfers between devices, facing(): return lax.ppermute(x, ALL, pairs)  3.57 us
  transfers between devices with their start and end apart: 14, of which 7 were waited for; matrix products, arithmetic and copies ran while one was open for 0% of the time, Pallas kernels for 39%

profile of v7, /device:TPU:1, one launch (start us, length us, event | category | flops | bytes accessed | tf_op | source)
XLA Modules:
  0.0 115.2 jit_solution(9638564413012844929)
XLA Ops:
  0.7 1.6 %pack_x_kernel.1 = (f32[20,8,128]{2,1,0:T(8,128)}, f32[20,8,128]{2,1,0:T(8,128)}) custom-call(f32[4,512,128]{2,1,0:T(8,128)} %refs_1_.3, f32[4,512,128]{2,1,0:T(8,128)} %refs_2_.3, f32[4,512,128]{2,1,0:T(8,128)} %refs_3_.3, f32[4,512,128]{2,1,0:T(8,128)} %refs_4_.3, f32[3,512,128]{2,1,0:T(8,128)} %refs_5_.3, s32[512,128]{1,0:T(8,128)} %refs_6_.3, ...), custom_call_target="tpu_custom_call" | custom-call | flops 1 | bytes 1000000 | tf_op jit(solution)/shard_map/pack_x_kernel/pallas_call | solution.py:722
  2.3 2.1 %collective-permute-start = (f32[20,8,128]{2,1,0:T(8,128)}, f32[20,8,128]{2,1,0:T(8,128)S(1)}, u32[]{:S(2)}, u32[]{:S(2)}) collective-permute-start(f32[20,8,128]{2,1,0:T(8,128)} %get-tuple-element.74), channel_id=1, source_target_pairs={{0,16},{16,32},{32,48},{48,64},{64,80},{80,96},{96,112},{112,0},{1... | collective-permute-start | bytes 245768 | tf_op jit(solution)/shard_map/ppermute | solution.py:664
  4.5 3.6 %collective-permute-start.1 = (f32[20,8,128]{2,1,0:T(8,128)}, f32[20,8,128]{2,1,0:T(8,128)S(1)}, u32[]{:S(2)}, u32[]{:S(2)}) collective-permute-start(f32[20,8,128]{2,1,0:T(8,128)} %get-tuple-element.75), channel_id=1, source_target_pairs={{0,112},{16,0},{32,16},{48,32},{64,48},{80,64},{96,80},{112,96},{1... | collective-permute-start | bytes 245768 | tf_op jit(solution)/shard_map/ppermute | solution.py:664
  8.0 3.2 %send_kernel.1 = (f32[2176,128]{1,0:T(8,128)}, s32[128]{0:T(128)S(1)}, f32[536,128]{1,0:T(8,128)}) custom-call(s32[128]{0:T(128)S(1)} %bitcast.9, s32[128]{0:T(128)S(1)} %copy-done.20, f32[128,8,128]{2,1,0:T(8,128)S(1)} %copy-done.13, f32[4,512,128]{2,1,0:T(8,128)} %refs_1_.3), custom_call_target="tpu_custom_call" | custom-call | flops 1000000 | bytes 1000000 | tf_op jit(solution)/shard_map/send_kernel/pallas_call | solution.py:47
  11.3 2.5 %collective-permute-start.4 = (f32[536,128]{1,0:T(8,128)}, f32[536,128]{1,0:T(8,128)S(1)}, u32[]{:S(2)}, u32[]{:S(2)}) collective-permute-start(f32[536,128]{1,0:T(8,128)} %get-tuple-element.83), channel_id=1, source_target_pairs={{0,8},{1,9},{2,10},{3,11},{4,12},{5,13},{6,14},{7,15},{8,0},{9,1},... | collective-permute-start | bytes 823304 | tf_op jit(solution)/shard_map/ppermute | solution.py:672
  13.9 1.7 %pack_y_kernel.1 = (f32[528,128]{1,0:T(8,128)S(1)}, f32[528,128]{1,0:T(8,128)S(1)}) custom-call(f32[4,512,128]{2,1,0:T(8,128)S(1)} %copy-done, f32[4,512,128]{2,1,0:T(8,128)S(1)} %copy-done.1, f32[4,512,128]{2,1,0:T(8,128)S(1)} %copy-done.2, f32[4,512,128]{2,1,0:T(8,128)S(1)} %copy-done.3, f32[3,512,128]{2,1,0:T(8,128)S(1)} %copy-done.4, ...), custom_call_target="tpu_custom_call" | custom-call | flops 1000000 | bytes 1000000 | tf_op jit(solution)/shard_map/pack_y_kernel/pallas_call | solution.py:47
  15.6 2.5 %collective-permute-start.2 = (f32[528,128]{1,0:T(8,128)S(1)}, f32[528,128]{1,0:T(8,128)S(1)}, u32[]{:S(2)}, u32[]{:S(2)}) collective-permute-start(f32[528,128]{1,0:T(8,128)S(1)} %get-tuple-element.81), channel_id=1, source_target_pairs={{0,1},{1,2},{2,3},{3,4},{4,5},{5,6},{6,7},{7,8},{8,9},{9,10},{10,1... | collective-permute-start | bytes 811016 | tf_op jit(solution)/shard_map/ppermute | solution.py:664
  18.1 3.4 %collective-permute-done.2.refs_10_ = f32[528,128]{1,0:T(8,128)S(1)} collective-permute-done((f32[528,128]{1,0:T(8,128)S(1)}, f32[528,128]{1,0:T(8,128)S(1)}, u32[]{:S(2)}, u32[]{:S(2)}) %collective-permute-start.2) | collective-permute-done | bytes 270368 | tf_op jit(solution)/shard_map/ppermute | solution.py:664
  21.5 2.8 %collective-permute-done.3.refs_11_ = f32[528,128]{1,0:T(8,128)S(1)} collective-permute-done((f32[528,128]{1,0:T(8,128)S(1)}, f32[528,128]{1,0:T(8,128)S(1)}, u32[]{:S(2)}, u32[]{:S(2)}) %collective-permute-start.3) | collective-permute-done | bytes 270368 | tf_op jit(solution)/shard_map/ppermute | solution.py:664
  24.3 0.7 copy-done.25
  25.0 10.8 %all-to-all-start = ((f32[128,17,1,128]{3,2,1,0:T(1,128)}), f32[128,17,1,128]{3,2,1,0:T(1,128)S(1)}, u32[]{:S(2)}, u32[]{:S(2)}) async-start(f32[128,17,1,128]{3,2,1,0:T(1,128)} %bitcast.1), calls=%async_computation | async-start | bytes 2228224 | tf_op jit(solution)/shard_map/all_to_all | solution.py:748
  35.8 0.6 pad_add_fusion.refs_0_
  36.4 14.5 %base_kernel.1 = (f32[544,256]{1,0:T(8,128)}, f32[544,256]{1,0:T(8,128)}, f32[544,256]{1,0:T(8,128)}, f32[544,256]{1,0:T(8,128)}, f32[544,256]{1,0:T(8,128)}, /*...) custom-call(s32[4]{0:T(128)} %pad_add_fusion.refs_0_, ...), custom_call_target="tpu_custom_call" | custom-call | flops 20000000 | bytes 20000000 | tf_op jit(solution)/shard_map/base_kernel/pallas_call | solution.py:47
  50.9 3.0 %collective-permute-start.5 = (f32[680,128]{1,0:T(8,128)}, f32[680,128]{1,0:T(8,128)S(1)}, u32[]{:S(2)}, u32[]{:S(2)}) collective-permute-start(f32[680,128]{1,0:T(8,128)} %get-tuple-element.89), channel_id=1, source_target_pairs={{0,8},{1,9},{2,10},{3,11},{4,12},{5,13},{6,14},{7,15},{8,0},{9,1},... | collective-permute-start | bytes 1044488 | tf_op jit(solution)/shard_map/ppermute | solution.py:672
  53.8 1.7 %all-to-all-done = f32[128,17,1,128]{3,2,1,0:T(1,128)S(1)} async-done(((f32[128,17,1,128]{3,2,1,0:T(1,128)}), f32[128,17,1,128]{3,2,1,0:T(1,128)S(1)}, u32[]{:S(2)}, u32[]{:S(2)}) %all-to-all-start) | async-done | bytes 1114144 | tf_op jit(solution)/shard_map/all_to_all | solution.py:748
  55.5 1.8 %map_kernel.1 = (f32[512,128]{1,0:T(8,128)S(1)}, f32[8,128]{1,0:T(8,128)S(1)}, f32[8,128]{1,0:T(8,128)S(1)}, s32[256]{0:T(256)S(1)}) custom-call(f32[2176,128]{1,0:T(8,128)S(1)} %bitcast.7), custom_call_target="tpu_custom_call" | custom-call | flops 1000000 | bytes 1000000 | tf_op jit(solution)/shard_map/map_kernel/pallas_call | solution.py:47
  57.3 0.3 collective-permute-start.6
  57.7 3.3 %collective-permute-start.7 = (f32[8,128]{1,0:T(8,128)S(1)}, f32[8,128]{1,0:T(8,128)S(1)}, u32[]{:S(2)}, u32[]{:S(2)}) collective-permute-start(f32[8,128]{1,0:T(8,128)S(1)} %get-tuple-element.93), channel_id=1, source_target_pairs={{0,112},{16,0},{32,16},{48,32},{64,48},{80,64},{96,80},{112,96},{1... | collective-permute-start | bytes 12296 | tf_op jit(solution)/shard_map/ppermute | solution.py:664
  61.0 0.3 collective-permute-done.5.part
  61.3 0.7 copy-done.21
  62.1 4.8 %first_top_kernel.1 = (f32[544,256]{1,0:T(8,128)}, f32[544,256]{1,0:T(8,128)}, f32[544,256]{1,0:T(8,128)}, f32[568,128]{1,0:T(8,128)S(1)}) custom-call(f32[680,128]{1,0:T(8,128)} %copy-done.21, f32[544,256]{1,0:T(8,128)} %get-tuple-element.97.refs_0_, f32[544,256]{1,0:T(8,128)} %get-tuple-element.98.refs_1_, f32[544,256]{1,0:T(8,128)} %get-tuple-element.99.refs_2_, ...), custom_call_target="tpu_custom_call" | custom-call | flops 1000000 | bytes 1000000 | tf_op jit(solution)/shard_map/first_top_kernel/pallas_call | solution.py:47
  67.1 3.7 %collective-permute-start.10 = (f32[568,128]{1,0:T(8,128)S(1)}, f32[568,128]{1,0:T(8,128)S(1)}, u32[]{:S(2)}, u32[]{:S(2)}) collective-permute-start(f32[568,128]{1,0:T(8,128)S(1)} %get-tuple-element.118), channel_id=1, source_target_pairs={{0,8},{1,9},{2,10},{3,11},{4,12},{5,13},{6,14},{7,15},{8,0},{9,1},... | collective-permute-start | bytes 872456 | tf_op jit(solution)/shard_map/ppermute | solution.py:672
  70.8 2.6 %collective-permute-start.8 = (f32[8,640]{1,0:T(8,128)S(1)}, f32[8,640]{1,0:T(8,128)S(1)}, u32[]{:S(2)}, u32[]{:S(2)}) collective-permute-start(f32[8,640]{1,0:T(8,128)S(1)} %get-tuple-element.106), channel_id=1, source_target_pairs={{0,1},{1,2},{2,3},{3,4},{4,5},{5,6},{6,7},{7,8},{8,9},{9,10},{10,1... | collective-permute-start | bytes 61448 | tf_op jit(solution)/shard_map/ppermute | solution.py:664
  73.4 0.9 collective-permute-done.8.f_left
  74.3 2.6 %collective-permute-done.9.f_right = f32[8,640]{1,0:T(8,128)S(1)} collective-permute-done((f32[8,640]{1,0:T(8,128)S(1)}, f32[8,640]{1,0:T(8,128)S(1)}, u32[]{:S(2)}, u32[]{:S(2)}) %collective-permute-start.9) | collective-permute-done | bytes 20512 | tf_op jit(solution)/shard_map/ppermute | solution.py:664
  77.0 5.0 %effect_kernel.1 = (f32[512,128]{1,0:T(8,128)}, f32[2048,128]{1,0:T(8,128)}, f32[544,256]{1,0:T(8,128)}, f32[544,256]{1,0:T(8,128)}, f32[512,128]{1,0:T(8,128)}, /*index=5*/f32[512,128]{1,0:T(8,128)}) custom-call(s32[256]{0:T(256)S(1)} %get-tuple-element.90.labels, f32[512,128]{1,0:T(8,128)S(1)} %get-tuple-element.91.cur, ...), custom_call_target="tpu_custom_call" | custom-call | flops 1000000 | bytes 1000000 | tf_op jit(solution)/shard_map/effect_kernel/pallas_call | solution.py:47
  82.0 11.3 %all-to-all-start.1 = ((f32[128,16,128]{2,1,0:T(8,128)}), f32[128,16,128]{2,1,0:T(8,128)S(1)}, u32[]{:S(2)}, u32[]{:S(2)}) async-start(f32[128,16,128]{2,1,0:T(8,128)} %bitcast.10), calls=%async_computation.1 | async-start | bytes 2097152 | tf_op jit(solution)/shard_map/all_to_all | solution.py:839
  93.3 4.9 %second_top_kernel.1 = (f32[544,256]{1,0:T(8,128)}, f32[544,256]{1,0:T(8,128)}, f32[512,128]{1,0:T(8,128)}, f32[512,128]{1,0:T(8,128)}) custom-call(f32[544,256]{1,0:T(8,128)} %get-tuple-element.123.low.b12, f32[544,256]{1,0:T(8,128)} %get-tuple-element.130.inv_low.inv2, f32[544,256]{1,0:T(8,128)} %get-tuple-element.131.delta, ...), custom_call_target="tpu_custom_call" | custom-call | flops 1000000 | bytes 1000000 | tf_op jit(solution)/shard_map/second_top_kernel/pallas_call | solution.py:47
  98.2 2.9 %collective-permute-start.11 = (f32[512,128]{1,0:T(8,128)}, f32[512,128]{1,0:T(8,128)S(1)}, u32[]{:S(2)}, u32[]{:S(2)}) collective-permute-start(f32[512,128]{1,0:T(8,128)} %get-tuple-element.140), channel_id=1, source_target_pairs={{0,8},{1,9},{2,10},{3,11},{4,12},{5,13},{6,14},{7,15},{8,0},{9,1},... | collective-permute-start | bytes 786440 | tf_op jit(solution)/shard_map/ppermute | solution.py:672
  101.1 8.8 %final_kernel.1.field = f32[4,512,128]{2,1,0:T(8,128)} custom-call(f32[512,128]{1,0:T(8,128)} %get-tuple-element.120.v0, f32[3,512,128]{2,1,0:T(8,128)} %get-tuple-element.121.vd0, f32[544,256]{1,0:T(8,128)} %get-tuple-element.122.d11, f32[544,256]{1,0:T(8,128)} %get-tuple-element.123.low.b12, f32[544,256]{1,0:T(8,128)} %get-tuple-element.124.z12, ...), custom_call_target="tpu_custom_call" | custom-call | flops 10000000 | bytes 10000000 | tf_op jit(solution)/shard_map/final_kernel/pallas_call | solution.py:47
  109.9 3.2 %collective-permute-done.11.part = f32[512,128]{1,0:T(8,128)S(1)} collective-permute-done((f32[512,128]{1,0:T(8,128)}, f32[512,128]{1,0:T(8,128)S(1)}, u32[]{:S(2)}, u32[]{:S(2)}) %collective-permute-start.11) | collective-permute-done | bytes 262176 | tf_op jit(solution)/shard_map/ppermute | solution.py:672
  113.2 2.0 %last_kernel.1 = (f32[128,8,128]{2,1,0:T(8,128)}, f32[4,512,128]{2,1,0:T(8,128)}) custom-call(s32[128]{0:T(128)S(1)} %get-tuple-element.73.dest, f32[2048,128]{1,0:T(8,128)S(1)} %bitcast.8, f32[4,512,128]{2,1,0:T(8,128)} %final_kernel.1.field, f32[512,128]{1,0:T(8,128)S(1)} %collective-permute-done.11.part, ...), custom_call_target="tpu_custom_call", output_to_operand_aliasing={{1}: (2, {})} | custom-call | tf_op jit(solution)/shard_map/last_kernel/pallas_call | solution.py:852
  (60 shorter events, 0.4 us)
Async XLA Ops:
  0.6 7.4 %copy-start.20 = (s32[128]{0:T(128)S(1)}, s32[128]{0:T(128)}, u32[]{:S(2)}) copy-start(s32[128]{0:T(128)} %slot_ref.1) | copy-start | bytes 1540
  0.7 13.2 %copy-start.1 = (f32[4,512,128]{2,1,0:T(8,128)S(1)}, f32[4,512,128]{2,1,0:T(8,128)}, u32[]{:S(2)}) copy-start(f32[4,512,128]{2,1,0:T(8,128)} %refs_2_.3) | copy-start | bytes 3145732
  0.7 13.2 %copy-start.2 = (f32[4,512,128]{2,1,0:T(8,128)S(1)}, f32[4,512,128]{2,1,0:T(8,128)}, u32[]{:S(2)}) copy-start(f32[4,512,128]{2,1,0:T(8,128)} %refs_3_.3) | copy-start | bytes 3145732
  0.7 13.1 %copy-start.3 = (f32[4,512,128]{2,1,0:T(8,128)S(1)}, f32[4,512,128]{2,1,0:T(8,128)}, u32[]{:S(2)}) copy-start(f32[4,512,128]{2,1,0:T(8,128)} %refs_4_.3) | copy-start | bytes 3145732
  0.7 13.1 %copy-start.4 = (f32[3,512,128]{2,1,0:T(8,128)S(1)}, f32[3,512,128]{2,1,0:T(8,128)}, u32[]{:S(2)}) copy-start(f32[3,512,128]{2,1,0:T(8,128)} %refs_5_.3) | copy-start | bytes 2359300
  2.3 11.5 %copy-start = (f32[4,512,128]{2,1,0:T(8,128)S(1)}, f32[4,512,128]{2,1,0:T(8,128)}, u32[]{:S(2)}) copy-start(f32[4,512,128]{2,1,0:T(8,128)} %refs_1_.3) | copy-start | bytes 3145732
  2.3 11.5 %copy-start.5 = (s32[512,128]{1,0:T(8,128)S(1)}, s32[512,128]{1,0:T(8,128)}, u32[]{:S(2)}) copy-start(s32[512,128]{1,0:T(8,128)} %refs_6_.3) | copy-start | bytes 786436
  2.3 8.9 %collective-permute-start = (f32[20,8,128]{2,1,0:T(8,128)}, f32[20,8,128]{2,1,0:T(8,128)S(1)}, u32[]{:S(2)}, u32[]{:S(2)}) collective-permute-start(f32[20,8,128]{2,1,0:T(8,128)} %get-tuple-element.74), channel_id=1, source_target_pairs={{0,16},{16,32},{32,48},{48,64},{64,80},{80,96},{96,112},{112,0},{1... | collective-permute-start | bytes 245768 | tf_op jit(solution)/shard_map/ppermute | solution.py:664
  4.5 6.8 %collective-permute-start.1 = (f32[20,8,128]{2,1,0:T(8,128)}, f32[20,8,128]{2,1,0:T(8,128)S(1)}, u32[]{:S(2)}, u32[]{:S(2)}) collective-permute-start(f32[20,8,128]{2,1,0:T(8,128)} %get-tuple-element.75), channel_id=1, source_target_pairs={{0,112},{16,0},{32,16},{48,32},{64,48},{80,64},{96,80},{112,96},{1... | collective-permute-start | bytes 245768 | tf_op jit(solution)/shard_map/ppermute | solution.py:664
  11.3 13.0 %collective-permute-start.4 = (f32[536,128]{1,0:T(8,128)}, f32[536,128]{1,0:T(8,128)S(1)}, u32[]{:S(2)}, u32[]{:S(2)}) collective-permute-start(f32[536,128]{1,0:T(8,128)} %get-tuple-element.83), channel_id=1, source_target_pairs={{0,8},{1,9},{2,10},{3,11},{4,12},{5,13},{6,14},{7,15},{8,0},{9,1},... | collective-permute-start | bytes 823304 | tf_op jit(solution)/shard_map/ppermute | solution.py:672
  15.6 5.9 %collective-permute-start.2 = (f32[528,128]{1,0:T(8,128)S(1)}, f32[528,128]{1,0:T(8,128)S(1)}, u32[]{:S(2)}, u32[]{:S(2)}) collective-permute-start(f32[528,128]{1,0:T(8,128)S(1)} %get-tuple-element.81), channel_id=1, source_target_pairs={{0,1},{1,2},{2,3},{3,4},{4,5},{5,6},{6,7},{7,8},{8,9},{9,10},{10,1... | collective-permute-start | bytes 811016 | tf_op jit(solution)/shard_map/ppermute | solution.py:664
  18.1 6.2 %collective-permute-start.3 = (f32[528,128]{1,0:T(8,128)S(1)}, f32[528,128]{1,0:T(8,128)S(1)}, u32[]{:S(2)}, u32[]{:S(2)}) collective-permute-start(f32[528,128]{1,0:T(8,128)S(1)} %get-tuple-element.82), channel_id=1, source_target_pairs={{0,15},{1,0},{2,1},{3,2},{4,3},{5,4},{6,5},{7,6},{8,7},{9,8},{10,9... | collective-permute-start | bytes 811016 | tf_op jit(solution)/shard_map/ppermute | solution.py:664
  25.0 30.5 %all-to-all-start = ((f32[128,17,1,128]{3,2,1,0:T(1,128)}), f32[128,17,1,128]{3,2,1,0:T(1,128)S(1)}, u32[]{:S(2)}, u32[]{:S(2)}) async-start(f32[128,17,1,128]{3,2,1,0:T(1,128)} %bitcast.1), calls=%async_computation | async-start | bytes 2228224 | tf_op jit(solution)/shard_map/all_to_all | solution.py:748
  50.9 10.5 %collective-permute-start.5 = (f32[680,128]{1,0:T(8,128)}, f32[680,128]{1,0:T(8,128)S(1)}, u32[]{:S(2)}, u32[]{:S(2)}) collective-permute-start(f32[680,128]{1,0:T(8,128)} %get-tuple-element.89), channel_id=1, source_target_pairs={{0,8},{1,9},{2,10},{3,11},{4,12},{5,13},{6,14},{7,15},{8,0},{9,1},... | collective-permute-start | bytes 1044488 | tf_op jit(solution)/shard_map/ppermute | solution.py:672
  57.3 9.6 %collective-permute-start.6 = (f32[8,128]{1,0:T(8,128)S(1)}, f32[8,128]{1,0:T(8,128)S(1)}, u32[]{:S(2)}, u32[]{:S(2)}) collective-permute-start(f32[8,128]{1,0:T(8,128)S(1)} %get-tuple-element.92), channel_id=1, source_target_pairs={{0,16},{16,32},{32,48},{48,64},{64,80},{80,96},{96,112},{112,0},{1... | collective-permute-start | bytes 12296 | tf_op jit(solution)/shard_map/ppermute | solution.py:664
  57.7 9.2 %collective-permute-start.7 = (f32[8,128]{1,0:T(8,128)S(1)}, f32[8,128]{1,0:T(8,128)S(1)}, u32[]{:S(2)}, u32[]{:S(2)}) collective-permute-start(f32[8,128]{1,0:T(8,128)S(1)} %get-tuple-element.93), channel_id=1, source_target_pairs={{0,112},{16,0},{32,16},{48,32},{64,48},{80,64},{96,80},{112,96},{1... | collective-permute-start | bytes 12296 | tf_op jit(solution)/shard_map/ppermute | solution.py:664
  62.0 14.9 %copy-start.6 = (f32[544,256]{1,0:T(8,128)S(1)}, f32[544,256]{1,0:T(8,128)}, u32[]{:S(2)}) copy-start(f32[544,256]{1,0:T(8,128)} %get-tuple-element.113.refs_5_.gx1) | copy-start | bytes 1671172
  62.1 14.9 %copy-start.7 = (f32[544,256]{1,0:T(8,128)S(1)}, f32[544,256]{1,0:T(8,128)}, u32[]{:S(2)}) copy-start(f32[544,256]{1,0:T(8,128)} %get-tuple-element.114.refs_6_.gy1) | copy-start | bytes 1671172
  62.1 14.9 %copy-start.8 = (f32[544,256]{1,0:T(8,128)S(1)}, f32[544,256]{1,0:T(8,128)}, u32[]{:S(2)}) copy-start(f32[544,256]{1,0:T(8,128)} %get-tuple-element.112.refs_4_.inv1) | copy-start | bytes 1671172
  62.1 14.9 %copy-start.9 = (f32[544,256]{1,0:T(8,128)S(1)}, f32[544,256]{1,0:T(8,128)}, u32[]{:S(2)}) copy-start(f32[544,256]{1,0:T(8,128)} %get-tuple-element.111.refs_3_.via0) | copy-start | bytes 1671172
  62.1 14.9 %copy-start.10 = (f32[544,256]{1,0:T(8,128)S(1)}, f32[544,256]{1,0:T(8,128)}, u32[]{:S(2)}) copy-start(f32[544,256]{1,0:T(8,128)} %get-tuple-element.109.refs_1_) | copy-start | bytes 1671172
  62.1 14.9 %copy-start.11 = (f32[544,256]{1,0:T(8,128)S(1)}, f32[544,256]{1,0:T(8,128)}, u32[]{:S(2)}) copy-start(f32[544,256]{1,0:T(8,128)} %get-tuple-element.110.refs_2_) | copy-start | bytes 1671172
  62.1 14.9 %copy-start.12 = (f32[544,256]{1,0:T(8,128)S(1)}, f32[544,256]{1,0:T(8,128)}, u32[]{:S(2)}) copy-start(f32[544,256]{1,0:T(8,128)} %get-tuple-element.108.refs_0_) | copy-start | bytes 1671172
  62.1 14.9 %copy-start.17 = (f32[512,128]{1,0:T(8,128)S(1)}, f32[512,128]{1,0:T(8,128)}, u32[]{:S(2)}) copy-start(f32[512,128]{1,0:T(8,128)} %get-tuple-element.116.refs_8_) | copy-start | bytes 786436
  62.1 14.9 %copy-start.18 = (f32[512,128]{1,0:T(8,128)S(1)}, f32[512,128]{1,0:T(8,128)}, u32[]{:S(2)}) copy-start(f32[512,128]{1,0:T(8,128)} %get-tuple-element.115.refs_7_) | copy-start | bytes 786436
  67.1 14.9 %collective-permute-start.10 = (f32[568,128]{1,0:T(8,128)S(1)}, f32[568,128]{1,0:T(8,128)S(1)}, u32[]{:S(2)}, u32[]{:S(2)}) collective-permute-start(f32[568,128]{1,0:T(8,128)S(1)} %get-tuple-element.118), channel_id=1, source_target_pairs={{0,8},{1,9},{2,10},{3,11},{4,12},{5,13},{6,14},{7,15},{8,0},{9,1},... | collective-permute-start | bytes 872456 | tf_op jit(solution)/shard_map/ppermute | solution.py:672
  70.8 3.5 %collective-permute-start.8 = (f32[8,640]{1,0:T(8,128)S(1)}, f32[8,640]{1,0:T(8,128)S(1)}, u32[]{:S(2)}, u32[]{:S(2)}) collective-permute-start(f32[8,640]{1,0:T(8,128)S(1)} %get-tuple-element.106), channel_id=1, source_target_pairs={{0,1},{1,2},{2,3},{3,4},{4,5},{5,6},{6,7},{7,8},{8,9},{9,10},{10,1... | collective-permute-start | bytes 61448 | tf_op jit(solution)/shard_map/ppermute | solution.py:664
  73.4 3.5 %collective-permute-start.9 = (f32[8,640]{1,0:T(8,128)S(1)}, f32[8,640]{1,0:T(8,128)S(1)}, u32[]{:S(2)}, u32[]{:S(2)}) collective-permute-start(f32[8,640]{1,0:T(8,128)S(1)} %get-tuple-element.107), channel_id=1, source_target_pairs={{0,15},{1,0},{2,1},{3,2},{4,3},{5,4},{6,5},{7,6},{8,7},{9,8},{10,9... | collective-permute-start | bytes 61448 | tf_op jit(solution)/shard_map/ppermute | solution.py:664
  82.0 11.3 %copy-start.22 = (f32[568,128]{1,0:T(8,128)}, f32[568,128]{1,0:T(8,128)S(1)}, u32[]{:S(2)}) copy-start(f32[568,128]{1,0:T(8,128)S(1)} %collective-permute-done.10.part) | copy-start | bytes 872452
  82.0 31.2 %all-to-all-start.1 = ((f32[128,16,128]{2,1,0:T(8,128)}), f32[128,16,128]{2,1,0:T(8,128)S(1)}, u32[]{:S(2)}, u32[]{:S(2)}) async-start(f32[128,16,128]{2,1,0:T(8,128)} %bitcast.10), calls=%async_computation.1 | async-start | bytes 2097152 | tf_op jit(solution)/shard_map/all_to_all | solution.py:839
  98.2 14.9 %collective-permute-start.11 = (f32[512,128]{1,0:T(8,128)}, f32[512,128]{1,0:T(8,128)S(1)}, u32[]{:S(2)}, u32[]{:S(2)}) collective-permute-start(f32[512,128]{1,0:T(8,128)} %get-tuple-element.140), channel_id=1, source_target_pairs={{0,8},{1,9},{2,10},{3,11},{4,12},{5,13},{6,14},{7,15},{8,0},{9,1},... | collective-permute-start | bytes 786440 | tf_op jit(solution)/shard_map/ppermute | solution.py:672
  101.1 12.0 %copy-start.16 = (f32[512,128]{1,0:T(8,128)S(1)}, f32[512,128]{1,0:T(8,128)}, u32[]{:S(2)}) copy-start(f32[512,128]{1,0:T(8,128)} %get-tuple-element.141.weight) | copy-start | bytes 786436
  (8 other events, 28.4 us)

commit v8 on v7

--- a/solution.py
+++ b/solution.py
@@ -27,6 +27,7 @@
 H = 8
 PAD = 16
 Q = 4
+LONG = 176
 WIDE = 88
 STEP = 128
 ROWS_MSG = CAP * 8 + 1
@@ -440,9 +441,9 @@
         halo(slice(first, first + n), edge, a[:n], b[:n], c[:n])
 
     def body(s):
-        a = pl.ds(s, WIDE)
-        r = pl.ds(pl.multiple_of(s - H, 8), WIDE)
-        nb = weighted(d0, s, WIDE, gx, gy) + via[a, :] * low[a, :] + bond[a, :] * ep[a, :]
+        a = pl.ds(s, LONG)
+        r = pl.ds(pl.multiple_of(s - H, 8), LONG)
+        nb = weighted(d0, s, LONG, gx, gy) + via[a, :] * low[a, :] + bond[a, :] * ep[a, :]
         x = inv[a, :] * nb
         d = A1 * d0[a, :] + B1 * x
         z_out[a, :] = x
@@ -450,7 +451,7 @@
         side[r, :] = d[:, W:]
         msg[r, :] = d[:, :W]
 
-    each_chunk(H, total, body, WIDE)
+    each_chunk(H, total, body, LONG)
     leaving = copies.start((d_out, d_hbm), (z_out, z_hbm), (delta, delta_hbm))
     pack_side(side, msg, total, total)
     wait(leaving)
@@ -590,34 +591,34 @@
         ec[H + W * j : H + W * j + n, edge] = u[...].T[:n]
 
     def zeroth(s):
-        a = pl.ds(s, WIDE)
+        a = pl.ds(s, LONG)
         e0[a, :] = inv0[a, :] * ec[a, :]
 
-    each_chunk(H, total, zeroth, WIDE)
+    each_chunk(H, total, zeroth, LONG)
     def first(s):
-        a = pl.ds(s, WIDE)
+        a = pl.ds(s, LONG)
         here = e0[a, :]
-        z = inv0[a, :] * weighted(e0, s, WIDE, gx0, gy0)
+        z = inv0[a, :] * weighted(e0, s, LONG, gx0, gy0)
         z10[a, :] = z
         e1[a, :] = A1 * here + B1 * z
         z = inv1[a, :] * via0[a, :] * here
         z11[a, :] = z
         e11[a, :] = B1 * z
 
-    each_chunk(H, total, first, WIDE)
+    each_chunk(H, total, first, LONG)
     def second(s):
-        a = pl.ds(s, WIDE)
+        a = pl.ds(s, LONG)
         low, high, between = e1[a, :], e11[a, :], via0[a, :]
-        nb = weighted(e1, s, WIDE, gx0, gy0) + between * high
+        nb = weighted(e1, s, LONG, gx0, gy0) + between * high
         z = z10[a, :] - low + inv0[a, :] * nb
         z20[a, :] = z
         e2[a, :] = A2 * low + B2 * z
-        nb = weighted(e11, s, WIDE, gx1, gy1) + between * low
+        nb = weighted(e11, s, LONG, gx1, gy1) + between * low
         z = z11[a, :] - high + inv1[a, :] * nb
         z11[a, :] = z
         e21[a, :] = A2 * high + B2 * z
 
-    each_chunk(H, total, second, WIDE)
+    each_chunk(H, total, second, LONG)
     copies.start((e11, e11_out), (e21, e21_out))
     def third(i):
         s = pl.multiple_of(i + PAD, 8)

time: 116 us -> 115 us (level)
  no operation moved by 1% of the time
where the time goes in v8:
time: 115 us
  starting transfers between devices  48.6 us (42%)
  Pallas kernels  48.2 us (42%)
  waiting for transfers between devices  14.9 us (13%)
  local copies, waits for them, and re-layouts  1.62 us (1%)
    pallas_call x9, Pallas kernels, call(): pl.pallas_call(kernel, out_shape=outs if many else outs[0], in_specs=in_s...  44.5 us
    ppermute x8, starting transfers between devices, shift(): return lax.ppermute(x, axis, ring(axis, step))  14.4 us
    ppermute x4, starting transfers between devices, facing(): return lax.ppermute(x, ALL, pairs)  12.1 us
    all_to_all x1, starting transfers between devices, on_device(): back = lax.all_to_all(picked, ALL, 0, 0, tiled=True)  11.3 us
    all_to_all x1, starting transfers between devices, on_device(): lax.all_to_all(outgoing.reshape(devices, ROWS_MSG, 1, W), ALL, 0, 0, tile...  10.8 us
    ppermute x8, waiting for transfers between devices, shift(): return lax.ppermute(x, axis, ring(axis, step))  9.68 us
    ppermute x4, waiting for transfers between devices, facing(): return lax.ppermute(x, ALL, pairs)  3.57 us
  transfers between devices with their start and end apart: 14, of which 7 were waited for; matrix products, arithmetic and copies ran while one was open for 0% of the time, Pallas kernels for 39%

profile of v8, /device:TPU:1, one launch (start us, length us, event | category | flops | bytes accessed | tf_op | source)
XLA Modules:
  0.0 114.9 jit_solution(3598335440231632618)
XLA Ops:
  0.7 1.6 %pack_x_kernel.1 = (f32[20,8,128]{2,1,0:T(8,128)}, f32[20,8,128]{2,1,0:T(8,128)}) custom-call(f32[4,512,128]{2,1,0:T(8,128)} %refs_1_.3, f32[4,512,128]{2,1,0:T(8,128)} %refs_2_.3, f32[4,512,128]{2,1,0:T(8,128)} %refs_3_.3, f32[4,512,128]{2,1,0:T(8,128)} %refs_4_.3, f32[3,512,128]{2,1,0:T(8,128)} %refs_5_.3, s32[512,128]{1,0:T(8,128)} %refs_6_.3, ...), custom_call_target="tpu_custom_call" | custom-call | flops 1 | bytes 1000000 | tf_op jit(solution)/shard_map/pack_x_kernel/pallas_call | solution.py:723
  2.3 2.1 %collective-permute-start = (f32[20,8,128]{2,1,0:T(8,128)}, f32[20,8,128]{2,1,0:T(8,128)S(1)}, u32[]{:S(2)}, u32[]{:S(2)}) collective-permute-start(f32[20,8,128]{2,1,0:T(8,128)} %get-tuple-element.74), channel_id=1, source_target_pairs={{0,16},{16,32},{32,48},{48,64},{64,80},{80,96},{96,112},{112,0},{1... | collective-permute-start | bytes 245768 | tf_op jit(solution)/shard_map/ppermute | solution.py:665
  4.5 3.6 %collective-permute-start.1 = (f32[20,8,128]{2,1,0:T(8,128)}, f32[20,8,128]{2,1,0:T(8,128)S(1)}, u32[]{:S(2)}, u32[]{:S(2)}) collective-permute-start(f32[20,8,128]{2,1,0:T(8,128)} %get-tuple-element.75), channel_id=1, source_target_pairs={{0,112},{16,0},{32,16},{48,32},{64,48},{80,64},{96,80},{112,96},{1... | collective-permute-start | bytes 245768 | tf_op jit(solution)/shard_map/ppermute | solution.py:665
  8.0 3.2 %send_kernel.1 = (f32[2176,128]{1,0:T(8,128)}, s32[128]{0:T(128)S(1)}, f32[536,128]{1,0:T(8,128)}) custom-call(s32[128]{0:T(128)S(1)} %bitcast.9, s32[128]{0:T(128)S(1)} %copy-done.20, f32[128,8,128]{2,1,0:T(8,128)S(1)} %copy-done.13, f32[4,512,128]{2,1,0:T(8,128)} %refs_1_.3), custom_call_target="tpu_custom_call" | custom-call | flops 1000000 | bytes 1000000 | tf_op jit(solution)/shard_map/send_kernel/pallas_call | solution.py:48
  11.3 2.5 %collective-permute-start.4 = (f32[536,128]{1,0:T(8,128)}, f32[536,128]{1,0:T(8,128)S(1)}, u32[]{:S(2)}, u32[]{:S(2)}) collective-permute-start(f32[536,128]{1,0:T(8,128)} %get-tuple-element.83), channel_id=1, source_target_pairs={{0,8},{1,9},{2,10},{3,11},{4,12},{5,13},{6,14},{7,15},{8,0},{9,1},... | collective-permute-start | bytes 823304 | tf_op jit(solution)/shard_map/ppermute | solution.py:673
  13.9 1.7 %pack_y_kernel.1 = (f32[528,128]{1,0:T(8,128)S(1)}, f32[528,128]{1,0:T(8,128)S(1)}) custom-call(f32[4,512,128]{2,1,0:T(8,128)S(1)} %copy-done, f32[4,512,128]{2,1,0:T(8,128)S(1)} %copy-done.1, f32[4,512,128]{2,1,0:T(8,128)S(1)} %copy-done.2, f32[4,512,128]{2,1,0:T(8,128)S(1)} %copy-done.3, f32[3,512,128]{2,1,0:T(8,128)S(1)} %copy-done.4, ...), custom_call_target="tpu_custom_call" | custom-call | flops 1000000 | bytes 1000000 | tf_op jit(solution)/shard_map/pack_y_kernel/pallas_call | solution.py:48
  15.6 2.5 %collective-permute-start.2 = (f32[528,128]{1,0:T(8,128)S(1)}, f32[528,128]{1,0:T(8,128)S(1)}, u32[]{:S(2)}, u32[]{:S(2)}) collective-permute-start(f32[528,128]{1,0:T(8,128)S(1)} %get-tuple-element.81), channel_id=1, source_target_pairs={{0,1},{1,2},{2,3},{3,4},{4,5},{5,6},{6,7},{7,8},{8,9},{9,10},{10,1... | collective-permute-start | bytes 811016 | tf_op jit(solution)/shard_map/ppermute | solution.py:665
  18.1 3.4 %collective-permute-done.2.refs_10_ = f32[528,128]{1,0:T(8,128)S(1)} collective-permute-done((f32[528,128]{1,0:T(8,128)S(1)}, f32[528,128]{1,0:T(8,128)S(1)}, u32[]{:S(2)}, u32[]{:S(2)}) %collective-permute-start.2) | collective-permute-done | bytes 270368 | tf_op jit(solution)/shard_map/ppermute | solution.py:665
  21.5 2.8 %collective-permute-done.3.refs_11_ = f32[528,128]{1,0:T(8,128)S(1)} collective-permute-done((f32[528,128]{1,0:T(8,128)S(1)}, f32[528,128]{1,0:T(8,128)S(1)}, u32[]{:S(2)}, u32[]{:S(2)}) %collective-permute-start.3) | collective-permute-done | bytes 270368 | tf_op jit(solution)/shard_map/ppermute | solution.py:665
  24.3 0.7 copy-done.25
  25.0 10.8 %all-to-all-start = ((f32[128,17,1,128]{3,2,1,0:T(1,128)}), f32[128,17,1,128]{3,2,1,0:T(1,128)S(1)}, u32[]{:S(2)}, u32[]{:S(2)}) async-start(f32[128,17,1,128]{3,2,1,0:T(1,128)} %bitcast.1), calls=%async_computation | async-start | bytes 2228224 | tf_op jit(solution)/shard_map/all_to_all | solution.py:749
  35.8 0.6 pad_add_fusion.refs_0_
  36.4 14.5 %base_kernel.1 = (f32[544,256]{1,0:T(8,128)}, f32[544,256]{1,0:T(8,128)}, f32[544,256]{1,0:T(8,128)}, f32[544,256]{1,0:T(8,128)}, f32[544,256]{1,0:T(8,128)}, /*...) custom-call(s32[4]{0:T(128)} %pad_add_fusion.refs_0_, ...), custom_call_target="tpu_custom_call" | custom-call | flops 20000000 | bytes 20000000 | tf_op jit(solution)/shard_map/base_kernel/pallas_call | solution.py:48
  50.9 3.0 %collective-permute-start.5 = (f32[680,128]{1,0:T(8,128)}, f32[680,128]{1,0:T(8,128)S(1)}, u32[]{:S(2)}, u32[]{:S(2)}) collective-permute-start(f32[680,128]{1,0:T(8,128)} %get-tuple-element.89), channel_id=1, source_target_pairs={{0,8},{1,9},{2,10},{3,11},{4,12},{5,13},{6,14},{7,15},{8,0},{9,1},... | collective-permute-start | bytes 1044488 | tf_op jit(solution)/shard_map/ppermute | solution.py:673
  53.8 1.7 %all-to-all-done = f32[128,17,1,128]{3,2,1,0:T(1,128)S(1)} async-done(((f32[128,17,1,128]{3,2,1,0:T(1,128)}), f32[128,17,1,128]{3,2,1,0:T(1,128)S(1)}, u32[]{:S(2)}, u32[]{:S(2)}) %all-to-all-start) | async-done | bytes 1114144 | tf_op jit(solution)/shard_map/all_to_all | solution.py:749
  55.5 1.8 %map_kernel.1 = (f32[512,128]{1,0:T(8,128)S(1)}, f32[8,128]{1,0:T(8,128)S(1)}, f32[8,128]{1,0:T(8,128)S(1)}, s32[256]{0:T(256)S(1)}) custom-call(f32[2176,128]{1,0:T(8,128)S(1)} %bitcast.7), custom_call_target="tpu_custom_call" | custom-call | flops 1000000 | bytes 1000000 | tf_op jit(solution)/shard_map/map_kernel/pallas_call | solution.py:48
  57.3 0.3 collective-permute-start.6
  57.7 3.3 %collective-permute-start.7 = (f32[8,128]{1,0:T(8,128)S(1)}, f32[8,128]{1,0:T(8,128)S(1)}, u32[]{:S(2)}, u32[]{:S(2)}) collective-permute-start(f32[8,128]{1,0:T(8,128)S(1)} %get-tuple-element.93), channel_id=1, source_target_pairs={{0,112},{16,0},{32,16},{48,32},{64,48},{80,64},{96,80},{112,96},{1... | collective-permute-start | bytes 12296 | tf_op jit(solution)/shard_map/ppermute | solution.py:665
  61.0 0.3 collective-permute-done.5.part
  61.3 0.7 copy-done.21
  62.1 4.6 %first_top_kernel.1 = (f32[544,256]{1,0:T(8,128)}, f32[544,256]{1,0:T(8,128)}, f32[544,256]{1,0:T(8,128)}, f32[568,128]{1,0:T(8,128)S(1)}) custom-call(f32[680,128]{1,0:T(8,128)} %copy-done.21, f32[544,256]{1,0:T(8,128)} %get-tuple-element.97.refs_0_, f32[544,256]{1,0:T(8,128)} %get-tuple-element.98.refs_1_, f32[544,256]{1,0:T(8,128)} %get-tuple-element.99.refs_2_, ...), custom_call_target="tpu_custom_call" | custom-call | flops 1000000 | bytes 1000000 | tf_op jit(solution)/shard_map/first_top_kernel/pallas_call | solution.py:48
  66.9 3.7 %collective-permute-start.10 = (f32[568,128]{1,0:T(8,128)S(1)}, f32[568,128]{1,0:T(8,128)S(1)}, u32[]{:S(2)}, u32[]{:S(2)}) collective-permute-start(f32[568,128]{1,0:T(8,128)S(1)} %get-tuple-element.118), channel_id=1, source_target_pairs={{0,8},{1,9},{2,10},{3,11},{4,12},{5,13},{6,14},{7,15},{8,0},{9,1},... | collective-permute-start | bytes 872456 | tf_op jit(solution)/shard_map/ppermute | solution.py:673
  70.6 2.6 %collective-permute-start.8 = (f32[8,640]{1,0:T(8,128)S(1)}, f32[8,640]{1,0:T(8,128)S(1)}, u32[]{:S(2)}, u32[]{:S(2)}) collective-permute-start(f32[8,640]{1,0:T(8,128)S(1)} %get-tuple-element.106), channel_id=1, source_target_pairs={{0,1},{1,2},{2,3},{3,4},{4,5},{5,6},{6,7},{7,8},{8,9},{9,10},{10,1... | collective-permute-start | bytes 61448 | tf_op jit(solution)/shard_map/ppermute | solution.py:665
  73.2 0.9 collective-permute-done.8.f_left
  74.1 2.6 %collective-permute-done.9.f_right = f32[8,640]{1,0:T(8,128)S(1)} collective-permute-done((f32[8,640]{1,0:T(8,128)S(1)}, f32[8,640]{1,0:T(8,128)S(1)}, u32[]{:S(2)}, u32[]{:S(2)}) %collective-permute-start.9) | collective-permute-done | bytes 20512 | tf_op jit(solution)/shard_map/ppermute | solution.py:665
  76.8 4.9 %effect_kernel.1 = (f32[512,128]{1,0:T(8,128)}, f32[2048,128]{1,0:T(8,128)}, f32[544,256]{1,0:T(8,128)}, f32[544,256]{1,0:T(8,128)}, f32[512,128]{1,0:T(8,128)}, /*index=5*/f32[512,128]{1,0:T(8,128)}) custom-call(s32[256]{0:T(256)S(1)} %get-tuple-element.90.labels, f32[512,128]{1,0:T(8,128)S(1)} %get-tuple-element.91.cur, ...), custom_call_target="tpu_custom_call" | custom-call | flops 1000000 | bytes 1000000 | tf_op jit(solution)/shard_map/effect_kernel/pallas_call | solution.py:48
  81.7 11.3 %all-to-all-start.1 = ((f32[128,16,128]{2,1,0:T(8,128)}), f32[128,16,128]{2,1,0:T(8,128)S(1)}, u32[]{:S(2)}, u32[]{:S(2)}) async-start(f32[128,16,128]{2,1,0:T(8,128)} %bitcast.10), calls=%async_computation.1 | async-start | bytes 2097152 | tf_op jit(solution)/shard_map/all_to_all | solution.py:840
  93.0 4.9 %second_top_kernel.1 = (f32[544,256]{1,0:T(8,128)}, f32[544,256]{1,0:T(8,128)}, f32[512,128]{1,0:T(8,128)}, f32[512,128]{1,0:T(8,128)}) custom-call(f32[544,256]{1,0:T(8,128)} %get-tuple-element.123.low.b12, f32[544,256]{1,0:T(8,128)} %get-tuple-element.130.inv_low.inv2, f32[544,256]{1,0:T(8,128)} %get-tuple-element.131.delta, ...), custom_call_target="tpu_custom_call" | custom-call | flops 1000000 | bytes 1000000 | tf_op jit(solution)/shard_map/second_top_kernel/pallas_call | solution.py:48
  97.9 2.9 %collective-permute-start.11 = (f32[512,128]{1,0:T(8,128)}, f32[512,128]{1,0:T(8,128)S(1)}, u32[]{:S(2)}, u32[]{:S(2)}) collective-permute-start(f32[512,128]{1,0:T(8,128)} %get-tuple-element.140), channel_id=1, source_target_pairs={{0,8},{1,9},{2,10},{3,11},{4,12},{5,13},{6,14},{7,15},{8,0},{9,1},... | collective-permute-start | bytes 786440 | tf_op jit(solution)/shard_map/ppermute | solution.py:673
  100.8 8.8 %final_kernel.1.field = f32[4,512,128]{2,1,0:T(8,128)} custom-call(f32[512,128]{1,0:T(8,128)} %get-tuple-element.120.v0, f32[3,512,128]{2,1,0:T(8,128)} %get-tuple-element.121.vd0, f32[544,256]{1,0:T(8,128)} %get-tuple-element.122.d11, f32[544,256]{1,0:T(8,128)} %get-tuple-element.123.low.b12, f32[544,256]{1,0:T(8,128)} %get-tuple-element.124.z12, ...), custom_call_target="tpu_custom_call" | custom-call | flops 10000000 | bytes 10000000 | tf_op jit(solution)/shard_map/final_kernel/pallas_call | solution.py:48
  109.6 3.2 %collective-permute-done.11.part = f32[512,128]{1,0:T(8,128)S(1)} collective-permute-done((f32[512,128]{1,0:T(8,128)}, f32[512,128]{1,0:T(8,128)S(1)}, u32[]{:S(2)}, u32[]{:S(2)}) %collective-permute-start.11) | collective-permute-done | bytes 262176 | tf_op jit(solution)/shard_map/ppermute | solution.py:673
  112.8 2.0 %last_kernel.1 = (f32[128,8,128]{2,1,0:T(8,128)}, f32[4,512,128]{2,1,0:T(8,128)}) custom-call(s32[128]{0:T(128)S(1)} %get-tuple-element.73.dest, f32[2048,128]{1,0:T(8,128)S(1)} %bitcast.8, f32[4,512,128]{2,1,0:T(8,128)} %final_kernel.1.field, f32[512,128]{1,0:T(8,128)S(1)} %collective-permute-done.11.part, ...), custom_call_target="tpu_custom_call", output_to_operand_aliasing={{1}: (2, {})} | custom-call | tf_op jit(solution)/shard_map/last_kernel/pallas_call | solution.py:853
  (60 shorter events, 0.4 us)
Async XLA Ops:
  0.6 7.4 %copy-start.20 = (s32[128]{0:T(128)S(1)}, s32[128]{0:T(128)}, u32[]{:S(2)}) copy-start(s32[128]{0:T(128)} %slot_ref.1) | copy-start | bytes 1540
  0.7 13.2 %copy-start.1 = (f32[4,512,128]{2,1,0:T(8,128)S(1)}, f32[4,512,128]{2,1,0:T(8,128)}, u32[]{:S(2)}) copy-start(f32[4,512,128]{2,1,0:T(8,128)} %refs_2_.3) | copy-start | bytes 3145732
  0.7 13.2 %copy-start.2 = (f32[4,512,128]{2,1,0:T(8,128)S(1)}, f32[4,512,128]{2,1,0:T(8,128)}, u32[]{:S(2)}) copy-start(f32[4,512,128]{2,1,0:T(8,128)} %refs_3_.3) | copy-start | bytes 3145732
  0.7 13.1 %copy-start.3 = (f32[4,512,128]{2,1,0:T(8,128)S(1)}, f32[4,512,128]{2,1,0:T(8,128)}, u32[]{:S(2)}) copy-start(f32[4,512,128]{2,1,0:T(8,128)} %refs_4_.3) | copy-start | bytes 3145732
  0.7 13.1 %copy-start.4 = (f32[3,512,128]{2,1,0:T(8,128)S(1)}, f32[3,512,128]{2,1,0:T(8,128)}, u32[]{:S(2)}) copy-start(f32[3,512,128]{2,1,0:T(8,128)} %refs_5_.3) | copy-start | bytes 2359300
  2.3 11.5 %copy-start = (f32[4,512,128]{2,1,0:T(8,128)S(1)}, f32[4,512,128]{2,1,0:T(8,128)}, u32[]{:S(2)}) copy-start(f32[4,512,128]{2,1,0:T(8,128)} %refs_1_.3) | copy-start | bytes 3145732
  2.3 11.5 %copy-start.5 = (s32[512,128]{1,0:T(8,128)S(1)}, s32[512,128]{1,0:T(8,128)}, u32[]{:S(2)}) copy-start(s32[512,128]{1,0:T(8,128)} %refs_6_.3) | copy-start | bytes 786436
  2.3 8.9 %collective-permute-start = (f32[20,8,128]{2,1,0:T(8,128)}, f32[20,8,128]{2,1,0:T(8,128)S(1)}, u32[]{:S(2)}, u32[]{:S(2)}) collective-permute-start(f32[20,8,128]{2,1,0:T(8,128)} %get-tuple-element.74), channel_id=1, source_target_pairs={{0,16},{16,32},{32,48},{48,64},{64,80},{80,96},{96,112},{112,0},{1... | collective-permute-start | bytes 245768 | tf_op jit(solution)/shard_map/ppermute | solution.py:665
  4.5 6.8 %collective-permute-start.1 = (f32[20,8,128]{2,1,0:T(8,128)}, f32[20,8,128]{2,1,0:T(8,128)S(1)}, u32[]{:S(2)}, u32[]{:S(2)}) collective-permute-start(f32[20,8,128]{2,1,0:T(8,128)} %get-tuple-element.75), channel_id=1, source_target_pairs={{0,112},{16,0},{32,16},{48,32},{64,48},{80,64},{96,80},{112,96},{1... | collective-permute-start | bytes 245768 | tf_op jit(solution)/shard_map/ppermute | solution.py:665
  11.3 13.0 %collective-permute-start.4 = (f32[536,128]{1,0:T(8,128)}, f32[536,128]{1,0:T(8,128)S(1)}, u32[]{:S(2)}, u32[]{:S(2)}) collective-permute-start(f32[536,128]{1,0:T(8,128)} %get-tuple-element.83), channel_id=1, source_target_pairs={{0,8},{1,9},{2,10},{3,11},{4,12},{5,13},{6,14},{7,15},{8,0},{9,1},... | collective-permute-start | bytes 823304 | tf_op jit(solution)/shard_map/ppermute | solution.py:673
  15.6 5.9 %collective-permute-start.2 = (f32[528,128]{1,0:T(8,128)S(1)}, f32[528,128]{1,0:T(8,128)S(1)}, u32[]{:S(2)}, u32[]{:S(2)}) collective-permute-start(f32[528,128]{1,0:T(8,128)S(1)} %get-tuple-element.81), channel_id=1, source_target_pairs={{0,1},{1,2},{2,3},{3,4},{4,5},{5,6},{6,7},{7,8},{8,9},{9,10},{10,1... | collective-permute-start | bytes 811016 | tf_op jit(solution)/shard_map/ppermute | solution.py:665
  18.1 6.2 %collective-permute-start.3 = (f32[528,128]{1,0:T(8,128)S(1)}, f32[528,128]{1,0:T(8,128)S(1)}, u32[]{:S(2)}, u32[]{:S(2)}) collective-permute-start(f32[528,128]{1,0:T(8,128)S(1)} %get-tuple-element.82), channel_id=1, source_target_pairs={{0,15},{1,0},{2,1},{3,2},{4,3},{5,4},{6,5},{7,6},{8,7},{9,8},{10,9... | collective-permute-start | bytes 811016 | tf_op jit(solution)/shard_map/ppermute | solution.py:665
  25.0 30.5 %all-to-all-start = ((f32[128,17,1,128]{3,2,1,0:T(1,128)}), f32[128,17,1,128]{3,2,1,0:T(1,128)S(1)}, u32[]{:S(2)}, u32[]{:S(2)}) async-start(f32[128,17,1,128]{3,2,1,0:T(1,128)} %bitcast.1), calls=%async_computation | async-start | bytes 2228224 | tf_op jit(solution)/shard_map/all_to_all | solution.py:749
  50.9 10.5 %collective-permute-start.5 = (f32[680,128]{1,0:T(8,128)}, f32[680,128]{1,0:T(8,128)S(1)}, u32[]{:S(2)}, u32[]{:S(2)}) collective-permute-start(f32[680,128]{1,0:T(8,128)} %get-tuple-element.89), channel_id=1, source_target_pairs={{0,8},{1,9},{2,10},{3,11},{4,12},{5,13},{6,14},{7,15},{8,0},{9,1},... | collective-permute-start | bytes 1044488 | tf_op jit(solution)/shard_map/ppermute | solution.py:673
  57.3 9.4 %collective-permute-start.6 = (f32[8,128]{1,0:T(8,128)S(1)}, f32[8,128]{1,0:T(8,128)S(1)}, u32[]{:S(2)}, u32[]{:S(2)}) collective-permute-start(f32[8,128]{1,0:T(8,128)S(1)} %get-tuple-element.92), channel_id=1, source_target_pairs={{0,16},{16,32},{32,48},{48,64},{64,80},{80,96},{96,112},{112,0},{1... | collective-permute-start | bytes 12296 | tf_op jit(solution)/shard_map/ppermute | solution.py:665
  57.7 9.1 %collective-permute-start.7 = (f32[8,128]{1,0:T(8,128)S(1)}, f32[8,128]{1,0:T(8,128)S(1)}, u32[]{:S(2)}, u32[]{:S(2)}) collective-permute-start(f32[8,128]{1,0:T(8,128)S(1)} %get-tuple-element.93), channel_id=1, source_target_pairs={{0,112},{16,0},{32,16},{48,32},{64,48},{80,64},{96,80},{112,96},{1... | collective-permute-start | bytes 12296 | tf_op jit(solution)/shard_map/ppermute | solution.py:665
  62.0 14.7 %copy-start.6 = (f32[544,256]{1,0:T(8,128)S(1)}, f32[544,256]{1,0:T(8,128)}, u32[]{:S(2)}) copy-start(f32[544,256]{1,0:T(8,128)} %get-tuple-element.113.refs_5_.gx1) | copy-start | bytes 1671172
  62.1 14.7 %copy-start.7 = (f32[544,256]{1,0:T(8,128)S(1)}, f32[544,256]{1,0:T(8,128)}, u32[]{:S(2)}) copy-start(f32[544,256]{1,0:T(8,128)} %get-tuple-element.114.refs_6_.gy1) | copy-start | bytes 1671172
  62.1 14.7 %copy-start.8 = (f32[544,256]{1,0:T(8,128)S(1)}, f32[544,256]{1,0:T(8,128)}, u32[]{:S(2)}) copy-start(f32[544,256]{1,0:T(8,128)} %get-tuple-element.112.refs_4_.inv1) | copy-start | bytes 1671172
  62.1 14.7 %copy-start.9 = (f32[544,256]{1,0:T(8,128)S(1)}, f32[544,256]{1,0:T(8,128)}, u32[]{:S(2)}) copy-start(f32[544,256]{1,0:T(8,128)} %get-tuple-element.111.refs_3_.via0) | copy-start | bytes 1671172
  62.1 14.7 %copy-start.10 = (f32[544,256]{1,0:T(8,128)S(1)}, f32[544,256]{1,0:T(8,128)}, u32[]{:S(2)}) copy-start(f32[544,256]{1,0:T(8,128)} %get-tuple-element.109.refs_1_) | copy-start | bytes 1671172
  62.1 14.7 %copy-start.11 = (f32[544,256]{1,0:T(8,128)S(1)}, f32[544,256]{1,0:T(8,128)}, u32[]{:S(2)}) copy-start(f32[544,256]{1,0:T(8,128)} %get-tuple-element.110.refs_2_) | copy-start | bytes 1671172
  62.1 14.7 %copy-start.12 = (f32[544,256]{1,0:T(8,128)S(1)}, f32[544,256]{1,0:T(8,128)}, u32[]{:S(2)}) copy-start(f32[544,256]{1,0:T(8,128)} %get-tuple-element.108.refs_0_) | copy-start | bytes 1671172
  62.1 14.7 %copy-start.17 = (f32[512,128]{1,0:T(8,128)S(1)}, f32[512,128]{1,0:T(8,128)}, u32[]{:S(2)}) copy-start(f32[512,128]{1,0:T(8,128)} %get-tuple-element.116.refs_8_) | copy-start | bytes 786436
  62.1 14.7 %copy-start.18 = (f32[512,128]{1,0:T(8,128)S(1)}, f32[512,128]{1,0:T(8,128)}, u32[]{:S(2)}) copy-start(f32[512,128]{1,0:T(8,128)} %get-tuple-element.115.refs_7_) | copy-start | bytes 786436
  66.9 14.8 %collective-permute-start.10 = (f32[568,128]{1,0:T(8,128)S(1)}, f32[568,128]{1,0:T(8,128)S(1)}, u32[]{:S(2)}, u32[]{:S(2)}) collective-permute-start(f32[568,128]{1,0:T(8,128)S(1)} %get-tuple-element.118), channel_id=1, source_target_pairs={{0,8},{1,9},{2,10},{3,11},{4,12},{5,13},{6,14},{7,15},{8,0},{9,1},... | collective-permute-start | bytes 872456 | tf_op jit(solution)/shard_map/ppermute | solution.py:673
  70.6 3.5 %collective-permute-start.8 = (f32[8,640]{1,0:T(8,128)S(1)}, f32[8,640]{1,0:T(8,128)S(1)}, u32[]{:S(2)}, u32[]{:S(2)}) collective-permute-start(f32[8,640]{1,0:T(8,128)S(1)} %get-tuple-element.106), channel_id=1, source_target_pairs={{0,1},{1,2},{2,3},{3,4},{4,5},{5,6},{6,7},{7,8},{8,9},{9,10},{10,1... | collective-permute-start | bytes 61448 | tf_op jit(solution)/shard_map/ppermute | solution.py:665
  73.2 3.5 %collective-permute-start.9 = (f32[8,640]{1,0:T(8,128)S(1)}, f32[8,640]{1,0:T(8,128)S(1)}, u32[]{:S(2)}, u32[]{:S(2)}) collective-permute-start(f32[8,640]{1,0:T(8,128)S(1)} %get-tuple-element.107), channel_id=1, source_target_pairs={{0,15},{1,0},{2,1},{3,2},{4,3},{5,4},{6,5},{7,6},{8,7},{9,8},{10,9... | collective-permute-start | bytes 61448 | tf_op jit(solution)/shard_map/ppermute | solution.py:665
  81.7 11.3 %copy-start.22 = (f32[568,128]{1,0:T(8,128)}, f32[568,128]{1,0:T(8,128)S(1)}, u32[]{:S(2)}) copy-start(f32[568,128]{1,0:T(8,128)S(1)} %collective-permute-done.10.part) | copy-start | bytes 872452
  81.7 31.2 %all-to-all-start.1 = ((f32[128,16,128]{2,1,0:T(8,128)}), f32[128,16,128]{2,1,0:T(8,128)S(1)}, u32[]{:S(2)}, u32[]{:S(2)}) async-start(f32[128,16,128]{2,1,0:T(8,128)} %bitcast.10), calls=%async_computation.1 | async-start | bytes 2097152 | tf_op jit(solution)/shard_map/all_to_all | solution.py:840
  97.9 14.9 %collective-permute-start.11 = (f32[512,128]{1,0:T(8,128)}, f32[512,128]{1,0:T(8,128)S(1)}, u32[]{:S(2)}, u32[]{:S(2)}) collective-permute-start(f32[512,128]{1,0:T(8,128)} %get-tuple-element.140), channel_id=1, source_target_pairs={{0,8},{1,9},{2,10},{3,11},{4,12},{5,13},{6,14},{7,15},{8,0},{9,1},... | collective-permute-start | bytes 786440 | tf_op jit(solution)/shard_map/ppermute | solution.py:673
  100.8 12.0 %copy-start.16 = (f32[512,128]{1,0:T(8,128)S(1)}, f32[512,128]{1,0:T(8,128)}, u32[]{:S(2)}) copy-start(f32[512,128]{1,0:T(8,128)} %get-tuple-element.141.weight) | copy-start | bytes 786436
  (8 other events, 28.4 us)
